TPU v7x, 32 devices: a whole 2x2x4 slice. The times are simulated.
32 devices in a mesh: dp: 4 (over x, core), bank: 8 (over z, y).
Axes of the slice: x: 2, y: 2, z: 4, core: 2. Of those that a mesh axis runs over, the one named last changes fastest.
Arguments:
- feature_map: bfloat16 [16384, 2048], P(('dp', 'bank')), may hold values from -6 to 6
- bank: bfloat16 [4096, 2048], P('bank'), may hold values from -6 to 6
- region_time: int32 [1024], P('dp'), may hold values from 0 to 4095, as said below
- roi_index: int32 [1024, 16], P(('dp', 'bank')), may hold values from 0 to 511, as said below
- roi_weight: bfloat16 [1024, 16], P(('dp', 'bank')), may hold values from 0.029907227 to 0.099609375
- conv_a: bfloat16 [6144, 512], P('bank'), may hold values from -0.078125 to 0.078125
- scale_a: float32 [512], replicated, may hold values from 0.1 to 1.9
- shift_a: float32 [512], replicated, may hold values from -3 to 3
- conv_b: bfloat16 [4608, 512], P('bank'), may hold values from -0.09375 to 0.09375
- scale_b: float32 [512], replicated, may hold values from 0.1 to 1.9
- shift_b: float32 [512], replicated, may hold values from -3 to 3
- conv_c: bfloat16 [512, 2048], P('bank'), may hold values from -0.25 to 0.25
- scale_c: float32 [2048], replicated, may hold values from 0.1 to 1.9
- shift_c: float32 [2048], replicated, may hold values from -3 to 3
- w_reduce: bfloat16 [2048, 512], replicated, may hold values from -0.125 to 0.125
- w_bank: bfloat16 [2048, 512], replicated, may hold values from -0.125 to 0.125
- w_query: bfloat16 [512, 512], replicated, may hold values from -0.25 to 0.25
- w_key: bfloat16 [512, 512], replicated, may hold values from -0.25 to 0.25
- w_value: bfloat16 [512, 512], replicated, may hold values from -0.25 to 0.25
- ln_gain: float32 [512], replicated, may hold values from 0.1 to 1.9
- ln_shift: float32 [512], replicated, may hold values from -3 to 3
- w_out: bfloat16 [512, 512], replicated, may hold values from -0.25 to 0.25
- w_head: bfloat16 [2560, 80], replicated, may hold values from -0.125 to 0.125
- logit_grad: bfloat16 [1024, 80], P('dp'), may hold values from -6 to 6
Outputs:
- logits: bfloat16 [1024, 80], P(('dp', 'bank'))
- map_grad: bfloat16 [16384, 2048], P(('dp', 'bank'))
- bank_grad: bfloat16 [4096, 2048], P('bank')
- conv_a_grad: float32 [6144, 512], P('bank')
- scale_a_grad: float32 [512], P('bank')
- shift_a_grad: float32 [512], P('bank')
- conv_b_grad: float32 [4608, 512], P('bank')
- scale_b_grad: float32 [512], P('bank')
- shift_b_grad: float32 [512], P('bank')
- conv_c_grad: float32 [512, 2048], P('bank')
- scale_c_grad: float32 [2048], P('bank')
- shift_c_grad: float32 [2048], P('bank')
- reduce_weight_grad: float32 [2048, 512], P('bank')
- bank_weight_grad: float32 [2048, 512], P('bank')
- query_weight_grad: float32 [512, 512], P('bank')
- key_weight_grad: float32 [512, 512], P('bank')
- value_weight_grad: float32 [512, 512], P('bank')
- gain_grad: float32 [512], P('bank')
- shift_grad: float32 [512], P('bank')
- out_weight_grad: float32 [512, 512], P('bank')
- head_weight_grad: float32 [2560, 80], P('bank')
Inputs may be any that keep to these rules, and one draw needn't show every extreme that they name: `region_time`: times lean toward the start of the bank; the first three regions of every block of 256 sit at times 4096 // 2, 4095 and 0. `roi_index`: A region's 16 entries are the distinct positions of a 4 x 4 window of rows and columns in one frame of one clip of its device's block of 512 positions, row by row; in every block of 32 regions the first reads the last window of the last frame of the last clip and the second the first window of the first frame of the first clip.
All inputs are finite; a program needn't handle non-finite values.
Results may differ from a plain program's by a relative error of at most 0.028.
Values may be sent and summed in bfloat16 or wider, within the bound.
No kernel may reach another device: no remote copies, remote signals or barrier semaphores. Data moves between devices by JAX's collectives and lax.ppermute only.
A program may use at most 192 MiB of HBM per device.

v0:
```python
import jax
import jax.numpy as jnp
from jax import lax
from jax.sharding import PartitionSpec as P

FRAMES = 4
SIDE = 8


epsilon = 1e-05
masked_score = -1e30
places = [(-1, -1), (-1, 0), (-1, 1), (0, -1), (0, 0), (0, 1), (1, -1), (1, 0), (1, 1)]


def product(left, right):
    return jnp.dot(left, right, preferred_element_type=jnp.float32)


def inner_rows(left, right):
    return lax.dot_general(
        left, right, (((0,), (0,)), ((), ())), preferred_element_type=jnp.float32
    )


def outer_cols(left, right):
    return lax.dot_general(
        left, right, (((1,), (1,)), ((), ())), preferred_element_type=jnp.float32
    )


def rows_of(left, right, first_col, col_count):
    return inner_rows(lax.dynamic_slice_in_dim(left, first_col, col_count, 1), right)


def shifted(field, axis, step):
    if step == 0:
        return field
    length = field.shape[axis]
    widths = [(0, 0)] * field.ndim
    if step > 0:
        widths[axis] = (0, step)
        return lax.slice_in_dim(jnp.pad(field, widths), step, step + length, axis=axis)
    widths[axis] = (-step, 0)
    return lax.slice_in_dim(jnp.pad(field, widths), 0, length, axis=axis)


def frame_stack(field):
    return jnp.concatenate([shifted(field, 1, offset - 1) for offset in range(3)], axis=-1)


def frame_unstack(stacked, width):
    summed = shifted(stacked[..., :width], 1, 1)
    for offset in range(1, 3):
        summed = summed + shifted(
            stacked[..., offset * width : (offset + 1) * width], 1, 1 - offset
        )
    return summed


def space_stack(field):
    return jnp.concatenate(
        [shifted(shifted(field, 2, rise), 3, slide) for rise, slide in places], axis=-1
    )


def space_unstack(stacked, width):
    summed = None
    for number, (rise, slide) in enumerate(places):
        back = shifted(
            shifted(stacked[..., number * width : (number + 1) * width], 3, -slide), 2, -rise
        )
        summed = back if summed is None else summed + back
    return summed


def norm_act(attended, ln_gain, ln_shift):
    row_mean = jnp.mean(attended, axis=1, keepdims=True)
    centred = attended - row_mean
    row_var = jnp.mean(centred * centred, axis=1, keepdims=True)
    normed = centred * lax.rsqrt(row_var + epsilon) * ln_gain + ln_shift
    return jax.nn.gelu(normed)


def gelu_back(linear, upstream):
    unused, pullback = jax.vjp(jax.nn.gelu, linear)
    return pullback(upstream)[0]


def body(
    feature_map,
    bank,
    region_time,
    roi_index,
    roi_weight,
    conv_a,
    scale_a,
    shift_a,
    conv_b,
    scale_b,
    shift_b,
    conv_c,
    scale_c,
    shift_c,
    w_reduce,
    w_bank,
    w_query,
    w_key,
    w_value,
    ln_gain,
    ln_shift,
    w_out,
    w_head,
    logit_grad,
):
    site_count = feature_map.shape[0]
    feature_count = feature_map.shape[1]
    channels = w_query.shape[0]
    keys_here = bank.shape[0]
    own_count = roi_index.shape[0]
    bank_count = lax.axis_size("bank")
    bank_place = lax.axis_index("bank")
    first_row = bank_place * own_count
    score_scale = channels ** (-0.5)
    half_span = keys_here * bank_count // 2
    clip_count = site_count // (FRAMES * SIDE * SIDE)
    layout = (clip_count, FRAMES, SIDE, SIDE)
    full_a, full_b, full_c = (
        lax.all_gather(conv_a, "bank", axis=0, tiled=True),
        lax.all_gather(conv_b, "bank", axis=0, tiled=True),
        lax.all_gather(conv_c, "bank", axis=0, tiled=True),
    )
    stack_a = frame_stack(feature_map.reshape(layout + (feature_count,))).reshape(
        site_count, 3 * feature_count
    )
    pre_a = product(stack_a, full_a)
    lin_a = pre_a * scale_a + shift_a
    act_a = jax.nn.gelu(lin_a).astype(jnp.bfloat16)
    stack_b = space_stack(act_a.reshape(layout + (channels,))).reshape(site_count, 9 * channels)
    pre_b = product(stack_b, full_b)
    lin_b = pre_b * scale_b + shift_b
    act_b = jax.nn.gelu(lin_b).astype(jnp.bfloat16)
    pre_c = product(act_b, full_c)
    lin_c = feature_map.astype(jnp.float32) + pre_c * scale_c + shift_c
    out_low = jax.nn.gelu(lin_c).astype(jnp.bfloat16)
    matches = roi_index[:, :, None] == jnp.arange(site_count, dtype=jnp.int32)[None, None, :]
    pooling = jnp.sum(
        jnp.where(matches, roi_weight.astype(jnp.float32)[:, :, None], 0.0), axis=1
    ).astype(jnp.bfloat16)
    pooled = product(pooling, out_low).astype(jnp.bfloat16)
    own_regions = lax.all_gather(pooled, "bank", axis=0, tiled=True)
    own_reduced = product(own_regions, w_reduce)
    own_reduced_low = own_reduced.astype(jnp.bfloat16)
    queries = product(own_reduced_low, w_query).astype(jnp.bfloat16)
    memory = product(bank, w_bank)
    memory_low = memory.astype(jnp.bfloat16)
    keys = product(memory_low, w_key).astype(jnp.bfloat16)
    values = product(memory_low, w_value).astype(jnp.bfloat16)
    positions = bank_place * keys_here + jnp.arange(keys_here, dtype=jnp.int32)
    visible = jnp.abs(region_time[:, None] - positions[None, :]) <= half_span
    scores = jnp.where(visible, outer_cols(queries, keys) * score_scale, masked_score)
    row_top = lax.pmax(jnp.max(scores, axis=1), "bank")
    weights = jnp.exp(scores - row_top[:, None])
    weights_low = weights.astype(jnp.bfloat16)
    local_total = jnp.sum(weights, axis=1)
    local_numer = product(weights_low, values)
    total, numer = (
        lax.psum(local_total.astype(jnp.bfloat16), "bank").astype(jnp.float32),
        lax.psum(local_numer.astype(jnp.bfloat16), "bank").astype(jnp.float32),
    )
    attended = numer / total[:, None]
    hidden, act_pull = jax.vjp(norm_act, attended, ln_gain, ln_shift)
    hidden_low = hidden.astype(jnp.bfloat16)
    merged = own_reduced + product(hidden_low, w_out)
    joined = jnp.concatenate([own_regions, merged.astype(jnp.bfloat16)], axis=1)
    logits = product(joined, w_head)
    joined_grad = outer_cols(logit_grad, w_head)
    direct_grad = joined_grad[:, :feature_count]
    merged_grad = joined_grad[:, feature_count:]
    branch_grad = merged_grad.astype(jnp.bfloat16)
    hidden_grad = outer_cols(branch_grad, w_out)
    attended_grad, gain_full, shift_full = act_pull(hidden_grad)
    numer_grad = (attended_grad / total[:, None]).astype(jnp.bfloat16)
    centre = jnp.sum(attended_grad * attended, axis=1) / total
    numer_grad_all, centre_all = (numer_grad, centre)
    prob_grad = outer_cols(numer_grad_all, values)
    score_grad = (weights * (prob_grad - centre_all[:, None]) * score_scale).astype(jnp.bfloat16)
    query_part = product(score_grad, keys)
    key_part = inner_rows(score_grad, queries)
    value_part = inner_rows(weights_low, numer_grad_all)
    key_sum, value_sum = (
        lax.psum(key_part.astype(jnp.bfloat16), "dp").astype(jnp.float32),
        lax.psum(value_part.astype(jnp.bfloat16), "dp").astype(jnp.float32),
    )
    query_sum = lax.psum(query_part.astype(jnp.bfloat16), "bank")
    reduced_grad = (merged_grad + outer_cols(query_sum, w_query)).astype(jnp.bfloat16)
    regions_full = (direct_grad + outer_cols(reduced_grad, w_reduce)).astype(jnp.bfloat16)
    feature_rows = feature_count // bank_count
    channel_rows = channels // bank_count
    joined_rows = joined.shape[1] // bank_count
    reduce_term = rows_of(own_regions, reduced_grad, bank_place * feature_rows, feature_rows)
    query_term = rows_of(own_reduced_low, query_sum, bank_place * channel_rows, channel_rows)
    gain_term = lax.dynamic_slice_in_dim(gain_full, bank_place * channel_rows, channel_rows, 0)
    shift_term = lax.dynamic_slice_in_dim(shift_full, bank_place * channel_rows, channel_rows, 0)
    out_term = rows_of(hidden_low, branch_grad, bank_place * channel_rows, channel_rows)
    head_term = rows_of(joined, logit_grad, bank_place * joined_rows, joined_rows)
    logits_out = lax.dynamic_slice_in_dim(logits, first_row, own_count, 0).astype(jnp.bfloat16)
    regions_grad = lax.dynamic_slice_in_dim(regions_full, first_row, own_count, 0)
    out_grad = inner_rows(pooling, regions_grad)
    lin_c_grad = gelu_back(lin_c, out_grad)
    pre_c_grad = (lin_c_grad * scale_c).astype(jnp.bfloat16)
    lin_b_grad = gelu_back(lin_b, outer_cols(pre_c_grad, full_c))
    pre_b_grad = (lin_b_grad * scale_b).astype(jnp.bfloat16)
    act_a_grad = space_unstack(
        outer_cols(pre_b_grad, full_b).reshape(layout + (9 * channels,)), channels
    )
    lin_a_grad = gelu_back(lin_a, act_a_grad.reshape(site_count, channels))
    pre_a_grad = (lin_a_grad * scale_a).astype(jnp.bfloat16)
    stack_a_grad = outer_cols(pre_a_grad, full_a).reshape(layout + (3 * feature_count,))
    map_grad = (
        lin_c_grad + frame_unstack(stack_a_grad, feature_count).reshape(site_count, feature_count)
    ).astype(jnp.bfloat16)
    key_low = key_sum.astype(jnp.bfloat16)
    value_low = value_sum.astype(jnp.bfloat16)
    memory_grad = (outer_cols(key_low, w_key) + outer_cols(value_low, w_value)).astype(jnp.bfloat16)
    bank_grad = outer_cols(memory_grad, w_bank).astype(jnp.bfloat16)
    (
        bank_weight_grad,
        key_weight_grad,
        value_weight_grad,
        conv_a_term,
        scale_a_term,
        shift_a_term,
        conv_b_term,
        scale_b_term,
        shift_b_term,
        conv_c_term,
        scale_c_term,
        shift_c_term,
    ) = (
        lax.psum_scatter(
            inner_rows(bank, memory_grad).astype(jnp.bfloat16),
            "bank",
            scatter_dimension=0,
            tiled=True,
        ).astype(jnp.float32),
        lax.psum_scatter(
            inner_rows(memory_low, key_low).astype(jnp.bfloat16),
            "bank",
            scatter_dimension=0,
            tiled=True,
        ).astype(jnp.float32),
        lax.psum_scatter(
            inner_rows(memory_low, value_low).astype(jnp.bfloat16),
            "bank",
            scatter_dimension=0,
            tiled=True,
        ).astype(jnp.float32),
        lax.psum_scatter(
            inner_rows(stack_a, pre_a_grad).astype(jnp.bfloat16),
            "bank",
            scatter_dimension=0,
            tiled=True,
        ).astype(jnp.float32),
        lax.psum_scatter(
            jnp.sum(lin_a_grad * pre_a, axis=0).astype(jnp.bfloat16),
            "bank",
            scatter_dimension=0,
            tiled=True,
        ).astype(jnp.float32),
        lax.psum_scatter(
            jnp.sum(lin_a_grad, axis=0).astype(jnp.bfloat16),
            "bank",
            scatter_dimension=0,
            tiled=True,
        ).astype(jnp.float32),
        lax.psum_scatter(
            inner_rows(stack_b, pre_b_grad).astype(jnp.bfloat16),
            "bank",
            scatter_dimension=0,
            tiled=True,
        ).astype(jnp.float32),
        lax.psum_scatter(
            jnp.sum(lin_b_grad * pre_b, axis=0).astype(jnp.bfloat16),
            "bank",
            scatter_dimension=0,
            tiled=True,
        ).astype(jnp.float32),
        lax.psum_scatter(
            jnp.sum(lin_b_grad, axis=0).astype(jnp.bfloat16),
            "bank",
            scatter_dimension=0,
            tiled=True,
        ).astype(jnp.float32),
        lax.psum_scatter(
            inner_rows(act_b, pre_c_grad).astype(jnp.bfloat16),
            "bank",
            scatter_dimension=0,
            tiled=True,
        ).astype(jnp.float32),
        lax.psum_scatter(
            jnp.sum(lin_c_grad * pre_c, axis=0).astype(jnp.bfloat16),
            "bank",
            scatter_dimension=0,
            tiled=True,
        ).astype(jnp.float32),
        lax.psum_scatter(
            jnp.sum(lin_c_grad, axis=0).astype(jnp.bfloat16),
            "bank",
            scatter_dimension=0,
            tiled=True,
        ).astype(jnp.float32),
    )
    (
        reduce_weight_grad,
        query_weight_grad,
        gain_grad,
        shift_grad,
        out_weight_grad,
        head_weight_grad,
        conv_a_grad,
        scale_a_grad,
        shift_a_grad,
        conv_b_grad,
        scale_b_grad,
        shift_b_grad,
        conv_c_grad,
        scale_c_grad,
        shift_c_grad,
    ) = (
        lax.psum(reduce_term.astype(jnp.bfloat16), "dp").astype(jnp.float32),
        lax.psum(query_term.astype(jnp.bfloat16), "dp").astype(jnp.float32),
        lax.psum(gain_term.astype(jnp.bfloat16), "dp").astype(jnp.float32),
        lax.psum(shift_term.astype(jnp.bfloat16), "dp").astype(jnp.float32),
        lax.psum(out_term.astype(jnp.bfloat16), "dp").astype(jnp.float32),
        lax.psum(head_term.astype(jnp.bfloat16), "dp").astype(jnp.float32),
        lax.psum(conv_a_term.astype(jnp.bfloat16), "dp").astype(jnp.float32),
        lax.psum(scale_a_term.astype(jnp.bfloat16), "dp").astype(jnp.float32),
        lax.psum(shift_a_term.astype(jnp.bfloat16), "dp").astype(jnp.float32),
        lax.psum(conv_b_term.astype(jnp.bfloat16), "dp").astype(jnp.float32),
        lax.psum(scale_b_term.astype(jnp.bfloat16), "dp").astype(jnp.float32),
        lax.psum(shift_b_term.astype(jnp.bfloat16), "dp").astype(jnp.float32),
        lax.psum(conv_c_term.astype(jnp.bfloat16), "dp").astype(jnp.float32),
        lax.psum(scale_c_term.astype(jnp.bfloat16), "dp").astype(jnp.float32),
        lax.psum(shift_c_term.astype(jnp.bfloat16), "dp").astype(jnp.float32),
    )
    return (
        logits_out,
        map_grad,
        bank_grad,
        conv_a_grad,
        scale_a_grad,
        shift_a_grad,
        conv_b_grad,
        scale_b_grad,
        shift_b_grad,
        conv_c_grad,
        scale_c_grad,
        shift_c_grad,
        reduce_weight_grad,
        bank_weight_grad,
        query_weight_grad,
        key_weight_grad,
        value_weight_grad,
        gain_grad,
        shift_grad,
        out_weight_grad,
        head_weight_grad,
    )


def solution(mesh):
    in_specs = (
        P(("dp", "bank"), None),
        P("bank", None),
        P("dp"),
        P(("dp", "bank"), None),
        P(("dp", "bank"), None),
        P("bank", None),
        P(),
        P(),
        P("bank", None),
        P(),
        P(),
        P("bank", None),
        P(),
        P(),
        P(),
        P(),
        P(),
        P(),
        P(),
        P(),
        P(),
        P(),
        P(),
        P("dp", None),
    )
    out_specs = (
        P(("dp", "bank"), None),
        P(("dp", "bank"), None),
        P("bank", None),
        P("bank", None),
        P("bank"),
        P("bank"),
        P("bank", None),
        P("bank"),
        P("bank"),
        P("bank", None),
        P("bank"),
        P("bank"),
        P("bank", None),
        P("bank", None),
        P("bank", None),
        P("bank", None),
        P("bank", None),
        P("bank"),
        P("bank"),
        P("bank", None),
        P("bank", None),
    )
    return jax.shard_map(body, mesh=mesh, in_specs=in_specs, out_specs=out_specs, check_vma=False)
```

profile of v0, /device:TPU:9, one launch (start us, length us, event | category | flops | bytes accessed | tf_op | source)
XLA Modules:
  0.0 1043.6 jit_solution(629452490961496523)
XLA Ops:
  15.9 92.3 %all-gather.5.cloned.1.call-done = bf16[6144,512]{1,0:T(8,128)(2,1)} async-done(((bf16[768,512]{1,0:T(8,128)(2,1)}), bf16[6144,512]{1,0:T(8,128)(2,1)}) %all-gather.5.cloned.1.call-update) | async-done | bytes 6291472 | tf_op jit(solution)/shard_map/all_gather | solution.py:128
  108.2 8.3 multiply_convert_fusion.6
  125.2 63.6 %all-gather.7.cloned.1.call-done = bf16[4608,512]{1,0:T(8,128)(2,1)} async-done(((bf16[576,512]{1,0:T(8,128)(2,1)}), bf16[4608,512]{1,0:T(8,128)(2,1)}) %all-gather.7.cloned.1.call-update) | async-done | bytes 4718608 | tf_op jit(solution)/shard_map/all_gather | solution.py:129
  188.8 5.9 fusion.91
  194.8 44.7 %all-gather.9.cloned.1.call-done = bf16[512,2048]{1,0:T(8,128)(2,1)} async-done(((bf16[64,2048]{1,0:T(8,128)(2,1)}), bf16[512,2048]{1,0:T(8,128)(2,1)}) %all-gather.9.cloned.1.call-update) | async-done | bytes 2097168 | tf_op jit(solution)/shard_map/all_gather | solution.py:130
  252.7 32.7 %all-gather.11.cloned.1.call-done = bf16[256,2048]{1,0:T(8,128)(2,1)} async-done(((bf16[32,2048]{1,0:T(8,128)(2,1)}), bf16[256,2048]{1,0:T(8,128)(2,1)}) %all-gather.11.cloned.1.call-update) | async-done | bytes 1048592 | tf_op jit(solution)/shard_map/all_gather | solution.py:150
  292.3 13.2 %pmax.7 = f32[256]{0:T(256)} all-reduce(f32[256]{0:T(256)} %get-tuple-element.145), channel_id=1, replica_groups=mesh['dp'=4,'bank'=8] {'bank'}, use_global_device_ids=true, to_apply=%region_2.3 | all-reduce | flops 256 | bytes 2048 | tf_op jit(solution)/shard_map/pmax | solution.py:161
  311.9 14.6 %psum.141 = bf16[256]{0:T(256)(128)(2,1)S(1)} all-reduce(bf16[256]{0:T(256)(128)(2,1)S(1)} %fusion.50), channel_id=1, replica_groups=mesh['dp'=4,'bank'=8] {'bank'}, use_global_device_ids=true, to_apply=%region_5.6 | all-reduce | flops 256 | bytes 1024 | tf_op jit(solution)/shard_map/psum | solution.py:167
  326.5 54.9 %all-reduce.37.cloned.1.call-done = bf16[256,512]{1,0:T(8,128)(2,1)} async-done(((bf16[256,512]{1,0:T(8,128)(2,1)}), bf16[256,512]{1,0:T(8,128)(2,1)}) %all-reduce.37.cloned.1.call-update) | async-done | bytes 262160 | tf_op jit(solution)/shard_map/psum | solution.py:168
  390.0 69.9 %all-reduce.39.cloned.1.call-done = bf16[256,512]{1,0:T(8,128)(2,1)} async-done(((bf16[256,512]{1,0:T(8,128)(2,1)}), bf16[256,512]{1,0:T(8,128)(2,1)}) %all-reduce.39.cloned.1.call-update) | async-done | bytes 262160 | tf_op jit(solution)/shard_map/psum | solution.py:194
  463.9 5.3 fusion.7
  474.2 5.8 fusion.83
  480.0 6.6 convolution_convert_fusion.1
  497.5 7.4 convolution_convert_fusion
  514.3 27.4 %reduce-scatter.11.cloned.1.call-done = bf16[64,2048]{1,0:T(8,128)(2,1)} async-done(((bf16[512,2048]{1,0:T(8,128)(2,1)}), bf16[64,2048]{1,0:T(8,128)(2,1)}) %reduce-scatter.11.cloned.1.call-update) | async-done | bytes 262160 | tf_op jit(solution)/shard_map/reduce_scatter | solution.py:294
  541.7 100.2 %reduce-scatter.9.cloned.1.call-done = bf16[576,512]{1,0:T(8,128)(2,1)} async-done(((bf16[4608,512]{1,0:T(8,128)(2,1)}), bf16[576,512]{1,0:T(8,128)(2,1)}) %reduce-scatter.9.cloned.1.call-update) | async-done | bytes 589840 | tf_op jit(solution)/shard_map/reduce_scatter | solution.py:276
  641.9 120.5 %reduce-scatter.7.cloned.1.call-done = bf16[768,512]{1,0:T(8,128)(2,1)} async-done(((bf16[6144,512]{1,0:T(8,128)(2,1)}), bf16[768,512]{1,0:T(8,128)(2,1)}) %reduce-scatter.7.cloned.1.call-update) | async-done | bytes 786448 | tf_op jit(solution)/shard_map/reduce_scatter | solution.py:258
  762.4 72.9 %all-reduce.41.cloned.1.call-done = (bf16[512,512]{1,0:T(8,128)(2,1)}, bf16[512,512]{1,0:T(8,128)(2,1)}, bf16[768,512]{1,0:T(8,128)(2,1)}, bf16[576,512]{1,0:T(8...) async-done(((bf16[512,512]{1,0:T(8,128)(2,1)}, bf16[512,512]{1,0:T(8,128)(2,1)}, ...) | async-done | bytes 3080208 | tf_op jit(solution)/shard_map/psum | solution.py:191
  854.6 5.6 fusion.54
  868.1 6.1 fusion.82
  874.2 27.7 %all-reduce.30 = (bf16[512]{0:T(512)(128)(2,1)}, bf16[512]{0:T(512)(128)(2,1)}, bf16[512]{0:T(512)(128)(2,1)}, bf16[512]{0:T(512)(128)(2,1)}, bf16[2048]{0:T(1024)(128)(2,1)}, /*index=5*/bf16[2048]{0:T(1024)(128)(2,1)}) all-reduce(bf16[512]{0:T(512)(128)(2,1)S(1)} %get-tuple-element.89, ...), channel_id=3, replica_groups=mesh['dp'=4,'bank'=8] {'bank'}, use_global_device_ids=true, to_apply=%region_17.18.clone | all-reduce | flops 6144 | bytes 24576
  906.9 18.7 %all-reduce.31 = (bf16[64]{0:T(256)(128)(2,1)}, bf16[64]{0:T(256)(128)(2,1)}, bf16[64]{0:T(256)(128)(2,1)}, bf16[64]{0:T(256)(128)(2,1)}, bf16[256]{0:T(256)(128...) all-reduce(bf16[64]{0:T(256)(128)(2,1)S(1)} %dynamic-slice.5, ...), channel_id=1, replica_groups=mesh['dp'=4,'bank'=8] {'dp'}, use_global_device_ids=true, to_apply=%region_18.19 | all-reduce | flops 26496 | bytes 105984 | tf_op jit(solution)/shard_map/psum | solution.py:337
  949.9 13.4 %reduce-scatter.17.cloned.1.call-done = bf16[64,512]{1,0:T(8,128)(2,1)} async-done(((bf16[512,512]{1,0:T(8,128)(2,1)}), bf16[64,512]{1,0:T(8,128)(2,1)}) %reduce-scatter.17.cloned.1.call-update) | async-done | bytes 65552 | tf_op jit(solution)/shard_map/reduce_scatter | solution.py:252
  964.9 69.9 %reduce-scatter.13.cloned.1.call-done = bf16[256,512]{0,1:T(8,128)(2,1)} async-done(((bf16[2048,512]{0,1:T(8,128)(2,1)}), bf16[256,512]{0,1:T(8,128)(2,1)}) %reduce-scatter.13.cloned.1.call-update) | async-done | bytes 262160 | tf_op jit(solution)/shard_map/reduce_scatter | solution.py:240
  (232 shorter events, 139.7 us)
Async XLA Ops:
  7.2 240.9 %copy-start = (bf16[512,2048]{1,0:T(8,128)(2,1)S(1)}, bf16[512,2048]{1,0:T(8,128)(2,1)}, u32[]{:S(2)}) copy-start(bf16[512,2048]{1,0:T(8,128)(2,1)} %param.25) | copy-start | bytes 6291460
  7.2 101.0 %copy-start.31 = (f32[512]{0:T(512)S(1)}, f32[512]{0:T(512)}, u32[]{:S(2)}) copy-start(f32[512]{0:T(512)} %param.30) | copy-start | bytes 6148
  7.2 101.0 %copy-start.41 = (f32[512]{0:T(512)S(1)}, f32[512]{0:T(512)}, u32[]{:S(2)}) copy-start(f32[512]{0:T(512)} %param.31) | copy-start | bytes 6148
  7.2 100.9 %all-gather.5.cloned.1.call-start = ((), (), s32[]{:S(2)}) async-start(), calls=%async_computation.6 | async-start | bytes 7077888 | tf_op jit(solution)/shard_map/all_gather | solution.py:128
  8.0 180.8 %all-gather.7.cloned.1.call-start = ((), (), s32[]{:S(2)}) async-start(), calls=%async_computation.7 | async-start | bytes 5308416 | tf_op jit(solution)/shard_map/all_gather | solution.py:129
  8.7 230.8 %all-gather.9.cloned.1.call-start = ((), (), s32[]{:S(2)}) async-start(), calls=%async_computation.8 | async-start | bytes 2359296 | tf_op jit(solution)/shard_map/all_gather | solution.py:130
  9.4 276.0 %all-gather.11.cloned.1.call-start = ((), (), s32[]{:S(2)}) async-start(), calls=%async_computation.9 | async-start | bytes 1179648 | tf_op jit(solution)/shard_map/all_gather | solution.py:150
  15.9 226.8 %copy-start.35 = (bf16[32,512]{1,0:T(8,128)(2,1)}, bf16[32,512]{1,0:T(8,128)(2,1)S(1)}, u32[]{:S(2)}) copy-start(bf16[32,512]{1,0:T(8,128)(2,1)S(1)} %select_reduce_fusion) | copy-start | bytes 98308
  125.2 114.3 %copy-start.33 = (f32[512]{0:T(512)S(1)}, f32[512]{0:T(512)}, u32[]{:S(2)}) copy-start(f32[512]{0:T(512)} %param.33) | copy-start | bytes 6148
  125.2 114.3 %copy-start.48 = (f32[512]{0:T(512)S(1)}, f32[512]{0:T(512)}, u32[]{:S(2)}) copy-start(f32[512]{0:T(512)} %param.34) | copy-start | bytes 6148
  247.4 134.0 %all-reduce.37.cloned.1.call-start = ((), (), s32[]{:S(2)}) async-start(), calls=%async_computation.10 | async-start | bytes 524288 | tf_op jit(solution)/shard_map/psum | solution.py:168
  307.8 152.0 %all-reduce.39.cloned.1.call-start = ((), (), s32[]{:S(2)}) async-start(), calls=%async_computation.11 | async-start | bytes 524288 | tf_op jit(solution)/shard_map/psum | solution.py:194
  310.7 75.5 %copy-start.38 = (f32[512]{0:T(512)S(1)}, f32[512]{0:T(512)}, u32[]{:S(2)}) copy-start(f32[512]{0:T(512)} %param.43) | copy-start | bytes 6148
  310.7 75.5 %copy-start.39 = (f32[512]{0:T(512)S(1)}, f32[512]{0:T(512)}, u32[]{:S(2)}) copy-start(f32[512]{0:T(512)} %param.44) | copy-start | bytes 6148
  389.9 73.9 %copy-start.36 = (bf16[32,512]{1,0:T(8,128)(2,1)S(1)}, bf16[32,512]{1,0:T(8,128)(2,1)}, u32[]{:S(2)}) copy-start(bf16[32,512]{1,0:T(8,128)(2,1)} %copy-done.35) | copy-start | bytes 98308
  389.9 151.8 %reduce-scatter.11.cloned.1.call-start = ((), (), s32[]{:S(2)}) async-start(), calls=%async_computation.14 | async-start | bytes 2359296 | tf_op jit(solution)/shard_map/reduce_scatter | solution.py:294
  474.2 167.7 %reduce-scatter.9.cloned.1.call-start = ((), (), s32[]{:S(2)}) async-start(), calls=%async_computation.13 | async-start | bytes 5308416 | tf_op jit(solution)/shard_map/reduce_scatter | solution.py:276
  486.7 275.7 %reduce-scatter.7.cloned.1.call-start = ((), (), s32[]{:S(2)}) async-start(), calls=%async_computation.12 | async-start | bytes 7077888 | tf_op jit(solution)/shard_map/reduce_scatter | solution.py:258
  504.9 330.4 %all-reduce.41.cloned.1.call-start = ((), (), s32[]{:S(2)}) async-start(), calls=%async_computation.18 | async-start | bytes 6160384 | tf_op jit(solution)/shard_map/psum | solution.py:191
  513.4 327.3 %copy-start.51 = (u32[32]{0:T(128)S(1)}, u32[32]{0:T(128)}, u32[]{:S(2)}) copy-start(u32[32]{0:T(128)} %constant.119) | copy-start | bytes 388
  762.4 186.0 %reduce-scatter.15.cloned.1.call-start = ((), (), s32[]{:S(2)}) async-start(), calls=%async_computation.16 | async-start | bytes 589824 | tf_op jit(solution)/shard_map/reduce_scatter | solution.py:246
  837.8 125.6 %reduce-scatter.17.cloned.1.call-start = ((), (), s32[]{:S(2)}) async-start(), calls=%async_computation.17 | async-start | bytes 589824 | tf_op jit(solution)/shard_map/reduce_scatter | solution.py:252
  840.3 194.4 %reduce-scatter.13.cloned.1.call-start = ((), (), s32[]{:S(2)}) async-start(), calls=%async_computation.15 | async-start | bytes 2359296 | tf_op jit(solution)/shard_map/reduce_scatter | solution.py:240
  868.1 75.1 %copy-start.25 = (bf16[768,512]{1,0:T(8,128)(2,1)S(1)}, bf16[768,512]{1,0:T(8,128)(2,1)}, u32[]{:S(2)}) copy-start(bf16[768,512]{1,0:T(8,128)(2,1)} %get-tuple-element.110) | copy-start | bytes 2359300
  (44 other events, 621.6 us)
Sparse Core Ops, SparseCore 0:
  10.2 97.8 all-gather.4
  110.4 78.3 all-gather.6
  190.9 48.5 all-gather.8
  247.6 37.8 all-gather.10
  307.9 73.4 all-reduce.36
  390.0 69.8 all-reduce.38
  474.3 67.3 reduce-scatter.10
  545.3 96.4 reduce-scatter.8
  645.5 116.8 reduce-scatter.6
  766.8 68.4 all-reduce.40
  839.0 60.1 reduce-scatter.14
  902.4 60.8 reduce-scatter.16
  967.3 67.3 reduce-scatter.12
where the time goes:
time: 1060 us; the launch traced here: 1040 us
  waiting for transfers between devices  764 us (72%)
  matrix products  107 us (10%)
  blocking collectives  74.1 us (7%)
  other arithmetic  41.3 us (4%)
  local copies, waits for them, and re-layouts  39.1 us (4%)
  between operations  16.3 us (2%)
    reduce_scatter x1, waiting for transfers between devices, body(): lax.psum_scatter(inner_rows(stack_a, pre_a_grad).astype(jnp.bfloat16), 'b...  120 us
    reduce_scatter x1, waiting for transfers between devices, body(): lax.psum_scatter(inner_rows(stack_b, pre_b_grad).astype(jnp.bfloat16), 'b...  100 us
    all_gather x1, waiting for transfers between devices, body(): lax.all_gather(conv_a, 'bank', axis=0, tiled=True)  92.3 us
    psum x1, waiting for transfers between devices, body(): lax.psum(key_part.astype(jnp.bfloat16), 'dp').astype(jnp.float32)  72.9 us
    psum x1, waiting for transfers between devices, body(): query_sum = lax.psum(query_part.astype(jnp.bfloat16), 'bank')  69.9 us
    reduce_scatter x1, waiting for transfers between devices, body(): lax.psum_scatter(inner_rows(bank, memory_grad).astype(jnp.bfloat16), 'ban...  69.9 us
    all_gather x1, waiting for transfers between devices, body(): lax.all_gather(conv_b, 'bank', axis=0, tiled=True)  63.6 us
    psum x1, waiting for transfers between devices, body(): lax.psum(local_numer.astype(jnp.bfloat16), 'bank').astype(jnp.float32)  54.9 us
  transfers between devices with their start and end apart: 13, of which 12 were waited for; matrix products, arithmetic and copies ran while one was open for 14% of the time, Pallas kernels for 0%

commit v1 on v0

v1 whole, which is shorter than its diff:
```python
import jax
import jax.numpy as jnp
from jax import lax
from jax.sharding import PartitionSpec as P

FRAMES = 4
SIDE = 8


epsilon = 1e-05
masked_score = -1e30
places = [(-1, -1), (-1, 0), (-1, 1), (0, -1), (0, 0), (0, 1), (1, -1), (1, 0), (1, 1)]


def product(left, right):
    return jnp.dot(left, right, preferred_element_type=jnp.float32)


def inner_rows(left, right):
    return lax.dot_general(
        left, right, (((0,), (0,)), ((), ())), preferred_element_type=jnp.float32
    )


def outer_cols(left, right):
    return lax.dot_general(
        left, right, (((1,), (1,)), ((), ())), preferred_element_type=jnp.float32
    )


def rows_of(left, right, first_col, col_count):
    return inner_rows(lax.dynamic_slice_in_dim(left, first_col, col_count, 1), right)


def shifted(field, axis, step):
    if step == 0:
        return field
    length = field.shape[axis]
    widths = [(0, 0)] * field.ndim
    if step > 0:
        widths[axis] = (0, step)
        return lax.slice_in_dim(jnp.pad(field, widths), step, step + length, axis=axis)
    widths[axis] = (-step, 0)
    return lax.slice_in_dim(jnp.pad(field, widths), 0, length, axis=axis)


def frame_stack(field):
    return jnp.concatenate([shifted(field, 1, offset - 1) for offset in range(3)], axis=-1)


def frame_unstack(stacked, width):
    summed = shifted(stacked[..., :width], 1, 1)
    for offset in range(1, 3):
        summed = summed + shifted(
            stacked[..., offset * width : (offset + 1) * width], 1, 1 - offset
        )
    return summed


def space_stack(field):
    return jnp.concatenate(
        [shifted(shifted(field, 2, rise), 3, slide) for rise, slide in places], axis=-1
    )


def space_unstack(stacked, width):
    summed = None
    for number, (rise, slide) in enumerate(places):
        back = shifted(
            shifted(stacked[..., number * width : (number + 1) * width], 3, -slide), 2, -rise
        )
        summed = back if summed is None else summed + back
    return summed


def norm_act(attended, ln_gain, ln_shift):
    row_mean = jnp.mean(attended, axis=1, keepdims=True)
    centred = attended - row_mean
    row_var = jnp.mean(centred * centred, axis=1, keepdims=True)
    normed = centred * lax.rsqrt(row_var + epsilon) * ln_gain + ln_shift
    return jax.nn.gelu(normed)


def gelu_back(linear, upstream):
    unused, pullback = jax.vjp(jax.nn.gelu, linear)
    return pullback(upstream)[0]


class SubAxis:
    def __init__(self, name, size, stride):
        self.name, self.size, self.stride = name, size, stride

    def place(self):
        return lax.rem(lax.axis_index(self.name) // self.stride, self.size)

    def swap(self, value, step):
        count = lax.axis_size(self.name)
        pairs = [(i, i ^ (step * self.stride)) for i in range(count)]
        return lax.ppermute(value, self.name, pairs)


def sub_axes(dp_count, bank_count):
    inner = 2 if bank_count <= 8 else 8
    return (
        SubAxis("bank", bank_count // inner, inner),
        SubAxis("bank", inner, 1),
        SubAxis("dp", dp_count // 2, 2),
        SubAxis("dp", 2, 1),
    )


def low(value):
    return value.astype(jnp.bfloat16)


def wide(value):
    return value.astype(jnp.float32)


def block_at(value, place, dim):
    return lax.dynamic_index_in_dim(value, place, dim, keepdims=False)


def reduce_over(value, axis, dim):
    me = axis.place()
    parts = [axis.swap(block_at(value, me ^ step, dim), step) for step in range(1, axis.size)]
    total = wide(block_at(value, me, dim))
    for part in parts:
        total = total + wide(part)
    return total


def reduce_all(value, axes):
    outer, inner, across, core = axes
    value = low(reduce_over(value, core, 3))
    half = outer.size // 2
    first = low(reduce_over(value[:half], across, 2))
    second = low(reduce_over(value[half:], inner, 1))
    first = low(reduce_over(first, inner, 1))
    second = low(reduce_over(second, across, 1))
    return reduce_over(jnp.concatenate([first, second], 0), outer, 0)


def sum_everywhere(value, names):
    for name in names:
        step = 1
        while step < lax.axis_size(name):
            pairs = [(i, i ^ step) for i in range(lax.axis_size(name))]
            value = value + lax.ppermute(value, name, pairs)
            step *= 2
    return value


def thirds(column):
    top = low(column)
    rest = column - wide(top)
    middle = low(rest)
    return jnp.concatenate([top, middle, low(rest - wide(middle))], axis=-1)


def from_thirds(columns):
    return jnp.sum(wide(columns), axis=-1, keepdims=True)


def to_owners(value):
    return lax.all_to_all(value, "bank", split_axis=0, concat_axis=0, tiled=True)


def to_group(value):
    count = lax.axis_size("bank")
    return to_owners(jnp.broadcast_to(value[None], (count,) + value.shape))


def body(
    feature_map,
    bank,
    region_time,
    roi_index,
    roi_weight,
    conv_a,
    scale_a,
    shift_a,
    conv_b,
    scale_b,
    shift_b,
    conv_c,
    scale_c,
    shift_c,
    w_reduce,
    w_bank,
    w_query,
    w_key,
    w_value,
    ln_gain,
    ln_shift,
    w_out,
    w_head,
    logit_grad,
):
    site_count = feature_map.shape[0]
    feature_count = feature_map.shape[1]
    channels = w_query.shape[0]
    keys_here = bank.shape[0]
    own_count = roi_index.shape[0]
    bank_count = lax.axis_size("bank")
    bank_place = lax.axis_index("bank")
    dp_count = lax.axis_size("dp")
    dp_place = lax.axis_index("dp")
    axes = sub_axes(dp_count, bank_count)
    first_row = bank_place * own_count
    score_scale = channels ** (-0.5)
    half_span = keys_here * bank_count // 2
    clip_count = site_count // (FRAMES * SIDE * SIDE)
    layout = (clip_count, FRAMES, SIDE, SIDE)
    grid = tuple(axis.size for axis in axes)
    blocks = bank_count * dp_count

    def own_quarter(shard):
        rows = shard.shape[0] // dp_count
        return lax.dynamic_slice_in_dim(shard, dp_place * rows, rows, 0)

    quarter_a, quarter_b, quarter_c = own_quarter(conv_a), own_quarter(conv_b), own_quarter(conv_c)
    rows_a, rows_b, rows_c = quarter_a.shape[0], quarter_b.shape[0], quarter_c.shape[0]
    wide_c = feature_count // channels
    packed = jnp.concatenate([quarter_a, quarter_b, quarter_c.reshape(rows_c * wide_c, channels)], 0)
    gathered = lax.all_gather(packed, ("bank", "dp"), axis=0, tiled=False)
    full_a = gathered[:, :rows_a].reshape(blocks * rows_a, channels)
    full_b = gathered[:, rows_a : rows_a + rows_b].reshape(blocks * rows_b, channels)
    full_c = gathered[:, rows_a + rows_b :].reshape(blocks * rows_c, feature_count)
    memory = product(bank, w_bank)
    memory_low = low(memory)
    keys = low(product(memory_low, w_key))
    values = low(product(memory_low, w_value))
    stack_a = frame_stack(feature_map.reshape(layout + (feature_count,))).reshape(
        site_count, 3 * feature_count
    )
    matches = roi_index[:, :, None] == jnp.arange(site_count, dtype=jnp.int32)[None, None, :]
    pooling = low(jnp.sum(jnp.where(matches, wide(roi_weight)[:, :, None], 0.0), axis=1))
    own_logit_grad = lax.dynamic_slice_in_dim(logit_grad, first_row, own_count, 0)
    joined_grad = outer_cols(own_logit_grad, w_head)
    direct_grad = joined_grad[:, :feature_count]
    merged_grad = joined_grad[:, feature_count:]
    branch_grad = low(merged_grad)
    hidden_grad = outer_cols(branch_grad, w_out)

    pre_a = product(stack_a, full_a)
    lin_a = pre_a * scale_a + shift_a
    act_a = low(jax.nn.gelu(lin_a))
    stack_b = space_stack(act_a.reshape(layout + (channels,))).reshape(site_count, 9 * channels)
    pre_b = product(stack_b, full_b)
    lin_b = pre_b * scale_b + shift_b
    act_b = low(jax.nn.gelu(lin_b))
    pre_c = product(act_b, full_c)
    lin_c = wide(feature_map) + pre_c * scale_c + shift_c
    out_low = low(jax.nn.gelu(lin_c))
    regions = low(product(pooling, out_low))
    reduced = product(regions, w_reduce)
    reduced_low = low(reduced)
    own_queries = low(product(reduced_low, w_query))
    queries = to_group(own_queries).reshape(bank_count * own_count, channels)

    positions = bank_place * keys_here + jnp.arange(keys_here, dtype=jnp.int32)
    visible = jnp.abs(region_time[:, None] - positions[None, :]) <= half_span
    scores = jnp.where(visible, outer_cols(queries, keys) * score_scale, masked_score)
    local_top = jnp.max(scores, axis=1, keepdims=True)
    local_weights = jnp.exp(scores - local_top)
    local_total = jnp.sum(local_weights, axis=1, keepdims=True)
    local_numer = product(low(local_weights), values)
    message = jnp.concatenate(
        [low(local_numer), thirds(local_top), thirds(local_total), jnp.zeros((scores.shape[0], 122), jnp.bfloat16)], 1
    )
    arrived = to_owners(message.reshape(bank_count, own_count, channels + 128))
    tops = from_thirds(arrived[:, :, channels : channels + 3])
    top = jnp.max(tops, axis=0)
    factors = jnp.exp(tops - top[None])
    total = jnp.sum(factors * from_thirds(arrived[:, :, channels + 3 : channels + 6]), axis=0)
    numer = jnp.sum(factors * wide(arrived[:, :, :channels]), axis=0)
    attended = numer / total
    hidden, act_pull = jax.vjp(norm_act, attended, ln_gain, ln_shift)
    hidden_low = low(hidden)
    attended_grad, gain_part, shift_part = act_pull(hidden_grad)
    own_numer_grad = low(attended_grad / total)
    own_centre = jnp.sum(attended_grad * attended, axis=1, keepdims=True) / total
    message = jnp.concatenate(
        [own_numer_grad, thirds(top), thirds(own_centre), jnp.zeros((own_count, 122), jnp.bfloat16)], 1
    )
    arrived = to_group(message).reshape(bank_count * own_count, channels + 128)
    numer_grad = arrived[:, :channels]
    row_top = from_thirds(arrived[:, channels : channels + 3])
    centre = from_thirds(arrived[:, channels + 3 : channels + 6])
    weights = jnp.exp(scores - row_top)
    weights_low = low(weights)
    prob_grad = outer_cols(numer_grad, values)
    score_grad = low(weights * (prob_grad - centre) * score_scale)
    query_part = low(product(score_grad, keys))
    arrived = to_owners(query_part.reshape(bank_count, own_count, channels))
    query_grad = low(jnp.sum(wide(arrived), axis=0))
    key_part = low(inner_rows(score_grad, queries))
    value_part = low(inner_rows(weights_low, numer_grad))
    reduced_grad = low(merged_grad + outer_cols(query_grad, w_query))
    regions_grad = low(direct_grad + outer_cols(reduced_grad, w_reduce))

    merged = reduced + product(hidden_low, w_out)
    joined = jnp.concatenate([regions, low(merged)], axis=1)
    logits_out = low(product(joined, w_head))

    out_grad = inner_rows(pooling, regions_grad)
    lin_c_grad = gelu_back(lin_c, out_grad)
    pre_c_grad = low(lin_c_grad * scale_c)
    part_c = low(inner_rows(act_b, pre_c_grad)).reshape(grid + (rows_c, feature_count))
    lin_b_grad = gelu_back(lin_b, outer_cols(pre_c_grad, full_c))
    pre_b_grad = low(lin_b_grad * scale_b)
    part_b = low(inner_rows(stack_b, pre_b_grad)).reshape(grid + (rows_b, channels))
    act_a_grad = space_unstack(
        outer_cols(pre_b_grad, full_b).reshape(layout + (9 * channels,)), channels
    )
    lin_a_grad = gelu_back(lin_a, act_a_grad.reshape(site_count, channels))
    pre_a_grad = low(lin_a_grad * scale_a)
    part_a = low(inner_rows(stack_a, pre_a_grad)).reshape(grid + (rows_a, channels))
    stack_a_grad = outer_cols(pre_a_grad, full_a).reshape(layout + (3 * feature_count,))
    map_grad = low(
        lin_c_grad + frame_unstack(stack_a_grad, feature_count).reshape(site_count, feature_count)
    )

    region_parts = [
        low(part).reshape(blocks, part.shape[0] // blocks, part.shape[1])
        for part in (
            inner_rows(regions, reduced_grad),
            inner_rows(reduced_low, query_grad),
            inner_rows(hidden_low, branch_grad),
            inner_rows(joined, own_logit_grad),
        )
    ]
    part_r = jnp.concatenate(region_parts[:3], axis=1)
    head_part = region_parts[3]
    rows_r, rows_h, classes = part_r.shape[1], head_part.shape[1], head_part.shape[2]

    def over_dp(block):
        rows, width = block.shape
        return lax.all_gather(low(block), "dp", axis=0, tiled=False)

    done_r = over_dp(reduce_all(part_r.reshape(grid + (rows_r, channels)), axes))
    done_h = over_dp(reduce_all(head_part.reshape(grid + (rows_h, classes)), axes))
    done_c = over_dp(reduce_all(part_c, axes))
    done_b = over_dp(reduce_all(part_b, axes))
    done_a = over_dp(reduce_all(part_a, axes))

    def whole(stacked, first, count):
        picked = wide(stacked[:, first : first + count])
        return picked.reshape(dp_count * count, stacked.shape[2])

    rows_reduce = feature_count // blocks
    rows_query = channels // blocks
    reduce_weight_grad = whole(done_r, 0, rows_reduce)
    query_weight_grad = whole(done_r, rows_reduce, rows_query)
    out_weight_grad = whole(done_r, rows_reduce + rows_query, rows_query)
    head_weight_grad = whole(done_h, 0, rows_h)
    conv_a_grad, conv_b_grad, conv_c_grad = (
        whole(done_a, 0, rows_a), whole(done_b, 0, rows_b), whole(done_c, 0, rows_c)
    )

    key_value = lax.psum(jnp.concatenate([key_part, value_part], 0), "dp")
    key_low, value_low = key_value[:keys_here], key_value[keys_here:]
    memory_grad = low(outer_cols(key_low, w_key) + outer_cols(value_low, w_value))
    bank_grad = low(outer_cols(memory_grad, w_bank))
    width = channels // dp_count

    def columns(value):
        return lax.dynamic_slice_in_dim(value, dp_place * width, width, 1)

    bank_parts = [
        low(part).reshape(bank_count, part.shape[0] // bank_count, width)
        for part in (
            inner_rows(bank, columns(memory_grad)),
            inner_rows(memory_low, columns(key_low)),
            inner_rows(memory_low, columns(value_low)),
        )
    ]
    bank_sum = jnp.sum(wide(to_owners(jnp.concatenate(bank_parts, 1))), axis=0)
    bank_done = wide(lax.all_gather(low(bank_sum), "dp", axis=1, tiled=True))
    bank_rows, channel_rows = feature_count // bank_count, channels // bank_count
    bank_weight_grad = bank_done[:bank_rows]
    key_weight_grad = bank_done[bank_rows : bank_rows + channel_rows]
    value_weight_grad = bank_done[bank_rows + channel_rows :]

    vectors = [
        gain_part,
        shift_part,
        jnp.sum(lin_a_grad * pre_a, axis=0),
        jnp.sum(lin_a_grad, axis=0),
        jnp.sum(lin_b_grad * pre_b, axis=0),
        jnp.sum(lin_b_grad, axis=0),
        jnp.sum(lin_c_grad * pre_c, axis=0),
        jnp.sum(lin_c_grad, axis=0),
    ]
    summed = sum_everywhere(jnp.concatenate(vectors).reshape(-1, channels), ("dp", "bank")).reshape(-1)
    pieces, start = [], 0
    for vector in vectors:
        count = vector.shape[0] // bank_count
        pieces.append(lax.dynamic_slice_in_dim(summed, start + bank_place * count, count, 0))
        start += vector.shape[0]
    gain_grad, shift_grad = pieces[:2]
    scale_a_grad, shift_a_grad, scale_b_grad, shift_b_grad, scale_c_grad, shift_c_grad = pieces[2:]
    return (
        logits_out,
        map_grad,
        bank_grad,
        conv_a_grad,
        scale_a_grad,
        shift_a_grad,
        conv_b_grad,
        scale_b_grad,
        shift_b_grad,
        conv_c_grad,
        scale_c_grad,
        shift_c_grad,
        reduce_weight_grad,
        bank_weight_grad,
        query_weight_grad,
        key_weight_grad,
        value_weight_grad,
        gain_grad,
        shift_grad,
        out_weight_grad,
        head_weight_grad,
    )


def solution(mesh):
    in_specs = (
        P(("dp", "bank"), None),
        P("bank", None),
        P("dp"),
        P(("dp", "bank"), None),
        P(("dp", "bank"), None),
        P("bank", None),
        P(),
        P(),
        P("bank", None),
        P(),
        P(),
        P("bank", None),
        P(),
        P(),
        P(),
        P(),
        P(),
        P(),
        P(),
        P(),
        P(),
        P(),
        P(),
        P("dp", None),
    )
    out_specs = (
        P(("dp", "bank"), None),
        P(("dp", "bank"), None),
        P("bank", None),
        P("bank", None),
        P("bank"),
        P("bank"),
        P("bank", None),
        P("bank"),
        P("bank"),
        P("bank", None),
        P("bank"),
        P("bank"),
        P("bank", None),
        P("bank", None),
        P("bank", None),
        P("bank", None),
        P("bank", None),
        P("bank"),
        P("bank"),
        P("bank", None),
        P("bank", None),
    )
    return jax.shard_map(body, mesh=mesh, in_specs=in_specs, out_specs=out_specs, check_vma=False)
```

time: 1060 us -> 563 us (0.53)
  waiting for transfers between devices: 764 us -> 180 us
  starting transfers between devices: 0.99 us -> 72.2 us
  local copies, waits for them, and re-layouts: 39.1 us -> 97.2 us
  blocking collectives: 74.1 us -> 53 us
  matrix products: 107 us -> 89.8 us
    reduce_scatter x6 -> x0, waiting for transfers between devices: 331 us -> none  [the longest x1 120 us: body(): lax.psum_scatter(inner_rows(stack_a, pre_a_grad).astype(jnp.bfloat16), 'b...]
    psum x3 -> x1, waiting for transfers between devices: 198 us -> 0.01 us  [body(): key_value = lax.psum(jnp.concatenate([key_part, value_part], 0), 'dp')]
    all_gather x4 -> x1, waiting for transfers between devices: 233 us -> 92 us  [body(): gathered = lax.all_gather(packed, ('bank', 'dp'), axis=0, tiled=False)]
    ppermute x0 -> x45, waiting for transfers between devices: none -> 77 us  [the longest x40 76.5 us: swap(): return lax.ppermute(value, self.name, pairs)]
    all_gather x0 -> x6, blocking collectives: none -> 53 us  [the longest x5 44.2 us: over_dp(): return lax.all_gather(low(block), 'dp', axis=0, tiled=False)]
    ppermute x0 -> x45, starting transfers between devices: none -> 46.2 us  [the longest x40 41.3 us: swap(): return lax.ppermute(value, self.name, pairs)]
    psum x2 -> x0, blocking collectives: 33.2 us -> none  [the longest x1 18.7 us: body(): lax.psum(scale_a_term.astype(jnp.bfloat16), 'dp').astype(jnp.float32)]
    unnamed x1 -> x0, blocking collectives: 27.7 us -> none
  transfers between devices with their start and end apart: 13 -> 52, of which waited for: 12 -> 22; matrix products, arithmetic and copies ran while one was open for 14% -> 25% of each run, Pallas kernels for 0% -> 0%
where the time goes in v1:
time: 563 us; the launch traced here: 552 us
  waiting for transfers between devices  180 us (32%)
  local copies, waits for them, and re-layouts  97.2 us (17%)
  matrix products  89.8 us (16%)
  starting transfers between devices  72.2 us (13%)
  blocking collectives  53 us (9%)
  other arithmetic  43.8 us (8%)
  between operations  15.8 us (3%)
    all_gather x1, waiting for transfers between devices, body(): gathered = lax.all_gather(packed, ('bank', 'dp'), axis=0, tiled=False)  92 us
    ppermute x40, waiting for transfers between devices, swap(): return lax.ppermute(value, self.name, pairs)  76.5 us
    all_gather x5, blocking collectives, over_dp(): return lax.all_gather(low(block), 'dp', axis=0, tiled=False)  44.2 us
    ppermute x40, starting transfers between devices, swap(): return lax.ppermute(value, self.name, pairs)  41.3 us
    dot_general x13, matrix products, inner_rows(): lax.dot_general(left, right, (((0,), (0,)), ((), ())), preferred_element_...  37.2 us
    dot_general x13, matrix products, product(): return jnp.dot(left, right, preferred_element_type=jnp.float32)  26.9 us
    dot_general x11, matrix products, outer_cols(): lax.dot_general(left, right, (((1,), (1,)), ((), ())), preferred_element_...  25.8 us
    all_to_all x5, starting transfers between devices, to_owners(): lax.all_to_all(value, 'bank', split_axis=0, concat_axis=0, tiled=True)  25.5 us
  transfers between devices with their start and end apart: 52, of which 22 were waited for; matrix products, arithmetic and copies ran while one was open for 25% of the time, Pallas kernels for 0%

profile of v1, /device:TPU:9, one launch (start us, length us, event | category | flops | bytes accessed | tf_op | source)
XLA Modules:
  0.0 552.3 jit_solution(3182875169645602378)
XLA Ops:
  18.9 92.0 %all-gather.8.cloned.1.call-done = bf16[12800,512]{1,0:T(8,128)(2,1)} async-done(((bf16[400,512]{1,0:T(8,128)(2,1)}), bf16[12800,512]{1,0:T(8,128)(2,1)}) %all-gather.8.cloned.1.call-update) | async-done | bytes 13107216 | tf_op jit(solution)/shard_map/all_gather | solution.py:226
  114.4 7.1 %slice.265 = bf16[32,144,512]{2,1,0:T(8,128)(2,1)} slice(bf16[32,400,512]{2,1,0:T(8,128)(2,1)} %bitcast.339), slice={[0:32], [192:336], [0:512]} | slice | bytes 9437184 | tf_op jit(solution)/shard_map/slice | solution.py:228
  147.2 6.1 %fusion.187 = f32[512,512]{1,0:T(8,128)S(1)} fusion(bf16[512,4608]{1,0:T(8,128)(2,1)} %constant_dynamic-update-slice_fusion, bf16[4608,512]{1,0:T(8,128)(2,1)} %bitcast.349), kind=kOutput, calls=%fused_computation.434 | convolution fusion | flops 2415919104 | bytes 10485760 | tf_op jit(solution)/shard_map/dot_general | solution.py:16
  160.4 4.9 all-to-all-start
  182.9 5.9 %all-to-all-start.1 = ((bf16[8,32,640]{2,1,0:T(8,128)(2,1)}), bf16[8,32,640]{2,1,0:T(8,128)(2,1)}, u32[]{:S(2)}, u32[]{:S(2)}) async-start(bf16[8,32,640]{2,1,0:T(8,128)(2,1)} %concatenate.91), calls=%async_computation.1 | async-start | bytes 655360 | tf_op jit(solution)/shard_map/all_to_all | solution.py:166
  190.9 4.9 all-to-all-done.1
  251.1 8.9 %all-gather.5 = bf16[320,80]{1,0:T(8,128)(2,1)S(1)} all-gather(bf16[80,80]{1,0:T(8,128)(2,1)S(1)} %fusion.132), channel_id=7, replica_groups=mesh['dp'=4,'bank'=8] {'dp'}, dimensions={0}, use_global_device_ids=true | all-gather | bytes 64000 | tf_op jit(solution)/shard_map/all_gather | solution.py:340
  266.1 5.9 %all-to-all-start.3 = ((bf16[8,32,512]{2,1,0:T(8,128)(2,1)}), bf16[8,32,512]{2,1,0:T(8,128)(2,1)}, u32[]{:S(2)}, u32[]{:S(2)}) async-start(bf16[8,32,512]{2,1,0:T(8,128)(2,1)} %bitcast.374), calls=%async_computation.3 | async-start | bytes 524288 | tf_op jit(solution)/shard_map/all_to_all | solution.py:166
  284.0 8.6 %fusion.9 = f32[512,2048]{1,0:T(8,128)} fusion(f32[512,2048]{1,0:T(8,128)} %copy-done.9, bf16[512,2048]{1,0:T(8,128)(2,1)} %param.24, f32[2048]{0:T(1024)S(1)} %copy-done.43, f32[2048]{0:T(1024)S(1)} %copy-done.45, bf16[32,512]{1,0:T(8,128)(2,1)S(1)} %fusion.25, bf16[2048,512]{1,0:T(8,128)(2,1)} %param.38, f32[32,2560]{1,0:T(8,128)} %fusion.144, ...), kind=kOutput, calls=%fused_computation.18 | convolution fusion | flops 158466048 | bytes 12926976 | tf_op jit(solution)/shard_map/dot_general | solution.py:20
  305.4 7.0 %convolution_convert_fusion.1 = bf16[4608,512]{1,0:T(8,128)(2,1)} fusion(bf16[512,4608]{1,0:T(8,128)(2,1)} %constant_dynamic-update-slice_fusion, bf16[512,512]{1,0:T(8,128)(2,1)S(1)} %get-tuple-element.152), kind=kOutput, calls=%fused_computation.1 | convolution fusion | flops 2418278400 | bytes 9961472 | tf_op jit(solution)/shard_map/dot_general | solution.py:20
  320.8 7.2 %convolution_convert_fusion = bf16[6144,512]{1,0:T(8,128)(2,1)} fusion(bf16[512,512]{1,0:T(8,128)(2,1)S(1)} %multiply_convert_fusion.3, bf16[512,2048]{1,0:T(8,128)(2,1)S(1)} %bitcast.360, bf16[512,2048]{1,0:T(8,128)(2,1)S(1)} %copy-done.14, bf16[512,2048]{1,0:T(8,128)(2,1)S(1)} %bitcast.358), kind=kOutput, calls=%fused_computation | convolution fusion | flops 3243245568 | bytes 13107200 | tf_op jit(solution)/shard_map/dot_general | solution.py:20
  328.0 6.7 %fusion.190 = f32[2,4,8,8,6144]{4,3,2,1,0:T(8,128)} fusion(bf16[2,4,8,8,512]{4,3,2,1,0:T(8,128)(2,1)S(1)} %bitcast.377, bf16[6144,512,1,1,1]{1,0,4,3,2:T(8,128)(2,1)S(1)} %bitcast.345), kind=kOutput, calls=%fused_computation.437 | convolution fusion | flops 3221225472 | bytes 19398656 | tf_op jit(solution)/shard_map/dot_general | solution.py:26
  342.3 4.8 fusion.168
  382.0 10.2 %collective-permute-done.24 = bf16[2,2,16,2048]{3,2,0,1:T(8,128)(2,1)S(1)} collective-permute-done((bf16[2,2,16,2048]{3,2,0,1:T(8,128)(2,1)S(1)}, bf16[2,2,16,2048]{3,2,0,1:T(8,128)(2,1)S(1)}, u32[]{:S(2)}, u32[]{:S(2)}) %collective-permute-start.24) | collective-permute-done | bytes 262176 | tf_op jit(solution)/shard_map/ppermute | solution.py:99
  394.6 8.8 %all_gather.49 = bf16[384,512]{0,1:T(8,128)(2,1)S(1)} all-gather(bf16[384,128]{0,1:T(8,128)(2,1)S(1)} %reduce_sum.254), channel_id=1, replica_groups=mesh['dp'=4,'bank'=8] {'dp'}, dimensions={1}, use_global_device_ids=true | all-gather | bytes 491520 | tf_op jit(solution)/shard_map/all_gather | solution.py:380
  416.7 6.6 %collective-permute-done.32 = bf16[2,2,96,512]{3,2,1,0:T(8,128)(2,1)S(1)} collective-permute-done((bf16[2,2,96,512]{3,2,1,0:T(8,128)(2,1)S(1)}, bf16[2,2,96,512]{3,2,1,0:T(8,128)(2,1)S(1)}, u32[]{:S(2)}, u32[]{:S(2)}) %collective-permute-start.32) | collective-permute-done | bytes 393248 | tf_op jit(solution)/shard_map/ppermute | solution.py:99
  433.0 9.0 %all-gather.3 = bf16[64,2048]{1,0:T(8,128)(2,1)S(1)} all-gather(bf16[16,2048]{1,0:T(8,128)(2,1)S(1)} %fusion.102), channel_id=5, replica_groups=mesh['dp'=4,'bank'=8] {'dp'}, dimensions={0}, use_global_device_ids=true | all-gather | bytes 327680 | tf_op jit(solution)/shard_map/all_gather | solution.py:340
  443.0 6.6 %all-gather.4 = bf16[384,512]{1,0:T(8,128)(2,1)S(1)} all-gather(bf16[96,512]{1,0:T(8,128)(2,1)S(1)} %fusion.89), channel_id=6, replica_groups=mesh['dp'=4,'bank'=8] {'dp'}, dimensions={0}, use_global_device_ids=true | all-gather | bytes 491520 | tf_op jit(solution)/shard_map/all_gather | solution.py:340
  456.6 11.3 %collective-permute-done.16 = bf16[2,2,144,512]{3,2,0,1:T(8,128)(2,1)S(1)} collective-permute-done((bf16[2,2,144,512]{3,2,0,1:T(8,128)(2,1)S(1)}, bf16[2,2,144,512]{3,2,0,1:T(8,128)(2,1)S(1)}, u32[]{:S(2)}, u32[]{:S(2)}) %collective-permute-start.16) | collective-permute-done | bytes 589856 | tf_op jit(solution)/shard_map/ppermute | solution.py:99
  475.9 21.4 %collective-permute-done.15 = bf16[2,144,512]{2,1,0:T(8,128)(2,1)S(1)} collective-permute-done((bf16[2,144,512]{2,1,0:T(8,128)(2,1)S(1)}, bf16[2,144,512]{2,1,0:T(8,128)(2,1)S(1)}, u32[]{:S(2)}, u32[]{:S(2)}) %collective-permute-start.15) | collective-permute-done | bytes 294944 | tf_op jit(solution)/shard_map/ppermute | solution.py:99
  506.0 7.7 %collective-permute-done.20 = bf16[144,512]{1,0:T(8,128)(2,1)S(1)} collective-permute-done((bf16[144,512]{1,0:T(8,128)(2,1)S(1)}, bf16[144,512]{1,0:T(8,128)(2,1)S(1)}, u32[]{:S(2)}, u32[]{:S(2)}) %collective-permute-start.20) | collective-permute-done | bytes 147488 | tf_op jit(solution)/shard_map/ppermute | solution.py:99
  517.1 9.6 %all-gather.2 = bf16[576,512]{1,0:T(8,128)(2,1)S(1)} all-gather(bf16[144,512]{1,0:T(8,128)(2,1)S(1)} %fusion.69), channel_id=4, replica_groups=mesh['dp'=4,'bank'=8] {'dp'}, dimensions={0}, use_global_device_ids=true | all-gather | bytes 737280 | tf_op jit(solution)/shard_map/all_gather | solution.py:340
  527.9 5.4 collective-permute-done.7
  533.5 10.2 %all-gather.1 = bf16[768,512]{1,0:T(8,128)(2,1)S(1)} all-gather(bf16[192,512]{1,0:T(8,128)(2,1)S(1)} %fusion.66), channel_id=3, replica_groups=mesh['dp'=4,'bank'=8] {'dp'}, dimensions={0}, use_global_device_ids=true | all-gather | bytes 983040 | tf_op jit(solution)/shard_map/all_gather | solution.py:340
  (440 shorter events, 259.7 us)
Async XLA Ops:
  7.2 103.7 %all-gather.8.cloned.1.call-start = ((), (), s32[]{:S(2)}) async-start(), calls=%async_computation.6 | async-start | bytes 13516800 | tf_op jit(solution)/shard_map/all_gather | solution.py:226
  182.9 12.9 %all-to-all-start.1 = ((bf16[8,32,640]{2,1,0:T(8,128)(2,1)}), bf16[8,32,640]{2,1,0:T(8,128)(2,1)}, u32[]{:S(2)}, u32[]{:S(2)}) async-start(bf16[8,32,640]{2,1,0:T(8,128)(2,1)} %concatenate.91), calls=%async_computation.1 | async-start | bytes 655360 | tf_op jit(solution)/shard_map/all_to_all | solution.py:166
  217.4 17.6 %collective-permute-start.37 = (bf16[4,2,2,80,80]{4,3,0,2,1:T(8,128)(2,1)}, bf16[4,2,2,80,80]{4,3,0,2,1:T(8,128)(2,1)}, u32[]{:S(2)}, u32[]{:S(2)}) collective-permute-start(bf16[4,2,2,80,80]{4,3,0,2,1:T(8,128)(2,1)} %bitcast.381), channel_id=1, source_target_pairs={{0,8},{8,0},{16,24},{24,16},{1,9},{9,1},{17,25},{25,17},{2,10},{10... | collective-permute-start | bytes 614408 | tf_op jit(solution)/shard_map/ppermute | solution.py:99
  227.2 33.4 %all-to-all-start.2 = ((bf16[8,32,640]{2,1,0:T(8,128)(2,1)}), bf16[8,32,640]{2,1,0:T(8,128)(2,1)}, u32[]{:S(2)}, u32[]{:S(2)}) async-start(bf16[8,32,640]{2,1,0:T(8,128)(2,1)} %broadcast_in_dim.36), calls=%async_computation.2 | async-start | bytes 655360 | tf_op jit(solution)/shard_map/all_to_all | solution.py:166
  266.1 13.2 %all-to-all-start.3 = ((bf16[8,32,512]{2,1,0:T(8,128)(2,1)}), bf16[8,32,512]{2,1,0:T(8,128)(2,1)}, u32[]{:S(2)}, u32[]{:S(2)}) async-start(bf16[8,32,512]{2,1,0:T(8,128)(2,1)} %bitcast.374), calls=%async_computation.3 | async-start | bytes 524288 | tf_op jit(solution)/shard_map/all_to_all | solution.py:166
  272.0 88.0 %all-reduce.26.cloned.1.call-start = ((), (), s32[]{:S(2)}) async-start(), calls=%async_computation.5 | async-start | bytes 2097152 | tf_op jit(solution)/shard_map/psum | solution.py:362
  301.1 108.9 %collective-permute-start.29 = (bf16[4,2,2,96,512]{4,3,2,1,0:T(8,128)(2,1)}, bf16[4,2,2,96,512]{4,3,2,1,0:T(8,128)(2,1)}, u32[]{:S(2)}, u32[]{:S(2)}) collective-permute-start(bf16[4,2,2,96,512]{4,3,2,1,0:T(8,128)(2,1)} %dynamic-slice_bitcast_fusion), channel_id=1, source_target_pairs={{0,8},{8,0},{16,24},{24,16},{1,9},{9,1},{17,25},{25,17},{2,10},{10... | collective-permute-start | bytes 4718600 | tf_op jit(solution)/shard_map/ppermute | solution.py:99
  305.4 71.9 %collective-permute-start.21 = (bf16[4,2,2,16,2048]{4,3,0,2,1:T(8,128)(2,1)}, bf16[4,2,2,16,2048]{4,3,0,2,1:T(8,128)(2,1)}, u32[]{:S(2)}, u32[]{:S(2)}) collective-permute-start(bf16[4,2,2,16,2048]{4,3,0,2,1:T(8,128)(2,1)} %bitcast.335), channel_id=1, source_target_pairs={{0,8},{8,0},{16,24},{24,16},{1,9},{9,1},{17,25},{25,17},{2,10},{10... | collective-permute-start | bytes 3145736 | tf_op jit(solution)/shard_map/ppermute | solution.py:99
  353.8 96.7 %collective-permute-start.13 = (bf16[4,2,2,144,512]{4,3,0,2,1:T(8,128)(2,1)}, bf16[4,2,2,144,512]{4,3,0,2,1:T(8,128)(2,1)}, u32[]{:S(2)}, u32[]{:S(2)}) collective-permute-start(bf16[4,2,2,144,512]{4,3,0,2,1:T(8,128)(2,1)} %bitcast.334), channel_id=1, source_target_pairs={{0,8},{8,0},{16,24},{24,16},{1,9},{9,1},{17,25},{25,17},{2,10},{10... | collective-permute-start | bytes 7077896 | tf_op jit(solution)/shard_map/ppermute | solution.py:99
  359.0 111.0 %collective-permute-start = (bf16[4,2,2,192,512]{4,3,0,2,1:T(8,128)(2,1)}, bf16[4,2,2,192,512]{4,3,0,2,1:T(8,128)(2,1)}, u32[]{:S(2)}, u32[]{:S(2)}) collective-permute-start(bf16[4,2,2,192,512]{4,3,0,2,1:T(8,128)(2,1)} %bitcast.333), channel_id=1, source_target_pairs={{0,8},{8,0},{16,24},{24,16},{1,9},{9,1},{17,25},{25,17},{2,10},{10... | collective-permute-start | bytes 9437192 | tf_op jit(solution)/shard_map/ppermute | solution.py:99
  372.5 21.9 %all-to-all-start.4 = ((bf16[8,384,128]{1,2,0:T(8,128)(2,1)}), bf16[8,384,128]{1,2,0:T(8,128)(2,1)S(1)}, u32[]{:S(2)}, u32[]{:S(2)}) async-start(bf16[8,384,128]{1,2,0:T(8,128)(2,1)} %pad_maximum_fusion.5), calls=%async_computation.4 | async-start | bytes 1572864 | tf_op jit(solution)/shard_map/all_to_all | solution.py:166
  379.4 12.7 %collective-permute-start.24 = (bf16[2,2,16,2048]{3,2,0,1:T(8,128)(2,1)S(1)}, bf16[2,2,16,2048]{3,2,0,1:T(8,128)(2,1)S(1)}, u32[]{:S(2)}, u32[]{:S(2)}) collective-permute-start(bf16[2,2,16,2048]{3,2,0,1:T(8,128)(2,1)S(1)} %dynamic-slice_bitcast_fusion.10), channel_id=1, source_target_pairs={{0,1},{1,0},{2,3},{3,2},{4,5},{5,4},{6,7},{7,6},{8,9},{9,8},{10,11... | collective-permute-start | bytes 786440 | tf_op jit(solution)/shard_map/ppermute | solution.py:99
  394.4 12.7 %collective-permute-start.23 = (bf16[2,16,2048]{2,1,0:T(8,128)(2,1)}, bf16[2,16,2048]{2,1,0:T(8,128)(2,1)S(1)}, u32[]{:S(2)}, u32[]{:S(2)}) collective-permute-start(bf16[2,16,2048]{2,1,0:T(8,128)(2,1)} %dynamic-slice_bitcast_fusion.15), channel_id=1, source_target_pairs={{0,1},{1,0},{2,3},{3,2},{4,5},{5,4},{6,7},{7,6},{8,9},{9,8},{10,11... | collective-permute-start | bytes 393224 | tf_op jit(solution)/shard_map/ppermute | solution.py:99
  429.7 13.2 %collective-permute-start.34 = (bf16[96,512]{1,0:T(8,128)(2,1)S(1)}, bf16[96,512]{1,0:T(8,128)(2,1)S(1)}, u32[]{:S(2)}, u32[]{:S(2)}) collective-permute-start(bf16[96,512]{1,0:T(8,128)(2,1)S(1)} %get-tuple-element.175), channel_id=1, source_target_pairs={{0,2},{1,3},{2,0},{3,1},{4,6},{5,7},{6,4},{7,5},{8,10},{9,11},{10,... | collective-permute-start | bytes 294920 | tf_op jit(solution)/shard_map/ppermute | solution.py:99
  430.5 12.4 %collective-permute-start.35 = (bf16[96,512]{1,0:T(8,128)(2,1)S(1)}, bf16[96,512]{1,0:T(8,128)(2,1)S(1)}, u32[]{:S(2)}, u32[]{:S(2)}) collective-permute-start(bf16[96,512]{1,0:T(8,128)(2,1)S(1)} %get-tuple-element.176), channel_id=1, source_target_pairs={{0,4},{1,5},{2,6},{3,7},{4,0},{5,1},{6,2},{7,3},{8,12},{9,13},{10,... | collective-permute-start | bytes 294920 | tf_op jit(solution)/shard_map/ppermute | solution.py:99
  453.2 14.8 %collective-permute-start.16 = (bf16[2,2,144,512]{3,2,0,1:T(8,128)(2,1)S(1)}, bf16[2,2,144,512]{3,2,0,1:T(8,128)(2,1)S(1)}, u32[]{:S(2)}, u32[]{:S(2)}) collective-permute-start(bf16[2,2,144,512]{3,2,0,1:T(8,128)(2,1)S(1)} %dynamic-slice_bitcast_fusion.3), channel_id=1, source_target_pairs={{0,1},{1,0},{2,3},{3,2},{4,5},{5,4},{6,7},{7,6},{8,9},{9,8},{10,11... | collective-permute-start | bytes 1769480 | tf_op jit(solution)/shard_map/ppermute | solution.py:99
  455.3 14.5 %collective-permute-start.14 = (bf16[2,2,144,512]{3,2,0,1:T(8,128)(2,1)S(1)}, bf16[2,2,144,512]{3,2,0,1:T(8,128)(2,1)S(1)}, u32[]{:S(2)}, u32[]{:S(2)}) collective-permute-start(bf16[2,2,144,512]{3,2,0,1:T(8,128)(2,1)S(1)} %dynamic-slice_bitcast_fusion.4), channel_id=1, source_target_pairs={{0,16},{8,24},{16,0},{24,8},{1,17},{9,25},{17,1},{25,9},{2,18},{10... | collective-permute-start | bytes 1769480 | tf_op jit(solution)/shard_map/ppermute | solution.py:99
  473.2 28.3 %collective-permute-start.3 = (bf16[2,2,192,512]{3,2,0,1:T(8,128)(2,1)S(1)}, bf16[2,2,192,512]{3,2,0,1:T(8,128)(2,1)S(1)}, u32[]{:S(2)}, u32[]{:S(2)}) collective-permute-start(bf16[2,2,192,512]{3,2,0,1:T(8,128)(2,1)S(1)} %dynamic-slice_bitcast_fusion.1), channel_id=1, source_target_pairs={{0,1},{1,0},{2,3},{3,2},{4,5},{5,4},{6,7},{7,6},{8,9},{9,8},{10,11... | collective-permute-start | bytes 2359304 | tf_op jit(solution)/shard_map/ppermute | solution.py:99
  473.7 23.6 %collective-permute-start.15 = (bf16[2,144,512]{2,1,0:T(8,128)(2,1)S(1)}, bf16[2,144,512]{2,1,0:T(8,128)(2,1)S(1)}, u32[]{:S(2)}, u32[]{:S(2)}) collective-permute-start(bf16[2,144,512]{2,1,0:T(8,128)(2,1)S(1)} %dynamic-slice_bitcast_fusion.9), channel_id=1, source_target_pairs={{0,1},{1,0},{2,3},{3,2},{4,5},{5,4},{6,7},{7,6},{8,9},{9,8},{10,11... | collective-permute-start | bytes 884744 | tf_op jit(solution)/shard_map/ppermute | solution.py:99
  474.9 27.6 %collective-permute-start.1 = (bf16[2,2,192,512]{3,2,0,1:T(8,128)(2,1)S(1)}, bf16[2,2,192,512]{3,2,0,1:T(8,128)(2,1)S(1)}, u32[]{:S(2)}, u32[]{:S(2)}) collective-permute-start(bf16[2,2,192,512]{3,2,0,1:T(8,128)(2,1)S(1)} %dynamic-slice_bitcast_fusion.2), channel_id=1, source_target_pairs={{0,16},{8,24},{16,0},{24,8},{1,17},{9,25},{17,1},{25,9},{2,18},{10... | collective-permute-start | bytes 2359304 | tf_op jit(solution)/shard_map/ppermute | solution.py:99
  501.3 12.5 %collective-permute-start.20 = (bf16[144,512]{1,0:T(8,128)(2,1)S(1)}, bf16[144,512]{1,0:T(8,128)(2,1)S(1)}, u32[]{:S(2)}, u32[]{:S(2)}) collective-permute-start(bf16[144,512]{1,0:T(8,128)(2,1)S(1)} %get-tuple-element.162), channel_id=1, source_target_pairs={{0,6},{1,7},{2,4},{3,5},{4,2},{5,3},{6,0},{7,1},{8,14},{9,15},{10,... | collective-permute-start | bytes 442376 | tf_op jit(solution)/shard_map/ppermute | solution.py:99
  514.4 13.5 %collective-permute-start.5 = (bf16[192,512]{1,0:T(8,128)(2,1)S(1)}, bf16[192,512]{1,0:T(8,128)(2,1)S(1)}, u32[]{:S(2)}, u32[]{:S(2)}) collective-permute-start(bf16[192,512]{1,0:T(8,128)(2,1)S(1)} %get-tuple-element.155), channel_id=1, source_target_pairs={{0,2},{1,3},{2,0},{3,1},{4,6},{5,7},{6,4},{7,5},{8,10},{9,11},{10,... | collective-permute-start | bytes 589832 | tf_op jit(solution)/shard_map/ppermute | solution.py:99
  514.5 13.4 %collective-permute-start.6 = (bf16[192,512]{1,0:T(8,128)(2,1)S(1)}, bf16[192,512]{1,0:T(8,128)(2,1)S(1)}, u32[]{:S(2)}, u32[]{:S(2)}) collective-permute-start(bf16[192,512]{1,0:T(8,128)(2,1)S(1)} %get-tuple-element.156), channel_id=1, source_target_pairs={{0,4},{1,5},{2,6},{3,7},{4,0},{5,1},{6,2},{7,3},{8,12},{9,13},{10,... | collective-permute-start | bytes 589832 | tf_op jit(solution)/shard_map/ppermute | solution.py:99
  516.7 16.6 %collective-permute-start.7 = (bf16[192,512]{1,0:T(8,128)(2,1)S(1)}, bf16[192,512]{1,0:T(8,128)(2,1)S(1)}, u32[]{:S(2)}, u32[]{:S(2)}) collective-permute-start(bf16[192,512]{1,0:T(8,128)(2,1)S(1)} %get-tuple-element.157), channel_id=1, source_target_pairs={{0,6},{1,7},{2,4},{3,5},{4,2},{5,3},{6,0},{7,1},{8,14},{9,15},{10,... | collective-permute-start | bytes 589832 | tf_op jit(solution)/shard_map/ppermute | solution.py:99
  (87 other events, 777.9 us)
Sparse Core Ops, SparseCore 0:
  11.5 99.3 all-gather.7
  276.4 36.1 all-reduce.25

commit v2 on v1

v2 whole, which is shorter than its diff:
```python
import functools

import jax
import jax.numpy as jnp
from jax import lax
from jax.experimental import pallas as pl
from jax.experimental.pallas import tpu as pltpu
from jax.sharding import PartitionSpec as P

FRAMES = 4
SIDE = 8
LANE_ROWS = 16
TILE = 128
ROOT = 0.7978845608028654
CUBIC = 0.044715

epsilon = 1e-05
masked_score = -1e30
places = [(-1, -1), (-1, 0), (-1, 1), (0, -1), (0, 0), (0, 1), (1, -1), (1, 0), (1, 1)]


def product(left, right):
    return jnp.dot(left, right, preferred_element_type=jnp.float32)


def low(value):
    return value.astype(jnp.bfloat16)


def wide(value):
    return value.astype(jnp.float32)


class SubAxis:
    def __init__(self, name, size, stride):
        self.name, self.size, self.stride = name, size, stride

    def place(self):
        return lax.rem(lax.axis_index(self.name) // self.stride, self.size)

    def swap(self, value, step):
        count = lax.axis_size(self.name)
        pairs = [(i, i ^ (step * self.stride)) for i in range(count)]
        return lax.ppermute(value, self.name, pairs)


def block_axes(split, dp_count, bank_count):
    if split:
        return (
            SubAxis("bank", bank_count // 2, 2),
            SubAxis("bank", 2, 1),
            SubAxis("dp", dp_count // 2, 2),
            SubAxis("dp", 2, 1),
        )
    return (
        SubAxis("bank", bank_count // 8, 8),
        SubAxis("bank", 2, 4),
        SubAxis("bank", 2, 2),
        SubAxis("bank", 2, 1),
    )


def block_at(value, place, dim):
    return lax.dynamic_index_in_dim(value, place, dim, keepdims=False)


def reduce_over(value, axis, dim):
    me = axis.place()
    parts = [axis.swap(block_at(value, me ^ step, dim), step) for step in range(1, axis.size)]
    total = wide(block_at(value, me, dim))
    for part in parts:
        total = total + wide(part)
    return total


def reduce_halves(send, keep, axes):
    outer, inner, across, last = axes
    value = low(wide(keep) + wide(last.swap(send, 1)))
    half = outer.size // 2
    first = low(reduce_over(value[:half], across, 2))
    second = low(reduce_over(value[half:], inner, 1))
    first = low(reduce_over(first, inner, 1))
    second = low(reduce_over(second, across, 1))
    return reduce_over(jnp.concatenate([first, second], 0), outer, 0)


def sum_everywhere(value, names):
    for name in names:
        step = 1
        while step < lax.axis_size(name):
            pairs = [(i, i ^ step) for i in range(lax.axis_size(name))]
            value = value + lax.ppermute(value, name, pairs)
            step *= 2
    return value


def to_owners(value):
    return lax.all_to_all(value, "bank", split_axis=0, concat_axis=0, tiled=True)


def to_group(value):
    count = lax.axis_size("bank")
    return to_owners(jnp.broadcast_to(value[None], (count,) + value.shape))


def whole_vmem(count):
    return [pl.BlockSpec(memory_space=pltpu.VMEM)] * count


def params(mib):
    return pltpu.CompilerParams(vmem_limit_bytes=mib * 1024 * 1024)


def gelu_of(x):
    return 0.5 * x * (1.0 + jnp.tanh(ROOT * (x + CUBIC * x * x * x)))


def gelu_slope(x):
    square = x * x
    bent = jnp.tanh(ROOT * x * (1.0 + CUBIC * square))
    return 0.5 * (1.0 + bent) + 0.5 * ROOT * x * (1.0 - bent * bent) * (1.0 + 3.0 * CUBIC * square)


def by_rows(count, step, work):
    def one(number, carry):
        work(pl.ds(pl.multiple_of(number * step, step), step))
        return carry

    lax.fori_loop(0, count // step, one, 0)


def dot_tn(left, right):
    return lax.dot_general(
        left, right, (((0,), (0,)), ((), ())), preferred_element_type=jnp.float32
    )


def dot_nt(left, right):
    return lax.dot_general(
        left, right, (((1,), (1,)), ((), ())), preferred_element_type=jnp.float32
    )


def in_rows(value, step):
    if step == 0:
        return value
    sites, width = value.shape
    tall = value.reshape(sites // (SIDE * SIDE), SIDE, SIDE, width)
    edge = jnp.zeros_like(tall[:, :1])
    if step > 0:
        tall = jnp.concatenate([tall[:, 1:], edge], axis=1)
    else:
        tall = jnp.concatenate([edge, tall[:, :-1]], axis=1)
    return tall.reshape(sites, width)


def in_columns(value, step):
    if step == 0:
        return value
    sites = value.shape[0]
    turned = pltpu.roll(value, (-step) % sites, 0)
    column = lax.broadcasted_iota(jnp.int32, value.shape, 0) % SIDE
    keep = column != (SIDE - 1 if step > 0 else 0)
    return jnp.where(keep, turned, 0.0)


def fetch(source, target, sems, first, groups):
    copies = []
    for block in range(source.shape[0]):
        copies.append(
            pltpu.make_async_copy(
                source.at[block, pl.ds(first, groups)],
                target.at[pl.ds(block * groups, groups)],
                sems.at[block],
            )
        )
    return copies


def fetch_columns(source, target, sems, first, groups):
    return [
        pltpu.make_async_copy(
            source.at[block, pl.ds(first, groups)], target.at[:, block], sems.at[block]
        )
        for block in range(source.shape[0])
    ]


def first_conv(fm_ref, packed_ref, scale_ref, shift_ref, pre_ref, act_ref, weight, sems):
    sites, features = fm_ref.shape
    channels = pre_ref.shape[1]
    groups = weight.shape[0] // packed_ref.shape[0]
    copies = fetch(packed_ref, weight, sems, 0, groups)
    for copy in copies:
        copy.start()
    block_rows = groups * LANE_ROWS
    clip = FRAMES * SIDE * SIDE
    frame = SIDE * SIDE
    waited = 0

    def tap(number):
        nonlocal waited
        end = (number + 1) * features
        while waited < len(copies) and waited * block_rows < end:
            copies[waited].wait()
            waited += 1
        begin = number * features // LANE_ROWS
        return weight[begin : begin + features // LANE_ROWS].reshape(features, channels)

    before = tap(0)
    for start in range(0, sites, clip):
        pre_ref[start : start + frame] = jnp.zeros((frame, channels), jnp.float32)
        pre_ref[start + frame : start + clip] = product(fm_ref[start : start + clip - frame], before)
    pre_ref[...] += product(fm_ref[...], tap(1))
    after = tap(2)
    for start in range(0, sites, clip):
        pre_ref[start : start + clip - frame] += product(fm_ref[start + frame : start + clip], after)

    def finish(rows):
        act_ref[rows] = low(gelu_of(pre_ref[rows] * scale_ref[...] + shift_ref[...]))

    by_rows(sites, 64, finish)


def later_convs(
    act_a_ref, fm_ref, packed_ref, scale_b_ref, shift_b_ref, scale_c_ref, shift_c_ref, pool_ref, w_reduce_ref, w_query_ref,
    pre_b_ref, act_b_ref, pre_c_ref, regions_ref, reduced_ref, queries_ref,
    weight_b, weight_c, out_low, sems_b, sems_c,
):
    sites, channels = act_a_ref.shape
    blocks = packed_ref.shape[0]
    groups_b = weight_b.shape[0] // blocks
    groups_c = weight_c.shape[0]
    groups_a = packed_ref.shape[1] - groups_b - groups_c
    copies_b = fetch(packed_ref, weight_b, sems_b, groups_a, groups_b)
    copies_c = fetch_columns(packed_ref, weight_c, sems_c, groups_a + groups_b, groups_c)
    for copy in copies_b + copies_c:
        copy.start()
    act_a = act_a_ref[...]
    block_rows = groups_b * LANE_ROWS
    sums = {-1: None, 0: None, 1: None}
    waited = 0
    for number, (rise, slide) in enumerate(places):
        while waited < len(copies_b) and waited * block_rows < (number + 1) * channels:
            copies_b[waited].wait()
            waited += 1
        begin = number * channels // LANE_ROWS
        tap = weight_b[begin : begin + channels // LANE_ROWS].reshape(channels, channels)
        part = in_rows(product(act_a, tap), rise)
        sums[slide] = part if sums[slide] is None else sums[slide] + part
    pre_b_ref[...] = sums[0] + in_columns(sums[1], 1) + in_columns(sums[-1], -1)

    def finish(rows):
        act_b_ref[rows] = low(gelu_of(pre_b_ref[rows] * scale_b_ref[...] + shift_b_ref[...]))

    by_rows(sites, 64, finish)
    for copy in copies_c:
        copy.wait()
    reduced_ref[...] = jnp.zeros_like(reduced_ref)

    def chunk(number, carry):
        columns = pl.ds(pl.multiple_of(number * channels, channels), channels)
        pre_c_ref[:, columns] = product(act_b_ref[...], weight_c[number].reshape(channels, channels))

        def finish_c(rows):
            linear = wide(fm_ref[rows, columns]) + pre_c_ref[rows, columns] * scale_c_ref[:, columns] + shift_c_ref[:, columns]
            out_low[rows] = low(gelu_of(linear))

        by_rows(sites, 64, finish_c)
        part = low(product(pool_ref[...], out_low[...]))
        regions_ref[:, columns] = part
        reduced_ref[...] += product(part, w_reduce_ref[columns])
        return carry

    lax.fori_loop(0, groups_c, chunk, 0)
    queries_ref[...] = low(product(low(reduced_ref[...]), w_query_ref[...]))


def column_tile(columns, shape):
    lane = lax.broadcasted_iota(jnp.int32, shape, len(shape) - 1)
    tile = jnp.zeros(shape, jnp.float32)
    for number, column in enumerate(columns):
        rest = column
        for third in range(3):
            piece = wide(low(rest))
            tile = jnp.where(lane == 3 * number + third, piece, tile)
            rest = rest - piece
    return low(tile)


def from_tile(tile, number):
    lane = lax.broadcasted_iota(jnp.int32, tile.shape, tile.ndim - 1)
    picked = jnp.where((lane >= 3 * number) & (lane < 3 * number + 3), wide(tile), 0.0)
    return jnp.sum(picked, axis=-1, keepdims=True)


def attend(half_span, start_ref, queries_ref, keys_ref, values_ref, time_ref, message_ref, scores_ref):
    channels = queries_ref.shape[1]
    positions = start_ref[0] + lax.broadcasted_iota(jnp.int32, scores_ref.shape, 1)
    visible = jnp.abs(time_ref[...] - positions) <= half_span
    scores = dot_nt(queries_ref[...], keys_ref[...]) * (channels ** (-0.5))
    scores = jnp.where(visible, scores, masked_score)
    scores_ref[...] = scores
    top = jnp.max(scores, axis=1, keepdims=True)
    weights = jnp.exp(scores - top)
    total = jnp.sum(weights, axis=1, keepdims=True)
    message_ref[:, :channels] = low(product(low(weights), values_ref[...]))
    message_ref[:, channels:] = column_tile([top, total], (scores.shape[0], TILE))


def merge_rows(arrived_ref, hidden_grad_ref, gain_ref, shift_ref, message_ref, hidden_ref, gain_out_ref, shift_out_ref):
    count, own, packed = arrived_ref.shape
    channels = hidden_grad_ref.shape[1]
    tops = from_tile(arrived_ref[:, :, channels:], 0)
    totals = from_tile(arrived_ref[:, :, channels:], 1)
    top = jnp.max(tops, axis=0)
    factors = jnp.exp(tops - top[None])
    total = jnp.sum(factors * totals, axis=0)
    numer = jnp.sum(factors * wide(arrived_ref[:, :, :channels]), axis=0)
    attended = numer / total
    centred = attended - jnp.mean(attended, axis=1, keepdims=True)
    spread = lax.rsqrt(jnp.mean(centred * centred, axis=1, keepdims=True) + epsilon)
    unit = centred * spread
    normed = unit * gain_ref[...] + shift_ref[...]
    hidden_ref[...] = low(gelu_of(normed))
    normed_grad = hidden_grad_ref[...] * gelu_slope(normed)
    gain_out_ref[...] = jnp.sum(normed_grad * unit, axis=0, keepdims=True)
    shift_out_ref[...] = jnp.sum(normed_grad, axis=0, keepdims=True)
    unit_grad = normed_grad * gain_ref[...]
    attended_grad = spread * (
        unit_grad
        - jnp.mean(unit_grad, axis=1, keepdims=True)
        - unit * jnp.mean(unit_grad * unit, axis=1, keepdims=True)
    )
    centre = jnp.sum(attended_grad * attended, axis=1, keepdims=True) / total
    numer_grad = low(attended_grad / total)
    tile = column_tile([top, centre], (own, TILE))
    for place in range(count):
        message_ref[place, :, :channels] = numer_grad
        message_ref[place, :, channels:] = tile


def attend_back(arrived_ref, scores_ref, keys_ref, values_ref, part_ref, score_grad_ref, weights_ref):
    channels = keys_ref.shape[1]
    top = from_tile(arrived_ref[:, channels:], 0)
    centre = from_tile(arrived_ref[:, channels:], 1)
    weights = jnp.exp(scores_ref[...] - top)
    weights_ref[...] = low(weights)
    prob_grad = dot_nt(arrived_ref[:, :channels], values_ref[...])
    score_grad = low(weights * (prob_grad - centre) * (channels ** (-0.5)))
    score_grad_ref[...] = score_grad
    part_ref[...] = low(product(score_grad, keys_ref[...]))


def half_of(place_ref, bit):
    return jnp.where(place_ref[0] == bit, 1, 0)


def hand_out(buffer, send_ref, keep_ref, sems):
    copies = [
        pltpu.make_async_copy(buffer.at[number], target, sems.at[number])
        for number, target in enumerate((send_ref, keep_ref))
    ]
    for copy in copies:
        copy.start()
    for copy in copies:
        copy.wait()


def store_rows(buffer, place_ref, value, first):
    rows = buffer.shape[2]
    at, end = first, first + value.shape[0]
    while at < end:
        block, offset = divmod(at, rows)
        count = min(rows - offset, end - at)
        buffer[half_of(place_ref, block % 2), block // 2, offset : offset + count] = value[at - first : at - first + count]
        at += count


def fold(value):
    return jnp.sum(value.reshape(value.shape[0] // 8, 8, value.shape[1]), axis=0)


def third_back(
    place_ref, arrived_ref, joined_grad_ref, w_query_ref, w_reduce_ref, pool_ref, pre_c_ref, fm_ref, scale_ref, shift_ref,
    act_b_ref, packed_ref,
    send_ref, keep_ref, lin_c_grad_ref, act_b_grad_ref, scale_out_ref, shift_out_ref, query_grad_ref, reduced_grad_ref,
    weight_c, buffer, out_grad, pre_grad, regions_grad, turned, sems, out_sems,
):
    sites, features = fm_ref.shape
    channels = act_b_ref.shape[1]
    groups_c = weight_c.shape[0]
    blocks = weight_c.shape[1]
    first = packed_ref.shape[1] - groups_c
    copies = fetch_columns(packed_ref, weight_c, sems, first, groups_c)
    for copy in copies:
        copy.start()
    query_grad = low(jnp.sum(wide(arrived_ref[...]), axis=0))
    query_grad_ref[...] = query_grad
    reduced_grad = low(joined_grad_ref[:, features:] + dot_nt(query_grad, w_query_ref[...]))
    reduced_grad_ref[...] = reduced_grad
    regions_grad[...] = low(joined_grad_ref[:, :features] + dot_nt(reduced_grad, w_reduce_ref[...]))
    turned[...] = act_b_ref[...].T
    act_b_grad_ref[...] = jnp.zeros_like(act_b_grad_ref)
    for copy in copies:
        copy.wait()

    def chunk(number, carry):
        columns = pl.ds(pl.multiple_of(number * channels, channels), channels)
        out_grad[...] = dot_tn(pool_ref[...], regions_grad[:, columns])

        def one(step, sums):
            rows = pl.ds(pl.multiple_of(step * 64, 64), 64)
            pre = pre_c_ref[rows, columns]
            scale = scale_ref[:, columns]
            linear = wide(fm_ref[rows, columns]) + pre * scale + shift_ref[:, columns]
            grad = out_grad[rows] * gelu_slope(linear)
            lin_c_grad_ref[rows, columns] = grad
            pre_grad[rows] = low(grad * scale)
            return sums[0] + fold(grad * pre), sums[1] + fold(grad)

        zero = jnp.zeros((8, channels), jnp.float32)
        scale_sum, shift_sum = lax.fori_loop(0, sites // 64, one, (zero, zero))
        scale_out_ref[:, columns] = jnp.sum(scale_sum, axis=0, keepdims=True)
        shift_out_ref[:, columns] = jnp.sum(shift_sum, axis=0, keepdims=True)
        part = low(product(turned[...], pre_grad[...])).reshape(blocks // 2, 2, LANE_ROWS, channels)
        rows = pl.ds(pl.multiple_of(number * LANE_ROWS, LANE_ROWS), LANE_ROWS)
        for bit in range(2):
            buffer[half_of(place_ref, bit), :, rows] = part[:, bit]
        act_b_grad_ref[...] += dot_nt(pre_grad[...], weight_c[number].reshape(channels, channels))
        return carry

    lax.fori_loop(0, groups_c, chunk, 0)
    hand_out(buffer, send_ref, keep_ref, out_sems)


def slope_back(upstream_ref, pre_ref, scale_ref, shift_ref, out_ref, scale_out_ref, shift_out_ref):
    sites, channels = pre_ref.shape

    def one(step, sums):
        rows = pl.ds(pl.multiple_of(step * 64, 64), 64)
        pre = pre_ref[rows]
        grad = upstream_ref[rows] * gelu_slope(pre * scale_ref[...] + shift_ref[...])
        out_ref[rows] = low(grad * scale_ref[...]).astype(out_ref.dtype)
        return sums[0] + fold(grad * pre), sums[1] + fold(grad)

    zero = jnp.zeros((8, channels), jnp.float32)
    scale_sum, shift_sum = lax.fori_loop(0, sites // 64, one, (zero, zero))
    scale_out_ref[...] = jnp.sum(scale_sum, axis=0, keepdims=True)
    shift_out_ref[...] = jnp.sum(shift_sum, axis=0, keepdims=True)


def second_back(
    first, place_ref, act_b_grad_ref, pre_b_ref, scale_b_ref, shift_b_ref, act_a_ref, pre_a_ref, scale_a_ref, shift_a_ref, packed_ref,
    send_ref, keep_ref, pre_a_grad_ref, scale_b_out_ref, shift_b_out_ref, scale_a_out_ref, shift_a_out_ref,
    weight_b, buffer, pre_grad, act_grad, turned, sems, out_sems,
):
    channels = act_a_ref.shape[1]
    blocks = packed_ref.shape[0]
    groups_b = weight_b.shape[0] // blocks
    copies = fetch(packed_ref, weight_b, sems, first, groups_b)
    for copy in copies:
        copy.start()
    slope_back(act_b_grad_ref, pre_b_ref, scale_b_ref, shift_b_ref, pre_grad, scale_b_out_ref, shift_b_out_ref)
    turned[...] = act_a_ref[...].T
    for copy in copies:
        copy.wait()
    for slide in (-1, 0, 1):
        slid = in_columns(pre_grad[...], -slide)
        for number, place in enumerate(places):
            if place[1] != slide:
                continue
            moved = low(in_rows(slid, -place[0]))
            store_rows(buffer, place_ref, low(product(turned[...], moved)), number * channels)
            begin = number * channels // LANE_ROWS
            tap = weight_b[begin : begin + channels // LANE_ROWS].reshape(channels, channels)
            part = dot_nt(moved, tap)
            if slide == -1 and place[0] == -1:
                act_grad[...] = part
            else:
                act_grad[...] += part
    slope_back(act_grad, pre_a_ref, scale_a_ref, shift_a_ref, pre_a_grad_ref, scale_a_out_ref, shift_a_out_ref)
    hand_out(buffer, send_ref, keep_ref, out_sems)


def by_frames(grad, offset):
    if offset == 0:
        return grad
    sites, width = grad.shape
    tall = grad.reshape(sites // (FRAMES * SIDE * SIDE), FRAMES, SIDE * SIDE, width)
    edge = jnp.zeros_like(tall[:, :1])
    if offset > 0:
        tall = jnp.concatenate([edge, tall[:, :-1]], axis=1)
    else:
        tall = jnp.concatenate([tall[:, 1:], edge], axis=1)
    return tall.reshape(sites, width)


def first_back(place_ref, grad_ref, turned_ref, send_ref, keep_ref, buffer, out_sems):
    features = turned_ref.shape[0]
    channels = grad_ref.shape[1]
    for tap in range(3):
        moved = by_frames(grad_ref[...], tap - 1)
        for start in range(0, features, channels):
            part = low(product(turned_ref[start : start + channels], moved))
            store_rows(buffer, place_ref, part, tap * features + start)
    hand_out(buffer, send_ref, keep_ref, out_sems)


def map_back(grad_ref, lin_c_grad_ref, packed_ref, out_ref, weight, moved, sems):
    sites, features = out_ref.shape
    channels = grad_ref.shape[1]
    blocks = packed_ref.shape[0]
    copies = fetch(packed_ref, weight, sems, 0, weight.shape[0] // blocks)
    for copy in copies:
        copy.start()
    for tap in range(3):
        moved[tap] = by_frames(grad_ref[...], tap - 1)
    for copy in copies:
        copy.wait()
    groups = channels // LANE_ROWS

    def chunk(number, carry):
        columns = pl.ds(pl.multiple_of(number * channels, channels), channels)
        total = lin_c_grad_ref[:, columns]
        for tap in range(3):
            rows = pl.ds(tap * (features // LANE_ROWS) + number * groups, groups)
            total = total + dot_nt(moved[tap], weight[rows].reshape(channels, channels))
        out_ref[:, columns] = low(total)
        return carry

    lax.fori_loop(0, features // channels, chunk, 0)

ANY = pl.BlockSpec(memory_space=pl.ANY)
SCALAR = pl.BlockSpec(memory_space=pltpu.SMEM)


def shape_of(dims, kind):
    return jax.ShapeDtypeStruct(dims, kind)


F32 = jnp.float32
BF16 = jnp.bfloat16


def run_first_conv(feature_map, packed, scale, shift, groups):
    sites, channels = feature_map.shape[0], packed.shape[3]
    blocks = packed.shape[0]
    return pl.pallas_call(
        first_conv,
        out_shape=[
            jax.ShapeDtypeStruct((sites, channels), jnp.float32),
            jax.ShapeDtypeStruct((sites, channels), jnp.bfloat16),
        ],
        in_specs=[pl.BlockSpec(memory_space=pltpu.VMEM), pl.BlockSpec(memory_space=pl.ANY)] + whole_vmem(2),
        out_specs=whole_vmem(2),
        scratch_shapes=[
            pltpu.VMEM((blocks * groups, LANE_ROWS, channels), jnp.bfloat16),
            pltpu.SemaphoreType.DMA((blocks,)),
        ],
        compiler_params=params(40),
        name="first_conv",
    )(feature_map, packed, scale.reshape(1, -1), shift.reshape(1, -1))


def run_later_convs(
    act_a, feature_map, packed, scale_b, shift_b, scale_c, shift_c, pooling, w_reduce, w_query, groups_b, groups_c
):
    sites, channels = act_a.shape
    features = feature_map.shape[1]
    blocks = packed.shape[0]
    own = pooling.shape[0]
    return pl.pallas_call(
        later_convs,
        out_shape=[
            jax.ShapeDtypeStruct((sites, channels), jnp.float32),
            jax.ShapeDtypeStruct((sites, channels), jnp.bfloat16),
            jax.ShapeDtypeStruct((sites, features), jnp.float32),
            jax.ShapeDtypeStruct((own, features), jnp.bfloat16),
            jax.ShapeDtypeStruct((own, channels), jnp.float32),
            jax.ShapeDtypeStruct((own, channels), jnp.bfloat16),
        ],
        in_specs=whole_vmem(2) + [pl.BlockSpec(memory_space=pl.ANY)] + whole_vmem(7),
        out_specs=whole_vmem(6),
        scratch_shapes=[
            pltpu.VMEM((blocks * groups_b, LANE_ROWS, channels), jnp.bfloat16),
            pltpu.VMEM((groups_c, blocks, LANE_ROWS, channels), jnp.bfloat16),
            pltpu.VMEM((sites, channels), jnp.bfloat16),
            pltpu.SemaphoreType.DMA((blocks,)),
            pltpu.SemaphoreType.DMA((blocks,)),
        ],
        compiler_params=params(52),
        name="later_convs",
    )(
        act_a, feature_map, packed, scale_b.reshape(1, -1), shift_b.reshape(1, -1), scale_c.reshape(1, -1),
        shift_c.reshape(1, -1), pooling, w_reduce, w_query,
    )


def run_attend(half_span, start, queries, keys, values, times):
    rows, channels = queries.shape
    return pl.pallas_call(
        functools.partial(attend, half_span),
        out_shape=[shape_of((rows, channels + TILE), BF16), shape_of((rows, keys.shape[0]), F32)],
        in_specs=[SCALAR] + whole_vmem(4),
        out_specs=whole_vmem(2),
        compiler_params=params(32),
        name="attend",
    )(start.reshape(1), queries, keys, values, times.reshape(-1, 1))


def run_merge_rows(arrived, hidden_grad, gain, shift):
    own, channels = hidden_grad.shape
    return pl.pallas_call(
        merge_rows,
        out_shape=[
            shape_of(arrived.shape, BF16),
            shape_of((own, channels), BF16),
            shape_of((1, channels), F32),
            shape_of((1, channels), F32),
        ],
        in_specs=whole_vmem(4),
        out_specs=whole_vmem(4),
        compiler_params=params(24),
        name="merge_rows",
    )(arrived, hidden_grad, gain.reshape(1, -1), shift.reshape(1, -1))


def run_attend_back(arrived, scores, keys, values):
    rows, count = scores.shape
    channels = keys.shape[1]
    return pl.pallas_call(
        attend_back,
        out_shape=[shape_of((rows, channels), BF16), shape_of((rows, count), BF16), shape_of((rows, count), BF16)],
        in_specs=whole_vmem(4),
        out_specs=whole_vmem(3),
        compiler_params=params(32),
        name="attend_back",
    )(arrived, scores, keys, values)


def run_third_back(
    place, arrived, joined_grad, w_query, w_reduce, pooling, pre_c, feature_map, scale, shift, act_b, packed, groups_c
):
    sites, features = feature_map.shape
    channels = act_b.shape[1]
    blocks, own = packed.shape[0], pooling.shape[0]
    rows_c = groups_c * LANE_ROWS
    return pl.pallas_call(
        third_back,
        out_shape=[shape_of((blocks // 2, rows_c, channels), BF16)] * 2
        + [
            shape_of((sites, features), F32),
            shape_of((sites, channels), F32),
            shape_of((1, features), F32),
            shape_of((1, features), F32),
            shape_of((own, channels), BF16),
            shape_of((own, channels), BF16),
        ],
        in_specs=[SCALAR] + whole_vmem(10) + [ANY],
        out_specs=[ANY] * 2 + whole_vmem(6),
        scratch_shapes=[
            pltpu.VMEM((groups_c, blocks, LANE_ROWS, channels), BF16),
            pltpu.VMEM((2, blocks // 2, rows_c, channels), BF16),
            pltpu.VMEM((sites, channels), F32),
            pltpu.VMEM((sites, channels), BF16),
            pltpu.VMEM((own, features), BF16),
            pltpu.VMEM((channels, sites), BF16),
            pltpu.SemaphoreType.DMA((blocks,)),
            pltpu.SemaphoreType.DMA((2,)),
        ],
        compiler_params=params(52),
        name="third_back",
    )(
        place.reshape(1), arrived, joined_grad, w_query, w_reduce, pooling, pre_c, feature_map, scale.reshape(1, -1),
        shift.reshape(1, -1), act_b, packed,
    )


def run_second_back(
    place, act_b_grad, pre_b, scale_b, shift_b, act_a, pre_a, scale_a, shift_a, packed, groups_a, groups_b
):
    sites, channels = act_a.shape
    blocks = packed.shape[0]
    rows_b = groups_b * LANE_ROWS
    row = shape_of((1, channels), F32)
    return pl.pallas_call(
        functools.partial(second_back, groups_a),
        out_shape=[shape_of((blocks // 2, rows_b, channels), BF16)] * 2
        + [shape_of((sites, channels), BF16), row, row, row, row],
        in_specs=[SCALAR] + whole_vmem(8) + [ANY],
        out_specs=[ANY] * 2 + whole_vmem(5),
        scratch_shapes=[
            pltpu.VMEM((blocks * groups_b, LANE_ROWS, channels), BF16),
            pltpu.VMEM((2, blocks // 2, rows_b, channels), BF16),
            pltpu.VMEM((sites, channels), F32),
            pltpu.VMEM((sites, channels), F32),
            pltpu.VMEM((channels, sites), BF16),
            pltpu.SemaphoreType.DMA((blocks,)),
            pltpu.SemaphoreType.DMA((2,)),
        ],
        compiler_params=params(52),
        name="second_back",
    )(
        place.reshape(1), act_b_grad, pre_b, scale_b.reshape(1, -1), shift_b.reshape(1, -1), act_a, pre_a,
        scale_a.reshape(1, -1), shift_a.reshape(1, -1), packed,
    )


def run_first_back(place, pre_a_grad, turned_map, blocks, rows_a):
    channels = pre_a_grad.shape[1]
    return pl.pallas_call(
        first_back,
        out_shape=[shape_of((blocks // 2, rows_a, channels), BF16)] * 2,
        in_specs=[SCALAR] + whole_vmem(2),
        out_specs=[ANY] * 2,
        scratch_shapes=[
            pltpu.VMEM((2, blocks // 2, rows_a, channels), BF16),
            pltpu.SemaphoreType.DMA((2,)),
        ],
        compiler_params=params(40),
        name="first_back",
    )(place.reshape(1), pre_a_grad, turned_map)


def run_map_back(pre_a_grad, lin_c_grad, packed, groups_a):
    sites, channels = pre_a_grad.shape
    blocks = packed.shape[0]
    return pl.pallas_call(
        map_back,
        out_shape=shape_of(lin_c_grad.shape, BF16),
        in_specs=whole_vmem(2) + [ANY],
        out_specs=pl.BlockSpec(memory_space=pltpu.VMEM),
        scratch_shapes=[
            pltpu.VMEM((blocks * groups_a, LANE_ROWS, channels), BF16),
            pltpu.VMEM((3, sites, channels), BF16),
            pltpu.SemaphoreType.DMA((blocks,)),
        ],
        compiler_params=params(40),
        name="map_back",
    )(pre_a_grad, lin_c_grad, packed)


def body(
    feature_map,
    bank,
    region_time,
    roi_index,
    roi_weight,
    conv_a,
    scale_a,
    shift_a,
    conv_b,
    scale_b,
    shift_b,
    conv_c,
    scale_c,
    shift_c,
    w_reduce,
    w_bank,
    w_query,
    w_key,
    w_value,
    ln_gain,
    ln_shift,
    w_out,
    w_head,
    logit_grad,
):
    site_count = feature_map.shape[0]
    feature_count = feature_map.shape[1]
    channels = w_query.shape[0]
    keys_here = bank.shape[0]
    own_count = roi_index.shape[0]
    bank_count = lax.axis_size("bank")
    bank_place = lax.axis_index("bank")
    dp_count = lax.axis_size("dp")
    dp_place = lax.axis_index("dp")
    first_row = bank_place * own_count
    half_span = keys_here * bank_count // 2
    group_rows = bank_count * own_count
    chunks = feature_count // channels
    shards = (conv_a, conv_b, conv_c)
    split = all(shard.shape[0] % (LANE_ROWS * dp_count) == 0 for shard in shards)
    axes = block_axes(split, dp_count, bank_count)
    blocks = bank_count * dp_count if split else bank_count
    halves = tuple(axis.size for axis in axes[:3])
    last_place = axes[3].place()

    def own_part(shard):
        if not split:
            return shard
        rows = shard.shape[0] // dp_count
        return lax.dynamic_slice_in_dim(shard, dp_place * rows, rows, 0)

    part_a, part_b, part_c = [own_part(shard) for shard in shards]
    rows_a, rows_b, rows_c = part_a.shape[0], part_b.shape[0], part_c.shape[0]
    groups_a, groups_b, groups_c = rows_a // LANE_ROWS, rows_b // LANE_ROWS, chunks
    pieces_c = [part_c[:, chunk * channels : (chunk + 1) * channels] for chunk in range(chunks)]
    own_packed = jnp.concatenate([part_a, part_b] + pieces_c, 0).reshape(-1, LANE_ROWS, channels)
    packed = lax.all_gather(own_packed, ("bank", "dp") if split else "bank", axis=0, tiled=False)
    packed = packed.reshape((blocks,) + own_packed.shape)

    memory = product(bank, w_bank)
    memory_low = low(memory)
    keys = low(product(memory_low, w_key))
    values = low(product(memory_low, w_value))
    turned_map = feature_map.T
    matches = roi_index[:, :, None] == jnp.arange(site_count, dtype=jnp.int32)[None, None, :]
    pooling = low(jnp.sum(jnp.where(matches, wide(roi_weight)[:, :, None], 0.0), axis=1))
    own_logit_grad = lax.dynamic_slice_in_dim(logit_grad, first_row, own_count, 0)
    joined_grad = dot_nt(own_logit_grad, w_head)
    branch_grad = low(joined_grad[:, feature_count:])
    hidden_grad = dot_nt(branch_grad, w_out)

    pre_a, act_a = run_first_conv(feature_map, packed, scale_a, shift_a, groups_a)
    pre_b, act_b, pre_c, regions, reduced, own_queries = run_later_convs(
        act_a, feature_map, packed, scale_b, shift_b, scale_c, shift_c, pooling, w_reduce, w_query, groups_b, groups_c
    )
    reduced_low = low(reduced)
    queries = to_group(own_queries).reshape(group_rows, channels)
    message, scores = run_attend(half_span, bank_place * keys_here, queries, keys, values, region_time)
    arrived = to_owners(message.reshape(bank_count, own_count, channels + TILE))
    message, hidden_low, gain_part, shift_part = run_merge_rows(arrived, hidden_grad, ln_gain, ln_shift)
    arrived = to_owners(message).reshape(group_rows, channels + TILE)
    query_part, score_grad, weights_low = run_attend_back(arrived, scores, keys, values)
    numer_grad = arrived[:, :channels]
    arrived = to_owners(query_part.reshape(bank_count, own_count, channels))
    key_part = low(dot_tn(score_grad, queries))
    value_part = low(dot_tn(weights_low, numer_grad))
    (
        send_c, keep_c, lin_c_grad, act_b_grad, scale_c_part, shift_c_part, query_grad, reduced_grad
    ) = run_third_back(
        last_place, arrived, joined_grad, w_query, w_reduce, pooling, pre_c, feature_map, scale_c, shift_c, act_b,
        packed, groups_c,
    )
    send_b, keep_b, pre_a_grad, scale_b_part, shift_b_part, scale_a_part, shift_a_part = run_second_back(
        last_place, act_b_grad, pre_b, scale_b, shift_b, act_a, pre_a, scale_a, shift_a, packed, groups_a, groups_b
    )
    send_a, keep_a = run_first_back(last_place, pre_a_grad, turned_map, blocks, rows_a)
    map_grad = run_map_back(pre_a_grad, lin_c_grad, packed, groups_a)

    merged = reduced + product(hidden_low, w_out)
    joined = jnp.concatenate([regions, low(merged)], axis=1)
    logits_out = low(product(joined, w_head))

    region_parts = [
        low(part).reshape(blocks, part.shape[0] // blocks, part.shape[1])
        for part in (
            dot_tn(regions, reduced_grad),
            dot_tn(reduced_low, query_grad),
            dot_tn(hidden_low, branch_grad),
            dot_tn(joined, own_logit_grad),
        )
    ]

    def over_dp(block):
        if split:
            return lax.all_gather(low(block), "dp", axis=0, tiled=False)
        return lax.psum(low(block), "dp")[None]

    def reduced_part(send, keep):
        rows, width = send.shape[-2:]
        dims = halves + (rows, width)
        return over_dp(reduce_halves(send.reshape(dims), keep.reshape(dims), axes))

    def halved(part):
        pairs = part.reshape((blocks // 2, 2) + part.shape[1:])
        return reduced_part(block_at(pairs, 1 - last_place, 1), block_at(pairs, last_place, 1))

    done_r = halved(jnp.concatenate(region_parts[:3], axis=1))
    done_h = halved(region_parts[3])
    done_c = reduced_part(send_c, keep_c)
    done_b = reduced_part(send_b, keep_b)
    done_a = reduced_part(send_a, keep_a)

    def whole(stacked, first, count):
        picked = wide(stacked[:, first : first + count])
        return picked.reshape(stacked.shape[0] * count, stacked.shape[2])

    rows_reduce = feature_count // blocks
    rows_query = channels // blocks
    reduce_weight_grad = whole(done_r, 0, rows_reduce)
    query_weight_grad = whole(done_r, rows_reduce, rows_query)
    out_weight_grad = whole(done_r, rows_reduce + rows_query, rows_query)
    head_weight_grad = whole(done_h, 0, done_h.shape[1])
    conv_a_grad = whole(done_a, 0, rows_a)
    conv_b_grad = whole(done_b, 0, rows_b)
    done_c = wide(done_c).reshape(-1, chunks, LANE_ROWS, channels).transpose(0, 2, 1, 3)
    conv_c_grad = done_c.reshape(-1, feature_count)

    key_value = lax.psum(jnp.concatenate([key_part, value_part], 0), "dp")
    key_low, value_low = key_value[:keys_here], key_value[keys_here:]
    memory_grad = low(dot_nt(key_low, w_key) + dot_nt(value_low, w_value))
    bank_grad = low(dot_nt(memory_grad, w_bank))
    width = channels // dp_count

    def columns(value):
        return lax.dynamic_slice_in_dim(value, dp_place * width, width, 1)

    bank_parts = [
        low(part).reshape(bank_count, part.shape[0] // bank_count, width)
        for part in (
            dot_tn(bank, columns(memory_grad)),
            dot_tn(memory_low, columns(key_low)),
            dot_tn(memory_low, columns(value_low)),
        )
    ]
    bank_sum = jnp.sum(wide(to_owners(jnp.concatenate(bank_parts, 1))), axis=0)
    bank_done = wide(lax.all_gather(low(bank_sum), "dp", axis=1, tiled=True))
    bank_rows, channel_rows = feature_count // bank_count, channels // bank_count
    bank_weight_grad = bank_done[:bank_rows]
    key_weight_grad = bank_done[bank_rows : bank_rows + channel_rows]
    value_weight_grad = bank_done[bank_rows + channel_rows :]

    vectors = [
        part.reshape(-1)
        for part in (
            gain_part, shift_part, scale_a_part, shift_a_part, scale_b_part, shift_b_part, scale_c_part, shift_c_part
        )
    ]
    summed = sum_everywhere(jnp.concatenate(vectors).reshape(-1, channels), ("dp", "bank")).reshape(-1)
    pieces, start = [], 0
    for vector in vectors:
        count = vector.shape[0] // bank_count
        pieces.append(lax.dynamic_slice_in_dim(summed, start + bank_place * count, count, 0))
        start += vector.shape[0]
    gain_grad, shift_grad = pieces[:2]
    scale_a_grad, shift_a_grad, scale_b_grad, shift_b_grad, scale_c_grad, shift_c_grad = pieces[2:]
    return (
        logits_out,
        map_grad,
        bank_grad,
        conv_a_grad,
        scale_a_grad,
        shift_a_grad,
        conv_b_grad,
        scale_b_grad,
        shift_b_grad,
        conv_c_grad,
        scale_c_grad,
        shift_c_grad,
        reduce_weight_grad,
        bank_weight_grad,
        query_weight_grad,
        key_weight_grad,
        value_weight_grad,
        gain_grad,
        shift_grad,
        out_weight_grad,
        head_weight_grad,
    )


def solution(mesh):
    in_specs = (
        P(("dp", "bank"), None),
        P("bank", None),
        P("dp"),
        P(("dp", "bank"), None),
        P(("dp", "bank"), None),
        P("bank", None),
        P(),
        P(),
        P("bank", None),
        P(),
        P(),
        P("bank", None),
        P(),
        P(),
        P(),
        P(),
        P(),
        P(),
        P(),
        P(),
        P(),
        P(),
        P(),
        P("dp", None),
    )
    out_specs = (
        P(("dp", "bank"), None),
        P(("dp", "bank"), None),
        P("bank", None),
        P("bank", None),
        P("bank"),
        P("bank"),
        P("bank", None),
        P("bank"),
        P("bank"),
        P("bank", None),
        P("bank"),
        P("bank"),
        P("bank", None),
        P("bank", None),
        P("bank", None),
        P("bank", None),
        P("bank", None),
        P("bank"),
        P("bank"),
        P("bank", None),
        P("bank", None),
    )
    return jax.shard_map(body, mesh=mesh, in_specs=in_specs, out_specs=out_specs, check_vma=False)
```

time: 563 us -> 508 us (0.902)
  Pallas kernels: 0 us -> 67.5 us
  matrix products: 89.8 us -> 26 us
  local copies, waits for them, and re-layouts: 97.2 us -> 59.9 us
  other arithmetic: 43.8 us -> 23.3 us
  starting transfers between devices: 72.2 us -> 85.6 us
  waiting for transfers between devices: 180 us -> 171 us
    pallas_call x0 -> x9, Pallas kernels: none -> 67.5 us  [the longest x1 17.3 us: run_third_back(): pl.pallas_call(third_back, out_shape=[shape_of((blocks // 2, rows_c, chan...]
    dot_general x24 -> x14, matrix products: 62.9 us -> 16.2 us  [the longest x5 8.19 us: dot_nt(): lax.dot_general(left, right, (((1,), (1,)), ((), ())), preferred_element_...]
    slice x18 -> x5, local copies, waits for them, and re-layouts: 28.8 us -> 0.64 us  [reduce_halves(): second = low(reduce_over(value[half:], inner, 1))]
    dot_general x13 -> x5, matrix products: 26.9 us -> 9.73 us  [product(): return jnp.dot(left, right, preferred_element_type=jnp.float32)]
    unnamed x142 -> x150, local copies, waits for them, and re-layouts: 23.4 us -> 37.7 us
    all_to_all x5, starting transfers between devices: 25.5 us -> 37.6 us  [to_owners(): lax.all_to_all(value, 'bank', split_axis=0, concat_axis=0, tiled=True)]
    reduce_sum x13 -> x0, other arithmetic: 10.6 us -> none  [the longest x1 4.78 us: body(): jnp.sum(lin_c_grad, axis=0)]
    dynamic_slice x9 -> x5, local copies, waits for them, and re-layouts: 17.1 us -> 6.52 us  [block_at(): return lax.dynamic_index_in_dim(value, place, dim, keepdims=False)]
  transfers between devices with their start and end apart: 52 -> 52, of which waited for: 22 -> 20; matrix products, arithmetic and copies ran while one was open for 25% -> 17% of each run, Pallas kernels for 0% -> 9%
where the time goes in v2:
time: 508 us; the launch traced here: 501 us
  waiting for transfers between devices  171 us (34%)
  starting transfers between devices  85.6 us (17%)
  Pallas kernels  67.5 us (13%)
  local copies, waits for them, and re-layouts  59.9 us (12%)
  blocking collectives  51.9 us (10%)
  matrix products  26 us (5%)
  other arithmetic  23.3 us (5%)
  between operations  15.7 us (3%)
    all_gather x1, waiting for transfers between devices, body(): lax.all_gather(own_packed, ('bank', 'dp') if split else 'bank', axis=0, t...  93.9 us
    ppermute x40, waiting for transfers between devices, swap(): return lax.ppermute(value, self.name, pairs)  69.7 us
    all_gather x5, blocking collectives, over_dp(): return lax.all_gather(low(block), 'dp', axis=0, tiled=False)  44.4 us
    ppermute x40, starting transfers between devices, swap(): return lax.ppermute(value, self.name, pairs)  41 us
    unnamed x150, local copies, waits for them, and re-layouts  37.7 us
    all_to_all x5, starting transfers between devices, to_owners(): lax.all_to_all(value, 'bank', split_axis=0, concat_axis=0, tiled=True)  37.6 us
    pallas_call x1, Pallas kernels, run_third_back(): pl.pallas_call(third_back, out_shape=[shape_of((blocks // 2, rows_c, chan...  17.3 us
    pallas_call x1, Pallas kernels, run_later_convs(): pl.pallas_call(later_convs, out_shape=[jax.ShapeDtypeStruct((sites, chann...  16.2 us
  transfers between devices with their start and end apart: 52, of which 20 were waited for; matrix products, arithmetic and copies ran while one was open for 17% of the time, Pallas kernels for 9%

profile of v2, /device:TPU:9, one launch (start us, length us, event | category | flops | bytes accessed | tf_op | source)
XLA Modules:
  0.0 500.9 jit_solution(5803190646328057315)
XLA Ops:
  18.6 93.9 %all-gather.7.cloned.1.call-done.packed_ref = bf16[32,25,16,512]{3,2,1,0:T(8,128)(2,1)} async-done(((bf16[1,25,16,512]{3,2,1,0:T(8,128)(2,1)}), bf16[32,25,16,512]{3,2,1,0:T(8,128)(2,1)}) %all-gather.7.cloned.1.call-update) | async-done | bytes 13107216 | tf_op jit(solution)/shard_map/all_gather | solution.py:801
  114.1 5.7 %first_conv.1 = (f32[512,512]{1,0:T(8,128)S(1)}, bf16[512,512]{1,0:T(8,128)(2,1)S(1)}) custom-call(bf16[512,2048]{1,0:T(8,128)(2,1)S(1)} %copy-done.1, bf16[32,25,16,512]{3,2,1,0:T(8,128)(2,1)} %all-gather.7.cloned.1.call-done.packed_ref, f32[1,512]{1,0:T(1,128)S(1)} %bitcast.270, f32[1,512]{1,0:T(1,128)S(1)} %bitcast.272), custom_call_target="tpu_custom_call" | custom-call | tf_op jit(solution)/shard_map/first_conv/pallas_call | solution.py:549
  120.8 16.2 %later_convs.1 = (f32[512,512]{1,0:T(8,128)}, bf16[512,512]{1,0:T(8,128)(2,1)S(1)}, f32[512,2048]{1,0:T(8,128)}, bf16[32,2048]{1,0:T(8,128)(2,1)S(1)}, f32[32,51...) custom-call(bf16[512,512]{1,0:T(8,128)(2,1)S(1)} %get-tuple-element.55.act_a_ref, bf16[512,2048]{1,0:T(8,128)(2,1)} %fm_ref.5, ...), custom_call_target="tpu_custom_call" | custom-call | tf_op jit(solution)/shard_map/later_convs/pallas_call | solution.py:573
  139.9 4.4 all-to-all-start
  153.0 6.0 %all-to-all-start.1 = ((bf16[8,32,640]{2,1,0:T(8,128)(2,1)}), bf16[8,32,640]{2,1,0:T(8,128)(2,1)}, u32[]{:S(2)}, u32[]{:S(2)}) async-start(bf16[8,32,640]{2,1,0:T(8,128)(2,1)} %bitcast.264), calls=%async_computation.1 | async-start | bytes 655360 | tf_op jit(solution)/shard_map/all_to_all | solution.py:98
  159.0 3.9 copy.99
  173.1 17.3 %all-to-all-start.2 = ((bf16[8,32,640]{2,1,0:T(8,128)(2,1)}), bf16[8,32,640]{2,1,0:T(8,128)(2,1)S(1)}, u32[]{:S(2)}, u32[]{:S(2)}) async-start(bf16[8,32,640]{2,1,0:T(8,128)(2,1)} %copy-done.21), calls=%async_computation.2 | async-start | bytes 655360 | tf_op jit(solution)/shard_map/all_to_all | solution.py:98
  223.0 9.1 %all-gather.4 = bf16[320,80]{1,0:T(8,128)(2,1)} all-gather(bf16[80,80]{1,0:T(8,128)(2,1)S(1)} %fusion.77), channel_id=6, replica_groups=mesh['dp'=4,'bank'=8] {'dp'}, dimensions={0}, use_global_device_ids=true | all-gather | bytes 64000 | tf_op jit(solution)/shard_map/all_gather | solution.py:859
  237.4 5.4 %all-to-all-start.3 = ((bf16[8,32,512]{2,1,0:T(8,128)(2,1)}), bf16[8,32,512]{2,1,0:T(8,128)(2,1)}, u32[]{:S(2)}, u32[]{:S(2)}) async-start(bf16[8,32,512]{2,1,0:T(8,128)(2,1)} %bitcast.265), calls=%async_computation.3 | async-start | bytes 524288 | tf_op jit(solution)/shard_map/all_to_all | solution.py:98
  250.2 17.3 %third_back.1 = (bf16[16,64,512]{2,1,0:T(8,128)(2,1)}, bf16[16,64,512]{2,1,0:T(8,128)(2,1)}, f32[512,2048]{1,0:T(8,128)}, f32[512,512]{1,0:T(8,128)}, f32[1,2048...) custom-call(s32[1]{0:T(128)} %bitcast.13.place_ref, ...), custom_call_target="tpu_custom_call" | custom-call | tf_op jit(solution)/shard_map/third_back/pallas_call | solution.py:649
  267.6 12.8 %second_back.1 = (bf16[16,144,512]{2,1,0:T(8,128)(2,1)}, bf16[16,144,512]{2,1,0:T(8,128)(2,1)}, bf16[512,512]{1,0:T(8,128)(2,1)S(1)}, f32[1,512]{1,0:T(1,128)S(1...) custom-call(s32[1]{0:T(128)} %bitcast.13.place_ref, ...), custom_call_target="tpu_custom_call" | custom-call | tf_op jit(solution)/shard_map/second_back/pallas_call | solution.py:687
  299.6 8.7 %map_back.1 = bf16[512,2048]{1,0:T(8,128)(2,1)} custom-call(bf16[512,512]{1,0:T(8,128)(2,1)S(1)} %get-tuple-element.69.grad_ref, f32[512,2048]{1,0:T(8,128)S(1)} %copy-done.3, bf16[32,25,16,512]{3,2,1,0:T(8,128)(2,1)} %all-gather.7.cloned.1.call-done.packed_ref), custom_call_target="tpu_custom_call" | custom-call | tf_op jit(solution)/shard_map/map_back/pallas_call | solution.py:729
  319.8 4.4 all-to-all-start.4
  333.1 7.2 %collective-permute-done.24 = bf16[2,2,64,512]{3,2,1,0:T(8,128)(2,1)S(1)} collective-permute-done((bf16[2,2,64,512]{3,2,1,0:T(8,128)(2,1)S(1)}, bf16[2,2,64,512]{3,2,1,0:T(8,128)(2,1)S(1)}, u32[]{:S(2)}, u32[]{:S(2)}) %collective-permute-start.24) | collective-permute-done | bytes 262176 | tf_op jit(solution)/shard_map/ppermute | solution.py:44
  345.3 7.4 %all_gather.45 = bf16[384,512]{0,1:T(8,128)(2,1)S(1)} all-gather(bf16[384,128]{0,1:T(8,128)(2,1)} %reduce_sum.22), channel_id=1, replica_groups=mesh['dp'=4,'bank'=8] {'dp'}, dimensions={1}, use_global_device_ids=true | all-gather | bytes 491520 | tf_op jit(solution)/shard_map/all_gather | solution.py:910
  372.5 7.0 %collective-permute-done.32 = bf16[2,2,96,512]{3,2,1,0:T(8,128)(2,1)S(1)} collective-permute-done((bf16[2,2,96,512]{3,2,1,0:T(8,128)(2,1)S(1)}, bf16[2,2,96,512]{3,2,1,0:T(8,128)(2,1)S(1)}, u32[]{:S(2)}, u32[]{:S(2)}) %collective-permute-start.32) | collective-permute-done | bytes 393248 | tf_op jit(solution)/shard_map/ppermute | solution.py:44
  388.9 8.4 %all-gather.2 = bf16[256,512]{1,0:T(8,128)(2,1)S(1)} all-gather(bf16[64,512]{1,0:T(8,128)(2,1)S(1)} %fusion.53), channel_id=4, replica_groups=mesh['dp'=4,'bank'=8] {'dp'}, dimensions={0}, use_global_device_ids=true | all-gather | bytes 327680 | tf_op jit(solution)/shard_map/all_gather | solution.py:859
  398.6 6.8 %all-gather.3 = bf16[384,512]{1,0:T(8,128)(2,1)S(1)} all-gather(bf16[96,512]{1,0:T(8,128)(2,1)S(1)} %fusion.40), channel_id=5, replica_groups=mesh['dp'=4,'bank'=8] {'dp'}, dimensions={0}, use_global_device_ids=true | all-gather | bytes 491520 | tf_op jit(solution)/shard_map/all_gather | solution.py:859
  411.1 12.8 %collective-permute-done.14 = bf16[2,2,144,512]{3,2,0,1:T(8,128)(2,1)S(1)} collective-permute-done((bf16[2,2,144,512]{3,2,0,1:T(8,128)(2,1)S(1)}, bf16[2,2,144,512]{3,2,0,1:T(8,128)(2,1)S(1)}, u32[]{:S(2)}, u32[]{:S(2)}) %collective-permute-start.14) | collective-permute-done | bytes 589856 | tf_op jit(solution)/shard_map/ppermute | solution.py:44
  431.8 18.6 %collective-permute-done.17 = bf16[2,144,512]{2,1,0:T(8,128)(2,1)S(1)} collective-permute-done((bf16[2,144,512]{2,1,0:T(8,128)(2,1)S(1)}, bf16[2,144,512]{2,1,0:T(8,128)(2,1)S(1)}, u32[]{:S(2)}, u32[]{:S(2)}) %collective-permute-start.17) | collective-permute-done | bytes 294944 | tf_op jit(solution)/shard_map/ppermute | solution.py:44
  457.1 7.0 %collective-permute-done.19 = bf16[144,512]{1,0:T(8,128)(2,1)S(1)} collective-permute-done((bf16[144,512]{1,0:T(8,128)(2,1)S(1)}, bf16[144,512]{1,0:T(8,128)(2,1)S(1)}, u32[]{:S(2)}, u32[]{:S(2)}) %collective-permute-start.19) | collective-permute-done | bytes 147488 | tf_op jit(solution)/shard_map/ppermute | solution.py:44
  465.4 4.0 collective-permute-start.6
  469.4 9.9 %all-gather.1 = bf16[576,512]{1,0:T(8,128)(2,1)S(1)} all-gather(bf16[144,512]{1,0:T(8,128)(2,1)S(1)} %fusion.26), channel_id=3, replica_groups=mesh['dp'=4,'bank'=8] {'dp'}, dimensions={0}, use_global_device_ids=true | all-gather | bytes 737280 | tf_op jit(solution)/shard_map/all_gather | solution.py:859
  482.1 10.2 %all-gather = bf16[768,512]{1,0:T(8,128)(2,1)S(1)} all-gather(bf16[192,512]{1,0:T(8,128)(2,1)S(1)} %fusion.23), channel_id=2, replica_groups=mesh['dp'=4,'bank'=8] {'dp'}, dimensions={0}, use_global_device_ids=true | all-gather | bytes 983040 | tf_op jit(solution)/shard_map/all_gather | solution.py:859
  (364 shorter events, 180.5 us)
Async XLA Ops:
  7.2 105.3 %all-gather.7.cloned.1.call-start = ((), (), s32[]{:S(2)}) async-start(), calls=%async_computation.5 | async-start | bytes 13516800 | tf_op jit(solution)/shard_map/all_gather | solution.py:801
  153.0 13.3 %all-to-all-start.1 = ((bf16[8,32,640]{2,1,0:T(8,128)(2,1)}), bf16[8,32,640]{2,1,0:T(8,128)(2,1)}, u32[]{:S(2)}, u32[]{:S(2)}) async-start(bf16[8,32,640]{2,1,0:T(8,128)(2,1)} %bitcast.264), calls=%async_computation.1 | async-start | bytes 655360 | tf_op jit(solution)/shard_map/all_to_all | solution.py:98
  173.1 60.6 %all-to-all-start.2 = ((bf16[8,32,640]{2,1,0:T(8,128)(2,1)}), bf16[8,32,640]{2,1,0:T(8,128)(2,1)S(1)}, u32[]{:S(2)}, u32[]{:S(2)}) async-start(bf16[8,32,640]{2,1,0:T(8,128)(2,1)} %copy-done.21), calls=%async_computation.2 | async-start | bytes 655360 | tf_op jit(solution)/shard_map/all_to_all | solution.py:98
  237.4 12.7 %all-to-all-start.3 = ((bf16[8,32,512]{2,1,0:T(8,128)(2,1)}), bf16[8,32,512]{2,1,0:T(8,128)(2,1)}, u32[]{:S(2)}, u32[]{:S(2)}) async-start(bf16[8,32,512]{2,1,0:T(8,128)(2,1)} %bitcast.265), calls=%async_computation.3 | async-start | bytes 524288 | tf_op jit(solution)/shard_map/all_to_all | solution.py:98
  242.9 65.7 %all-reduce.2.cloned.1.call-start = ((), (), s32[]{:S(2)}) async-start(), calls=%async_computation.6 | async-start | bytes 2097152 | tf_op jit(solution)/shard_map/psum | solution.py:892
  280.5 15.5 %collective-permute-start.8 = (f32[14,512]{1,0:T(8,128)S(1)}, f32[14,512]{1,0:T(8,128)S(1)}, u32[]{:S(2)}, u32[]{:S(2)}) collective-permute-start(f32[14,512]{1,0:T(8,128)S(1)} %reshape.303), channel_id=1, source_target_pairs={{0,8},{8,0},{16,24},{24,16},{1,9},{9,1},{17,25},{25,17},{2,10},{10... | collective-permute-start | bytes 86024 | tf_op jit(solution)/shard_map/ppermute | solution.py:92
  286.3 120.0 %collective-permute-start.13 = (bf16[4,2,2,144,512]{4,3,0,2,1:T(8,128)(2,1)}, bf16[4,2,2,144,512]{4,3,0,2,1:T(8,128)(2,1)}, u32[]{:S(2)}, u32[]{:S(2)}) collective-permute-start(bf16[4,2,2,144,512]{4,3,0,2,1:T(8,128)(2,1)} %copy.102), channel_id=1, source_target_pairs={{0,8},{8,0},{16,24},{24,16},{1,9},{9,1},{17,25},{25,17},{2,10},{10... | collective-permute-start | bytes 7077896 | tf_op jit(solution)/shard_map/ppermute | solution.py:44
  295.6 28.6 %collective-permute-start.21 = (bf16[4,2,2,64,512]{4,3,2,1,0:T(8,128)(2,1)}, bf16[4,2,2,64,512]{4,3,2,1,0:T(8,128)(2,1)}, u32[]{:S(2)}, u32[]{:S(2)}) collective-permute-start(bf16[4,2,2,64,512]{4,3,2,1,0:T(8,128)(2,1)} %bitcast.54), channel_id=1, source_target_pairs={{0,8},{8,0},{16,24},{24,16},{1,9},{9,1},{17,25},{25,17},{2,10},{10... | collective-permute-start | bytes 3145736 | tf_op jit(solution)/shard_map/ppermute | solution.py:44
  296.0 12.3 %collective-permute-start.9 = (f32[14,512]{1,0:T(8,128)S(1)}, f32[14,512]{1,0:T(8,128)S(1)}, u32[]{:S(2)}, u32[]{:S(2)}) collective-permute-start(f32[14,512]{1,0:T(8,128)S(1)} %add.334), channel_id=1, source_target_pairs={{0,16},{8,24},{16,0},{24,8},{1,17},{9,25},{17,1},{25,9},{2,18},{10... | collective-permute-start | bytes 86024 | tf_op jit(solution)/shard_map/ppermute | solution.py:92
  299.3 55.3 %collective-permute-start.29 = (bf16[4,2,2,96,512]{4,3,2,1,0:T(8,128)(2,1)}, bf16[4,2,2,96,512]{4,3,2,1,0:T(8,128)(2,1)}, u32[]{:S(2)}, u32[]{:S(2)}) collective-permute-start(bf16[4,2,2,96,512]{4,3,2,1,0:T(8,128)(2,1)} %bitcast.73), channel_id=1, source_target_pairs={{0,8},{8,0},{16,24},{24,16},{1,9},{9,1},{17,25},{25,17},{2,10},{10... | collective-permute-start | bytes 4718600 | tf_op jit(solution)/shard_map/ppermute | solution.py:44
  319.8 21.4 %all-to-all-start.4 = ((bf16[8,384,128]{1,2,0:T(8,128)(2,1)}), bf16[8,384,128]{1,2,0:T(8,128)(2,1)S(1)}, u32[]{:S(2)}, u32[]{:S(2)}) async-start(bf16[8,384,128]{1,2,0:T(8,128)(2,1)} %pad_maximum_fusion.2), calls=%async_computation.4 | async-start | bytes 1572864 | tf_op jit(solution)/shard_map/all_to_all | solution.py:98
  331.9 12.5 %collective-permute-start.23 = (bf16[2,64,512]{2,1,0:T(8,128)(2,1)S(1)}, bf16[2,64,512]{2,1,0:T(8,128)(2,1)}, u32[]{:S(2)}, u32[]{:S(2)}) collective-permute-start(bf16[2,64,512]{2,1,0:T(8,128)(2,1)S(1)} %dynamic-slice_bitcast_fusion.13), channel_id=1, source_target_pairs={{0,1},{1,0},{2,3},{3,2},{4,5},{5,4},{6,7},{7,6},{8,9},{9,8},{10,11... | collective-permute-start | bytes 393224 | tf_op jit(solution)/shard_map/ppermute | solution.py:44
  367.8 57.1 %collective-permute-start = (bf16[4,2,2,192,512]{4,3,0,2,1:T(8,128)(2,1)}, bf16[4,2,2,192,512]{4,3,0,2,1:T(8,128)(2,1)S(1)}, u32[]{:S(2)}, u32[]{:S(2)}) collective-permute-start(bf16[4,2,2,192,512]{4,3,0,2,1:T(8,128)(2,1)} %copy.100), channel_id=1, source_target_pairs={{0,8},{8,0},{16,24},{24,16},{1,9},{9,1},{17,25},{25,17},{2,10},{10... | collective-permute-start | bytes 9437192 | tf_op jit(solution)/shard_map/ppermute | solution.py:44
  385.0 13.5 %collective-permute-start.36 = (bf16[96,512]{1,0:T(8,128)(2,1)S(1)}, bf16[96,512]{1,0:T(8,128)(2,1)S(1)}, u32[]{:S(2)}, u32[]{:S(2)}) collective-permute-start(bf16[96,512]{1,0:T(8,128)(2,1)S(1)} %get-tuple-element.182), channel_id=1, source_target_pairs={{0,6},{1,7},{2,4},{3,5},{4,2},{5,3},{6,0},{7,1},{8,14},{9,15},{10,... | collective-permute-start | bytes 294920 | tf_op jit(solution)/shard_map/ppermute | solution.py:44
  386.3 12.2 %collective-permute-start.35 = (bf16[96,512]{1,0:T(8,128)(2,1)S(1)}, bf16[96,512]{1,0:T(8,128)(2,1)S(1)}, u32[]{:S(2)}, u32[]{:S(2)}) collective-permute-start(bf16[96,512]{1,0:T(8,128)(2,1)S(1)} %get-tuple-element.181), channel_id=1, source_target_pairs={{0,4},{1,5},{2,6},{3,7},{4,0},{5,1},{6,2},{7,3},{8,12},{9,13},{10,... | collective-permute-start | bytes 294920 | tf_op jit(solution)/shard_map/ppermute | solution.py:44
  409.0 14.8 %collective-permute-start.14 = (bf16[2,2,144,512]{3,2,0,1:T(8,128)(2,1)S(1)}, bf16[2,2,144,512]{3,2,0,1:T(8,128)(2,1)S(1)}, u32[]{:S(2)}, u32[]{:S(2)}) collective-permute-start(bf16[2,2,144,512]{3,2,0,1:T(8,128)(2,1)S(1)} %dynamic-slice_bitcast_fusion.3), channel_id=1, source_target_pairs={{0,16},{8,24},{16,0},{24,8},{1,17},{9,25},{17,1},{25,9},{2,18},{10... | collective-permute-start | bytes 1769480 | tf_op jit(solution)/shard_map/ppermute | solution.py:44
  410.0 14.7 %collective-permute-start.16 = (bf16[2,2,144,512]{3,2,0,1:T(8,128)(2,1)S(1)}, bf16[2,2,144,512]{3,2,0,1:T(8,128)(2,1)S(1)}, u32[]{:S(2)}, u32[]{:S(2)}) collective-permute-start(bf16[2,2,144,512]{3,2,0,1:T(8,128)(2,1)S(1)} %dynamic-slice_bitcast_fusion.2), channel_id=1, source_target_pairs={{0,1},{1,0},{2,3},{3,2},{4,5},{5,4},{6,7},{7,6},{8,9},{9,8},{10,11... | collective-permute-start | bytes 1769480 | tf_op jit(solution)/shard_map/ppermute | solution.py:44
  426.2 28.4 %collective-permute-start.1 = (bf16[2,2,192,512]{3,2,0,1:T(8,128)(2,1)S(1)}, bf16[2,2,192,512]{3,2,0,1:T(8,128)(2,1)S(1)}, u32[]{:S(2)}, u32[]{:S(2)}) collective-permute-start(bf16[2,2,192,512]{3,2,0,1:T(8,128)(2,1)S(1)} %dynamic-slice_bitcast_fusion.1), channel_id=1, source_target_pairs={{0,16},{8,24},{16,0},{24,8},{1,17},{9,25},{17,1},{25,9},{2,18},{10... | collective-permute-start | bytes 2359304 | tf_op jit(solution)/shard_map/ppermute | solution.py:44
  426.9 23.5 %collective-permute-start.17 = (bf16[2,144,512]{2,1,0:T(8,128)(2,1)S(1)}, bf16[2,144,512]{2,1,0:T(8,128)(2,1)S(1)}, u32[]{:S(2)}, u32[]{:S(2)}) collective-permute-start(bf16[2,144,512]{2,1,0:T(8,128)(2,1)S(1)} %dynamic-slice_bitcast_fusion.7), channel_id=1, source_target_pairs={{0,16},{8,24},{16,0},{24,8},{1,17},{9,25},{17,1},{25,9},{2,18},{10... | collective-permute-start | bytes 884744 | tf_op jit(solution)/shard_map/ppermute | solution.py:44
  427.9 27.9 %collective-permute-start.3 = (bf16[2,2,192,512]{3,2,0,1:T(8,128)(2,1)S(1)}, bf16[2,2,192,512]{3,2,0,1:T(8,128)(2,1)S(1)}, u32[]{:S(2)}, u32[]{:S(2)}) collective-permute-start(bf16[2,2,192,512]{3,2,0,1:T(8,128)(2,1)S(1)} %dynamic-slice_bitcast_fusion), channel_id=1, source_target_pairs={{0,1},{1,0},{2,3},{3,2},{4,5},{5,4},{6,7},{7,6},{8,9},{9,8},{10,11... | collective-permute-start | bytes 2359304 | tf_op jit(solution)/shard_map/ppermute | solution.py:44
  451.8 12.4 %collective-permute-start.19 = (bf16[144,512]{1,0:T(8,128)(2,1)S(1)}, bf16[144,512]{1,0:T(8,128)(2,1)S(1)}, u32[]{:S(2)}, u32[]{:S(2)}) collective-permute-start(bf16[144,512]{1,0:T(8,128)(2,1)S(1)} %get-tuple-element.172), channel_id=1, source_target_pairs={{0,4},{1,5},{2,6},{3,7},{4,0},{5,1},{6,2},{7,3},{8,12},{9,13},{10,... | collective-permute-start | bytes 442376 | tf_op jit(solution)/shard_map/ppermute | solution.py:44
  464.8 15.7 %collective-permute-start.7 = (bf16[192,512]{1,0:T(8,128)(2,1)S(1)}, bf16[192,512]{1,0:T(8,128)(2,1)S(1)}, u32[]{:S(2)}, u32[]{:S(2)}) collective-permute-start(bf16[192,512]{1,0:T(8,128)(2,1)S(1)} %get-tuple-element.168), channel_id=1, source_target_pairs={{0,6},{1,7},{2,4},{3,5},{4,2},{5,3},{6,0},{7,1},{8,14},{9,15},{10,... | collective-permute-start | bytes 589832 | tf_op jit(solution)/shard_map/ppermute | solution.py:44
  465.4 16.6 %collective-permute-start.6 = (bf16[192,512]{1,0:T(8,128)(2,1)S(1)}, bf16[192,512]{1,0:T(8,128)(2,1)S(1)}, u32[]{:S(2)}, u32[]{:S(2)}) collective-permute-start(bf16[192,512]{1,0:T(8,128)(2,1)S(1)} %get-tuple-element.167), channel_id=1, source_target_pairs={{0,4},{1,5},{2,6},{3,7},{4,0},{5,1},{6,2},{7,3},{8,12},{9,13},{10,... | collective-permute-start | bytes 589832 | tf_op jit(solution)/shard_map/ppermute | solution.py:44
  469.4 12.6 %collective-permute-start.5 = (bf16[192,512]{1,0:T(8,128)(2,1)S(1)}, bf16[192,512]{1,0:T(8,128)(2,1)S(1)}, u32[]{:S(2)}, u32[]{:S(2)}) collective-permute-start(bf16[192,512]{1,0:T(8,128)(2,1)S(1)} %get-tuple-element.166), channel_id=1, source_target_pairs={{0,2},{1,3},{2,0},{3,1},{4,6},{5,7},{6,4},{7,5},{8,10},{9,11},{10,... | collective-permute-start | bytes 589832 | tf_op jit(solution)/shard_map/ppermute | solution.py:44
  (91 other events, 986.7 us)
Sparse Core Ops, SparseCore 0:
  13.1 99.3 all-gather.6
  246.8 36.3 all-reduce.1

commit v3 on v2

v3 whole, which is shorter than its diff:
```python
import functools

import jax
import jax.numpy as jnp
from jax import lax
from jax.experimental import pallas as pl
from jax.experimental.pallas import tpu as pltpu
from jax.sharding import PartitionSpec as P

FRAMES = 4
SIDE = 8
LANE_ROWS = 16
TILE = 128
ROOT = 0.7978845608028654
CUBIC = 0.044715

epsilon = 1e-05
masked_score = -1e30
places = [(-1, -1), (-1, 0), (-1, 1), (0, -1), (0, 0), (0, 1), (1, -1), (1, 0), (1, 1)]


def product(left, right):
    return jnp.dot(left, right, preferred_element_type=jnp.float32)


def low(value):
    return value.astype(jnp.bfloat16)


def wide(value):
    return value.astype(jnp.float32)


class SubAxis:
    def __init__(self, name, size, stride):
        self.name, self.size, self.stride = name, size, stride

    def place(self):
        return lax.rem(lax.axis_index(self.name) // self.stride, self.size)

    def swap(self, value, step):
        count = lax.axis_size(self.name)
        pairs = [(i, i ^ (step * self.stride)) for i in range(count)]
        return lax.ppermute(value, self.name, pairs)


def block_axes(split, dp_count, bank_count):
    if split:
        return (
            SubAxis("bank", bank_count // 2, 2),
            SubAxis("bank", 2, 1),
            SubAxis("dp", dp_count // 2, 2),
            SubAxis("dp", 2, 1),
        )
    return (
        SubAxis("bank", bank_count // 8, 8),
        SubAxis("bank", 2, 4),
        SubAxis("bank", 2, 2),
        SubAxis("bank", 2, 1),
    )


def to_owners(value):
    return lax.all_to_all(value, "bank", split_axis=0, concat_axis=0, tiled=True)


def to_group(value):
    count = lax.axis_size("bank")
    return to_owners(jnp.broadcast_to(value[None], (count,) + value.shape))


def params(mib):
    return pltpu.CompilerParams(vmem_limit_bytes=mib * 1024 * 1024)


def gelu_of(x):
    return 0.5 * x * (1.0 + jnp.tanh(ROOT * (x + CUBIC * x * x * x)))


def gelu_slope(x):
    square = x * x
    bent = jnp.tanh(ROOT * x * (1.0 + CUBIC * square))
    return 0.5 * (1.0 + bent) + 0.5 * ROOT * x * (1.0 - bent * bent) * (1.0 + 3.0 * CUBIC * square)


def by_rows(count, step, work):
    def one(number, carry):
        work(pl.ds(pl.multiple_of(number * step, step), step))
        return carry

    lax.fori_loop(0, count // step, one, 0)


def dot_tn(left, right):
    return lax.dot_general(
        left, right, (((0,), (0,)), ((), ())), preferred_element_type=jnp.float32
    )


def dot_nt(left, right):
    return lax.dot_general(
        left, right, (((1,), (1,)), ((), ())), preferred_element_type=jnp.float32
    )


def in_rows(value, step):
    if step == 0:
        return value
    sites, width = value.shape
    tall = value.reshape(sites // (SIDE * SIDE), SIDE, SIDE, width)
    edge = jnp.zeros_like(tall[:, :1])
    if step > 0:
        tall = jnp.concatenate([tall[:, 1:], edge], axis=1)
    else:
        tall = jnp.concatenate([edge, tall[:, :-1]], axis=1)
    return tall.reshape(sites, width)


def in_columns(value, step):
    if step == 0:
        return value
    sites = value.shape[0]
    turned = pltpu.roll(value, (-step) % sites, 0)
    column = lax.broadcasted_iota(jnp.int32, value.shape, 0) % SIDE
    keep = column != (SIDE - 1 if step > 0 else 0)
    return jnp.where(keep, turned, 0.0)


def fetch(source, target, sems, first, groups):
    copies = []
    for block in range(source.shape[0]):
        copies.append(
            pltpu.make_async_copy(
                source.at[block, pl.ds(first, groups)],
                target.at[pl.ds(block * groups, groups)],
                sems.at[block],
            )
        )
    return copies


def fetch_columns(source, target, sems, first, groups):
    return [
        pltpu.make_async_copy(
            source.at[block, pl.ds(first, groups)], target.at[:, block], sems.at[block]
        )
        for block in range(source.shape[0])
    ]


def start_all(copies):
    for copy in copies:
        copy.start()
    return copies


def wait_all(copies):
    for copy in copies:
        copy.wait()


def first_conv(fm_ref, packed_ref, scale_ref, shift_ref, pre_out_ref, act_ref, weight_out_ref, weight, pre_ref, sems, out_sems):
    sites, features = fm_ref.shape
    channels = pre_ref.shape[1]
    groups = weight.shape[0] // packed_ref.shape[0]
    copies = fetch(packed_ref, weight, sems, 0, groups)
    for copy in copies:
        copy.start()
    block_rows = groups * LANE_ROWS
    clip = FRAMES * SIDE * SIDE
    frame = SIDE * SIDE
    waited = 0

    def tap(number):
        nonlocal waited
        end = (number + 1) * features
        while waited < len(copies) and waited * block_rows < end:
            copies[waited].wait()
            waited += 1
        begin = number * features // LANE_ROWS
        return weight[begin : begin + features // LANE_ROWS].reshape(features, channels)

    before = tap(0)
    for start in range(0, sites, clip):
        pre_ref[start : start + frame] = jnp.zeros((frame, channels), jnp.float32)
        pre_ref[start + frame : start + clip] = product(fm_ref[start : start + clip - frame], before)
    pre_ref[...] += product(fm_ref[...], tap(1))
    after = tap(2)
    out = start_all([pltpu.make_async_copy(weight, weight_out_ref, out_sems.at[1])])
    for start in range(0, sites, clip):
        pre_ref[start : start + clip - frame] += product(fm_ref[start + frame : start + clip], after)

    def finish(rows):
        act_ref[rows] = low(gelu_of(pre_ref[rows] * scale_ref[...] + shift_ref[...]))

    out += start_all([pltpu.make_async_copy(pre_ref, pre_out_ref, out_sems.at[0])])
    by_rows(sites, 64, finish)
    wait_all(out)


def later_convs(
    act_a_ref, fm_ref, packed_ref, scale_b_ref, shift_b_ref, scale_c_ref, shift_c_ref, pool_ref, w_reduce_ref, w_query_ref,
    pre_b_out_ref, act_b_out_ref, pre_c_ref, regions_ref, reduced_ref, queries_ref,
    weight_b, weight_c, out_low, held_map, held_pre, held_reduce, pre_b_ref, act_b_ref, sems_b, sems_c, sems,
):
    sites, channels = act_a_ref.shape
    blocks = packed_ref.shape[0]
    groups_b = weight_b.shape[0] // blocks
    groups_c = weight_c.shape[0]
    groups_a = packed_ref.shape[1] - groups_b - groups_c
    copies_b = start_all(fetch(packed_ref, weight_b, sems_b, groups_a, groups_b))
    copies_c = start_all(fetch_columns(packed_ref, weight_c, sems_c, groups_a + groups_b, groups_c))
    others = start_all(
        [
            pltpu.make_async_copy(fm_ref, held_map, sems.at[0]),
            pltpu.make_async_copy(w_reduce_ref, held_reduce, sems.at[1]),
        ]
    )
    act_a = act_a_ref[...]
    block_rows = groups_b * LANE_ROWS
    sums = {-1: None, 0: None, 1: None}
    waited = 0
    for number, (rise, slide) in enumerate(places):
        while waited < len(copies_b) and waited * block_rows < (number + 1) * channels:
            copies_b[waited].wait()
            waited += 1
        begin = number * channels // LANE_ROWS
        tap = weight_b[begin : begin + channels // LANE_ROWS].reshape(channels, channels)
        part = in_rows(product(act_a, tap), rise)
        sums[slide] = part if sums[slide] is None else sums[slide] + part
    pre_b_ref[...] = sums[0] + in_columns(sums[1], 1) + in_columns(sums[-1], -1)

    outs = start_all([pltpu.make_async_copy(pre_b_ref, pre_b_out_ref, sems.at[2 + groups_c])])

    def finish(rows):
        act_b_ref[rows] = low(gelu_of(pre_b_ref[rows] * scale_b_ref[...] + shift_b_ref[...]))

    by_rows(sites, 64, finish)
    outs += start_all([pltpu.make_async_copy(act_b_ref, act_b_out_ref, sems.at[3 + groups_c])])
    wait_all(copies_c + others)
    reduced_ref[...] = jnp.zeros_like(reduced_ref)

    def chunk(number, carry):
        columns = pl.ds(pl.multiple_of(number * channels, channels), channels)
        held_pre[:, columns] = product(act_b_ref[...], weight_c[number].reshape(channels, channels))
        pltpu.make_async_copy(held_pre.at[:, columns], pre_c_ref.at[:, columns], sems.at[2 + number]).start()

        def finish_c(rows):
            linear = wide(held_map[rows, columns]) + held_pre[rows, columns] * scale_c_ref[:, columns] + shift_c_ref[:, columns]
            out_low[rows] = low(gelu_of(linear))

        by_rows(sites, 64, finish_c)
        part = low(product(pool_ref[...], out_low[...]))
        regions_ref[:, columns] = part
        reduced_ref[...] += product(part, held_reduce[columns])
        return carry

    lax.fori_loop(0, groups_c, chunk, 0)
    queries = low(product(low(reduced_ref[...]), w_query_ref[...]))
    for place in range(queries_ref.shape[0]):
        queries_ref[place] = queries
    for number in range(groups_c):
        columns = pl.ds(number * channels, channels)
        outs.append(pltpu.make_async_copy(held_pre.at[:, columns], pre_c_ref.at[:, columns], sems.at[2 + number]))
    wait_all(outs)


def column_tile(columns, shape):
    lane = lax.broadcasted_iota(jnp.int32, shape, len(shape) - 1)
    tile = jnp.zeros(shape, jnp.float32)
    for number, column in enumerate(columns):
        rest = column
        for third in range(3):
            piece = wide(low(rest))
            tile = jnp.where(lane == 3 * number + third, piece, tile)
            rest = rest - piece
    return low(tile)


def from_tile(tile, number):
    lane = lax.broadcasted_iota(jnp.int32, tile.shape, tile.ndim - 1)
    picked = jnp.where((lane >= 3 * number) & (lane < 3 * number + 3), wide(tile), 0.0)
    return jnp.sum(picked, axis=-1, keepdims=True)


def attend(half_span, places_ref, queries_ref, keys_ref, values_ref, time_ref, message_ref, scores_ref):
    channels = queries_ref.shape[1]
    positions = places_ref[5] + lax.broadcasted_iota(jnp.int32, scores_ref.shape, 1)
    visible = jnp.abs(time_ref[...] - positions) <= half_span
    scores = dot_nt(queries_ref[...], keys_ref[...]) * (channels ** (-0.5))
    scores = jnp.where(visible, scores, masked_score)
    scores_ref[...] = scores
    top = jnp.max(scores, axis=1, keepdims=True)
    weights = jnp.exp(scores - top)
    total = jnp.sum(weights, axis=1, keepdims=True)
    message_ref[:, :channels] = low(product(low(weights), values_ref[...]))
    message_ref[:, channels:] = column_tile([top, total], (scores.shape[0], TILE))


def merge_rows(places_ref, arrived_ref, hidden_grad_ref, gain_ref, shift_ref, message_ref, hidden_ref, gain_out_ref, shift_out_ref):
    count, own, packed = arrived_ref.shape
    channels = hidden_grad_ref.shape[1]
    tops = from_tile(arrived_ref[:, :, channels:], 0)
    totals = from_tile(arrived_ref[:, :, channels:], 1)
    top = jnp.max(tops, axis=0)
    factors = jnp.exp(tops - top[None])
    total = jnp.sum(factors * totals, axis=0)
    numer = jnp.sum(factors * wide(arrived_ref[:, :, :channels]), axis=0)
    attended = numer / total
    centred = attended - jnp.mean(attended, axis=1, keepdims=True)
    spread = lax.rsqrt(jnp.mean(centred * centred, axis=1, keepdims=True) + epsilon)
    unit = centred * spread
    normed = unit * gain_ref[...] + shift_ref[...]
    hidden_ref[...] = low(gelu_of(normed))
    normed_grad = hidden_grad_ref[...] * gelu_slope(normed)
    gain_out_ref[...] = jnp.sum(normed_grad * unit, axis=0, keepdims=True)
    shift_out_ref[...] = jnp.sum(normed_grad, axis=0, keepdims=True)
    unit_grad = normed_grad * gain_ref[...]
    attended_grad = spread * (
        unit_grad
        - jnp.mean(unit_grad, axis=1, keepdims=True)
        - unit * jnp.mean(unit_grad * unit, axis=1, keepdims=True)
    )
    centre = jnp.sum(attended_grad * attended, axis=1, keepdims=True) / total
    numer_grad = low(attended_grad / total)
    tile = column_tile([top, centre], (own, TILE))
    for place in range(count):
        message_ref[place, :, :channels] = numer_grad
        message_ref[place, :, channels:] = tile


def attend_back(places_ref, arrived_ref, scores_ref, keys_ref, values_ref, part_ref, score_grad_ref, weights_ref):
    channels = keys_ref.shape[1]
    top = from_tile(arrived_ref[:, channels:], 0)
    centre = from_tile(arrived_ref[:, channels:], 1)
    weights = jnp.exp(scores_ref[...] - top)
    weights_ref[...] = low(weights)
    prob_grad = dot_nt(arrived_ref[:, :channels], values_ref[...])
    score_grad = low(weights * (prob_grad - centre) * (channels ** (-0.5)))
    score_grad_ref[...] = score_grad
    part_ref[...] = low(product(score_grad, keys_ref[...]))


def half_of(place_ref, bit):
    return jnp.where(place_ref[3] == bit, 1, 0)


def fold(value):
    return jnp.sum(value.reshape(value.shape[0] // 8, 8, value.shape[1]), axis=0)


def region_back(
    places_ref, arrived_ref, joined_grad_ref, w_query_ref, w_reduce_ref, query_grad_ref, reduced_grad_ref, regions_grad_ref
):
    features = regions_grad_ref.shape[1]
    query_grad = low(jnp.sum(wide(arrived_ref[...]), axis=0))
    query_grad_ref[...] = query_grad
    reduced_grad = low(joined_grad_ref[:, features:] + dot_nt(query_grad, w_query_ref[...]))
    reduced_grad_ref[...] = reduced_grad
    regions_grad_ref[...] = low(joined_grad_ref[:, :features] + dot_nt(reduced_grad, w_reduce_ref[...]))


def hand_out(buffer, send_ref, keep_ref, sems):
    copies = [
        pltpu.make_async_copy(buffer.at[number], target, sems.at[number])
        for number, target in enumerate((send_ref, keep_ref))
    ]
    for copy in copies:
        copy.start()
    for copy in copies:
        copy.wait()


def store_rows(buffer, place_ref, value, first, rows):
    at, end = first, first + value.shape[0]
    while at < end:
        block, offset = divmod(at, rows)
        count = min(rows - offset, end - at)
        buffer[half_of(place_ref, block % 2), block // 2, offset : offset + count] = value[at - first : at - first + count]
        at += count


def slope_back(upstream_ref, pre_ref, scale_ref, shift_ref, out_ref, scale_out_ref, shift_out_ref):
    sites, channels = pre_ref.shape

    def one(step, sums):
        rows = pl.ds(pl.multiple_of(step * 64, 64), 64)
        pre = pre_ref[rows]
        grad = upstream_ref[rows] * gelu_slope(pre * scale_ref[...] + shift_ref[...])
        out_ref[rows] = low(grad * scale_ref[...]).astype(out_ref.dtype)
        return sums[0] + fold(grad * pre), sums[1] + fold(grad)

    zero = jnp.zeros((8, channels), jnp.float32)
    scale_sum, shift_sum = lax.fori_loop(0, sites // 64, one, (zero, zero))
    scale_out_ref[...] = jnp.sum(scale_sum, axis=0, keepdims=True)
    shift_out_ref[...] = jnp.sum(shift_sum, axis=0, keepdims=True)


def later_back(
    groups_a, groups_b, place_ref, regions_grad_ref, pool_ref, scale_ref, shift_ref, scales_ref, pre_c_ref, fm_ref, act_b_ref,
    pre_b_ref, act_a_ref, pre_a_ref, packed_ref,
    send_ref, keep_ref, lin_c_grad_ref, pre_a_grad_ref, scale_c_out_ref, shift_c_out_ref, scale_b_out_ref, shift_b_out_ref,
    scale_a_out_ref, shift_a_out_ref,
    weight_b, weight_c, buffer, out_grad, pre_grad, turned, act_grad, wide_grad,
    held_pre_c, held_map, held_act_b, held_pre_b, held_act_a, held_pre_a, held_lin, sems_b, sems_c, out_sems, sems,
):
    sites, features = held_map.shape
    channels = held_act_b.shape[1]
    chunks, blocks = weight_c.shape[0], weight_c.shape[1]
    rows_b = groups_b * LANE_ROWS

    def part_of(source, target, number, sem):
        columns = pl.ds(pl.multiple_of(number * channels, channels), channels)
        return pltpu.make_async_copy(source.at[:, columns], target.at[:, columns], sems.at[sem + number])

    early = start_all([pltpu.make_async_copy(act_b_ref, held_act_b, sems.at[0])])
    copies_c = start_all(fetch_columns(packed_ref, weight_c, sems_c, groups_a + groups_b, chunks))
    for number in range(chunks):
        part_of(pre_c_ref, held_pre_c, number, 4).start()
        part_of(fm_ref, held_map, number, 4 + chunks).start()
    late = start_all(
        [
            pltpu.make_async_copy(pre_b_ref, held_pre_b, sems.at[1]),
            pltpu.make_async_copy(act_a_ref, held_act_a, sems.at[2]),
            pltpu.make_async_copy(pre_a_ref, held_pre_a, sems.at[3]),
        ]
    )
    copies_b = start_all(fetch(packed_ref, weight_b, sems_b, groups_a, groups_b))
    scale_b_ref, shift_b_ref, scale_a_ref, shift_a_ref = [scales_ref.at[pl.ds(number, 1)] for number in range(4)]
    act_grad[...] = jnp.zeros_like(act_grad)
    wait_all(early)
    turned[...] = held_act_b[...].T
    wait_all(copies_c)

    def chunk(number, carry):
        columns = pl.ds(pl.multiple_of(number * channels, channels), channels)
        out_grad[...] = dot_tn(pool_ref[...], regions_grad_ref[:, columns])
        part_of(pre_c_ref, held_pre_c, number, 4).wait()
        part_of(fm_ref, held_map, number, 4 + chunks).wait()

        def one(step, sums):
            rows = pl.ds(pl.multiple_of(step * 64, 64), 64)
            pre = held_pre_c[rows, columns]
            scale = scale_ref[:, columns]
            linear = wide(held_map[rows, columns]) + pre * scale + shift_ref[:, columns]
            grad = out_grad[rows] * gelu_slope(linear)
            held_lin[rows, columns] = low(grad)
            pre_grad[rows] = low(grad * scale)
            return sums[0] + fold(grad * pre), sums[1] + fold(grad)

        zero = jnp.zeros((8, channels), jnp.float32)
        scale_sum, shift_sum = lax.fori_loop(0, sites // 64, one, (zero, zero))
        part_of(held_lin, lin_c_grad_ref, number, 4 + 2 * chunks).start()
        scale_c_out_ref[:, columns] = jnp.sum(scale_sum, axis=0, keepdims=True)
        shift_c_out_ref[:, columns] = jnp.sum(shift_sum, axis=0, keepdims=True)
        part = low(product(turned[...], pre_grad[...])).reshape(blocks // 2, 2, LANE_ROWS, channels)
        rows = pl.ds(pl.multiple_of(rows_b + number * LANE_ROWS, LANE_ROWS), LANE_ROWS)
        for bit in range(2):
            buffer[half_of(place_ref, bit), :, rows] = part[:, bit]
        act_grad[...] += dot_nt(pre_grad[...], weight_c[number].reshape(channels, channels))
        return carry

    lax.fori_loop(0, chunks, chunk, 0)
    wait_all(late)
    slope_back(act_grad, held_pre_b, scale_b_ref, shift_b_ref, wide_grad, scale_b_out_ref, shift_b_out_ref)
    turned[...] = held_act_a[...].T
    wait_all(copies_b)
    for slide in (-1, 0, 1):
        slid = in_columns(wide_grad[...], -slide)
        for number, place in enumerate(places):
            if place[1] != slide:
                continue
            moved = low(in_rows(slid, -place[0]))
            store_rows(buffer, place_ref, low(product(turned[...], moved)), number * channels, rows_b)
            begin = number * channels // LANE_ROWS
            tap = weight_b[begin : begin + channels // LANE_ROWS].reshape(channels, channels)
            part = dot_nt(moved, tap)
            if slide == -1 and place[0] == -1:
                act_grad[...] = part
            else:
                act_grad[...] += part
    slope_back(act_grad, held_pre_a, scale_a_ref, shift_a_ref, pre_a_grad_ref, scale_a_out_ref, shift_a_out_ref)
    hand_out(buffer, send_ref, keep_ref, out_sems)
    for number in range(chunks):
        part_of(held_lin, lin_c_grad_ref, number, 4 + 2 * chunks).wait()


def by_frames(grad, offset):
    if offset == 0:
        return grad
    sites, width = grad.shape
    tall = grad.reshape(sites // (FRAMES * SIDE * SIDE), FRAMES, SIDE * SIDE, width)
    edge = jnp.zeros_like(tall[:, :1])
    if offset > 0:
        tall = jnp.concatenate([edge, tall[:, :-1]], axis=1)
    else:
        tall = jnp.concatenate([tall[:, 1:], edge], axis=1)
    return tall.reshape(sites, width)


def first_back(place_ref, grad_ref, own_ref, got_ref, turned_ref, send_ref, keep_ref, sum_ref, buffer, held, sems, out_sems):
    features, sites = held.shape
    channels = grad_ref.shape[1]
    copies = [
        pltpu.make_async_copy(turned_ref.at[pl.ds(start, channels)], held.at[pl.ds(start, channels)], sems.at[start // channels])
        for start in range(0, features, channels)
    ]
    start_all(copies)
    sum_ref[...] = add_low(own_ref[...], got_ref[...])
    for tap in range(3):
        moved = by_frames(grad_ref[...], tap - 1)
        for start in range(0, features, channels):
            if tap == 0:
                copies[start // channels].wait()
            part = low(product(held[start : start + channels], moved))
            store_rows(buffer, place_ref, part, tap * features + start, buffer.shape[2])
    hand_out(buffer, send_ref, keep_ref, out_sems)


def map_back(places_ref, grad_ref, weight_ref, lin_c_grad_ref, out_ref, moved, held_lin, held_out, sems):
    sites, features = held_out.shape
    channels = grad_ref.shape[1]
    copies = start_all([pltpu.make_async_copy(lin_c_grad_ref, held_lin, sems.at[0])])
    for tap in range(3):
        moved[tap] = by_frames(grad_ref[...], tap - 1)
    wait_all(copies)
    groups = channels // LANE_ROWS

    def chunk(number, carry):
        columns = pl.ds(pl.multiple_of(number * channels, channels), channels)
        total = wide(held_lin[:, columns])
        for tap in range(3):
            rows = pl.ds(tap * (features // LANE_ROWS) + number * groups, groups)
            total = total + dot_nt(moved[tap], weight_ref[rows].reshape(channels, channels))
        held_out[:, columns] = low(total)
        pltpu.make_async_copy(held_out.at[:, columns], out_ref.at[:, columns], sems.at[1 + number]).start()
        return carry

    lax.fori_loop(0, features // channels, chunk, 0)
    copies = []
    for number in range(features // channels):
        columns = pl.ds(number * channels, channels)
        copies.append(pltpu.make_async_copy(held_out.at[:, columns], out_ref.at[:, columns], sems.at[1 + number]))
    wait_all(copies)


COST = 6e9
WINDOW = 0.1
F32 = jnp.float32
BF16 = jnp.bfloat16
ANY = pl.BlockSpec(memory_space=pl.ANY)
SCALAR = pl.BlockSpec(memory_space=pltpu.SMEM)
HELD = pl.BlockSpec(memory_space=pltpu.VMEM)


def shape_of(dims, kind):
    return jax.ShapeDtypeStruct(dims, kind)


def add_low(left, right):
    return low(wide(left) + wide(right))


class Blocks:
    def __init__(self, ref, first, dims, rows):
        self.ref, self.first, self.dims, self.rows = ref, first, dims, rows

    def span(self, index):
        index = index if isinstance(index, tuple) else (index,)
        flat = 0
        for place, size in zip(index, self.dims):
            flat = flat * size + place
        return pl.ds(pl.multiple_of(self.first + flat * self.rows, LANE_ROWS), self.rows)

    def __getitem__(self, index):
        return self.ref[self.span(index)]

    def __setitem__(self, index, value):
        self.ref[self.span(index)] = value


def after_last(places_ref, keep_ref, got_ref, keep_one, send_one, keep_two, send_two):
    half = keep_ref.shape[0] // 2
    across, inner = places_ref[0], places_ref[1]

    def one(number, carry):
        for place in range(2):
            keep_one[number, place] = add_low(keep_ref[number, place, across], got_ref[number, place, across])
            send_one[number, place] = add_low(keep_ref[number, place, 1 - across], got_ref[number, place, 1 - across])
            later = number + half
            keep_two[number, place] = add_low(keep_ref[later, inner, place], got_ref[later, inner, place])
            send_two[number, place] = add_low(keep_ref[later, 1 - inner, place], got_ref[later, 1 - inner, place])
        return carry

    lax.fori_loop(0, half, one, 0)


def after_cross(places_ref, keep_one, got_one, keep_two, got_two, kept_one, send_one, kept_two, send_two):
    across, inner = places_ref[0], places_ref[1]

    def one(number, carry):
        kept_one[number] = add_low(keep_one[number, inner], got_one[number, inner])
        send_one[number] = add_low(keep_one[number, 1 - inner], got_one[number, 1 - inner])
        kept_two[number] = add_low(keep_two[number, across], got_two[number, across])
        send_two[number] = add_low(keep_two[number, 1 - across], got_two[number, 1 - across])
        return carry

    lax.fori_loop(0, keep_two.shape[0], one, 0)


def after_plane(places_ref, keep_one, got_one, keep_two, got_two, kept_ref, sends):
    half = keep_one.shape[0]
    outer = places_ref[2]

    def block(place, target):
        @pl.when(place < half)
        def _():
            target[...] = add_low(keep_one[lax.rem(place, half)], got_one[lax.rem(place, half)])

        @pl.when(place >= half)
        def _():
            target[...] = add_low(keep_two[lax.rem(place, half)], got_two[lax.rem(place, half)])

    block(outer, kept_ref)
    for step, target in enumerate(sends):
        block(outer ^ (step + 1), target)


def total_of(refs):
    total = wide(refs[0][...])
    for ref in refs[1:]:
        total = total + wide(ref[...])
    return total


def round_two(
    places_ref, keep_one, got_one, keep_two, got_two, keep_a, got_a,
    kept_one, kept_two, keep_a_one, keep_a_two, across_ref, inner_ref,
):
    half, rows = kept_one.shape[:2]
    rows_a = keep_a_one.shape[2]
    below = 2 * half * rows_a
    after_last(
        places_ref, keep_a, got_a, keep_a_one, Blocks(across_ref, 0, (half, 2), rows_a), keep_a_two,
        Blocks(inner_ref, 0, (half, 2), rows_a),
    )
    after_cross(
        places_ref, keep_one, got_one, keep_two, got_two, kept_one, Blocks(inner_ref, below, (half,), rows), kept_two,
        Blocks(across_ref, below, (half,), rows),
    )


def bank_spans(lines, width, channels):
    groups = channels // width
    step = -(-lines // (groups * LANE_ROWS)) * LANE_ROWS
    return [(first, min(first + step, lines)) for first in range(0, lines, step)], step


def store_narrow(target, first, value, channels):
    lines, width = value.shape
    spans, step = bank_spans(lines, width, channels)
    target[first : first + step] = jnp.zeros((step, channels), BF16)
    for number, (begin, end) in enumerate(spans):
        target[first : first + end - begin, number * width : (number + 1) * width] = value[begin:end]


def load_narrow(value, first, lines, width):
    spans, _ = bank_spans(lines, width, value.shape[1])
    pieces = [
        value[first : first + end - begin, number * width : (number + 1) * width]
        for number, (begin, end) in enumerate(spans)
    ]
    return jnp.concatenate(pieces, axis=0)


def round_three(count, split, places_ref, kept_one, kept_two, keep_a_one, keep_a_two, got_across, got_inner, *refs):
    bank_refs, refs = (refs[:count], refs[count:]) if split else (refs[:1], refs[1:])
    kept_ref, sends, refs = refs[0], refs[1 : count], refs[count:]
    kept_a_one, kept_a_two, bank_keep_ref, across_ref, inner_ref = refs
    half, rows, channels = kept_one.shape
    rows_a = keep_a_one.shape[2]
    below = 2 * half * rows_a
    after_plane(
        places_ref, kept_one, Blocks(got_inner, below, (half,), rows), kept_two, Blocks(got_across, below, (half,), rows),
        kept_ref, sends,
    )
    after_cross(
        places_ref, keep_a_one, Blocks(got_across, 0, (half, 2), rows_a), keep_a_two,
        Blocks(got_inner, 0, (half, 2), rows_a), kept_a_one, Blocks(inner_ref, 0, (half,), rows_a), kept_a_two,
        Blocks(across_ref, 0, (half,), rows_a),
    )
    inner = places_ref[7] if split else 0
    keep = total_of([ref.at[inner] for ref in bank_refs])
    store_narrow(bank_keep_ref, 0, low(keep), channels)
    if split:
        send = total_of([ref.at[1 - inner] for ref in bank_refs])
        store_narrow(inner_ref, half * rows_a, low(send), channels)
    else:
        inner_ref[half * rows_a :] = bank_keep_ref[...]


def round_four(count, split, places_ref, *refs):
    plane_refs, refs = refs[:count], refs[count:]
    kept_a_one, kept_a_two, bank_keep_ref, got_across, got_inner = refs[:5]
    region_refs, refs = (refs[5:7], refs[7:]) if split else (refs[5:6], refs[6:])
    done_ref, region_ref, kept_a_ref, *sends = refs
    half, rows_a, channels = kept_a_one.shape
    rows = plane_refs[0].shape[0]
    below = half * rows_a
    after_plane(
        places_ref, kept_a_one, Blocks(got_inner, 0, (half,), rows_a), kept_a_two,
        Blocks(got_across, 0, (half,), rows_a), kept_a_ref, sends,
    )
    done_ref[:rows] = low(total_of(plane_refs))
    done_ref[rows:] = add_low(bank_keep_ref[...], got_inner[below:]) if split else bank_keep_ref[...]
    region_ref[...] = low(total_of(region_refs))


def round_last(count, split, widths, places_ref, *refs):
    outer_refs, refs = refs[:count], refs[count:]
    region_refs, refs = (refs[:2], refs[2:]) if split else (refs[:1], refs[1:])
    done_refs, refs = (refs[:2], refs[2:]) if split else ((), refs)
    part_ref, reduce_ref, query_ref, out_ref, head_ref, *both = refs
    part_ref[...] = low(total_of(outer_refs))
    region = total_of(region_refs)
    _, _, feature_rows, channel_rows, _, joined_rows = widths
    reduce_ref[...] = region[:feature_rows]
    query_ref[...] = region[feature_rows : feature_rows + channel_rows]
    out_ref[...] = region[feature_rows + channel_rows : feature_rows + 2 * channel_rows]
    head = load_narrow(region, feature_rows + 2 * channel_rows, joined_rows, TILE)
    head_ref[...] = head[:, : head_ref.shape[1]]
    for number, ref in enumerate(done_refs):
        both[0][number] = ref[...]


def sum_swap(places_ref, *refs):
    refs[-1][...] = low(total_of(refs[:-1]))


def region_pack(
    places_ref, regions_ref, reduced_ref, hidden_ref, query_grad_ref, reduced_grad_ref, w_out_ref, w_head_ref,
    logits_ref, message_ref,
):
    count = message_ref.shape[0]
    channels = reduced_ref.shape[1]
    reduced = reduced_ref[...]
    merged = low(reduced + product(hidden_ref[...], w_out_ref[...]))
    joined = jnp.concatenate([regions_ref[...], merged], axis=1)
    logits_ref[...] = low(product(joined, w_head_ref[...]))[:, : logits_ref.shape[1]]
    reduced_low = low(reduced)
    parts = [regions_ref[...], reduced_low, hidden_ref[...], joined]
    shared = [reduced_grad_ref[...], query_grad_ref[...]]
    for place in range(count):
        pieces = list(shared)
        for part in parts:
            width = part.shape[1] // count
            pieces.append(part[:, place * width : (place + 1) * width])
        spare = message_ref.shape[2] - sum(piece.shape[1] for piece in pieces)
        if spare:
            pieces.append(jnp.zeros((reduced.shape[0], spare), BF16))
        message_ref[place] = jnp.concatenate(pieces, axis=1)


def key_value_parts(places_ref, score_grad_ref, queries_ref, weights_ref, arrived_ref, out_ref):
    keys_here = score_grad_ref.shape[1]
    out_ref[:keys_here] = low(dot_tn(score_grad_ref[...], queries_ref[...]))
    out_ref[keys_here:] = low(dot_tn(weights_ref[...], arrived_ref[:, : queries_ref.shape[1]]))


def region_sums(widths, places_ref, group_ref, branch_grad_ref, logit_grad_ref, out_ref):
    ends, start = [], 0
    for width in widths:
        ends.append((start, start + width))
        start += width
    reduced_grad, query_grad, regions, reduced, hidden, joined = [group_ref[:, begin:end] for begin, end in ends]
    first, second = widths[2], widths[2] + widths[3]
    third = second + widths[4]
    channels = reduced_grad.shape[1]
    out_ref[:first] = low(dot_tn(regions, reduced_grad))
    out_ref[first:second] = low(dot_tn(reduced, query_grad))
    out_ref[second:third] = low(dot_tn(hidden, branch_grad_ref[...]))
    head = low(dot_tn(joined, logit_grad_ref[...]))
    store_narrow(out_ref, third, head, channels)


def bank_back(
    places_ref, sums_ref, w_key_ref, w_value_ref, w_bank_ref, turned_bank_ref, turned_memory_ref, *refs
):
    vectors, bank_grad_ref, outs, (message_ref, grads) = refs[:8], refs[8], refs[9:-2], refs[-2:]
    keys_here, features = bank_grad_ref.shape
    channels = sums_ref.shape[1]
    count, _, width = message_ref.shape
    key_low, value_low = sums_ref[:keys_here], sums_ref[keys_here:]
    memory_grad = low(dot_nt(key_low, w_key_ref[...]) + dot_nt(value_low, w_value_ref[...]))
    for start in range(0, features, channels):
        bank_grad_ref[:, start : start + channels] = low(dot_nt(memory_grad, w_bank_ref[start : start + channels]))
    grads[:keys_here] = memory_grad
    grads[keys_here : 2 * keys_here] = key_low
    grads[2 * keys_here :] = value_low

    def columns(rows):
        if width % TILE == 0:
            return grads[rows, pl.ds(pl.multiple_of(places_ref[4] * width, width), width)]
        picked = grads[rows, :width]
        for number in range(1, channels // width):
            picked = jnp.where(places_ref[4] == number, grads[rows, number * width : (number + 1) * width], picked)
        return picked

    feature_rows, channel_rows = features // count, channels // count
    part = low(product(turned_bank_ref[...], columns(pl.ds(0, keys_here))))
    message_ref[:, :feature_rows] = part.reshape(count, feature_rows, width)
    at = feature_rows
    for number in (1, 2):
        part = low(product(turned_memory_ref[...], columns(pl.ds(number * keys_here, keys_here))))
        message_ref[:, at : at + channel_rows] = part.reshape(count, channel_rows, width)
        at += channel_rows
    spare = message_ref.shape[1] - at
    for place in range(count):
        row = []
        for vector_ref in vectors:
            share = vector_ref.shape[1] // count
            row.append(vector_ref[:, place * share : (place + 1) * share])
        total = sum(piece.shape[1] for piece in row)
        lines = -(-total // width)
        if lines * width > total:
            row.append(jnp.zeros((1, lines * width - total), F32))
        row = jnp.concatenate(row, axis=1)
        tile = [row[:, line * width : (line + 1) * width] for line in range(lines)]
        tile.append(jnp.zeros((spare - lines, width), F32))
        message_ref[place, at:] = low(jnp.concatenate(tile, axis=0))
    inner = outs[0].shape[0]
    for step, out_ref in enumerate(outs):
        out_ref[...] = message_ref[pl.ds((places_ref[6] ^ step) * inner, inner)]


def finish(shape_info, places_ref, part_ref, *refs):
    rows_b, rows_c, feature_rows, channel_rows, lines, split = shape_info
    if split:
        own_ref, got_ref, refs = refs[0], refs[1], refs[2:]
        weight_refs = [own_ref.at[0], got_ref.at[0], own_ref.at[1], got_ref.at[1]]
        bank_refs, first = weight_refs, rows_b + rows_c
    else:
        weight_refs, bank_refs, refs, first = refs[:1], refs[1:-14], refs[-14:], 0
    conv_a_ref, conv_b_ref, conv_c_ref, bank_out_ref, key_ref, value_ref = refs[:6]
    vectors = refs[6:]
    conv_a_ref[...] = wide(part_ref[...]).reshape(conv_a_ref.shape)
    channels = weight_refs[0].shape[1]
    width = channels // len(bank_refs)

    def spot(number, size):
        if not split:
            return pl.ds(number * size, size)
        return pl.ds(pl.multiple_of((places_ref[4] ^ number) * size, size), size)

    for number, ref in enumerate(weight_refs):
        conv_b_ref[spot(number, rows_b)] = wide(ref[:rows_b])
        for chunk in range(rows_c // LANE_ROWS):
            begin = rows_b + chunk * LANE_ROWS
            conv_c_ref[spot(number, LANE_ROWS), chunk * channels : (chunk + 1) * channels] = wide(
                ref[begin : begin + LANE_ROWS]
            )
    tile = None
    at = feature_rows + 2 * channel_rows
    for number, ref in enumerate(bank_refs):
        bank = wide(load_narrow(ref, first, lines, width))
        columns = spot(number, width)
        bank_out_ref[:, columns] = bank[:feature_rows]
        key_ref[:, columns] = bank[feature_rows : feature_rows + channel_rows]
        value_ref[:, columns] = bank[feature_rows + channel_rows : at]
        tile = bank[at:] if tile is None else tile + bank[at:]
    total = sum(ref.shape[1] for ref in vectors)
    row = jnp.concatenate([tile[line : line + 1] for line in range(-(-total // width))], axis=1)
    at = 0
    for ref in vectors:
        ref[...] = row[:, at : at + ref.shape[1]]
        at += ref.shape[1]


def run_kernel(
    kernel, places, arrays, shapes, name, micros, scratch=(), raw_in=(), raw_out=(), fetched=(), limit=8
):
    count_in, count_out, fetched = len(arrays), len(shapes), list(fetched)

    def wrapped(*refs):
        places_ref, ins = refs[0], list(refs[1 : 1 + count_in])
        out_places, outs = refs[1 + count_in], list(refs[2 + count_in : 2 + count_in + count_out])
        extra = refs[2 + count_in + count_out :]
        if fetched:
            held, sems, extra = extra[: len(fetched)], extra[len(fetched)], extra[len(fetched) + 1 :]
            copies = start_all(
                [
                    pltpu.make_async_copy(ins[number], held[slot], sems.at[slot])
                    for slot, number in enumerate(fetched)
                ]
            )
        for number in range(places.shape[0]):
            out_places[number] = places_ref[number]
        if fetched:
            wait_all(copies)
            for slot, number in enumerate(fetched):
                ins[number] = held[slot]
        kernel(places_ref, *ins, *outs, *extra)

    outside = [*raw_in, *fetched]
    buffers = [pltpu.VMEM(arrays[number].shape, arrays[number].dtype) for number in fetched]
    if fetched:
        buffers.append(pltpu.SemaphoreType.DMA((len(fetched),)))
    return pl.pallas_call(
        wrapped,
        out_shape=[shape_of(places.shape, jnp.int32)] + list(shapes),
        in_specs=[SCALAR] + [ANY if number in outside else HELD for number in range(count_in)],
        out_specs=[SCALAR] + [ANY if number in raw_out else HELD for number in range(count_out)],
        scratch_shapes=buffers + list(scratch),
        compiler_params=params(limit),
        cost_estimate=pl.CostEstimate(
            flops=int(micros * COST), bytes_accessed=int(micros * COST / 1000), transcendentals=0
        ),
        name=name,
    )(places, *arrays)


def run_first_conv(feature_map, packed, scale, shift, groups):
    sites, channels = feature_map.shape[0], packed.shape[3]
    blocks = packed.shape[0]
    return pl.pallas_call(
        first_conv,
        out_shape=[
            jax.ShapeDtypeStruct((sites, channels), jnp.float32),
            jax.ShapeDtypeStruct((sites, channels), jnp.bfloat16),
            jax.ShapeDtypeStruct((blocks * groups, LANE_ROWS, channels), jnp.bfloat16),
        ],
        in_specs=[pl.BlockSpec(memory_space=pltpu.VMEM), pl.BlockSpec(memory_space=pl.ANY)] + [HELD] * 2,
        out_specs=[ANY, HELD, ANY],
        scratch_shapes=[
            pltpu.VMEM((blocks * groups, LANE_ROWS, channels), jnp.bfloat16),
            pltpu.VMEM((sites, channels), jnp.float32),
            pltpu.SemaphoreType.DMA((blocks,)),
            pltpu.SemaphoreType.DMA((2,)),
        ],
        compiler_params=params(52),
        cost_estimate=pl.CostEstimate(flops=int(6 * COST), bytes_accessed=int(6 * COST / 1000), transcendentals=0),
        name="first_conv",
    )(feature_map, packed, scale.reshape(1, -1), shift.reshape(1, -1))


def run_later_convs(
    act_a, feature_map, packed, scale_b, shift_b, scale_c, shift_c, pooling, w_reduce, w_query, groups_b, groups_c
):
    sites, channels = act_a.shape
    features = feature_map.shape[1]
    blocks = packed.shape[0]
    own = pooling.shape[0]
    group = lax.axis_size("bank")
    return pl.pallas_call(
        later_convs,
        out_shape=[
            jax.ShapeDtypeStruct((sites, channels), jnp.float32),
            jax.ShapeDtypeStruct((sites, channels), jnp.bfloat16),
            jax.ShapeDtypeStruct((sites, features), jnp.float32),
            jax.ShapeDtypeStruct((own, features), jnp.bfloat16),
            jax.ShapeDtypeStruct((own, channels), jnp.float32),
            jax.ShapeDtypeStruct((group, own, channels), jnp.bfloat16),
        ],
        in_specs=[HELD] + [ANY] * 2 + [HELD] * 5 + [ANY, HELD],
        out_specs=[ANY] * 3 + [HELD] * 3,
        scratch_shapes=[
            pltpu.VMEM((blocks * groups_b, LANE_ROWS, channels), jnp.bfloat16),
            pltpu.VMEM((groups_c, blocks, LANE_ROWS, channels), jnp.bfloat16),
            pltpu.VMEM((sites, channels), jnp.bfloat16),
            pltpu.VMEM((sites, features), jnp.bfloat16),
            pltpu.VMEM((sites, features), jnp.float32),
            pltpu.VMEM(w_reduce.shape, jnp.bfloat16),
            pltpu.VMEM((sites, channels), jnp.float32),
            pltpu.VMEM((sites, channels), jnp.bfloat16),
            pltpu.SemaphoreType.DMA((blocks,)),
            pltpu.SemaphoreType.DMA((blocks,)),
            pltpu.SemaphoreType.DMA((4 + groups_c,)),
        ],
        compiler_params=params(52),
        cost_estimate=pl.CostEstimate(flops=int(15 * COST), bytes_accessed=int(15 * COST / 1000), transcendentals=0),
        name="later_convs",
    )(
        act_a, feature_map, packed, scale_b.reshape(1, -1), shift_b.reshape(1, -1), scale_c.reshape(1, -1),
        shift_c.reshape(1, -1), pooling, w_reduce, w_query,
    )


def body(
    feature_map,
    bank,
    region_time,
    roi_index,
    roi_weight,
    conv_a,
    scale_a,
    shift_a,
    conv_b,
    scale_b,
    shift_b,
    conv_c,
    scale_c,
    shift_c,
    w_reduce,
    w_bank,
    w_query,
    w_key,
    w_value,
    ln_gain,
    ln_shift,
    w_out,
    w_head,
    logit_grad,
):
    site_count = feature_map.shape[0]
    feature_count = feature_map.shape[1]
    channels = w_query.shape[0]
    classes = w_head.shape[1]
    keys_here = bank.shape[0]
    own_count = roi_index.shape[0]
    bank_count = lax.axis_size("bank")
    bank_place = lax.axis_index("bank")
    dp_count = lax.axis_size("dp")
    dp_place = lax.axis_index("dp")
    first_row = bank_place * own_count
    half_span = keys_here * bank_count // 2
    group_rows = bank_count * own_count
    chunks = feature_count // channels
    shards = (conv_a, conv_b, conv_c)
    split = dp_count // 2 == 2 and all(shard.shape[0] % (LANE_ROWS * dp_count) == 0 for shard in shards)
    axes = block_axes(split, dp_count, bank_count)
    outer, inner, across, last = axes
    outer_count = outer.size if split else 1
    blocks = bank_count * dp_count if split else bank_count
    halves = tuple(axis.size for axis in axes[:3])
    places_here = jnp.stack([across.place(), inner.place(), outer.place(), last.place(), dp_place, bank_place * keys_here, outer.place() if split else 0 * bank_place, inner.place()])

    def own_part(shard):
        if not split:
            return shard
        rows = shard.shape[0] // dp_count
        return lax.dynamic_slice_in_dim(shard, dp_place * rows, rows, 0)

    part_a, part_b, part_c = [own_part(shard) for shard in shards]
    rows_a, rows_b, rows_c = part_a.shape[0], part_b.shape[0], part_c.shape[0]
    groups_a, groups_b, groups_c = rows_a // LANE_ROWS, rows_b // LANE_ROWS, chunks
    pieces_c = [part_c[:, chunk * channels : (chunk + 1) * channels] for chunk in range(chunks)]
    own_packed = jnp.concatenate([part_a, part_b] + pieces_c, 0).reshape(-1, LANE_ROWS, channels)
    packed = lax.all_gather(own_packed, ("bank", "dp") if split else "bank", axis=0, tiled=False)
    packed = packed.reshape((blocks,) + own_packed.shape)

    memory = product(bank, w_bank)
    memory_low = low(memory)
    keys = low(product(memory_low, w_key))
    values = low(product(memory_low, w_value))
    turned_map, turned_bank, turned_memory = feature_map.T, bank.T, memory_low.T
    matches = roi_index[:, :, None] == jnp.arange(site_count, dtype=jnp.int32)[None, None, :]
    pooling = low(jnp.sum(jnp.where(matches, wide(roi_weight)[:, :, None], 0.0), axis=1))
    own_logit_grad = lax.dynamic_slice_in_dim(logit_grad, first_row, own_count, 0)
    joined_grad = dot_nt(own_logit_grad, w_head)
    branch_grad = low(joined_grad[:, feature_count:])
    hidden_grad = dot_nt(branch_grad, w_out)
    group_branch_grad = low(dot_nt(logit_grad, w_head[feature_count:]))
    spare = ((0, 0), (0, TILE - classes))
    wide_head, wide_logit_grad = jnp.pad(w_head, spare), jnp.pad(logit_grad, spare)
    time_column = region_time.reshape(-1, 1)
    scales = jnp.stack([scale_b, shift_b, scale_a, shift_a])
    (
        packed, turned_bank, turned_memory, keys, values, turned_map, pooling, joined_grad, hidden_grad,
        group_branch_grad, wide_head, wide_logit_grad, time_column, scales, places_here,
    ) = lax.optimization_barrier(
        (
            packed, turned_bank, turned_memory, keys, values, turned_map, pooling, joined_grad, hidden_grad,
            group_branch_grad, wide_head, wide_logit_grad, time_column, scales, places_here,
        )
    )

    pre_a, act_a, weight_a = run_first_conv(feature_map, packed, scale_a, shift_a, groups_a)
    pre_b, act_b, pre_c, regions, reduced, own_queries = run_later_convs(
        act_a, feature_map, packed, scale_b, shift_b, scale_c, shift_c, pooling, w_reduce, w_query, groups_b, groups_c
    )
    queries = to_owners(own_queries).reshape(group_rows, channels)
    places, message, scores = run_kernel(
        functools.partial(attend, half_span),
        places_here,
        [queries, keys, values, time_column],
        [shape_of((group_rows, channels + TILE), BF16), shape_of((group_rows, keys_here), F32)],
        "attend",
        2,
    )
    arrived = to_owners(message.reshape(bank_count, own_count, channels + TILE))
    row = shape_of((1, channels), F32)
    places, message, hidden_low, gain_part, shift_part = run_kernel(
        merge_rows,
        places,
        [arrived, hidden_grad, ln_gain.reshape(1, -1), ln_shift.reshape(1, -1)],
        [shape_of(arrived.shape, BF16), shape_of((own_count, channels), BF16), row, row],
        "merge_rows",
        2,
    )
    arrived = to_owners(message).reshape(group_rows, channels + TILE)
    group_shape = shape_of((group_rows, channels), BF16)
    weight_shape = shape_of((group_rows, keys_here), BF16)
    places, query_part, score_grad, weights_low = run_kernel(
        attend_back,
        places,
        [arrived, scores, keys, values],
        [group_shape, weight_shape, weight_shape],
        "attend_back",
        2,
    )
    query_parts = to_owners(query_part.reshape(bank_count, own_count, channels))
    places, key_value = run_kernel(
        key_value_parts,
        places,
        [score_grad, queries, weights_low, arrived],
        [shape_of((2 * keys_here, channels), BF16)],
        "key_value_parts",
        3,
    )

    def dp_swap(value, step):
        return lax.ppermute(value, "dp", [(i, i ^ step) for i in range(dp_count)])

    key_value_got = dp_swap(key_value, 1)

    def summed_swap(places, own, got):
        places, own = run_kernel(
            sum_swap, places, [own, got], [shape_of(own.shape, BF16)], "sum_swap", 2
        )
        return places, own

    places, key_value = summed_swap(places, key_value, key_value_got)
    step = 2
    while step * 2 < dp_count:
        places, key_value = summed_swap(places, key_value, dp_swap(key_value, step))
        step *= 2
    key_value_got = dp_swap(key_value, step)
    own_shape = shape_of((own_count, channels), BF16)
    places, query_grad, reduced_grad, regions_grad = run_kernel(
        region_back,
        places,
        [query_parts, joined_grad, w_query, w_reduce],
        [own_shape, own_shape, shape_of((own_count, feature_count), BF16)],
        "region_back",
        3,
    )
    half_blocks = blocks // 2
    rows_bc = rows_b + groups_c * LANE_ROWS
    wide_row = shape_of((1, feature_count), F32)
    maps = (site_count, feature_count)
    inside = (site_count, channels)
    (
        places, send_bc, keep_bc, lin_c_grad, pre_a_grad,
        scale_c_part, shift_c_part, scale_b_part, shift_b_part, scale_a_part, shift_a_part,
    ) = run_kernel(
        functools.partial(later_back, groups_a, groups_b),
        places,
        [
            regions_grad, pooling, scale_c.reshape(1, -1), shift_c.reshape(1, -1),
            scales, pre_c, feature_map, act_b, pre_b, act_a, pre_a, packed,
        ],
        [shape_of((half_blocks, rows_bc, channels), BF16)] * 2
        + [shape_of(maps, BF16), shape_of(inside, BF16), wide_row, wide_row]
        + [row] * 4,
        "later_back",
        28,
        scratch=[
            pltpu.VMEM((blocks * groups_b, LANE_ROWS, channels), BF16),
            pltpu.VMEM((groups_c, blocks, LANE_ROWS, channels), BF16),
            pltpu.VMEM((2, half_blocks, rows_bc, channels), BF16),
            pltpu.VMEM(inside, F32),
            pltpu.VMEM(inside, BF16),
            pltpu.VMEM((channels, site_count), BF16),
            pltpu.VMEM(inside, F32),
            pltpu.VMEM(inside, F32),
            pltpu.VMEM(maps, F32),
            pltpu.VMEM(maps, BF16),
            pltpu.VMEM(inside, BF16),
            pltpu.VMEM(inside, F32),
            pltpu.VMEM(inside, BF16),
            pltpu.VMEM(inside, F32),
            pltpu.VMEM(maps, BF16),
            pltpu.SemaphoreType.DMA((blocks,)),
            pltpu.SemaphoreType.DMA((blocks,)),
            pltpu.SemaphoreType.DMA((2,)),
            pltpu.SemaphoreType.DMA((4 + 3 * chunks,)),
        ],
        raw_in=range(5, 12),
        raw_out=(0, 1, 2),
        limit=40,
    )
    got_bc = last.swap(send_bc, 1)

    def parted(value):
        return value.reshape(halves + value.shape[1:])

    places, send_a, keep_a, key_value = run_kernel(
        first_back,
        places,
        [pre_a_grad, key_value, key_value_got, turned_map],
        [shape_of((half_blocks, rows_a, channels), BF16)] * 2 + [shape_of(key_value.shape, BF16)],
        "first_back",
        6,
        scratch=[
            pltpu.VMEM((2, half_blocks, rows_a, channels), BF16),
            pltpu.VMEM(turned_map.shape, BF16),
            pltpu.SemaphoreType.DMA((chunks,)),
            pltpu.SemaphoreType.DMA((2,)),
        ],
        raw_in=(3,),
        raw_out=(0, 1),
        limit=20,
    )
    got_a = last.swap(send_a, 1)
    half = outer.size // 2
    plane_shape = (half, 2, rows_bc, channels)
    places, keep_one, send_one, keep_two, send_two = run_kernel(
        after_last, places, [parted(keep_bc), parted(got_bc)], [shape_of(plane_shape, BF16)] * 4, "round_one", 4
    )
    got_one, got_two = across.swap(send_one, 1), inner.swap(send_two, 1)
    places, map_grad = run_kernel(
        map_back,
        places,
        [pre_a_grad, weight_a, lin_c_grad],
        [shape_of(maps, BF16)],
        "map_back",
        WINDOW,
        scratch=[
            pltpu.VMEM((3,) + inside, BF16),
            pltpu.VMEM(maps, BF16),
            pltpu.VMEM(maps, BF16),
            pltpu.SemaphoreType.DMA((1 + chunks,)),
        ],
        raw_in=(2,),
        raw_out=(0,),
        limit=12,
    )
    block_bc, block_a = shape_of((half, rows_bc, channels), BF16), shape_of((half, 2, rows_a, channels), BF16)
    both = shape_of((half * (2 * rows_a + rows_bc), channels), BF16)
    places, kept_one, kept_two, keep_a_one, keep_a_two, send_across, send_inner = run_kernel(
        round_two,
        places,
        [keep_one, got_one, keep_two, got_two, parted(keep_a), parted(got_a)],
        [block_bc, block_bc, block_a, block_a, both, both],
        "round_two",
        5,
    )
    got_across, got_inner = across.swap(send_across, 1), inner.swap(send_inner, 1)
    feature_rows, channel_rows = feature_count // bank_count, channels // bank_count
    joined_rows = (feature_count + channels) // bank_count
    widths = (channels, channels, feature_rows, channel_rows, channel_rows, joined_rows)
    message_width = -(-sum(widths) // TILE) * TILE
    places, logits_out, message = run_kernel(
        region_pack,
        places,
        [regions, reduced, hidden_low, query_grad, reduced_grad, w_out, wide_head],
        [shape_of((own_count, classes), BF16), shape_of((bank_count, own_count, message_width), BF16)],
        "region_pack",
        WINDOW,
    )
    group = to_owners(message).reshape(group_rows, message_width)

    vectors = [
        gain_part, shift_part, scale_a_part, shift_a_part, scale_b_part, shift_b_part, scale_c_part, shift_c_part
    ]
    width = channels // dp_count
    lines = -(-sum(vector.shape[1] for vector in vectors) // (bank_count * width))
    lines = -(-lines // LANE_ROWS) * LANE_ROWS
    bank_lines = feature_rows + 2 * channel_rows + lines
    bank_step = bank_spans(bank_lines, width, channels)[1]
    region_lines = feature_rows + 2 * channel_rows + bank_spans(joined_rows, TILE, channels)[1]
    places, bank_grad, *bank_pieces = run_kernel(
        bank_back,
        places,
        [key_value, w_key, w_value, w_bank, turned_bank, turned_memory] + vectors,
        [shape_of(bank.shape, BF16)]
        + [shape_of((bank_count // outer_count, bank_lines, width), BF16)] * outer_count,
        "bank_back",
        WINDOW,
        scratch=[
            pltpu.VMEM((bank_count, bank_lines, width), BF16),
            pltpu.VMEM((3 * keys_here, channels), BF16),
        ],
        limit=8,
    )
    if split:
        bank_parts = [bank_pieces[0]] + [outer.swap(piece, step + 1) for step, piece in enumerate(bank_pieces[1:])]
    else:
        bank_parts = [low(jnp.sum(wide(to_owners(bank_pieces[0])), axis=0, keepdims=True))]
    one_bc, half_a = shape_of((rows_bc, channels), BF16), shape_of((half, rows_a, channels), BF16)
    results = run_kernel(
        functools.partial(round_three, outer.size, split),
        places,
        [kept_one, kept_two, keep_a_one, keep_a_two, got_across, got_inner] + bank_parts,
        [one_bc] * outer.size
        + [half_a, half_a, shape_of((bank_step, channels), BF16)]
        + [
            shape_of((half * rows_a, channels), BF16),
            shape_of((half * rows_a + bank_step, channels), BF16),
        ],
        "round_three",
        5,
    )
    places, pieces_bc = results[0], results[1 : 1 + outer.size]
    kept_a_one, kept_a_two, bank_keep, send_across, send_inner = results[1 + outer.size :]
    got_across, got_inner = across.swap(send_across, 1), inner.swap(send_inner, 1)
    got_bc = [outer.swap(piece, step + 1) for step, piece in enumerate(pieces_bc[1:])]
    places, region_parts = run_kernel(
        functools.partial(region_sums, widths),
        places,
        [group, group_branch_grad, wide_logit_grad],
        [shape_of((region_lines, channels), BF16)],
        "region_sums",
        WINDOW,
    )
    region_both = [region_parts, dp_swap(region_parts, 1)] if split else [lax.psum(region_parts, "dp")]
    results = run_kernel(
        functools.partial(round_four, outer.size, split),
        places,
        [pieces_bc[0], *got_bc, kept_a_one, kept_a_two, bank_keep, got_across, got_inner, *region_both],
        [shape_of((rows_bc + bank_step, channels), BF16), shape_of(region_parts.shape, BF16)]
        + [shape_of((rows_a, channels), BF16)] * outer.size,
        "round_four",
        4,
    )
    places, done, region_parts, kept_a, *pieces_a = results
    got_a = [outer.swap(piece, step + 1) for step, piece in enumerate(pieces_a)]
    region_both = [region_parts, across.swap(region_parts, 1)] if split else [region_parts]
    done_both = [done, across.swap(done, 1)] if split else []
    row_block = shape_of((channel_rows, channels), F32)
    results = run_kernel(
        functools.partial(round_last, outer.size, split, widths),
        places,
        [kept_a, *got_a, *region_both, *done_both],
        [shape_of((rows_a, channels), BF16), shape_of((feature_rows, channels), F32), row_block, row_block]
        + [shape_of((joined_rows, classes), F32)]
        + [shape_of((2,) + done.shape, BF16)] * len(done_both[1:]),
        "round_last",
        2,
    )
    places, part_a, reduce_weight_grad, query_weight_grad, out_weight_grad, head_weight_grad = results[:6]
    if split:
        done_a = lax.all_gather(part_a, "dp", axis=0, tiled=False)
        done_all = [results[6], last.swap(results[6], 1)]
    else:
        done_a = lax.psum(part_a, "dp")
        bank_all = lax.all_gather(done[rows_bc:], "dp", axis=0, tiled=False)
        done_all = [lax.psum(done[:rows_bc], "dp")] + [bank_all[place] for place in range(dp_count)]
    info = (rows_b, groups_c * LANE_ROWS, feature_rows, channel_rows, bank_lines, split)
    results = run_kernel(
        functools.partial(finish, info),
        places,
        [done_a, *done_all],
        [shape_of(conv_a.shape, F32), shape_of(conv_b.shape, F32), shape_of(conv_c.shape, F32)]
        + [shape_of((feature_rows, channels), F32), row_block, row_block]
        + [shape_of((1, vector.shape[1] // bank_count), F32) for vector in vectors],
        "finish",
        3,
    )
    places, conv_a_grad, conv_b_grad, conv_c_grad, bank_weight_grad, key_weight_grad, value_weight_grad = results[:7]
    small = [value.reshape(-1) for value in results[7:]]
    gain_grad, shift_grad = small[:2]
    scale_a_grad, shift_a_grad, scale_b_grad, shift_b_grad, scale_c_grad, shift_c_grad = small[2:]
    return (
        logits_out,
        map_grad,
        bank_grad,
        conv_a_grad,
        scale_a_grad,
        shift_a_grad,
        conv_b_grad,
        scale_b_grad,
        shift_b_grad,
        conv_c_grad,
        scale_c_grad,
        shift_c_grad,
        reduce_weight_grad,
        bank_weight_grad,
        query_weight_grad,
        key_weight_grad,
        value_weight_grad,
        gain_grad,
        shift_grad,
        out_weight_grad,
        head_weight_grad,
    )


def solution(mesh):
    in_specs = (
        P(("dp", "bank"), None),
        P("bank", None),
        P("dp"),
        P(("dp", "bank"), None),
        P(("dp", "bank"), None),
        P("bank", None),
        P(),
        P(),
        P("bank", None),
        P(),
        P(),
        P("bank", None),
        P(),
        P(),
        P(),
        P(),
        P(),
        P(),
        P(),
        P(),
        P(),
        P(),
        P(),
        P("dp", None),
    )
    out_specs = (
        P(("dp", "bank"), None),
        P(("dp", "bank"), None),
        P("bank", None),
        P("bank", None),
        P("bank"),
        P("bank"),
        P("bank", None),
        P("bank"),
        P("bank"),
        P("bank", None),
        P("bank"),
        P("bank"),
        P("bank", None),
        P("bank", None),
        P("bank", None),
        P("bank", None),
        P("bank", None),
        P("bank"),
        P("bank"),
        P("bank", None),
        P("bank", None),
    )
    return jax.shard_map(body, mesh=mesh, in_specs=in_specs, out_specs=out_specs, check_vma=False)
```

time: 508 us -> 391 us (0.77); the launches traced: 501 us -> 389 us
  starting transfers between devices: 85.6 us -> 48.7 us
  waiting for transfers between devices: 171 us -> 146 us
  other arithmetic: 23.3 us -> 0.99 us
  Pallas kernels: 67.5 us -> 89.8 us
  matrix products: 26 us -> 9.53 us
  local copies, waits for them, and re-layouts: 59.9 us -> 43.7 us
  blocking collectives: 51.9 us -> 36.1 us
    all_gather x6 -> x1, blocking collectives: 51.9 us -> 8.7 us  [body(): done_a = lax.all_gather(part_a, 'dp', axis=0, tiled=False)]
    all_to_all x0 -> x2, blocking collectives: none -> 27.4 us  [to_owners(): lax.all_to_all(value, 'bank', split_axis=0, concat_axis=0, tiled=True)]
    pallas_call x7 -> x18, Pallas kernels: 45.6 us -> 67.6 us  [run_kernel(): pl.pallas_call(wrapped, out_shape=[shape_of(places.shape, jnp.int32)] + l...]
    all_to_all x5 -> x3, starting transfers between devices: 37.6 us -> 15.6 us  [to_owners(): lax.all_to_all(value, 'bank', split_axis=0, concat_axis=0, tiled=True)]
    all_gather x1, waiting for transfers between devices: 93.9 us -> 74.9 us  [body(): lax.all_gather(own_packed, ('bank', 'dp') if split else 'bank', axis=0, t...]
    ppermute x40 -> x20, starting transfers between devices: 41 us -> 22.4 us  [swap(): return lax.ppermute(value, self.name, pairs)]
    convert_element_type x30 -> x0, other arithmetic: 14.3 us -> none  [low(): return value.astype(jnp.bfloat16)]
    dot_general x9 -> x0, matrix products: 8.06 us -> none  [dot_tn(): lax.dot_general(left, right, (((0,), (0,)), ((), ())), preferred_element_...]
  transfers between devices with their start and end apart: 52 -> 27, of which waited for: 20 -> 14; matrix products, arithmetic and copies ran while one was open for 17% -> 7% of each run, Pallas kernels for 9% -> 13%
where the time goes in v3:
time: 391 us; the launch traced here: 389 us
  waiting for transfers between devices  146 us (37%)
  Pallas kernels  89.8 us (23%)
  starting transfers between devices  48.7 us (12%)
  local copies, waits for them, and re-layouts  43.7 us (11%)
  blocking collectives  36.1 us (9%)
  between operations  14.9 us (4%)
  matrix products  9.53 us (2%)
    all_gather x1, waiting for transfers between devices, body(): lax.all_gather(own_packed, ('bank', 'dp') if split else 'bank', axis=0, t...  74.9 us
    pallas_call x18, Pallas kernels, run_kernel(): pl.pallas_call(wrapped, out_shape=[shape_of(places.shape, jnp.int32)] + l...  67.6 us
    ppermute x20, waiting for transfers between devices, swap(): return lax.ppermute(value, self.name, pairs)  62.3 us
    unnamed x169, local copies, waits for them, and re-layouts  39.4 us
    all_to_all x2, blocking collectives, to_owners(): lax.all_to_all(value, 'bank', split_axis=0, concat_axis=0, tiled=True)  27.4 us
    ppermute x20, starting transfers between devices, swap(): return lax.ppermute(value, self.name, pairs)  22.4 us
    all_to_all x3, starting transfers between devices, to_owners(): lax.all_to_all(value, 'bank', split_axis=0, concat_axis=0, tiled=True)  15.6 us
    pallas_call x1, Pallas kernels, run_later_convs(): pl.pallas_call(later_convs, out_shape=[jax.ShapeDtypeStruct((sites, chann...  13.7 us
  transfers between devices with their start and end apart: 27, of which 14 were waited for; matrix products, arithmetic and copies ran while one was open for 7% of the time, Pallas kernels for 13%

profile of v3, /device:TPU:9, one launch (start us, length us, event | category | flops | bytes accessed | tf_op | source)
XLA Modules:
  0.0 389.5 jit_solution(6424735290701932671)
XLA Ops:
  21.5 4.1 %copy.73 = bf16[512,2048]{0,1:T(8,128)(2,1)} copy(bf16[512,2048]{1,0:T(8,128)(2,1)} %refs_7_.1) | data formatting | bytes 4194304 | tf_op args[0]
  37.6 74.9 %all-gather.3.cloned.1.call-done.packed_ref.refs_12_ = bf16[32,25,16,512]{3,2,1,0:T(8,128)(2,1)} async-done(((bf16[1,25,16,512]{3,2,1,0:T(8,128)(2,1)}), bf16[32,25,16,512]{3,2,1,0:T(8,128)(2,1)}) %all-gather.3.cloned.1.call-update) | async-done | bytes 13107216 | tf_op jit(solution)/shard_map/all_gather | solution.py:1048
  112.5 8.5 %first_conv.1 = (f32[512,512]{1,0:T(8,128)S(1)}, bf16[512,512]{1,0:T(8,128)(2,1)S(1)}, bf16[384,16,512]{2,1,0:T(8,128)(2,1)}) custom-call(bf16[512,2048]{1,0:T(8,128)(2,1)} %refs_7_.1, bf16[32,25,16,512]{3,2,1,0:T(8,128)(2,1)} %all-gather.3.cloned.1.call-done.packed_ref.refs_12_, f32[1,512]{1,0:T(1,128)S(1)} %bitcast.58, f32[1,512]{1,0:T(1,128)S(1)} %bitcast.60), custom_call_target="tpu_custom_call" | custom-call | flops 35999997952 | bytes 36000000 | tf_op jit(solution)/shard_map/first_conv/pallas_call | solution.py:925
  122.0 13.7 %later_convs.1 = (f32[512,512]{1,0:T(8,128)}, bf16[512,512]{1,0:T(8,128)(2,1)S(1)}, f32[512,2048]{1,0:T(8,128)}, bf16[32,2048]{1,0:T(8,128)(2,1)S(1)}, f32[32,51...) custom-call(bf16[512,512]{1,0:T(8,128)(2,1)S(1)} %get-tuple-element.145.act_a_ref.refs_10_, bf16[512,2048]{1,0:T(8,128)(2,1)} %refs_7_.1, ...), custom_call_target="tpu_custom_call" | custom-call | flops 89999998976 | bytes 90000000 | tf_op jit(solution)/shard_map/later_convs/pallas_call | solution.py:954
  138.5 4.9 %all-to-all-start = ((bf16[8,32,512]{2,1,0:T(8,128)(2,1)}), bf16[8,32,512]{2,1,0:T(8,128)(2,1)}, u32[]{:S(2)}, u32[]{:S(2)}) async-start(bf16[8,32,512]{2,1,0:T(8,128)(2,1)} %copy-done.12), calls=%async_computation | async-start | bytes 524288 | tf_op jit(solution)/shard_map/all_to_all | solution.py:64
  144.2 6.1 %all-to-all-done = bf16[8,32,512]{2,1,0:T(8,128)(2,1)} async-done(((bf16[8,32,512]{2,1,0:T(8,128)(2,1)}), bf16[8,32,512]{2,1,0:T(8,128)(2,1)}, u32[]{:S(2)}, u32[]{:S(2)}) %all-to-all-start) | async-done | bytes 262176 | tf_op jit(solution)/shard_map/all_to_all | solution.py:64
  155.1 13.8 %all_to_all.25.refs_1_ = bf16[8,32,640]{2,1,0:T(8,128)(2,1)S(1)} all-to-all(bf16[8,32,640]{2,1,0:T(8,128)(2,1)S(1)} %bitcast.55), channel_id=1, replica_groups=mesh['dp'=4,'bank'=8] {'bank'}, dimensions={0} | all-to-all | bytes 655360 | tf_op jit(solution)/shard_map/all_to_all | solution.py:64
  170.5 13.6 %all_to_all.26 = bf16[8,32,640]{2,1,0:T(8,128)(2,1)S(1)} all-to-all(bf16[8,32,640]{2,1,0:T(8,128)(2,1)S(1)} %get-tuple-element.155), channel_id=1, replica_groups=mesh['dp'=4,'bank'=8] {'bank'}, dimensions={0} | all-to-all | bytes 655360 | tf_op jit(solution)/shard_map/all_to_all | solution.py:64
  191.5 4.9 %all-to-all-start.3 = ((bf16[8,32,512]{2,1,0:T(8,128)(2,1)}), bf16[8,32,512]{2,1,0:T(8,128)(2,1)}, u32[]{:S(2)}, u32[]{:S(2)}) async-start(bf16[8,32,512]{2,1,0:T(8,128)(2,1)} %bitcast.56), calls=%async_computation.3 | async-start | bytes 524288 | tf_op jit(solution)/shard_map/all_to_all | solution.py:64
  210.8 21.4 %later_back.1 = (s32[8]{0:T(128)S(1)}, bf16[16,208,512]{2,1,0:T(8,128)(2,1)S(1)}, bf16[16,208,512]{2,1,0:T(8,128)(2,1)}, bf16[512,2048]{1,0:T(8,128)(2,1)S(1)}, ...) custom-call(s32[8]{0:T(128)S(1)} %get-tuple-element.165.refs_0_, ...), custom_call_target="tpu_custom_call" | custom-call | flops 167999995904 | bytes 168000000 | tf_op jit(solution)/shard_map/later_back/pallas_call | solution.py:908
  234.1 7.1 %first_back.1 = (s32[8]{0:T(128)S(1)}, bf16[16,192,512]{2,1,0:T(8,128)(2,1)S(1)}, bf16[16,192,512]{2,1,0:T(8,128)(2,1)S(1)}, bf16[1024,512]{1,0:T(8,128)(2,1)S(1)}) custom-call(s32[8]{0:T(128)S(1)} %get-tuple-element.172.refs_0_, bf16[512,512]{1,0:T(8,128)(2,1)S(1)} %get-tuple-element.173.refs_1_, bf16[1024,512]{1,0:T(8,128)(2,1)} %get-tuple-element.174.refs_2_, ...), custom_call_target="tpu_custom_call" | custom-call | flops 35999997952 | bytes 36000000 | tf_op jit(solution)/shard_map/first_back/pallas_call | solution.py:908
  244.5 6.3 %map_back.1 = (s32[8]{0:T(128)S(1)}, bf16[512,2048]{1,0:T(8,128)(2,1)}) custom-call(s32[8]{0:T(128)S(1)} %get-tuple-element.179.refs_0_, bf16[512,512]{1,0:T(8,128)(2,1)S(1)} %get-tuple-element.173.refs_1_, bf16[384,16,512]{2,1,0:T(8,128)(2,1)S(1)} %bitcast.48, bf16[512,2048]{1,0:T(8,128)(2,1)S(1)} %get-tuple-element.181.refs_3_), custom_call_target="tpu_custom_call" | custom-call | flops 600000000 | bytes 600000 | tf_op jit(solution)/shard_map/map_back/pallas_call | solution.py:908
  250.8 12.5 %collective-permute-done.3.refs_2_ = bf16[2,2,208,512]{3,2,1,0:T(8,128)(2,1)S(1)} collective-permute-done((bf16[2,2,208,512]{3,2,1,0:T(8,128)(2,1)S(1)}, bf16[2,2,208,512]{3,2,1,0:T(8,128)(2,1)S(1)}, u32[]{:S(2)}, u32[]{:S(2)}) %collective-permute-start.3) | collective-permute-done | bytes 852000 | tf_op jit(solution)/shard_map/ppermute | solution.py:44
  271.2 4.0 %bank_back.1 = (s32[8]{0:T(128)S(1)}, bf16[512,2048]{1,0:T(8,128)(2,1)}, bf16[2,400,128]{2,1,0:T(8,128)(2,1)S(1)}, bf16[2,400,128]{2,1,0:T(8,128)(2,1)S(1)}, bf1...) custom-call(s32[8]{0:T(128)S(1)} %get-tuple-element.198.refs_0_, ...), custom_call_target="tpu_custom_call" | custom-call | flops 600000000 | bytes 600000 | tf_op jit(solution)/shard_map/bank_back/pallas_call | solution.py:908
  278.2 5.7 %all-to-all-start.4 = ((bf16[8,32,1792]{2,1,0:T(8,128)(2,1)}), bf16[8,32,1792]{2,1,0:T(8,128)(2,1)S(1)}, u32[]{:S(2)}, u32[]{:S(2)}) async-start(bf16[8,32,1792]{2,1,0:T(8,128)(2,1)} %get-tuple-element.223), calls=%async_computation.4 | async-start | bytes 1835008 | tf_op jit(solution)/shard_map/all_to_all | solution.py:64
  284.6 12.3 %collective-permute-done.10.refs_10_ = bf16[2,400,128]{2,1,0:T(8,128)(2,1)S(1)} collective-permute-done((bf16[2,400,128]{2,1,0:T(8,128)(2,1)}, bf16[2,400,128]{2,1,0:T(8,128)(2,1)S(1)}, u32[]{:S(2)}, u32[]{:S(2)}) %collective-permute-start.10) | collective-permute-done | bytes 204832 | tf_op jit(solution)/shard_map/ppermute | solution.py:44
  309.1 5.2 %collective-permute-start.15 = (bf16[496,512]{1,0:T(8,128)(2,1)S(1)}, bf16[496,512]{1,0:T(8,128)(2,1)S(1)}, u32[]{:S(2)}, u32[]{:S(2)}) collective-permute-start(bf16[496,512]{1,0:T(8,128)(2,1)S(1)} %get-tuple-element.235), channel_id=1, source_target_pairs={{0,1},{1,0},{2,3},{3,2},{4,5},{5,4},{6,7},{7,6},{8,9},{9,8},{10,11... | collective-permute-start | bytes 1523720 | tf_op jit(solution)/shard_map/ppermute | solution.py:44
  315.7 6.8 %collective-permute-start.16 = (bf16[464,512]{1,0:T(8,128)(2,1)S(1)}, bf16[464,512]{1,0:T(8,128)(2,1)S(1)}, u32[]{:S(2)}, u32[]{:S(2)}) collective-permute-start(bf16[464,512]{1,0:T(8,128)(2,1)S(1)} %get-tuple-element.236.refs_10_), channel_id=1, source_target_pairs={{0,8},{8,0},{16,24},{24,16},{1,9},{9,1},{17,25},{25,17},{2,10},{10... | collective-permute-start | bytes 1425416 | tf_op jit(solution)/shard_map/ppermute | solution.py:1122
  325.5 4.2 %collective-permute-done.11.refs_2_ = bf16[208,512]{1,0:T(8,128)(2,1)S(1)} collective-permute-done((bf16[208,512]{1,0:T(8,128)(2,1)S(1)}, bf16[208,512]{1,0:T(8,128)(2,1)S(1)}, u32[]{:S(2)}, u32[]{:S(2)}) %collective-permute-start.11) | collective-permute-done | bytes 213024 | tf_op jit(solution)/shard_map/ppermute | solution.py:44
  330.4 3.9 %collective-permute-done.12.refs_3_ = bf16[208,512]{1,0:T(8,128)(2,1)S(1)} collective-permute-done((bf16[208,512]{1,0:T(8,128)(2,1)S(1)}, bf16[208,512]{1,0:T(8,128)(2,1)S(1)}, u32[]{:S(2)}, u32[]{:S(2)}) %collective-permute-start.12) | collective-permute-done | bytes 213024 | tf_op jit(solution)/shard_map/ppermute | solution.py:44
  334.4 10.3 %collective-permute-done.13.refs_4_ = bf16[208,512]{1,0:T(8,128)(2,1)S(1)} collective-permute-done((bf16[208,512]{1,0:T(8,128)(2,1)S(1)}, bf16[208,512]{1,0:T(8,128)(2,1)S(1)}, u32[]{:S(2)}, u32[]{:S(2)}) %collective-permute-start.13) | collective-permute-done | bytes 213024 | tf_op jit(solution)/shard_map/ppermute | solution.py:44
  352.5 4.0 %collective-permute-done.18.refs_3_ = bf16[192,512]{1,0:T(8,128)(2,1)S(1)} collective-permute-done((bf16[192,512]{1,0:T(8,128)(2,1)S(1)}, bf16[192,512]{1,0:T(8,128)(2,1)S(1)}, u32[]{:S(2)}, u32[]{:S(2)}) %collective-permute-start.18) | collective-permute-done | bytes 196640 | tf_op jit(solution)/shard_map/ppermute | solution.py:44
  356.5 10.1 %collective-permute-done.19.refs_4_ = bf16[192,512]{1,0:T(8,128)(2,1)S(1)} collective-permute-done((bf16[192,512]{1,0:T(8,128)(2,1)S(1)}, bf16[192,512]{1,0:T(8,128)(2,1)S(1)}, u32[]{:S(2)}, u32[]{:S(2)}) %collective-permute-start.19) | collective-permute-done | bytes 196640 | tf_op jit(solution)/shard_map/ppermute | solution.py:44
  371.3 8.7 %all-gather = bf16[768,512]{1,0:T(8,128)(2,1)S(1)} all-gather(bf16[192,512]{1,0:T(8,128)(2,1)S(1)} %get-tuple-element.245), channel_id=2, replica_groups=mesh['dp'=4,'bank'=8] {'dp'}, dimensions={0}, use_global_device_ids=true | all-gather | bytes 983040 | tf_op jit(solution)/shard_map/all_gather | solution.py:1343
  (238 shorter events, 107.6 us)
Async XLA Ops:
  7.2 105.3 %all-gather.3.cloned.1.call-start = ((), (), s32[]{:S(2)}) async-start(), calls=%async_computation.5 | async-start | bytes 13516800 | tf_op jit(solution)/shard_map/all_gather | solution.py:1048
  138.5 11.8 %all-to-all-start = ((bf16[8,32,512]{2,1,0:T(8,128)(2,1)}), bf16[8,32,512]{2,1,0:T(8,128)(2,1)}, u32[]{:S(2)}, u32[]{:S(2)}) async-start(bf16[8,32,512]{2,1,0:T(8,128)(2,1)} %copy-done.12), calls=%async_computation | async-start | bytes 524288 | tf_op jit(solution)/shard_map/all_to_all | solution.py:64
  188.7 7.7 %collective-permute-start = (bf16[1024,512]{1,0:T(8,128)(2,1)}, bf16[1024,512]{1,0:T(8,128)(2,1)}, u32[]{:S(2)}, u32[]{:S(2)}) collective-permute-start(bf16[1024,512]{1,0:T(8,128)(2,1)} %get-tuple-element.161.refs_1_), channel_id=1, source_target_pairs={{0,8},{8,0},{16,24},{24,16},{1,9},{9,1},{17,25},{25,17},{2,10},{10... | collective-permute-start | bytes 3145736 | tf_op jit(solution)/shard_map/ppermute | solution.py:1122
  191.5 12.4 %all-to-all-start.3 = ((bf16[8,32,512]{2,1,0:T(8,128)(2,1)}), bf16[8,32,512]{2,1,0:T(8,128)(2,1)}, u32[]{:S(2)}, u32[]{:S(2)}) async-start(bf16[8,32,512]{2,1,0:T(8,128)(2,1)} %bitcast.56), calls=%async_computation.3 | async-start | bytes 524288 | tf_op jit(solution)/shard_map/all_to_all | solution.py:64
  200.3 33.8 %collective-permute-start.1 = (bf16[1024,512]{1,0:T(8,128)(2,1)}, bf16[1024,512]{1,0:T(8,128)(2,1)}, u32[]{:S(2)}, u32[]{:S(2)}) collective-permute-start(bf16[1024,512]{1,0:T(8,128)(2,1)} %get-tuple-element.174.refs_2_), channel_id=1, source_target_pairs={{0,16},{8,24},{16,0},{24,8},{1,17},{9,25},{17,1},{25,9},{2,18},{10... | collective-permute-start | bytes 3145736 | tf_op jit(solution)/shard_map/ppermute | solution.py:1122
  232.2 9.1 %collective-permute-start.2 = (bf16[16,208,512]{2,1,0:T(8,128)(2,1)S(1)}, bf16[16,208,512]{2,1,0:T(8,128)(2,1)S(1)}, u32[]{:S(2)}, u32[]{:S(2)}) collective-permute-start(bf16[16,208,512]{2,1,0:T(8,128)(2,1)S(1)} %get-tuple-element.178), channel_id=1, source_target_pairs={{0,8},{8,0},{16,24},{24,16},{1,9},{9,1},{17,25},{25,17},{2,10},{10... | collective-permute-start | bytes 10223624 | tf_op jit(solution)/shard_map/ppermute | solution.py:44
  241.3 9.5 %collective-permute-start.5 = (bf16[16,192,512]{2,1,0:T(8,128)(2,1)S(1)}, bf16[16,192,512]{2,1,0:T(8,128)(2,1)S(1)}, u32[]{:S(2)}, u32[]{:S(2)}) collective-permute-start(bf16[16,192,512]{2,1,0:T(8,128)(2,1)S(1)} %get-tuple-element.188), channel_id=1, source_target_pairs={{0,8},{8,0},{16,24},{24,16},{1,9},{9,1},{17,25},{25,17},{2,10},{10... | collective-permute-start | bytes 9437192 | tf_op jit(solution)/shard_map/ppermute | solution.py:44
  243.2 20.1 %collective-permute-start.3 = (bf16[2,2,208,512]{3,2,1,0:T(8,128)(2,1)S(1)}, bf16[2,2,208,512]{3,2,1,0:T(8,128)(2,1)S(1)}, u32[]{:S(2)}, u32[]{:S(2)}) collective-permute-start(bf16[2,2,208,512]{3,2,1,0:T(8,128)(2,1)S(1)} %get-tuple-element.184), channel_id=1, source_target_pairs={{0,16},{8,24},{16,0},{24,8},{1,17},{9,25},{17,1},{25,9},{2,18},{10... | collective-permute-start | bytes 2555912 | tf_op jit(solution)/shard_map/ppermute | solution.py:44
  244.4 19.7 %collective-permute-start.4 = (bf16[2,2,208,512]{3,2,1,0:T(8,128)(2,1)S(1)}, bf16[2,2,208,512]{3,2,1,0:T(8,128)(2,1)S(1)}, u32[]{:S(2)}, u32[]{:S(2)}) collective-permute-start(bf16[2,2,208,512]{3,2,1,0:T(8,128)(2,1)S(1)} %get-tuple-element.186), channel_id=1, source_target_pairs={{0,1},{1,0},{2,3},{3,2},{4,5},{5,4},{6,7},{7,6},{8,9},{9,8},{10,11... | collective-permute-start | bytes 2555912 | tf_op jit(solution)/shard_map/ppermute | solution.py:44
  268.9 28.0 %collective-permute-start.6 = (bf16[1184,512]{1,0:T(8,128)(2,1)}, bf16[1184,512]{1,0:T(8,128)(2,1)}, u32[]{:S(2)}, u32[]{:S(2)}) collective-permute-start(bf16[1184,512]{1,0:T(8,128)(2,1)} %get-tuple-element.216), channel_id=1, source_target_pairs={{0,16},{8,24},{16,0},{24,8},{1,17},{9,25},{17,1},{25,9},{2,18},{10... | collective-permute-start | bytes 3637256 | tf_op jit(solution)/shard_map/ppermute | solution.py:44
  269.2 29.0 %collective-permute-start.7 = (bf16[1184,512]{1,0:T(8,128)(2,1)}, bf16[1184,512]{1,0:T(8,128)(2,1)}, u32[]{:S(2)}, u32[]{:S(2)}) collective-permute-start(bf16[1184,512]{1,0:T(8,128)(2,1)} %get-tuple-element.217), channel_id=1, source_target_pairs={{0,1},{1,0},{2,3},{3,2},{4,5},{5,4},{6,7},{7,6},{8,9},{9,8},{10,11... | collective-permute-start | bytes 3637256 | tf_op jit(solution)/shard_map/ppermute | solution.py:44
  275.2 8.7 %collective-permute-start.8 = (bf16[2,400,128]{2,1,0:T(8,128)(2,1)S(1)}, bf16[2,400,128]{2,1,0:T(8,128)(2,1)S(1)}, u32[]{:S(2)}, u32[]{:S(2)}) collective-permute-start(bf16[2,400,128]{2,1,0:T(8,128)(2,1)S(1)} %get-tuple-element.219), channel_id=1, source_target_pairs={{0,2},{1,3},{2,0},{3,1},{4,6},{5,7},{6,4},{7,5},{8,10},{9,11},{10,... | collective-permute-start | bytes 614408 | tf_op jit(solution)/shard_map/ppermute | solution.py:44
  277.0 19.8 %collective-permute-start.10 = (bf16[2,400,128]{2,1,0:T(8,128)(2,1)}, bf16[2,400,128]{2,1,0:T(8,128)(2,1)S(1)}, u32[]{:S(2)}, u32[]{:S(2)}) collective-permute-start(bf16[2,400,128]{2,1,0:T(8,128)(2,1)} %get-tuple-element.221), channel_id=1, source_target_pairs={{0,6},{1,7},{2,4},{3,5},{4,2},{5,3},{6,0},{7,1},{8,14},{9,15},{10,... | collective-permute-start | bytes 614408 | tf_op jit(solution)/shard_map/ppermute | solution.py:44
  278.2 36.1 %all-to-all-start.4 = ((bf16[8,32,1792]{2,1,0:T(8,128)(2,1)}), bf16[8,32,1792]{2,1,0:T(8,128)(2,1)S(1)}, u32[]{:S(2)}, u32[]{:S(2)}) async-start(bf16[8,32,1792]{2,1,0:T(8,128)(2,1)} %get-tuple-element.223), calls=%async_computation.4 | async-start | bytes 1835008 | tf_op jit(solution)/shard_map/all_to_all | solution.py:64
  309.1 35.6 %collective-permute-start.15 = (bf16[496,512]{1,0:T(8,128)(2,1)S(1)}, bf16[496,512]{1,0:T(8,128)(2,1)S(1)}, u32[]{:S(2)}, u32[]{:S(2)}) collective-permute-start(bf16[496,512]{1,0:T(8,128)(2,1)S(1)} %get-tuple-element.235), channel_id=1, source_target_pairs={{0,1},{1,0},{2,3},{3,2},{4,5},{5,4},{6,7},{7,6},{8,9},{9,8},{10,11... | collective-permute-start | bytes 1523720 | tf_op jit(solution)/shard_map/ppermute | solution.py:44
  315.7 29.1 %collective-permute-start.16 = (bf16[464,512]{1,0:T(8,128)(2,1)S(1)}, bf16[464,512]{1,0:T(8,128)(2,1)S(1)}, u32[]{:S(2)}, u32[]{:S(2)}) collective-permute-start(bf16[464,512]{1,0:T(8,128)(2,1)S(1)} %get-tuple-element.236.refs_10_), channel_id=1, source_target_pairs={{0,8},{8,0},{16,24},{24,16},{1,9},{9,1},{17,25},{25,17},{2,10},{10... | collective-permute-start | bytes 1425416 | tf_op jit(solution)/shard_map/ppermute | solution.py:1122
  322.4 22.3 %collective-permute-start.14 = (bf16[384,512]{1,0:T(8,128)(2,1)S(1)}, bf16[384,512]{1,0:T(8,128)(2,1)S(1)}, u32[]{:S(2)}, u32[]{:S(2)}) collective-permute-start(bf16[384,512]{1,0:T(8,128)(2,1)S(1)} %get-tuple-element.234), channel_id=1, source_target_pairs={{0,16},{8,24},{16,0},{24,8},{1,17},{9,25},{17,1},{25,9},{2,18},{10... | collective-permute-start | bytes 1179656 | tf_op jit(solution)/shard_map/ppermute | solution.py:44
  323.6 10.8 %collective-permute-start.12 = (bf16[208,512]{1,0:T(8,128)(2,1)S(1)}, bf16[208,512]{1,0:T(8,128)(2,1)S(1)}, u32[]{:S(2)}, u32[]{:S(2)}) collective-permute-start(bf16[208,512]{1,0:T(8,128)(2,1)S(1)} %get-tuple-element.229), channel_id=1, source_target_pairs={{0,4},{1,5},{2,6},{3,7},{4,0},{5,1},{6,2},{7,3},{8,12},{9,13},{10,... | collective-permute-start | bytes 638984 | tf_op jit(solution)/shard_map/ppermute | solution.py:44
  329.7 15.0 %collective-permute-start.13 = (bf16[208,512]{1,0:T(8,128)(2,1)S(1)}, bf16[208,512]{1,0:T(8,128)(2,1)S(1)}, u32[]{:S(2)}, u32[]{:S(2)}) collective-permute-start(bf16[208,512]{1,0:T(8,128)(2,1)S(1)} %get-tuple-element.230), channel_id=1, source_target_pairs={{0,6},{1,7},{2,4},{3,5},{4,2},{5,3},{6,0},{7,1},{8,14},{9,15},{10,... | collective-permute-start | bytes 638984 | tf_op jit(solution)/shard_map/ppermute | solution.py:44
  346.2 20.4 %collective-permute-start.20 = (bf16[464,512]{1,0:T(8,128)(2,1)S(1)}, bf16[464,512]{1,0:T(8,128)(2,1)S(1)}, u32[]{:S(2)}, u32[]{:S(2)}) collective-permute-start(bf16[464,512]{1,0:T(8,128)(2,1)S(1)} %get-tuple-element.242.refs_5_), channel_id=1, source_target_pairs={{0,16},{8,24},{16,0},{24,8},{1,17},{9,25},{17,1},{25,9},{2,18},{10... | collective-permute-start | bytes 1425416 | tf_op jit(solution)/shard_map/ppermute | solution.py:44
  346.7 19.9 %collective-permute-start.21 = (bf16[320,512]{1,0:T(8,128)(2,1)S(1)}, bf16[320,512]{1,0:T(8,128)(2,1)S(1)}, u32[]{:S(2)}, u32[]{:S(2)}) collective-permute-start(bf16[320,512]{1,0:T(8,128)(2,1)S(1)} %get-tuple-element.243.refs_7_), channel_id=1, source_target_pairs={{0,16},{8,24},{16,0},{24,8},{1,17},{9,25},{17,1},{25,9},{2,18},{10... | collective-permute-start | bytes 983048 | tf_op jit(solution)/shard_map/ppermute | solution.py:44
  347.7 8.8 %collective-permute-start.18 = (bf16[192,512]{1,0:T(8,128)(2,1)S(1)}, bf16[192,512]{1,0:T(8,128)(2,1)S(1)}, u32[]{:S(2)}, u32[]{:S(2)}) collective-permute-start(bf16[192,512]{1,0:T(8,128)(2,1)S(1)} %get-tuple-element.240), channel_id=1, source_target_pairs={{0,4},{1,5},{2,6},{3,7},{4,0},{5,1},{6,2},{7,3},{8,12},{9,13},{10,... | collective-permute-start | bytes 589832 | tf_op jit(solution)/shard_map/ppermute | solution.py:44
  349.7 16.9 %collective-permute-start.19 = (bf16[192,512]{1,0:T(8,128)(2,1)S(1)}, bf16[192,512]{1,0:T(8,128)(2,1)S(1)}, u32[]{:S(2)}, u32[]{:S(2)}) collective-permute-start(bf16[192,512]{1,0:T(8,128)(2,1)S(1)} %get-tuple-element.241), channel_id=1, source_target_pairs={{0,6},{1,7},{2,4},{3,5},{4,2},{5,3},{6,0},{7,1},{8,14},{9,15},{10,... | collective-permute-start | bytes 589832 | tf_op jit(solution)/shard_map/ppermute | solution.py:44
  368.2 11.8 %collective-permute-start.22 = (bf16[2,320,512]{2,1,0:T(8,128)(2,1)S(1)}, bf16[2,320,512]{2,1,0:T(8,128)(2,1)S(1)}, u32[]{:S(2)}, u32[]{:S(2)}) collective-permute-start(bf16[2,320,512]{2,1,0:T(8,128)(2,1)S(1)} %get-tuple-element.246.refs_2_), channel_id=1, source_target_pairs={{0,8},{8,0},{16,24},{24,16},{1,9},{9,1},{17,25},{25,17},{2,10},{10... | collective-permute-start | bytes 1966088 | tf_op jit(solution)/shard_map/ppermute | solution.py:44
  (82 other events, 563.4 us)
Sparse Core Ops, SparseCore 0:
  12.9 99.4 all-gather.2

commit v4 on v3

--- a/solution.py
+++ b/solution.py
@@ -60,6 +60,25 @@
     )
 
 
+def gather_blocks(own, axes, places, steps):
+    outer, inner, across, last = axes
+    blocks = [own] + [outer.swap(own, step) for step in range(1, outer.size)]
+    places = steps[0](places)
+    *blocks, places = lax.optimization_barrier((*blocks, places))
+    blocks = jnp.stack(blocks)
+    half = outer.size // 2
+    first, second = blocks[:half], blocks[half:]
+    got_first, got_second = across.swap(first, 1), inner.swap(second, 1)
+    places = steps[1](places)
+    first, got_first, second, got_second, places = lax.optimization_barrier((first, got_first, second, got_second, places))
+    first, second = jnp.concatenate([first, got_first]), jnp.concatenate([second, got_second])
+    got_first, got_second = inner.swap(first, 1), across.swap(second, 1)
+    places = steps[2](places)
+    first, got_first, second, got_second, places = lax.optimization_barrier((first, got_first, second, got_second, places))
+    near = jnp.concatenate([first, got_first, second, got_second])
+    return places, [near, last.swap(near, 1)]
+
+
 def to_owners(value):
     return lax.all_to_all(value, "bank", split_axis=0, concat_axis=0, tiled=True)
 
@@ -159,24 +178,34 @@
         copy.wait()
 
 
-def first_conv(fm_ref, packed_ref, scale_ref, shift_ref, pre_out_ref, act_ref, weight_out_ref, weight, pre_ref, sems, out_sems):
+def gathered_spot(places_ref, number, far):
+    second, rest = divmod(number, 8)
+    high, low_bits = divmod(rest, 4)
+    middle, step = divmod(low_bits, 2)
+    across, inner = (high, middle) if second else (middle, high)
+    outer = (places_ref[2] ^ (2 * second + step)) * 2 + (places_ref[1] ^ inner)
+    return (outer * 2 + (places_ref[0] ^ across)) * 2 + (places_ref[3] ^ far)
+
+
+def first_conv(places_ref, fm_ref, *refs):
+    sources, refs = refs[:-9], refs[-9:]
+    scale_ref, shift_ref, pre_out_ref, act_ref, weight_out_ref, weight, pre_ref, sems, out_sems = refs
     sites, features = fm_ref.shape
-    channels = pre_ref.shape[1]
-    groups = weight.shape[0] // packed_ref.shape[0]
-    copies = fetch(packed_ref, weight, sems, 0, groups)
-    for copy in copies:
-        copy.start()
-    block_rows = groups * LANE_ROWS
+    channels = act_ref.shape[1]
+    groups = sources[0].shape[1]
+    copies = []
+    for far, source in enumerate(sources):
+        for number in range(source.shape[0]):
+            block = gathered_spot(places_ref, number, far) if len(sources) > 1 else number
+            target = weight.at[pl.ds(block * groups, groups)]
+            copies.append(pltpu.make_async_copy(source.at[number], target, sems.at[len(copies)]))
+    start_all(copies)
     clip = FRAMES * SIDE * SIDE
     frame = SIDE * SIDE
-    waited = 0
+    wait_all(copies)
+    out = start_all([pltpu.make_async_copy(weight, weight_out_ref, out_sems.at[1])])
 
     def tap(number):
-        nonlocal waited
-        end = (number + 1) * features
-        while waited < len(copies) and waited * block_rows < end:
-            copies[waited].wait()
-            waited += 1
         begin = number * features // LANE_ROWS
         return weight[begin : begin + features // LANE_ROWS].reshape(features, channels)
 
@@ -186,7 +215,6 @@
         pre_ref[start + frame : start + clip] = product(fm_ref[start : start + clip - frame], before)
     pre_ref[...] += product(fm_ref[...], tap(1))
     after = tap(2)
-    out = start_all([pltpu.make_async_copy(weight, weight_out_ref, out_sems.at[1])])
     for start in range(0, sites, clip):
         pre_ref[start : start + clip - frame] += product(fm_ref[start + frame : start + clip], after)
 
@@ -194,14 +222,14 @@
         act_ref[rows] = low(gelu_of(pre_ref[rows] * scale_ref[...] + shift_ref[...]))
 
     out += start_all([pltpu.make_async_copy(pre_ref, pre_out_ref, out_sems.at[0])])
-    by_rows(sites, 64, finish)
+    by_rows(sites, 128, finish)
     wait_all(out)
 
 
 def later_convs(
     act_a_ref, fm_ref, packed_ref, scale_b_ref, shift_b_ref, scale_c_ref, shift_c_ref, pool_ref, w_reduce_ref, w_query_ref,
-    pre_b_out_ref, act_b_out_ref, pre_c_ref, regions_ref, reduced_ref, queries_ref,
-    weight_b, weight_c, out_low, held_map, held_pre, held_reduce, pre_b_ref, act_b_ref, sems_b, sems_c, sems,
+    pre_b_out_ref, act_b_out_ref, pre_c_ref, regions_out_ref, reduced_out_ref, queries_ref,
+    weight_b, weight_c, out_low, held_map, held_pre, held_reduce, pre_b_ref, act_b_ref, regions_ref, reduced_ref, sems_b, sems_c, sems,
 ):
     sites, channels = act_a_ref.shape
     blocks = packed_ref.shape[0]
@@ -235,7 +263,7 @@
     def finish(rows):
         act_b_ref[rows] = low(gelu_of(pre_b_ref[rows] * scale_b_ref[...] + shift_b_ref[...]))
 
-    by_rows(sites, 64, finish)
+    by_rows(sites, 128, finish)
     outs += start_all([pltpu.make_async_copy(act_b_ref, act_b_out_ref, sems.at[3 + groups_c])])
     wait_all(copies_c + others)
     reduced_ref[...] = jnp.zeros_like(reduced_ref)
@@ -249,13 +277,19 @@
             linear = wide(held_map[rows, columns]) + held_pre[rows, columns] * scale_c_ref[:, columns] + shift_c_ref[:, columns]
             out_low[rows] = low(gelu_of(linear))
 
-        by_rows(sites, 64, finish_c)
+        by_rows(sites, 128, finish_c)
         part = low(product(pool_ref[...], out_low[...]))
         regions_ref[:, columns] = part
         reduced_ref[...] += product(part, held_reduce[columns])
         return carry
 
     lax.fori_loop(0, groups_c, chunk, 0)
+    outs += start_all(
+        [
+            pltpu.make_async_copy(regions_ref, regions_out_ref, sems.at[4 + groups_c]),
+            pltpu.make_async_copy(reduced_ref, reduced_out_ref, sems.at[5 + groups_c]),
+        ]
+    )
     queries = low(product(low(reduced_ref[...]), w_query_ref[...]))
     for place in range(queries_ref.shape[0]):
         queries_ref[place] = queries
@@ -384,14 +418,14 @@
     sites, channels = pre_ref.shape
 
     def one(step, sums):
-        rows = pl.ds(pl.multiple_of(step * 64, 64), 64)
+        rows = pl.ds(pl.multiple_of(step * 128, 128), 128)
         pre = pre_ref[rows]
         grad = upstream_ref[rows] * gelu_slope(pre * scale_ref[...] + shift_ref[...])
         out_ref[rows] = low(grad * scale_ref[...]).astype(out_ref.dtype)
         return sums[0] + fold(grad * pre), sums[1] + fold(grad)
 
     zero = jnp.zeros((8, channels), jnp.float32)
-    scale_sum, shift_sum = lax.fori_loop(0, sites // 64, one, (zero, zero))
+    scale_sum, shift_sum = lax.fori_loop(0, sites // 128, one, (zero, zero))
     scale_out_ref[...] = jnp.sum(scale_sum, axis=0, keepdims=True)
     shift_out_ref[...] = jnp.sum(shift_sum, axis=0, keepdims=True)
 
@@ -439,7 +473,7 @@
         part_of(fm_ref, held_map, number, 4 + chunks).wait()
 
         def one(step, sums):
-            rows = pl.ds(pl.multiple_of(step * 64, 64), 64)
+            rows = pl.ds(pl.multiple_of(step * 128, 128), 128)
             pre = held_pre_c[rows, columns]
             scale = scale_ref[:, columns]
             linear = wide(held_map[rows, columns]) + pre * scale + shift_ref[:, columns]
@@ -449,7 +483,7 @@
             return sums[0] + fold(grad * pre), sums[1] + fold(grad)
 
         zero = jnp.zeros((8, channels), jnp.float32)
-        scale_sum, shift_sum = lax.fori_loop(0, sites // 64, one, (zero, zero))
+        scale_sum, shift_sum = lax.fori_loop(0, sites // 128, one, (zero, zero))
         part_of(held_lin, lin_c_grad_ref, number, 4 + 2 * chunks).start()
         scale_c_out_ref[:, columns] = jnp.sum(scale_sum, axis=0, keepdims=True)
         shift_c_out_ref[:, columns] = jnp.sum(shift_sum, axis=0, keepdims=True)
@@ -546,6 +580,7 @@
 
 COST = 6e9
 WINDOW = 0.1
+FIRST_LIMIT = 52
 F32 = jnp.float32
 BF16 = jnp.bfloat16
 ANY = pl.BlockSpec(memory_space=pl.ANY)
@@ -558,7 +593,7 @@
 
 
 def add_low(left, right):
-    return low(wide(left) + wide(right))
+    return left + right
 
 
 class Blocks:
@@ -674,6 +709,7 @@
 
 
 def round_three(count, split, places_ref, kept_one, kept_two, keep_a_one, keep_a_two, got_across, got_inner, *refs):
+    region_refs, refs = (refs[:2], refs[2:]) if split else (refs[:1], refs[1:])
     bank_refs, refs = (refs[:count], refs[count:]) if split else (refs[:1], refs[1:])
     kept_ref, sends, refs = refs[0], refs[1 : count], refs[count:]
     kept_a_one, kept_a_two, bank_keep_ref, across_ref, inner_ref = refs
@@ -689,6 +725,7 @@
         Blocks(got_inner, 0, (half, 2), rows_a), kept_a_one, Blocks(inner_ref, 0, (half,), rows_a), kept_a_two,
         Blocks(across_ref, 0, (half,), rows_a),
     )
+    across_ref[half * rows_a :] = low(total_of(region_refs))
     inner = places_ref[7] if split else 0
     keep = total_of([ref.at[inner] for ref in bank_refs])
     store_narrow(bank_keep_ref, 0, low(keep), channels)
@@ -699,11 +736,10 @@
         inner_ref[half * rows_a :] = bank_keep_ref[...]
 
 
-def round_four(count, split, places_ref, *refs):
+def round_four(count, split, widths, places_ref, *refs):
     plane_refs, refs = refs[:count], refs[count:]
-    kept_a_one, kept_a_two, bank_keep_ref, got_across, got_inner = refs[:5]
-    region_refs, refs = (refs[5:7], refs[7:]) if split else (refs[5:6], refs[6:])
-    done_ref, region_ref, kept_a_ref, *sends = refs
+    kept_a_one, kept_a_two, bank_keep_ref, across_ref, got_across, got_inner, done_ref, kept_a_ref = refs[:8]
+    sends, (reduce_ref, query_ref, out_ref, head_ref) = refs[8 : 7 + count], refs[7 + count :]
     half, rows_a, channels = kept_a_one.shape
     rows = plane_refs[0].shape[0]
     below = half * rows_a
@@ -713,28 +749,77 @@
     )
     done_ref[:rows] = low(total_of(plane_refs))
     done_ref[rows:] = add_low(bank_keep_ref[...], got_inner[below:]) if split else bank_keep_ref[...]
-    region_ref[...] = low(total_of(region_refs))
-
-
-def round_last(count, split, widths, places_ref, *refs):
-    outer_refs, refs = refs[:count], refs[count:]
-    region_refs, refs = (refs[:2], refs[2:]) if split else (refs[:1], refs[1:])
-    done_refs, refs = (refs[:2], refs[2:]) if split else ((), refs)
-    part_ref, reduce_ref, query_ref, out_ref, head_ref, *both = refs
-    part_ref[...] = low(total_of(outer_refs))
-    region = total_of(region_refs)
+    region = wide(across_ref[below:]) + wide(got_across[below:]) if split else wide(across_ref[below:])
     _, _, feature_rows, channel_rows, _, joined_rows = widths
     reduce_ref[...] = region[:feature_rows]
     query_ref[...] = region[feature_rows : feature_rows + channel_rows]
     out_ref[...] = region[feature_rows + channel_rows : feature_rows + 2 * channel_rows]
     head = load_narrow(region, feature_rows + 2 * channel_rows, joined_rows, TILE)
     head_ref[...] = head[:, : head_ref.shape[1]]
-    for number, ref in enumerate(done_refs):
-        both[0][number] = ref[...]
+
+
+def round_last(count, places_ref, *refs):
+    part_ref, both = refs[-1 if len(refs) == count + 1 else -2], refs[-1]
+    part_ref[...] = low(total_of(refs[:count]))
+    if len(refs) > count + 1:
+        for number, ref in enumerate(refs[count : count + 2]):
+            both[number] = ref[...]
 
 
 def sum_swap(places_ref, *refs):
     refs[-1][...] = low(total_of(refs[:-1]))
+
+
+def front_pack(groups_a, groups_b, places_ref, conv_a_ref, conv_b_ref, conv_c_ref, own_a_ref, own_ref, sems):
+    place = places_ref[9]
+    chunks = own_ref.shape[0] - groups_b
+    channels = own_ref.shape[2]
+    copies = [
+        pltpu.make_async_copy(conv_b_ref.at[pl.ds(place * groups_b, groups_b)], own_ref.at[pl.ds(0, groups_b)], sems.at[0]),
+        pltpu.make_async_copy(conv_a_ref.at[pl.ds(place * groups_a, groups_a)], own_a_ref, sems.at[1]),
+    ]
+    for chunk in range(chunks):
+        copies.append(
+            pltpu.make_async_copy(
+                conv_c_ref.at[place, :, pl.ds(chunk * channels, channels)], own_ref.at[groups_b + chunk], sems.at[2 + chunk]
+            )
+        )
+    wait_all(start_all(copies))
+
+
+def front_turn(places_ref, map_ref, bank_ref, turned_map_ref, turned_bank_ref):
+    sites, features = map_ref.shape
+    for start in range(0, features, sites):
+        turned_map_ref[start : start + sites] = map_ref[:, start : start + sites].T
+        turned_bank_ref[start : start + sites] = bank_ref[:, start : start + sites].T
+
+
+def front_bank(places_ref, bank_ref, w_bank_ref, w_key_ref, w_value_ref, keys_ref, values_ref, turned_memory_ref):
+    memory = low(product(bank_ref[...], w_bank_ref[...]))
+    keys_ref[...] = low(product(memory, w_key_ref[...]))
+    values_ref[...] = low(product(memory, w_value_ref[...]))
+    turned_memory_ref[...] = memory.T
+
+
+def front_head(
+    places_ref, index_ref, weight_ref, logit_grad_ref, w_head_ref, w_out_ref,
+    pool_ref, joined_grad_ref, hidden_grad_ref, branch_grad_ref,
+):
+    own, taps = index_ref.shape
+    sites = pool_ref.shape[1]
+    channels = hidden_grad_ref.shape[1]
+    features = w_head_ref.shape[0] - channels
+    column = lax.broadcasted_iota(jnp.int32, (own, sites), 1)
+    pool = jnp.zeros((own, sites), F32)
+    for tap in range(taps):
+        weight = wide(weight_ref[:, tap : tap + 1])
+        pool = pool + jnp.where(column == index_ref[:, tap : tap + 1], weight, 0.0)
+    pool_ref[...] = low(pool)
+    logit_grad = logit_grad_ref[pl.ds(pl.multiple_of(places_ref[8], LANE_ROWS), own)]
+    joined_grad = dot_nt(logit_grad, w_head_ref[...])
+    joined_grad_ref[...] = joined_grad
+    hidden_grad_ref[...] = dot_nt(low(joined_grad[:, features:]), w_out_ref[...])
+    branch_grad_ref[...] = low(dot_nt(logit_grad_ref[...], w_head_ref[features:]))
 
 
 def region_pack(
@@ -883,15 +968,12 @@
 
     def wrapped(*refs):
         places_ref, ins = refs[0], list(refs[1 : 1 + count_in])
-        out_places, outs = refs[1 + count_in], list(refs[2 + count_in : 2 + count_in + count_out])
+        out_places, outs = refs[1 + count_in], refs[2 + count_in : 2 + count_in + count_out]
         extra = refs[2 + count_in + count_out :]
         if fetched:
             held, sems, extra = extra[: len(fetched)], extra[len(fetched)], extra[len(fetched) + 1 :]
             copies = start_all(
-                [
-                    pltpu.make_async_copy(ins[number], held[slot], sems.at[slot])
-                    for slot, number in enumerate(fetched)
-                ]
+                [pltpu.make_async_copy(ins[number], held[slot], sems.at[slot]) for slot, number in enumerate(fetched)]
             )
         for number in range(places.shape[0]):
             out_places[number] = places_ref[number]
@@ -919,28 +1001,29 @@
     )(places, *arrays)
 
 
-def run_first_conv(feature_map, packed, scale, shift, groups):
-    sites, channels = feature_map.shape[0], packed.shape[3]
-    blocks = packed.shape[0]
+def run_first_conv(places, feature_map, sources, scale, shift):
+    sites, channels = feature_map.shape[0], sources[0].shape[3]
+    groups = sources[0].shape[1]
+    blocks = sum(source.shape[0] for source in sources)
     return pl.pallas_call(
         first_conv,
         out_shape=[
-            jax.ShapeDtypeStruct((sites, channels), jnp.float32),
-            jax.ShapeDtypeStruct((sites, channels), jnp.bfloat16),
-            jax.ShapeDtypeStruct((blocks * groups, LANE_ROWS, channels), jnp.bfloat16),
+            shape_of((sites, channels), F32),
+            shape_of((sites, channels), BF16),
+            shape_of((blocks * groups, LANE_ROWS, channels), BF16),
         ],
-        in_specs=[pl.BlockSpec(memory_space=pltpu.VMEM), pl.BlockSpec(memory_space=pl.ANY)] + [HELD] * 2,
+        in_specs=[SCALAR, HELD] + [ANY] * len(sources) + [HELD] * 2,
         out_specs=[ANY, HELD, ANY],
         scratch_shapes=[
-            pltpu.VMEM((blocks * groups, LANE_ROWS, channels), jnp.bfloat16),
-            pltpu.VMEM((sites, channels), jnp.float32),
+            pltpu.VMEM((blocks * groups, LANE_ROWS, channels), BF16),
+            pltpu.VMEM((sites, channels), F32),
             pltpu.SemaphoreType.DMA((blocks,)),
             pltpu.SemaphoreType.DMA((2,)),
         ],
-        compiler_params=params(52),
+        compiler_params=params(FIRST_LIMIT),
         cost_estimate=pl.CostEstimate(flops=int(6 * COST), bytes_accessed=int(6 * COST / 1000), transcendentals=0),
         name="first_conv",
-    )(feature_map, packed, scale.reshape(1, -1), shift.reshape(1, -1))
+    )(places, feature_map, *sources, scale.reshape(1, -1), shift.reshape(1, -1))
 
 
 def run_later_convs(
@@ -962,7 +1045,7 @@
             jax.ShapeDtypeStruct((group, own, channels), jnp.bfloat16),
         ],
         in_specs=[HELD] + [ANY] * 2 + [HELD] * 5 + [ANY, HELD],
-        out_specs=[ANY] * 3 + [HELD] * 3,
+        out_specs=[ANY] * 5 + [HELD],
         scratch_shapes=[
             pltpu.VMEM((blocks * groups_b, LANE_ROWS, channels), jnp.bfloat16),
             pltpu.VMEM((groups_c, blocks, LANE_ROWS, channels), jnp.bfloat16),
@@ -972,9 +1055,11 @@
             pltpu.VMEM(w_reduce.shape, jnp.bfloat16),
             pltpu.VMEM((sites, channels), jnp.float32),
             pltpu.VMEM((sites, channels), jnp.bfloat16),
+            pltpu.VMEM((own, features), jnp.bfloat16),
+            pltpu.VMEM((own, channels), jnp.float32),
             pltpu.SemaphoreType.DMA((blocks,)),
             pltpu.SemaphoreType.DMA((blocks,)),
-            pltpu.SemaphoreType.DMA((4 + groups_c,)),
+            pltpu.SemaphoreType.DMA((6 + groups_c,)),
         ],
         compiler_params=params(52),
         cost_estimate=pl.CostEstimate(flops=int(15 * COST), bytes_accessed=int(15 * COST / 1000), transcendentals=0),
@@ -1026,62 +1111,95 @@
     group_rows = bank_count * own_count
     chunks = feature_count // channels
     shards = (conv_a, conv_b, conv_c)
-    split = dp_count // 2 == 2 and all(shard.shape[0] % (LANE_ROWS * dp_count) == 0 for shard in shards)
+    split = dp_count // 2 == 2 and bank_count // 2 == 4 and all(shard.shape[0] % (LANE_ROWS * dp_count) == 0 for shard in shards)
     axes = block_axes(split, dp_count, bank_count)
     outer, inner, across, last = axes
     outer_count = outer.size if split else 1
     blocks = bank_count * dp_count if split else bank_count
     halves = tuple(axis.size for axis in axes[:3])
-    places_here = jnp.stack([across.place(), inner.place(), outer.place(), last.place(), dp_place, bank_place * keys_here, outer.place() if split else 0 * bank_place, inner.place()])
-
-    def own_part(shard):
-        if not split:
-            return shard
-        rows = shard.shape[0] // dp_count
-        return lax.dynamic_slice_in_dim(shard, dp_place * rows, rows, 0)
-
-    part_a, part_b, part_c = [own_part(shard) for shard in shards]
-    rows_a, rows_b, rows_c = part_a.shape[0], part_b.shape[0], part_c.shape[0]
+    places_here = jnp.stack([across.place(), inner.place(), outer.place(), last.place(), dp_place, bank_place * keys_here, outer.place() if split else 0 * bank_place, inner.place(), first_row, dp_place if split else 0 * dp_place])
+
+    parts = dp_count if split else 1
+    rows_a, rows_b, rows_c = [shard.shape[0] // parts for shard in shards]
     groups_a, groups_b, groups_c = rows_a // LANE_ROWS, rows_b // LANE_ROWS, chunks
-    pieces_c = [part_c[:, chunk * channels : (chunk + 1) * channels] for chunk in range(chunks)]
-    own_packed = jnp.concatenate([part_a, part_b] + pieces_c, 0).reshape(-1, LANE_ROWS, channels)
+    places, own_a, own_packed = run_kernel(
+        functools.partial(front_pack, groups_a, groups_b),
+        places_here,
+        [shard.reshape(-1, LANE_ROWS, shard.shape[1]) for shard in shards],
+        [shape_of((groups_a, LANE_ROWS, channels), BF16), shape_of((groups_b + chunks, LANE_ROWS, channels), BF16)],
+        "front_pack",
+        1,
+        scratch=[pltpu.SemaphoreType.DMA((2 + chunks,))],
+        raw_in=(0, 1, 2),
+        raw_out=(0, 1),
+    )
     packed = lax.all_gather(own_packed, ("bank", "dp") if split else "bank", axis=0, tiled=False)
     packed = packed.reshape((blocks,) + own_packed.shape)
-
-    memory = product(bank, w_bank)
-    memory_low = low(memory)
-    keys = low(product(memory_low, w_key))
-    values = low(product(memory_low, w_value))
-    turned_map, turned_bank, turned_memory = feature_map.T, bank.T, memory_low.T
-    matches = roi_index[:, :, None] == jnp.arange(site_count, dtype=jnp.int32)[None, None, :]
-    pooling = low(jnp.sum(jnp.where(matches, wide(roi_weight)[:, :, None], 0.0), axis=1))
-    own_logit_grad = lax.dynamic_slice_in_dim(logit_grad, first_row, own_count, 0)
-    joined_grad = dot_nt(own_logit_grad, w_head)
-    branch_grad = low(joined_grad[:, feature_count:])
-    hidden_grad = dot_nt(branch_grad, w_out)
-    group_branch_grad = low(dot_nt(logit_grad, w_head[feature_count:]))
     spare = ((0, 0), (0, TILE - classes))
     wide_head, wide_logit_grad = jnp.pad(w_head, spare), jnp.pad(logit_grad, spare)
+    front = {}
+
+    def turn(places):
+        places, front["turned_map"], front["turned_bank"] = run_kernel(
+            front_turn,
+            places,
+            [feature_map, bank],
+            [shape_of((feature_count, site_count), BF16), shape_of((feature_count, keys_here), BF16)],
+            "front_turn",
+            6,
+            limit=16,
+        )
+        return places
+
+    def project(places):
+        inside = shape_of((keys_here, channels), BF16)
+        places, front["keys"], front["values"], front["turned_memory"] = run_kernel(
+            front_bank,
+            places,
+            [bank, w_bank, w_key, w_value],
+            [inside, inside, shape_of((channels, keys_here), BF16)],
+            "front_bank",
+            6,
+            limit=16,
+        )
+        return places
+
+    def head(places):
+        places, front["pooling"], front["joined_grad"], front["hidden_grad"], front["group_branch_grad"] = run_kernel(
+            front_head,
+            places,
+            [roi_index, roi_weight, wide_logit_grad, wide_head, w_out],
+            [
+                shape_of((own_count, site_count), BF16),
+                shape_of((own_count, w_head.shape[0]), F32),
+                shape_of((own_count, channels), F32),
+                shape_of((group_rows, channels), BF16),
+            ],
+            "front_head",
+            4,
+            limit=16,
+        )
+        return places
+
+    if split:
+        places, sources = gather_blocks(own_a, axes, places, [turn, project, head])
+    else:
+        places, sources = head(project(turn(places))), [lax.all_gather(own_a, "bank", axis=0, tiled=False)]
+    turned_map, turned_bank, turned_memory = front["turned_map"], front["turned_bank"], front["turned_memory"]
+    keys, values, pooling = front["keys"], front["values"], front["pooling"]
+    joined_grad, hidden_grad, group_branch_grad = front["joined_grad"], front["hidden_grad"], front["group_branch_grad"]
     time_column = region_time.reshape(-1, 1)
     scales = jnp.stack([scale_b, shift_b, scale_a, shift_a])
-    (
-        packed, turned_bank, turned_memory, keys, values, turned_map, pooling, joined_grad, hidden_grad,
-        group_branch_grad, wide_head, wide_logit_grad, time_column, scales, places_here,
-    ) = lax.optimization_barrier(
-        (
-            packed, turned_bank, turned_memory, keys, values, turned_map, pooling, joined_grad, hidden_grad,
-            group_branch_grad, wide_head, wide_logit_grad, time_column, scales, places_here,
-        )
-    )
-
-    pre_a, act_a, weight_a = run_first_conv(feature_map, packed, scale_a, shift_a, groups_a)
+    places, time_column, scales, *sources = lax.optimization_barrier((places, time_column, scales, *sources))
+
+    pre_a, act_a, weight_a = run_first_conv(places, feature_map, sources, scale_a, shift_a)
     pre_b, act_b, pre_c, regions, reduced, own_queries = run_later_convs(
         act_a, feature_map, packed, scale_b, shift_b, scale_c, shift_c, pooling, w_reduce, w_query, groups_b, groups_c
     )
     queries = to_owners(own_queries).reshape(group_rows, channels)
     places, message, scores = run_kernel(
         functools.partial(attend, half_span),
-        places_here,
+        places,
         [queries, keys, values, time_column],
         [shape_of((group_rows, channels + TILE), BF16), shape_of((group_rows, keys_here), F32)],
         "attend",
@@ -1153,7 +1271,7 @@
         places, send_bc, keep_bc, lin_c_grad, pre_a_grad,
         scale_c_part, shift_c_part, scale_b_part, shift_b_part, scale_a_part, shift_a_part,
     ) = run_kernel(
-        functools.partial(later_back, groups_a, groups_b),
+        functools.partial(later_back, 0, groups_b),
         places,
         [
             regions_grad, pooling, scale_c.reshape(1, -1), shift_c.reshape(1, -1),
@@ -1218,6 +1336,20 @@
         after_last, places, [parted(keep_bc), parted(got_bc)], [shape_of(plane_shape, BF16)] * 4, "round_one", 4
     )
     got_one, got_two = across.swap(send_one, 1), inner.swap(send_two, 1)
+    feature_rows, channel_rows = feature_count // bank_count, channels // bank_count
+    joined_rows = (feature_count + channels) // bank_count
+    widths = (channels, channels, feature_rows, channel_rows, channel_rows, joined_rows)
+    message_width = -(-sum(widths) // TILE) * TILE
+    places, logits_out, message = run_kernel(
+        region_pack,
+        places,
+        [regions, reduced, hidden_low, query_grad, reduced_grad, w_out, wide_head],
+        [shape_of((own_count, classes), BF16), shape_of((bank_count, own_count, message_width), BF16)],
+        "region_pack",
+        WINDOW,
+    )
+    group = to_owners(message).reshape(group_rows, message_width)
+
     places, map_grad = run_kernel(
         map_back,
         places,
@@ -1246,20 +1378,6 @@
         5,
     )
     got_across, got_inner = across.swap(send_across, 1), inner.swap(send_inner, 1)
-    feature_rows, channel_rows = feature_count // bank_count, channels // bank_count
-    joined_rows = (feature_count + channels) // bank_count
-    widths = (channels, channels, feature_rows, channel_rows, channel_rows, joined_rows)
-    message_width = -(-sum(widths) // TILE) * TILE
-    places, logits_out, message = run_kernel(
-        region_pack,
-        places,
-        [regions, reduced, hidden_low, query_grad, reduced_grad, w_out, wide_head],
-        [shape_of((own_count, classes), BF16), shape_of((bank_count, own_count, message_width), BF16)],
-        "region_pack",
-        WINDOW,
-    )
-    group = to_owners(message).reshape(group_rows, message_width)
-
     vectors = [
         gain_part, shift_part, scale_a_part, shift_a_part, scale_b_part, shift_b_part, scale_c_part, shift_c_part
     ]
@@ -1283,6 +1401,15 @@
         ],
         limit=8,
     )
+    places, region_parts = run_kernel(
+        functools.partial(region_sums, widths),
+        places,
+        [group, group_branch_grad, wide_logit_grad],
+        [shape_of((region_lines, channels), BF16)],
+        "region_sums",
+        WINDOW,
+    )
+    region_both = [region_parts, dp_swap(region_parts, 1)] if split else [lax.psum(region_parts, "dp")]
     if split:
         bank_parts = [bank_pieces[0]] + [outer.swap(piece, step + 1) for step, piece in enumerate(bank_pieces[1:])]
     else:
@@ -1291,11 +1418,11 @@
     results = run_kernel(
         functools.partial(round_three, outer.size, split),
         places,
-        [kept_one, kept_two, keep_a_one, keep_a_two, got_across, got_inner] + bank_parts,
+        [kept_one, kept_two, keep_a_one, keep_a_two, got_across, got_inner] + region_both + bank_parts,
         [one_bc] * outer.size
         + [half_a, half_a, shape_of((bank_step, channels), BF16)]
         + [
-            shape_of((half * rows_a, channels), BF16),
+            shape_of((half * rows_a + region_lines, channels), BF16),
             shape_of((half * rows_a + bank_step, channels), BF16),
         ],
         "round_three",
@@ -1305,43 +1432,33 @@
     kept_a_one, kept_a_two, bank_keep, send_across, send_inner = results[1 + outer.size :]
     got_across, got_inner = across.swap(send_across, 1), inner.swap(send_inner, 1)
     got_bc = [outer.swap(piece, step + 1) for step, piece in enumerate(pieces_bc[1:])]
-    places, region_parts = run_kernel(
-        functools.partial(region_sums, widths),
+    row_block = shape_of((channel_rows, channels), F32)
+    results = run_kernel(
+        functools.partial(round_four, outer.size, split, widths),
         places,
-        [group, group_branch_grad, wide_logit_grad],
-        [shape_of((region_lines, channels), BF16)],
-        "region_sums",
-        WINDOW,
-    )
-    region_both = [region_parts, dp_swap(region_parts, 1)] if split else [lax.psum(region_parts, "dp")]
-    results = run_kernel(
-        functools.partial(round_four, outer.size, split),
-        places,
-        [pieces_bc[0], *got_bc, kept_a_one, kept_a_two, bank_keep, got_across, got_inner, *region_both],
-        [shape_of((rows_bc + bank_step, channels), BF16), shape_of(region_parts.shape, BF16)]
-        + [shape_of((rows_a, channels), BF16)] * outer.size,
+        [pieces_bc[0], *got_bc, kept_a_one, kept_a_two, bank_keep, send_across, got_across, got_inner],
+        [shape_of((rows_bc + bank_step, channels), BF16)]
+        + [shape_of((rows_a, channels), BF16)] * outer.size
+        + [shape_of((feature_rows, channels), F32), row_block, row_block, shape_of((joined_rows, classes), F32)],
         "round_four",
         4,
     )
-    places, done, region_parts, kept_a, *pieces_a = results
+    places, done, kept_a, *pieces_a = results[: 2 + outer.size]
+    reduce_weight_grad, query_weight_grad, out_weight_grad, head_weight_grad = results[2 + outer.size :]
     got_a = [outer.swap(piece, step + 1) for step, piece in enumerate(pieces_a)]
-    region_both = [region_parts, across.swap(region_parts, 1)] if split else [region_parts]
     done_both = [done, across.swap(done, 1)] if split else []
     row_block = shape_of((channel_rows, channels), F32)
-    results = run_kernel(
-        functools.partial(round_last, outer.size, split, widths),
+    places, part_a, *both = run_kernel(
+        functools.partial(round_last, outer.size),
         places,
-        [kept_a, *got_a, *region_both, *done_both],
-        [shape_of((rows_a, channels), BF16), shape_of((feature_rows, channels), F32), row_block, row_block]
-        + [shape_of((joined_rows, classes), F32)]
-        + [shape_of((2,) + done.shape, BF16)] * len(done_both[1:]),
+        [kept_a, *got_a, *done_both],
+        [shape_of((rows_a, channels), BF16)] + [shape_of((2,) + done.shape, BF16)] * len(done_both[1:]),
         "round_last",
         2,
     )
-    places, part_a, reduce_weight_grad, query_weight_grad, out_weight_grad, head_weight_grad = results[:6]
     if split:
         done_a = lax.all_gather(part_a, "dp", axis=0, tiled=False)
-        done_all = [results[6], last.swap(results[6], 1)]
+        done_all = [both[0], last.swap(both[0], 1)]
     else:
         done_a = lax.psum(part_a, "dp")
         bank_all = lax.all_gather(done[rows_bc:], "dp", axis=0, tiled=False)

time: 391 us -> 348 us (0.89)
  waiting for transfers between devices: 146 us -> 110 us
  matrix products: 9.53 us -> 0 us
  local copies, waits for them, and re-layouts: 43.7 us -> 35.8 us
  Pallas kernels: 89.8 us -> 97.4 us
    all_gather x1, waiting for transfers between devices: 74.9 us -> 7.8 us  [body(): lax.all_gather(own_packed, ('bank', 'dp') if split else 'bank', axis=0, t...]
    ppermute x20 -> x27, waiting for transfers between devices: 62.3 us -> 94.7 us  [swap(): return lax.ppermute(value, self.name, pairs)]
    dot_general x6 -> x0, matrix products: 9.53 us -> none  [the longest x3 6.16 us: product(): return jnp.dot(left, right, preferred_element_type=jnp.float32)]
    pallas_call x18 -> x22, Pallas kernels: 67.6 us -> 75 us  [run_kernel(): pl.pallas_call(wrapped, out_shape=[shape_of(places.shape, jnp.int32)] + l...]
    ppermute x20 -> x27, starting transfers between devices: 22.4 us -> 28.4 us  [swap(): return lax.ppermute(value, self.name, pairs)]
    unnamed x169 -> x168, local copies, waits for them, and re-layouts: 39.4 us -> 34.3 us
  transfers between devices with their start and end apart: 27 -> 34, of which waited for: 14 -> 20; matrix products, arithmetic and copies ran while one was open for 7% -> 2% of each run, Pallas kernels for 13% -> 20%
where the time goes in v4:
time: 348 us; the launch traced here: 346 us
  waiting for transfers between devices  110 us (32%)
  Pallas kernels  97.4 us (28%)
  starting transfers between devices  50.8 us (15%)
  local copies, waits for them, and re-layouts  35.8 us (10%)
  blocking collectives  35.3 us (10%)
  between operations  14.9 us (4%)
    ppermute x27, waiting for transfers between devices, swap(): return lax.ppermute(value, self.name, pairs)  94.7 us
    pallas_call x22, Pallas kernels, run_kernel(): pl.pallas_call(wrapped, out_shape=[shape_of(places.shape, jnp.int32)] + l...  75 us
    unnamed x168, local copies, waits for them, and re-layouts  34.3 us
    ppermute x27, starting transfers between devices, swap(): return lax.ppermute(value, self.name, pairs)  28.4 us
    all_to_all x2, blocking collectives, to_owners(): lax.all_to_all(value, 'bank', split_axis=0, concat_axis=0, tiled=True)  26.6 us
    all_to_all x3, starting transfers between devices, to_owners(): lax.all_to_all(value, 'bank', split_axis=0, concat_axis=0, tiled=True)  14.1 us
    pallas_call x1, Pallas kernels, run_later_convs(): pl.pallas_call(later_convs, out_shape=[jax.ShapeDtypeStruct((sites, chann...  14.1 us
    all_gather x1, blocking collectives, body(): done_a = lax.all_gather(part_a, 'dp', axis=0, tiled=False)  8.7 us
  transfers between devices with their start and end apart: 34, of which 20 were waited for; matrix products, arithmetic and copies ran while one was open for 2% of the time, Pallas kernels for 20%

profile of v4, /device:TPU:9, one launch (start us, length us, event | category | flops | bytes accessed | tf_op | source)
XLA Modules:
  0.0 346.3 jit_solution(40623189158063398)
XLA Ops:
  27.1 4.5 %collective-permute-done.1 = bf16[12,16,512]{2,1,0:T(8,128)(2,1)} collective-permute-done((bf16[12,16,512]{2,1,0:T(8,128)(2,1)S(1)}, bf16[12,16,512]{2,1,0:T(8,128)(2,1)}, u32[]{:S(2)}, u32[]{:S(2)}) %collective-permute-start.1) | collective-permute-done | bytes 196640 | tf_op jit(solution)/shard_map/ppermute | solution.py:44
  47.0 20.5 %collective-permute-done.6 = bf16[4,12,16,512]{3,2,1,0:T(8,128)(2,1)S(1)} collective-permute-done((bf16[4,12,16,512]{3,2,1,0:T(8,128)(2,1)S(1)}, bf16[4,12,16,512]{3,2,1,0:T(8,128)(2,1)S(1)}, u32[]{:S(2)}, u32[]{:S(2)}) %collective-permute-start.6) | collective-permute-done | bytes 786464 | tf_op jit(solution)/shard_map/ppermute | solution.py:44
  70.1 7.1 %collective-permute-done.7.refs_1_ = bf16[16,12,16,512]{3,2,1,0:T(8,128)(2,1)S(1)} collective-permute-done((bf16[16,12,16,512]{3,2,1,0:T(8,128)(2,1)S(1)}, bf16[16,12,16,512]{3,2,1,0:T(8,128)(2,1)S(1)}, u32[]{:S(2)}, u32[]{:S(2)}) %collective-permute-start.7) | collective-permute-done | bytes 3145760 | tf_op jit(solution)/shard_map/ppermute | solution.py:44
  78.9 8.3 %first_conv.1 = (f32[512,512]{1,0:T(8,128)S(1)}, bf16[512,512]{1,0:T(8,128)(2,1)S(1)}, bf16[384,16,512]{2,1,0:T(8,128)(2,1)}) custom-call(s32[10]{0:T(128)S(1)} %get-tuple-element.182.places_ref.refs_0_, bf16[512,2048]{1,0:T(8,128)(2,1)} %refs_7_.1, bf16[16,12,16,512]{3,2,1,0:T(8,128)(2,1)} %copy-done.73, bf16[16,12,16,512]{3,2,1,0:T(8,128)(2,1)} %copy-done.78, ...), custom_call_target="tpu_custom_call" | custom-call | flops 35999997952 | bytes 36000000 | tf_op jit(solution)/shard_map/first_conv/pallas_call | solution.py:1008
  88.1 7.8 %all-gather.4.cloned.1.call-done = bf16[416,16,512]{2,1,0:T(8,128)(2,1)} async-done(((bf16[13,16,512]{2,1,0:T(8,128)(2,1)}), bf16[416,16,512]{2,1,0:T(8,128)(2,1)}) %all-gather.4.cloned.1.call-update) | async-done | bytes 6815760 | tf_op jit(solution)/shard_map/all_gather | solution.py:1136
  95.9 14.1 %later_convs.1 = (f32[512,512]{1,0:T(8,128)}, bf16[512,512]{1,0:T(8,128)(2,1)S(1)}, f32[512,2048]{1,0:T(8,128)}, bf16[32,2048]{1,0:T(8,128)(2,1)S(1)}, f32[32,51...) custom-call(bf16[512,512]{1,0:T(8,128)(2,1)S(1)} %get-tuple-element.185.act_a_ref.refs_10_, bf16[512,2048]{1,0:T(8,128)(2,1)} %refs_7_.1, ...), custom_call_target="tpu_custom_call" | custom-call | flops 89999998976 | bytes 90000000 | tf_op jit(solution)/shard_map/later_convs/pallas_call | solution.py:1037
  110.8 4.0 %all-to-all-start = ((bf16[8,32,512]{2,1,0:T(8,128)(2,1)}), bf16[8,32,512]{2,1,0:T(8,128)(2,1)S(1)}, u32[]{:S(2)}, u32[]{:S(2)}) async-start(bf16[8,32,512]{2,1,0:T(8,128)(2,1)} %get-tuple-element.188), calls=%async_computation | async-start | bytes 524288 | tf_op jit(solution)/shard_map/all_to_all | solution.py:83
  115.0 6.4 %all-to-all-done = bf16[8,32,512]{2,1,0:T(8,128)(2,1)S(1)} async-done(((bf16[8,32,512]{2,1,0:T(8,128)(2,1)}), bf16[8,32,512]{2,1,0:T(8,128)(2,1)S(1)}, u32[]{:S(2)}, u32[]{:S(2)}) %all-to-all-start) | async-done | bytes 262176 | tf_op jit(solution)/shard_map/all_to_all | solution.py:83
  122.6 14.0 %all_to_all.25.refs_1_ = bf16[8,32,640]{2,1,0:T(8,128)(2,1)S(1)} all-to-all(bf16[8,32,640]{2,1,0:T(8,128)(2,1)S(1)} %bitcast.45), channel_id=1, replica_groups=mesh['dp'=4,'bank'=8] {'bank'}, dimensions={0} | all-to-all | bytes 655360 | tf_op jit(solution)/shard_map/all_to_all | solution.py:83
  138.2 12.6 %all_to_all.26 = bf16[8,32,640]{2,1,0:T(8,128)(2,1)S(1)} all-to-all(bf16[8,32,640]{2,1,0:T(8,128)(2,1)S(1)} %get-tuple-element.196), channel_id=1, replica_groups=mesh['dp'=4,'bank'=8] {'bank'}, dimensions={0} | all-to-all | bytes 655360 | tf_op jit(solution)/shard_map/all_to_all | solution.py:83
  158.5 4.3 %all-to-all-start.3 = ((bf16[8,32,512]{2,1,0:T(8,128)(2,1)}), bf16[8,32,512]{2,1,0:T(8,128)(2,1)S(1)}, u32[]{:S(2)}, u32[]{:S(2)}) async-start(bf16[8,32,512]{2,1,0:T(8,128)(2,1)} %bitcast.27), calls=%async_computation.3 | async-start | bytes 524288 | tf_op jit(solution)/shard_map/all_to_all | solution.py:83
  173.6 21.0 %later_back.1 = (s32[10]{0:T(128)S(1)}, bf16[16,208,512]{2,1,0:T(8,128)(2,1)S(1)}, bf16[16,208,512]{2,1,0:T(8,128)(2,1)}, bf16[512,2048]{1,0:T(8,128)(2,1)S(1)},...) custom-call(s32[10]{0:T(128)S(1)} %get-tuple-element.206.refs_0_, ...), custom_call_target="tpu_custom_call" | custom-call | flops 167999995904 | bytes 168000000 | tf_op jit(solution)/shard_map/later_back/pallas_call | solution.py:990
  196.6 8.2 %first_back.1 = (s32[10]{0:T(128)S(1)}, bf16[16,192,512]{2,1,0:T(8,128)(2,1)}, bf16[16,192,512]{2,1,0:T(8,128)(2,1)S(1)}, bf16[1024,512]{1,0:T(8,128)(2,1)S(1)}) custom-call(s32[10]{0:T(128)S(1)} %get-tuple-element.213.refs_0_, bf16[512,512]{1,0:T(8,128)(2,1)S(1)} %get-tuple-element.214.refs_1_, bf16[1024,512]{1,0:T(8,128)(2,1)} %get-tuple-element.215.refs_2_, ...), custom_call_target="tpu_custom_call" | custom-call | flops 35999997952 | bytes 36000000 | tf_op jit(solution)/shard_map/first_back/pallas_call | solution.py:990
  210.8 5.8 %all-to-all-start.4 = ((bf16[8,32,1792]{2,1,0:T(8,128)(2,1)}), bf16[8,32,1792]{2,1,0:T(8,128)(2,1)}, u32[]{:S(2)}, u32[]{:S(2)}) async-start(bf16[8,32,1792]{2,1,0:T(8,128)(2,1)} %copy-done.5), calls=%async_computation.4 | async-start | bytes 1835008 | tf_op jit(solution)/shard_map/all_to_all | solution.py:83
  220.4 6.3 %map_back.1 = (s32[10]{0:T(128)S(1)}, bf16[512,2048]{1,0:T(8,128)(2,1)}) custom-call(s32[10]{0:T(128)S(1)} %get-tuple-element.227.refs_0_, bf16[512,512]{1,0:T(8,128)(2,1)S(1)} %copy-done.15, bf16[384,16,512]{2,1,0:T(8,128)(2,1)S(1)} %copy-done, bf16[512,2048]{1,0:T(8,128)(2,1)S(1)} %get-tuple-element.229.refs_3_), custom_call_target="tpu_custom_call" | custom-call | flops 600000000 | bytes 600000 | tf_op jit(solution)/shard_map/map_back/pallas_call | solution.py:990
  227.6 6.6 %collective-permute-done.12.refs_4_ = bf16[2,2,208,512]{3,2,1,0:T(8,128)(2,1)} collective-permute-done((bf16[2,2,208,512]{3,2,1,0:T(8,128)(2,1)}, bf16[2,2,208,512]{3,2,1,0:T(8,128)(2,1)}, u32[]{:S(2)}, u32[]{:S(2)}) %collective-permute-start.12) | collective-permute-done | bytes 852000 | tf_op jit(solution)/shard_map/ppermute | solution.py:44
  234.2 4.6 %round_two.1 = (s32[10]{0:T(128)S(1)}, bf16[2,208,512]{2,1,0:T(8,128)(2,1)S(1)}, bf16[2,208,512]{2,1,0:T(8,128)(2,1)S(1)}, bf16[2,2,192,512]{3,2,1,0:T(8,128)(2,...) custom-call(s32[10]{0:T(128)S(1)} %get-tuple-element.231.refs_0_, ...), custom_call_target="tpu_custom_call" | custom-call | flops 30000001024 | bytes 30000000 | tf_op jit(solution)/shard_map/round_two/pallas_call | solution.py:990
  244.3 3.7 %bank_back.1 = (s32[10]{0:T(128)S(1)}, bf16[512,2048]{1,0:T(8,128)(2,1)}, bf16[2,400,128]{2,1,0:T(8,128)(2,1)S(1)}, bf16[2,400,128]{2,1,0:T(8,128)(2,1)S(1)}, bf...) custom-call(s32[10]{0:T(128)S(1)} %get-tuple-element.238.refs_0_, ...), custom_call_target="tpu_custom_call" | custom-call | flops 600000000 | bytes 600000 | tf_op jit(solution)/shard_map/bank_back/pallas_call | solution.py:990
  255.2 7.3 %collective-permute-done.17.refs_10_ = bf16[2,400,128]{2,1,0:T(8,128)(2,1)S(1)} collective-permute-done((bf16[2,400,128]{2,1,0:T(8,128)(2,1)S(1)}, bf16[2,400,128]{2,1,0:T(8,128)(2,1)S(1)}, u32[]{:S(2)}, u32[]{:S(2)}) %collective-permute-start.17) | collective-permute-done | bytes 204832 | tf_op jit(solution)/shard_map/ppermute | solution.py:44
  265.0 9.3 %collective-permute-done.19.refs_12_ = bf16[2,400,128]{2,1,0:T(8,128)(2,1)S(1)} collective-permute-done((bf16[2,400,128]{2,1,0:T(8,128)(2,1)S(1)}, bf16[2,400,128]{2,1,0:T(8,128)(2,1)S(1)}, u32[]{:S(2)}, u32[]{:S(2)}) %collective-permute-start.19) | collective-permute-done | bytes 204832 | tf_op jit(solution)/shard_map/ppermute | solution.py:44
  287.6 5.1 %collective-permute-done.21.refs_3_ = bf16[208,512]{1,0:T(8,128)(2,1)S(1)} collective-permute-done((bf16[208,512]{1,0:T(8,128)(2,1)S(1)}, bf16[208,512]{1,0:T(8,128)(2,1)S(1)}, u32[]{:S(2)}, u32[]{:S(2)}) %collective-permute-start.21) | collective-permute-done | bytes 213024 | tf_op jit(solution)/shard_map/ppermute | solution.py:44
  292.7 10.0 %collective-permute-done.22.refs_4_ = bf16[208,512]{1,0:T(8,128)(2,1)S(1)} collective-permute-done((bf16[208,512]{1,0:T(8,128)(2,1)S(1)}, bf16[208,512]{1,0:T(8,128)(2,1)S(1)}, u32[]{:S(2)}, u32[]{:S(2)}) %collective-permute-start.22) | collective-permute-done | bytes 213024 | tf_op jit(solution)/shard_map/ppermute | solution.py:44
  313.0 10.8 %collective-permute-done.27.refs_4_ = bf16[192,512]{1,0:T(8,128)(2,1)S(1)} collective-permute-done((bf16[192,512]{1,0:T(8,128)(2,1)S(1)}, bf16[192,512]{1,0:T(8,128)(2,1)S(1)}, u32[]{:S(2)}, u32[]{:S(2)}) %collective-permute-start.27) | collective-permute-done | bytes 196640 | tf_op jit(solution)/shard_map/ppermute | solution.py:44
  328.1 8.7 %all-gather.1 = bf16[768,512]{1,0:T(8,128)(2,1)S(1)} all-gather(bf16[192,512]{1,0:T(8,128)(2,1)S(1)} %get-tuple-element.283), channel_id=3, replica_groups=mesh['dp'=4,'bank'=8] {'dp'}, dimensions={0}, use_global_device_ids=true | all-gather | bytes 983040 | tf_op jit(solution)/shard_map/all_gather | solution.py:1460
  (250 shorter events, 120.3 us)
Async XLA Ops:
  7.2 88.7 %all-gather.4.cloned.1.call-start = ((), (), s32[]{:S(2)}) async-start(), calls=%async_computation.5 | async-start | bytes 7028736 | tf_op jit(solution)/shard_map/all_gather | solution.py:1136
  12.6 14.6 %collective-permute-start.2 = (bf16[12,16,512]{2,1,0:T(8,128)(2,1)S(1)}, bf16[12,16,512]{2,1,0:T(8,128)(2,1)}, u32[]{:S(2)}, u32[]{:S(2)}) collective-permute-start(bf16[12,16,512]{2,1,0:T(8,128)(2,1)S(1)} %get-tuple-element.165), channel_id=1, source_target_pairs={{0,6},{1,7},{2,4},{3,5},{4,2},{5,3},{6,0},{7,1},{8,14},{9,15},{10,... | collective-permute-start | bytes 589832 | tf_op jit(solution)/shard_map/ppermute | solution.py:44
  14.0 17.7 %collective-permute-start.1 = (bf16[12,16,512]{2,1,0:T(8,128)(2,1)S(1)}, bf16[12,16,512]{2,1,0:T(8,128)(2,1)}, u32[]{:S(2)}, u32[]{:S(2)}) collective-permute-start(bf16[12,16,512]{2,1,0:T(8,128)(2,1)S(1)} %get-tuple-element.165), channel_id=1, source_target_pairs={{0,4},{1,5},{2,6},{3,7},{4,0},{5,1},{6,2},{7,3},{8,12},{9,13},{10,... | collective-permute-start | bytes 589832 | tf_op jit(solution)/shard_map/ppermute | solution.py:44
  15.0 16.6 %collective-permute-start = (bf16[12,16,512]{2,1,0:T(8,128)(2,1)S(1)}, bf16[12,16,512]{2,1,0:T(8,128)(2,1)}, u32[]{:S(2)}, u32[]{:S(2)}) collective-permute-start(bf16[12,16,512]{2,1,0:T(8,128)(2,1)S(1)} %get-tuple-element.165), channel_id=1, source_target_pairs={{0,2},{1,3},{2,0},{3,1},{4,6},{5,7},{6,4},{7,5},{8,10},{9,11},{10,... | collective-permute-start | bytes 589832 | tf_op jit(solution)/shard_map/ppermute | solution.py:44
  43.6 23.9 %collective-permute-start.6 = (bf16[4,12,16,512]{3,2,1,0:T(8,128)(2,1)S(1)}, bf16[4,12,16,512]{3,2,1,0:T(8,128)(2,1)S(1)}, u32[]{:S(2)}, u32[]{:S(2)}) collective-permute-start(bf16[4,12,16,512]{3,2,1,0:T(8,128)(2,1)S(1)} %constant_dynamic-update-slice_fusion.2), channel_id=1, source_target_pairs={{0,16},{8,24},{16,0},{24,8},{1,17},{9,25},{17,1},{25,9},{2,18},{10... | collective-permute-start | bytes 2359304 | tf_op jit(solution)/shard_map/ppermute | solution.py:44
  44.9 22.6 %collective-permute-start.5 = (bf16[4,12,16,512]{3,2,1,0:T(8,128)(2,1)S(1)}, bf16[4,12,16,512]{3,2,1,0:T(8,128)(2,1)S(1)}, u32[]{:S(2)}, u32[]{:S(2)}) collective-permute-start(bf16[4,12,16,512]{3,2,1,0:T(8,128)(2,1)S(1)} %constant_dynamic-update-slice_fusion), channel_id=1, source_target_pairs={{0,1},{1,0},{2,3},{3,2},{4,5},{5,4},{6,7},{7,6},{8,9},{9,8},{10,11... | collective-permute-start | bytes 2359304 | tf_op jit(solution)/shard_map/ppermute | solution.py:44
  110.8 10.5 %all-to-all-start = ((bf16[8,32,512]{2,1,0:T(8,128)(2,1)}), bf16[8,32,512]{2,1,0:T(8,128)(2,1)S(1)}, u32[]{:S(2)}, u32[]{:S(2)}) async-start(bf16[8,32,512]{2,1,0:T(8,128)(2,1)} %get-tuple-element.188), calls=%async_computation | async-start | bytes 524288 | tf_op jit(solution)/shard_map/all_to_all | solution.py:83
  158.5 11.7 %all-to-all-start.3 = ((bf16[8,32,512]{2,1,0:T(8,128)(2,1)}), bf16[8,32,512]{2,1,0:T(8,128)(2,1)S(1)}, u32[]{:S(2)}, u32[]{:S(2)}) async-start(bf16[8,32,512]{2,1,0:T(8,128)(2,1)} %bitcast.27), calls=%async_computation.3 | async-start | bytes 524288 | tf_op jit(solution)/shard_map/all_to_all | solution.py:83
  168.0 28.5 %collective-permute-start.9 = (bf16[1024,512]{1,0:T(8,128)(2,1)}, bf16[1024,512]{1,0:T(8,128)(2,1)}, u32[]{:S(2)}, u32[]{:S(2)}) collective-permute-start(bf16[1024,512]{1,0:T(8,128)(2,1)} %get-tuple-element.215.refs_2_), channel_id=1, source_target_pairs={{0,16},{8,24},{16,0},{24,8},{1,17},{9,25},{17,1},{25,9},{2,18},{10... | collective-permute-start | bytes 3145736 | tf_op jit(solution)/shard_map/ppermute | solution.py:1240
  204.8 21.9 %collective-permute-start.13 = (bf16[16,192,512]{2,1,0:T(8,128)(2,1)}, bf16[16,192,512]{2,1,0:T(8,128)(2,1)}, u32[]{:S(2)}, u32[]{:S(2)}) collective-permute-start(bf16[16,192,512]{2,1,0:T(8,128)(2,1)} %get-tuple-element.237), channel_id=1, source_target_pairs={{0,8},{8,0},{16,24},{24,16},{1,9},{9,1},{17,25},{25,17},{2,10},{10... | collective-permute-start | bytes 9437192 | tf_op jit(solution)/shard_map/ppermute | solution.py:44
  207.2 20.4 %collective-permute-start.11 = (bf16[2,2,208,512]{3,2,1,0:T(8,128)(2,1)}, bf16[2,2,208,512]{3,2,1,0:T(8,128)(2,1)}, u32[]{:S(2)}, u32[]{:S(2)}) collective-permute-start(bf16[2,2,208,512]{3,2,1,0:T(8,128)(2,1)} %get-tuple-element.233), channel_id=1, source_target_pairs={{0,16},{8,24},{16,0},{24,8},{1,17},{9,25},{17,1},{25,9},{2,18},{10... | collective-permute-start | bytes 2555912 | tf_op jit(solution)/shard_map/ppermute | solution.py:44
  208.2 26.0 %collective-permute-start.12 = (bf16[2,2,208,512]{3,2,1,0:T(8,128)(2,1)}, bf16[2,2,208,512]{3,2,1,0:T(8,128)(2,1)}, u32[]{:S(2)}, u32[]{:S(2)}) collective-permute-start(bf16[2,2,208,512]{3,2,1,0:T(8,128)(2,1)} %get-tuple-element.235), channel_id=1, source_target_pairs={{0,1},{1,0},{2,3},{3,2},{4,5},{5,4},{6,7},{7,6},{8,9},{9,8},{10,11... | collective-permute-start | bytes 2555912 | tf_op jit(solution)/shard_map/ppermute | solution.py:44
  210.8 37.2 %all-to-all-start.4 = ((bf16[8,32,1792]{2,1,0:T(8,128)(2,1)}), bf16[8,32,1792]{2,1,0:T(8,128)(2,1)}, u32[]{:S(2)}, u32[]{:S(2)}) async-start(bf16[8,32,1792]{2,1,0:T(8,128)(2,1)} %copy-done.5), calls=%async_computation.4 | async-start | bytes 1835008 | tf_op jit(solution)/shard_map/all_to_all | solution.py:83
  242.1 32.1 %collective-permute-start.14 = (bf16[1184,512]{1,0:T(8,128)(2,1)}, bf16[1184,512]{1,0:T(8,128)(2,1)S(1)}, u32[]{:S(2)}, u32[]{:S(2)}) collective-permute-start(bf16[1184,512]{1,0:T(8,128)(2,1)} %get-tuple-element.259), channel_id=1, source_target_pairs={{0,16},{8,24},{16,0},{24,8},{1,17},{9,25},{17,1},{25,9},{2,18},{10... | collective-permute-start | bytes 3637256 | tf_op jit(solution)/shard_map/ppermute | solution.py:44
  242.6 31.6 %collective-permute-start.15 = (bf16[1184,512]{1,0:T(8,128)(2,1)}, bf16[1184,512]{1,0:T(8,128)(2,1)}, u32[]{:S(2)}, u32[]{:S(2)}) collective-permute-start(bf16[1184,512]{1,0:T(8,128)(2,1)} %get-tuple-element.260), channel_id=1, source_target_pairs={{0,1},{1,0},{2,3},{3,2},{4,5},{5,4},{6,7},{7,6},{8,9},{9,8},{10,11... | collective-permute-start | bytes 3637256 | tf_op jit(solution)/shard_map/ppermute | solution.py:44
  250.0 24.2 %collective-permute-start.16 = (bf16[464,512]{1,0:T(8,128)(2,1)S(1)}, bf16[464,512]{1,0:T(8,128)(2,1)S(1)}, u32[]{:S(2)}, u32[]{:S(2)}) collective-permute-start(bf16[464,512]{1,0:T(8,128)(2,1)S(1)} %get-tuple-element.261.refs_7_), channel_id=1, source_target_pairs={{0,8},{8,0},{16,24},{24,16},{1,9},{9,1},{17,25},{25,17},{2,10},{10... | collective-permute-start | bytes 1425416 | tf_op jit(solution)/shard_map/ppermute | solution.py:1240
  254.6 10.4 %collective-permute-start.18 = (bf16[2,400,128]{2,1,0:T(8,128)(2,1)S(1)}, bf16[2,400,128]{2,1,0:T(8,128)(2,1)S(1)}, u32[]{:S(2)}, u32[]{:S(2)}) collective-permute-start(bf16[2,400,128]{2,1,0:T(8,128)(2,1)S(1)} %get-tuple-element.264), channel_id=1, source_target_pairs={{0,4},{1,5},{2,6},{3,7},{4,0},{5,1},{6,2},{7,3},{8,12},{9,13},{10,... | collective-permute-start | bytes 614408 | tf_op jit(solution)/shard_map/ppermute | solution.py:44
  262.5 11.7 %collective-permute-start.19 = (bf16[2,400,128]{2,1,0:T(8,128)(2,1)S(1)}, bf16[2,400,128]{2,1,0:T(8,128)(2,1)S(1)}, u32[]{:S(2)}, u32[]{:S(2)}) collective-permute-start(bf16[2,400,128]{2,1,0:T(8,128)(2,1)S(1)} %get-tuple-element.265), channel_id=1, source_target_pairs={{0,6},{1,7},{2,4},{3,5},{4,2},{5,3},{6,0},{7,1},{8,14},{9,15},{10,... | collective-permute-start | bytes 614408 | tf_op jit(solution)/shard_map/ppermute | solution.py:44
  280.7 22.0 %collective-permute-start.23 = (bf16[848,512]{1,0:T(8,128)(2,1)S(1)}, bf16[848,512]{1,0:T(8,128)(2,1)S(1)}, u32[]{:S(2)}, u32[]{:S(2)}) collective-permute-start(bf16[848,512]{1,0:T(8,128)(2,1)S(1)} %get-tuple-element.274.refs_8_), channel_id=1, source_target_pairs={{0,16},{8,24},{16,0},{24,8},{1,17},{9,25},{17,1},{25,9},{2,18},{10... | collective-permute-start | bytes 2605064 | tf_op jit(solution)/shard_map/ppermute | solution.py:44
  281.7 21.0 %collective-permute-start.24 = (bf16[496,512]{1,0:T(8,128)(2,1)S(1)}, bf16[496,512]{1,0:T(8,128)(2,1)S(1)}, u32[]{:S(2)}, u32[]{:S(2)}) collective-permute-start(bf16[496,512]{1,0:T(8,128)(2,1)S(1)} %get-tuple-element.275), channel_id=1, source_target_pairs={{0,1},{1,0},{2,3},{3,2},{4,5},{5,4},{6,7},{7,6},{8,9},{9,8},{10,11... | collective-permute-start | bytes 1523720 | tf_op jit(solution)/shard_map/ppermute | solution.py:44
  284.4 18.3 %collective-permute-start.22 = (bf16[208,512]{1,0:T(8,128)(2,1)S(1)}, bf16[208,512]{1,0:T(8,128)(2,1)S(1)}, u32[]{:S(2)}, u32[]{:S(2)}) collective-permute-start(bf16[208,512]{1,0:T(8,128)(2,1)S(1)} %get-tuple-element.270), channel_id=1, source_target_pairs={{0,6},{1,7},{2,4},{3,5},{4,2},{5,3},{6,0},{7,1},{8,14},{9,15},{10,... | collective-permute-start | bytes 638984 | tf_op jit(solution)/shard_map/ppermute | solution.py:44
  304.4 19.4 %collective-permute-start.28 = (bf16[320,512]{1,0:T(8,128)(2,1)S(1)}, bf16[320,512]{1,0:T(8,128)(2,1)S(1)}, u32[]{:S(2)}, u32[]{:S(2)}) collective-permute-start(bf16[320,512]{1,0:T(8,128)(2,1)S(1)} %get-tuple-element.281.refs_5_), channel_id=1, source_target_pairs={{0,16},{8,24},{16,0},{24,8},{1,17},{9,25},{17,1},{25,9},{2,18},{10... | collective-permute-start | bytes 983048 | tf_op jit(solution)/shard_map/ppermute | solution.py:44
  306.8 17.0 %collective-permute-start.27 = (bf16[192,512]{1,0:T(8,128)(2,1)S(1)}, bf16[192,512]{1,0:T(8,128)(2,1)S(1)}, u32[]{:S(2)}, u32[]{:S(2)}) collective-permute-start(bf16[192,512]{1,0:T(8,128)(2,1)S(1)} %get-tuple-element.280), channel_id=1, source_target_pairs={{0,6},{1,7},{2,4},{3,5},{4,2},{5,3},{6,0},{7,1},{8,14},{9,15},{10,... | collective-permute-start | bytes 589832 | tf_op jit(solution)/shard_map/ppermute | solution.py:44
  324.9 11.9 %collective-permute-start.29 = (bf16[2,320,512]{2,1,0:T(8,128)(2,1)S(1)}, bf16[2,320,512]{2,1,0:T(8,128)(2,1)S(1)}, u32[]{:S(2)}, u32[]{:S(2)}) collective-permute-start(bf16[2,320,512]{2,1,0:T(8,128)(2,1)S(1)} %get-tuple-element.284.refs_2_), channel_id=1, source_target_pairs={{0,8},{8,0},{16,24},{24,16},{1,9},{9,1},{17,25},{25,17},{2,10},{10... | collective-permute-start | bytes 1966088 | tf_op jit(solution)/shard_map/ppermute | solution.py:44
  (89 other events, 627.9 us)
Sparse Core Ops, SparseCore 0:
  16.3 79.5 all-gather.3

commit v5 on v4

--- a/solution.py
+++ b/solution.py
@@ -395,14 +395,12 @@
 
 
 def hand_out(buffer, send_ref, keep_ref, sems):
-    copies = [
-        pltpu.make_async_copy(buffer.at[number], target, sems.at[number])
-        for number, target in enumerate((send_ref, keep_ref))
-    ]
-    for copy in copies:
-        copy.start()
-    for copy in copies:
-        copy.wait()
+    return start_all(
+        [
+            pltpu.make_async_copy(buffer.at[number], target, sems.at[number])
+            for number, target in enumerate((send_ref, keep_ref))
+        ]
+    )
 
 
 def store_rows(buffer, place_ref, value, first, rows):
@@ -414,6 +412,34 @@
         at += count
 
 
+def slopes_outer(places_ref, scale_ref, shift_ref, pre_ref, map_ref, out_ref, held_pre, held_map, held_out, sems):
+    sites, features = held_map.shape
+    chunks = sems.shape[1]
+    width = features // chunks
+
+    def part_of(source, target, number, row):
+        columns = pl.ds(pl.multiple_of(number * width, width), width)
+        return pltpu.make_async_copy(source.at[:, columns], target.at[:, columns], sems.at[row, number])
+
+    for number in range(chunks):
+        start_all([part_of(pre_ref, held_pre, number, 0), part_of(map_ref, held_map, number, 1)])
+
+    def chunk(number, carry):
+        columns = pl.ds(pl.multiple_of(number * width, width), width)
+        wait_all([part_of(pre_ref, held_pre, number, 0), part_of(map_ref, held_map, number, 1)])
+
+        def one(rows):
+            linear = wide(held_map[rows, columns]) + held_pre[rows, columns] * scale_ref[:, columns] + shift_ref[:, columns]
+            held_out[rows, columns] = low(gelu_slope(linear))
+
+        by_rows(sites, 128, one)
+        part_of(held_out, out_ref, number, 2).start()
+        return carry
+
+    lax.fori_loop(0, chunks, chunk, 0)
+    wait_all([part_of(held_out, out_ref, number, 2) for number in range(chunks)])
+
+
 def slope_back(upstream_ref, pre_ref, scale_ref, shift_ref, out_ref, scale_out_ref, shift_out_ref):
     sites, channels = pre_ref.shape
 
@@ -431,7 +457,7 @@
 
 
 def later_back(
-    groups_a, groups_b, place_ref, regions_grad_ref, pool_ref, scale_ref, shift_ref, scales_ref, pre_c_ref, fm_ref, act_b_ref,
+    groups_a, groups_b, place_ref, regions_grad_ref, pool_ref, scale_ref, scales_ref, pre_c_ref, slope_ref, act_b_ref,
     pre_b_ref, act_a_ref, pre_a_ref, packed_ref,
     send_ref, keep_ref, lin_c_grad_ref, pre_a_grad_ref, scale_c_out_ref, shift_c_out_ref, scale_b_out_ref, shift_b_out_ref,
     scale_a_out_ref, shift_a_out_ref,
@@ -451,7 +477,7 @@
     copies_c = start_all(fetch_columns(packed_ref, weight_c, sems_c, groups_a + groups_b, chunks))
     for number in range(chunks):
         part_of(pre_c_ref, held_pre_c, number, 4).start()
-        part_of(fm_ref, held_map, number, 4 + chunks).start()
+        part_of(slope_ref, held_map, number, 4 + chunks).start()
     late = start_all(
         [
             pltpu.make_async_copy(pre_b_ref, held_pre_b, sems.at[1]),
@@ -470,14 +496,13 @@
         columns = pl.ds(pl.multiple_of(number * channels, channels), channels)
         out_grad[...] = dot_tn(pool_ref[...], regions_grad_ref[:, columns])
         part_of(pre_c_ref, held_pre_c, number, 4).wait()
-        part_of(fm_ref, held_map, number, 4 + chunks).wait()
+        part_of(slope_ref, held_map, number, 4 + chunks).wait()
 
         def one(step, sums):
             rows = pl.ds(pl.multiple_of(step * 128, 128), 128)
             pre = held_pre_c[rows, columns]
             scale = scale_ref[:, columns]
-            linear = wide(held_map[rows, columns]) + pre * scale + shift_ref[:, columns]
-            grad = out_grad[rows] * gelu_slope(linear)
+            grad = out_grad[rows] * wide(held_map[rows, columns])
             held_lin[rows, columns] = low(grad)
             pre_grad[rows] = low(grad * scale)
             return sums[0] + fold(grad * pre), sums[1] + fold(grad)
@@ -513,8 +538,9 @@
                 act_grad[...] = part
             else:
                 act_grad[...] += part
+    copies = hand_out(buffer, send_ref, keep_ref, out_sems)
     slope_back(act_grad, held_pre_a, scale_a_ref, shift_a_ref, pre_a_grad_ref, scale_a_out_ref, shift_a_out_ref)
-    hand_out(buffer, send_ref, keep_ref, out_sems)
+    wait_all(copies)
     for number in range(chunks):
         part_of(held_lin, lin_c_grad_ref, number, 4 + 2 * chunks).wait()
 
@@ -548,7 +574,7 @@
                 copies[start // channels].wait()
             part = low(product(held[start : start + channels], moved))
             store_rows(buffer, place_ref, part, tap * features + start, buffer.shape[2])
-    hand_out(buffer, send_ref, keep_ref, out_sems)
+    wait_all(hand_out(buffer, send_ref, keep_ref, out_sems))
 
 
 def map_back(places_ref, grad_ref, weight_ref, lin_c_grad_ref, out_ref, moved, held_lin, held_out, sems):
@@ -578,7 +604,7 @@
     wait_all(copies)
 
 
-COST = 6e9
+COST = 1.5e10
 WINDOW = 0.1
 FIRST_LIMIT = 52
 F32 = jnp.float32
@@ -599,6 +625,10 @@
 class Blocks:
     def __init__(self, ref, first, dims, rows):
         self.ref, self.first, self.dims, self.rows = ref, first, dims, rows
+
+    @property
+    def shape(self):
+        return self.dims
 
     def span(self, index):
         index = index if isinstance(index, tuple) else (index,)
@@ -668,13 +698,22 @@
     return total
 
 
+def kept_blocks(ref, half, rows, rows_a):
+    pairs = 2 * half * rows_a
+    return (
+        Blocks(ref, 0, (half, 2), rows_a),
+        Blocks(ref, pairs, (half, 2), rows_a),
+        Blocks(ref, 2 * pairs, (half,), rows),
+        Blocks(ref, 2 * pairs + half * rows, (half,), rows),
+    )
+
+
 def round_two(
-    places_ref, keep_one, got_one, keep_two, got_two, keep_a, got_a,
-    kept_one, kept_two, keep_a_one, keep_a_two, across_ref, inner_ref,
+    places_ref, keep_one, got_one, keep_two, got_two, keep_a, got_a, kept_ref, across_ref, inner_ref
 ):
-    half, rows = kept_one.shape[:2]
-    rows_a = keep_a_one.shape[2]
+    half, rows, rows_a = keep_one.shape[0], keep_one.shape[2], keep_a.shape[3]
     below = 2 * half * rows_a
+    keep_a_one, keep_a_two, kept_one, kept_two = kept_blocks(kept_ref, half, rows, rows_a)
     after_last(
         places_ref, keep_a, got_a, keep_a_one, Blocks(across_ref, 0, (half, 2), rows_a), keep_a_two,
         Blocks(inner_ref, 0, (half, 2), rows_a),
@@ -708,47 +747,51 @@
     return jnp.concatenate(pieces, axis=0)
 
 
-def round_three(count, split, places_ref, kept_one, kept_two, keep_a_one, keep_a_two, got_across, got_inner, *refs):
+def round_three(sizes, count, split, places_ref, held_ref, got_across, got_inner, *refs):
+    half, rows, rows_a = sizes
     region_refs, refs = (refs[:2], refs[2:]) if split else (refs[:1], refs[1:])
     bank_refs, refs = (refs[:count], refs[count:]) if split else (refs[:1], refs[1:])
-    kept_ref, sends, refs = refs[0], refs[1 : count], refs[count:]
-    kept_a_one, kept_a_two, bank_keep_ref, across_ref, inner_ref = refs
-    half, rows, channels = kept_one.shape
-    rows_a = keep_a_one.shape[2]
+    kept_ref, across_ref, inner_ref, *sends = refs
+    channels = kept_ref.shape[1]
     below = 2 * half * rows_a
+    keep_a_one, keep_a_two, kept_one, kept_two = kept_blocks(held_ref, half, rows, rows_a)
     after_plane(
         places_ref, kept_one, Blocks(got_inner, below, (half,), rows), kept_two, Blocks(got_across, below, (half,), rows),
-        kept_ref, sends,
+        kept_ref.at[pl.ds(0, rows)], sends,
     )
     after_cross(
         places_ref, keep_a_one, Blocks(got_across, 0, (half, 2), rows_a), keep_a_two,
-        Blocks(got_inner, 0, (half, 2), rows_a), kept_a_one, Blocks(inner_ref, 0, (half,), rows_a), kept_a_two,
+        Blocks(got_inner, 0, (half, 2), rows_a), Blocks(kept_ref, rows, (half,), rows_a),
+        Blocks(inner_ref, 0, (half,), rows_a), Blocks(kept_ref, rows + half * rows_a, (half,), rows_a),
         Blocks(across_ref, 0, (half,), rows_a),
     )
     across_ref[half * rows_a :] = low(total_of(region_refs))
     inner = places_ref[7] if split else 0
     keep = total_of([ref.at[inner] for ref in bank_refs])
-    store_narrow(bank_keep_ref, 0, low(keep), channels)
+    at = rows + 2 * half * rows_a
+    store_narrow(kept_ref, at, low(keep), channels)
     if split:
         send = total_of([ref.at[1 - inner] for ref in bank_refs])
         store_narrow(inner_ref, half * rows_a, low(send), channels)
     else:
-        inner_ref[half * rows_a :] = bank_keep_ref[...]
-
-
-def round_four(count, split, widths, places_ref, *refs):
-    plane_refs, refs = refs[:count], refs[count:]
-    kept_a_one, kept_a_two, bank_keep_ref, across_ref, got_across, got_inner, done_ref, kept_a_ref = refs[:8]
-    sends, (reduce_ref, query_ref, out_ref, head_ref) = refs[8 : 7 + count], refs[7 + count :]
-    half, rows_a, channels = kept_a_one.shape
-    rows = plane_refs[0].shape[0]
+        inner_ref[half * rows_a :] = kept_ref[at:]
+
+
+def round_four(sizes, count, split, widths, places_ref, held_ref, *refs):
+    half, rows, rows_a = sizes
+    plane_refs, refs = [held_ref.at[pl.ds(0, rows)], *refs[: count - 1]], refs[count - 1 :]
+    across_ref, got_across, got_inner, done_ref, kept_a_ref = refs[:5]
+    sends, (reduce_ref, query_ref, out_ref, head_ref) = refs[5 : 4 + count], refs[4 + count :]
+    kept_a_one = Blocks(held_ref, rows, (half,), rows_a)
+    kept_a_two = Blocks(held_ref, rows + half * rows_a, (half,), rows_a)
+    bank_keep = held_ref[rows + 2 * half * rows_a :]
     below = half * rows_a
     after_plane(
         places_ref, kept_a_one, Blocks(got_inner, 0, (half,), rows_a), kept_a_two,
         Blocks(got_across, 0, (half,), rows_a), kept_a_ref, sends,
     )
     done_ref[:rows] = low(total_of(plane_refs))
-    done_ref[rows:] = add_low(bank_keep_ref[...], got_inner[below:]) if split else bank_keep_ref[...]
+    done_ref[rows:] = add_low(bank_keep, got_inner[below:]) if split else bank_keep
     region = wide(across_ref[below:]) + wide(got_across[below:]) if split else wide(across_ref[below:])
     _, _, feature_rows, channel_rows, _, joined_rows = widths
     reduce_ref[...] = region[:feature_rows]
@@ -1216,6 +1259,22 @@
         2,
     )
     arrived = to_owners(message).reshape(group_rows, channels + TILE)
+    maps = (site_count, feature_count)
+    inside = (site_count, channels)
+    places, slope_c = run_kernel(
+        slopes_outer,
+        places,
+        [scale_c.reshape(1, -1), shift_c.reshape(1, -1), pre_c, feature_map],
+        [shape_of(maps, BF16)],
+        "slopes_outer",
+        WINDOW,
+        scratch=[
+            pltpu.VMEM(maps, F32), pltpu.VMEM(maps, BF16), pltpu.VMEM(maps, BF16), pltpu.SemaphoreType.DMA((3, chunks))
+        ],
+        raw_in=(2, 3),
+        raw_out=(0,),
+        limit=52,
+    )
     group_shape = shape_of((group_rows, channels), BF16)
     weight_shape = shape_of((group_rows, keys_here), BF16)
     places, query_part, score_grad, weights_low = run_kernel(
@@ -1265,8 +1324,6 @@
     half_blocks = blocks // 2
     rows_bc = rows_b + groups_c * LANE_ROWS
     wide_row = shape_of((1, feature_count), F32)
-    maps = (site_count, feature_count)
-    inside = (site_count, channels)
     (
         places, send_bc, keep_bc, lin_c_grad, pre_a_grad,
         scale_c_part, shift_c_part, scale_b_part, shift_b_part, scale_a_part, shift_a_part,
@@ -1274,8 +1331,7 @@
         functools.partial(later_back, 0, groups_b),
         places,
         [
-            regions_grad, pooling, scale_c.reshape(1, -1), shift_c.reshape(1, -1),
-            scales, pre_c, feature_map, act_b, pre_b, act_a, pre_a, packed,
+            regions_grad, pooling, scale_c.reshape(1, -1), scales, pre_c, slope_c, act_b, pre_b, act_a, pre_a, packed,
         ],
         [shape_of((half_blocks, rows_bc, channels), BF16)] * 2
         + [shape_of(maps, BF16), shape_of(inside, BF16), wide_row, wide_row]
@@ -1303,7 +1359,7 @@
             pltpu.SemaphoreType.DMA((2,)),
             pltpu.SemaphoreType.DMA((4 + 3 * chunks,)),
         ],
-        raw_in=range(5, 12),
+        raw_in=range(4, 11),
         raw_out=(0, 1, 2),
         limit=40,
     )
@@ -1367,13 +1423,13 @@
         raw_out=(0,),
         limit=12,
     )
-    block_bc, block_a = shape_of((half, rows_bc, channels), BF16), shape_of((half, 2, rows_a, channels), BF16)
+    kept_shape = shape_of((2 * half * (2 * rows_a + rows_bc), channels), BF16)
     both = shape_of((half * (2 * rows_a + rows_bc), channels), BF16)
-    places, kept_one, kept_two, keep_a_one, keep_a_two, send_across, send_inner = run_kernel(
+    places, held, send_across, send_inner = run_kernel(
         round_two,
         places,
         [keep_one, got_one, keep_two, got_two, parted(keep_a), parted(got_a)],
-        [block_bc, block_bc, block_a, block_a, both, both],
+        [kept_shape, both, both],
         "round_two",
         5,
     )
@@ -1414,29 +1470,27 @@
         bank_parts = [bank_pieces[0]] + [outer.swap(piece, step + 1) for step, piece in enumerate(bank_pieces[1:])]
     else:
         bank_parts = [low(jnp.sum(wide(to_owners(bank_pieces[0])), axis=0, keepdims=True))]
-    one_bc, half_a = shape_of((rows_bc, channels), BF16), shape_of((half, rows_a, channels), BF16)
-    results = run_kernel(
-        functools.partial(round_three, outer.size, split),
+    sizes = (half, rows_bc, rows_a)
+    places, held, send_across, send_inner, *pieces_bc = run_kernel(
+        functools.partial(round_three, sizes, outer.size, split),
         places,
-        [kept_one, kept_two, keep_a_one, keep_a_two, got_across, got_inner] + region_both + bank_parts,
-        [one_bc] * outer.size
-        + [half_a, half_a, shape_of((bank_step, channels), BF16)]
-        + [
+        [held, got_across, got_inner] + region_both + bank_parts,
+        [
+            shape_of((rows_bc + 2 * half * rows_a + bank_step, channels), BF16),
             shape_of((half * rows_a + region_lines, channels), BF16),
             shape_of((half * rows_a + bank_step, channels), BF16),
-        ],
+        ]
+        + [shape_of((rows_bc, channels), BF16)] * (outer.size - 1),
         "round_three",
         5,
     )
-    places, pieces_bc = results[0], results[1 : 1 + outer.size]
-    kept_a_one, kept_a_two, bank_keep, send_across, send_inner = results[1 + outer.size :]
     got_across, got_inner = across.swap(send_across, 1), inner.swap(send_inner, 1)
-    got_bc = [outer.swap(piece, step + 1) for step, piece in enumerate(pieces_bc[1:])]
+    got_bc = [outer.swap(piece, step + 1) for step, piece in enumerate(pieces_bc)]
     row_block = shape_of((channel_rows, channels), F32)
     results = run_kernel(
-        functools.partial(round_four, outer.size, split, widths),
+        functools.partial(round_four, sizes, outer.size, split, widths),
         places,
-        [pieces_bc[0], *got_bc, kept_a_one, kept_a_two, bank_keep, send_across, got_across, got_inner],
+        [held, *got_bc, send_across, got_across, got_inner],
         [shape_of((rows_bc + bank_step, channels), BF16)]
         + [shape_of((rows_a, channels), BF16)] * outer.size
         + [shape_of((feature_rows, channels), F32), row_block, row_block, shape_of((joined_rows, classes), F32)],

time: 348 us -> 339 us (0.974)
  blocking collectives: 35.3 us -> 22.7 us
  local copies, waits for them, and re-layouts: 35.8 us -> 29 us
  starting transfers between devices: 50.8 us -> 56.4 us
  Pallas kernels: 97.4 us -> 101 us
    all_to_all x2 -> x1, blocking collectives: 26.6 us -> 14 us  [to_owners(): lax.all_to_all(value, 'bank', split_axis=0, concat_axis=0, tiled=True)]
    unnamed x168 -> x160, local copies, waits for them, and re-layouts: 34.3 us -> 27.4 us
    all_to_all x3 -> x4, starting transfers between devices: 14.1 us -> 18.2 us  [to_owners(): lax.all_to_all(value, 'bank', split_axis=0, concat_axis=0, tiled=True)]
    pallas_call x22 -> x23, Pallas kernels: 75 us -> 78.4 us  [run_kernel(): pl.pallas_call(wrapped, out_shape=[shape_of(places.shape, jnp.int32)] + l...]
    all_to_all x3 -> x4, waiting for transfers between devices: 7.49 us -> 7.19 us  [to_owners(): lax.all_to_all(value, 'bank', split_axis=0, concat_axis=0, tiled=True)]
  transfers between devices with their start and end apart: 34 -> 35, of which waited for: 20 -> 21; matrix products, arithmetic and copies ran while one was open for 2% -> 2% of each run, Pallas kernels for 20% -> 21%
where the time goes in v5:
time: 339 us; the launch traced here: 337 us
  waiting for transfers between devices  112 us (33%)
  Pallas kernels  101 us (30%)
  starting transfers between devices  56.4 us (17%)
  local copies, waits for them, and re-layouts  29 us (9%)
  blocking collectives  22.7 us (7%)
  between operations  14.9 us (4%)
    ppermute x27, waiting for transfers between devices, swap(): return lax.ppermute(value, self.name, pairs)  96.6 us
    pallas_call x23, Pallas kernels, run_kernel(): pl.pallas_call(wrapped, out_shape=[shape_of(places.shape, jnp.int32)] + l...  78.4 us
    ppermute x27, starting transfers between devices, swap(): return lax.ppermute(value, self.name, pairs)  30.8 us
    unnamed x160, local copies, waits for them, and re-layouts  27.4 us
    all_to_all x4, starting transfers between devices, to_owners(): lax.all_to_all(value, 'bank', split_axis=0, concat_axis=0, tiled=True)  18.2 us
    pallas_call x1, Pallas kernels, run_later_convs(): pl.pallas_call(later_convs, out_shape=[jax.ShapeDtypeStruct((sites, chann...  14.1 us
    all_to_all x1, blocking collectives, to_owners(): lax.all_to_all(value, 'bank', split_axis=0, concat_axis=0, tiled=True)  14 us
    all_gather x1, blocking collectives, body(): done_a = lax.all_gather(part_a, 'dp', axis=0, tiled=False)  8.7 us
  transfers between devices with their start and end apart: 35, of which 21 were waited for; matrix products, arithmetic and copies ran while one was open for 2% of the time, Pallas kernels for 21%

profile of v5, /device:TPU:9, one launch (start us, length us, event | category | flops | bytes accessed | tf_op | source)
XLA Modules:
  0.0 337.4 jit_solution(12928954538638536516)
XLA Ops:
  27.1 4.5 %collective-permute-done.1 = bf16[12,16,512]{2,1,0:T(8,128)(2,1)} collective-permute-done((bf16[12,16,512]{2,1,0:T(8,128)(2,1)S(1)}, bf16[12,16,512]{2,1,0:T(8,128)(2,1)}, u32[]{:S(2)}, u32[]{:S(2)}) %collective-permute-start.1) | collective-permute-done | bytes 196640 | tf_op jit(solution)/shard_map/ppermute | solution.py:44
  47.0 20.6 %collective-permute-done.6 = bf16[4,12,16,512]{3,2,1,0:T(8,128)(2,1)S(1)} collective-permute-done((bf16[4,12,16,512]{3,2,1,0:T(8,128)(2,1)S(1)}, bf16[4,12,16,512]{3,2,1,0:T(8,128)(2,1)S(1)}, u32[]{:S(2)}, u32[]{:S(2)}) %collective-permute-start.6) | collective-permute-done | bytes 786464 | tf_op jit(solution)/shard_map/ppermute | solution.py:44
  70.1 7.1 %collective-permute-done.7.refs_1_ = bf16[16,12,16,512]{3,2,1,0:T(8,128)(2,1)S(1)} collective-permute-done((bf16[16,12,16,512]{3,2,1,0:T(8,128)(2,1)S(1)}, bf16[16,12,16,512]{3,2,1,0:T(8,128)(2,1)S(1)}, u32[]{:S(2)}, u32[]{:S(2)}) %collective-permute-start.7) | collective-permute-done | bytes 3145760 | tf_op jit(solution)/shard_map/ppermute | solution.py:44
  78.9 8.3 %first_conv.1 = (f32[512,512]{1,0:T(8,128)S(1)}, bf16[512,512]{1,0:T(8,128)(2,1)S(1)}, bf16[384,16,512]{2,1,0:T(8,128)(2,1)}) custom-call(s32[10]{0:T(128)S(1)} %get-tuple-element.178.places_ref.refs_0_, bf16[512,2048]{1,0:T(8,128)(2,1)} %refs_4_.5, bf16[16,12,16,512]{3,2,1,0:T(8,128)(2,1)} %copy-done.69, bf16[16,12,16,512]{3,2,1,0:T(8,128)(2,1)} %copy-done.74, ...), custom_call_target="tpu_custom_call" | custom-call | flops 89999998976 | bytes 90000000 | tf_op jit(solution)/shard_map/first_conv/pallas_call | solution.py:1051
  88.1 7.8 %all-gather.4.cloned.1.call-done = bf16[416,16,512]{2,1,0:T(8,128)(2,1)} async-done(((bf16[13,16,512]{2,1,0:T(8,128)(2,1)}), bf16[416,16,512]{2,1,0:T(8,128)(2,1)}) %all-gather.4.cloned.1.call-update) | async-done | bytes 6815760 | tf_op jit(solution)/shard_map/all_gather | solution.py:1179
  96.0 14.1 %later_convs.1 = (f32[512,512]{1,0:T(8,128)}, bf16[512,512]{1,0:T(8,128)(2,1)S(1)}, f32[512,2048]{1,0:T(8,128)}, bf16[32,2048]{1,0:T(8,128)(2,1)S(1)}, f32[32,51...) custom-call(bf16[512,512]{1,0:T(8,128)(2,1)S(1)} %get-tuple-element.181.act_a_ref.refs_9_, bf16[512,2048]{1,0:T(8,128)(2,1)} %refs_4_.5, ...), custom_call_target="tpu_custom_call" | custom-call | flops 224999997440 | bytes 225000000 | tf_op jit(solution)/shard_map/later_convs/pallas_call | solution.py:1080
  110.1 4.0 %all-to-all-start = ((bf16[8,32,512]{2,1,0:T(8,128)(2,1)}), bf16[8,32,512]{2,1,0:T(8,128)(2,1)S(1)}, u32[]{:S(2)}, u32[]{:S(2)}) async-start(bf16[8,32,512]{2,1,0:T(8,128)(2,1)} %get-tuple-element.184), calls=%async_computation | async-start | bytes 524288 | tf_op jit(solution)/shard_map/all_to_all | solution.py:83
  114.2 6.4 %all-to-all-done = bf16[8,32,512]{2,1,0:T(8,128)(2,1)S(1)} async-done(((bf16[8,32,512]{2,1,0:T(8,128)(2,1)}), bf16[8,32,512]{2,1,0:T(8,128)(2,1)S(1)}, u32[]{:S(2)}, u32[]{:S(2)}) %all-to-all-start) | async-done | bytes 262176 | tf_op jit(solution)/shard_map/all_to_all | solution.py:83
  121.9 14.0 %all_to_all.25.refs_1_ = bf16[8,32,640]{2,1,0:T(8,128)(2,1)S(1)} all-to-all(bf16[8,32,640]{2,1,0:T(8,128)(2,1)S(1)} %bitcast.45), channel_id=1, replica_groups=mesh['dp'=4,'bank'=8] {'bank'}, dimensions={0} | all-to-all | bytes 655360 | tf_op jit(solution)/shard_map/all_to_all | solution.py:83
  137.8 5.6 %all-to-all-start.2 = ((bf16[8,32,640]{2,1,0:T(8,128)(2,1)}), bf16[8,32,640]{2,1,0:T(8,128)(2,1)S(1)}, u32[]{:S(2)}, u32[]{:S(2)}) async-start(bf16[8,32,640]{2,1,0:T(8,128)(2,1)} %get-tuple-element.194), calls=%async_computation.2 | async-start | bytes 655360 | tf_op jit(solution)/shard_map/all_to_all | solution.py:83
  143.3 6.4 %slopes_outer.1 = (s32[10]{0:T(128)S(1)}, bf16[512,2048]{1,0:T(8,128)(2,1)}) custom-call(s32[10]{0:T(128)S(1)} %get-tuple-element.191.refs_0_, f32[1,2048]{1,0:T(1,128)S(1)} %bitcast.52, f32[1,2048]{1,0:T(1,128)S(1)} %bitcast.50, f32[512,2048]{1,0:T(8,128)} %get-tuple-element.192.refs_3_.refs_5_, bf16[512,2048]{1,0:T(8,128)(2,1)} %refs_4_.5), custom_call_target="tpu_custom_call" | custom-call | flops 1500000000 | bytes 1500000 | tf_op jit(solution)/shard_map/slopes_outer/pallas_call | solution.py:1033
  157.9 4.0 %all-to-all-start.3 = ((bf16[8,32,512]{2,1,0:T(8,128)(2,1)}), bf16[8,32,512]{2,1,0:T(8,128)(2,1)S(1)}, u32[]{:S(2)}, u32[]{:S(2)}) async-start(bf16[8,32,512]{2,1,0:T(8,128)(2,1)} %bitcast.27), calls=%async_computation.3 | async-start | bytes 524288 | tf_op jit(solution)/shard_map/all_to_all | solution.py:83
  172.2 17.5 %later_back.1 = (s32[10]{0:T(128)S(1)}, bf16[16,208,512]{2,1,0:T(8,128)(2,1)S(1)}, bf16[16,208,512]{2,1,0:T(8,128)(2,1)}, bf16[512,2048]{1,0:T(8,128)(2,1)S(1)},...) custom-call(s32[10]{0:T(128)S(1)} %get-tuple-element.204.refs_0_, ...), custom_call_target="tpu_custom_call" | custom-call | flops 420000006144 | bytes 420000000 | tf_op jit(solution)/shard_map/later_back/pallas_call | solution.py:1033
  192.3 8.2 %first_back.1 = (s32[10]{0:T(128)S(1)}, bf16[16,192,512]{2,1,0:T(8,128)(2,1)}, bf16[16,192,512]{2,1,0:T(8,128)(2,1)S(1)}, bf16[1024,512]{1,0:T(8,128)(2,1)S(1)}) custom-call(s32[10]{0:T(128)S(1)} %get-tuple-element.211.refs_0_, bf16[512,512]{1,0:T(8,128)(2,1)S(1)} %get-tuple-element.212.refs_1_, bf16[1024,512]{1,0:T(8,128)(2,1)} %get-tuple-element.213.refs_2_, ...), custom_call_target="tpu_custom_call" | custom-call | flops 89999998976 | bytes 90000000 | tf_op jit(solution)/shard_map/first_back/pallas_call | solution.py:1033
  208.4 4.5 %all-to-all-start.4 = ((bf16[8,32,1792]{2,1,0:T(8,128)(2,1)}), bf16[8,32,1792]{2,1,0:T(8,128)(2,1)}, u32[]{:S(2)}, u32[]{:S(2)}) async-start(bf16[8,32,1792]{2,1,0:T(8,128)(2,1)} %copy-done.6), calls=%async_computation.4 | async-start | bytes 1835008 | tf_op jit(solution)/shard_map/all_to_all | solution.py:83
  216.8 6.3 %map_back.1 = (s32[10]{0:T(128)S(1)}, bf16[512,2048]{1,0:T(8,128)(2,1)}) custom-call(s32[10]{0:T(128)S(1)} %get-tuple-element.225.refs_0_, bf16[512,512]{1,0:T(8,128)(2,1)S(1)} %copy-done.16, bf16[384,16,512]{2,1,0:T(8,128)(2,1)S(1)} %copy-done, bf16[512,2048]{1,0:T(8,128)(2,1)S(1)} %get-tuple-element.227.refs_3_), custom_call_target="tpu_custom_call" | custom-call | flops 1500000000 | bytes 1500000 | tf_op jit(solution)/shard_map/map_back/pallas_call | solution.py:1033
  224.6 7.0 %collective-permute-done.12.refs_4_ = bf16[2,2,208,512]{3,2,1,0:T(8,128)(2,1)} collective-permute-done((bf16[2,2,208,512]{3,2,1,0:T(8,128)(2,1)}, bf16[2,2,208,512]{3,2,1,0:T(8,128)(2,1)}, u32[]{:S(2)}, u32[]{:S(2)}) %collective-permute-start.12) | collective-permute-done | bytes 852000 | tf_op jit(solution)/shard_map/ppermute | solution.py:44
  231.7 4.6 %round_two.1 = (s32[10]{0:T(128)S(1)}, bf16[2368,512]{1,0:T(8,128)(2,1)S(1)}, bf16[1184,512]{1,0:T(8,128)(2,1)}, bf16[1184,512]{1,0:T(8,128)(2,1)}) custom-call(s32[10]{0:T(128)S(1)} %get-tuple-element.229.refs_0_, bf16[2,2,208,512]{3,2,1,0:T(8,128)(2,1)S(1)} %copy-done.55, bf16[2,2,208,512]{3,2,1,0:T(8,128)(2,1)} %collective-permute-done.11.refs_2_, ...), custom_call_target="tpu_custom_call" | custom-call | flops 74999996416 | bytes 75000000 | tf_op jit(solution)/shard_map/round_two/pallas_call | solution.py:1033
  251.2 6.4 %collective-permute-done.17.refs_7_ = bf16[2,400,128]{2,1,0:T(8,128)(2,1)S(1)} collective-permute-done((bf16[2,400,128]{2,1,0:T(8,128)(2,1)S(1)}, bf16[2,400,128]{2,1,0:T(8,128)(2,1)S(1)}, u32[]{:S(2)}, u32[]{:S(2)}) %collective-permute-start.17) | collective-permute-done | bytes 204832 | tf_op jit(solution)/shard_map/ppermute | solution.py:44
  260.9 9.3 %collective-permute-done.19.refs_9_ = bf16[2,400,128]{2,1,0:T(8,128)(2,1)S(1)} collective-permute-done((bf16[2,400,128]{2,1,0:T(8,128)(2,1)S(1)}, bf16[2,400,128]{2,1,0:T(8,128)(2,1)S(1)}, u32[]{:S(2)}, u32[]{:S(2)}) %collective-permute-start.19) | collective-permute-done | bytes 204832 | tf_op jit(solution)/shard_map/ppermute | solution.py:44
  279.2 4.4 %collective-permute-done.21.refs_3_ = bf16[208,512]{1,0:T(8,128)(2,1)S(1)} collective-permute-done((bf16[208,512]{1,0:T(8,128)(2,1)S(1)}, bf16[208,512]{1,0:T(8,128)(2,1)S(1)}, u32[]{:S(2)}, u32[]{:S(2)}) %collective-permute-start.21) | collective-permute-done | bytes 213024 | tf_op jit(solution)/shard_map/ppermute | solution.py:44
  283.7 10.3 %collective-permute-done.22.refs_4_ = bf16[208,512]{1,0:T(8,128)(2,1)S(1)} collective-permute-done((bf16[208,512]{1,0:T(8,128)(2,1)S(1)}, bf16[208,512]{1,0:T(8,128)(2,1)S(1)}, u32[]{:S(2)}, u32[]{:S(2)}) %collective-permute-start.22) | collective-permute-done | bytes 213024 | tf_op jit(solution)/shard_map/ppermute | solution.py:44
  303.5 11.8 %collective-permute-done.27.refs_4_ = bf16[192,512]{1,0:T(8,128)(2,1)S(1)} collective-permute-done((bf16[192,512]{1,0:T(8,128)(2,1)S(1)}, bf16[192,512]{1,0:T(8,128)(2,1)S(1)}, u32[]{:S(2)}, u32[]{:S(2)}) %collective-permute-start.27) | collective-permute-done | bytes 196640 | tf_op jit(solution)/shard_map/ppermute | solution.py:44
  319.2 8.7 %all-gather.1 = bf16[768,512]{1,0:T(8,128)(2,1)S(1)} all-gather(bf16[192,512]{1,0:T(8,128)(2,1)S(1)} %get-tuple-element.275), channel_id=3, replica_groups=mesh['dp'=4,'bank'=8] {'dp'}, dimensions={0}, use_global_device_ids=true | all-gather | bytes 983040 | tf_op jit(solution)/shard_map/all_gather | solution.py:1514
  (244 shorter events, 120.6 us)
Async XLA Ops:
  7.2 88.7 %all-gather.4.cloned.1.call-start = ((), (), s32[]{:S(2)}) async-start(), calls=%async_computation.5 | async-start | bytes 7028736 | tf_op jit(solution)/shard_map/all_gather | solution.py:1179
  12.6 14.6 %collective-permute-start.2 = (bf16[12,16,512]{2,1,0:T(8,128)(2,1)S(1)}, bf16[12,16,512]{2,1,0:T(8,128)(2,1)}, u32[]{:S(2)}, u32[]{:S(2)}) collective-permute-start(bf16[12,16,512]{2,1,0:T(8,128)(2,1)S(1)} %get-tuple-element.161), channel_id=1, source_target_pairs={{0,6},{1,7},{2,4},{3,5},{4,2},{5,3},{6,0},{7,1},{8,14},{9,15},{10,... | collective-permute-start | bytes 589832 | tf_op jit(solution)/shard_map/ppermute | solution.py:44
  14.0 17.7 %collective-permute-start.1 = (bf16[12,16,512]{2,1,0:T(8,128)(2,1)S(1)}, bf16[12,16,512]{2,1,0:T(8,128)(2,1)}, u32[]{:S(2)}, u32[]{:S(2)}) collective-permute-start(bf16[12,16,512]{2,1,0:T(8,128)(2,1)S(1)} %get-tuple-element.161), channel_id=1, source_target_pairs={{0,4},{1,5},{2,6},{3,7},{4,0},{5,1},{6,2},{7,3},{8,12},{9,13},{10,... | collective-permute-start | bytes 589832 | tf_op jit(solution)/shard_map/ppermute | solution.py:44
  15.0 16.6 %collective-permute-start = (bf16[12,16,512]{2,1,0:T(8,128)(2,1)S(1)}, bf16[12,16,512]{2,1,0:T(8,128)(2,1)}, u32[]{:S(2)}, u32[]{:S(2)}) collective-permute-start(bf16[12,16,512]{2,1,0:T(8,128)(2,1)S(1)} %get-tuple-element.161), channel_id=1, source_target_pairs={{0,2},{1,3},{2,0},{3,1},{4,6},{5,7},{6,4},{7,5},{8,10},{9,11},{10,... | collective-permute-start | bytes 589832 | tf_op jit(solution)/shard_map/ppermute | solution.py:44
  43.6 23.9 %collective-permute-start.6 = (bf16[4,12,16,512]{3,2,1,0:T(8,128)(2,1)S(1)}, bf16[4,12,16,512]{3,2,1,0:T(8,128)(2,1)S(1)}, u32[]{:S(2)}, u32[]{:S(2)}) collective-permute-start(bf16[4,12,16,512]{3,2,1,0:T(8,128)(2,1)S(1)} %constant_dynamic-update-slice_fusion.2), channel_id=1, source_target_pairs={{0,16},{8,24},{16,0},{24,8},{1,17},{9,25},{17,1},{25,9},{2,18},{10... | collective-permute-start | bytes 2359304 | tf_op jit(solution)/shard_map/ppermute | solution.py:44
  44.9 22.7 %collective-permute-start.5 = (bf16[4,12,16,512]{3,2,1,0:T(8,128)(2,1)S(1)}, bf16[4,12,16,512]{3,2,1,0:T(8,128)(2,1)S(1)}, u32[]{:S(2)}, u32[]{:S(2)}) collective-permute-start(bf16[4,12,16,512]{3,2,1,0:T(8,128)(2,1)S(1)} %constant_dynamic-update-slice_fusion), channel_id=1, source_target_pairs={{0,1},{1,0},{2,3},{3,2},{4,5},{5,4},{6,7},{7,6},{8,9},{9,8},{10,11... | collective-permute-start | bytes 2359304 | tf_op jit(solution)/shard_map/ppermute | solution.py:44
  137.8 12.3 %all-to-all-start.2 = ((bf16[8,32,640]{2,1,0:T(8,128)(2,1)}), bf16[8,32,640]{2,1,0:T(8,128)(2,1)S(1)}, u32[]{:S(2)}, u32[]{:S(2)}) async-start(bf16[8,32,640]{2,1,0:T(8,128)(2,1)} %get-tuple-element.194), calls=%async_computation.2 | async-start | bytes 655360 | tf_op jit(solution)/shard_map/all_to_all | solution.py:83
  167.2 25.1 %collective-permute-start.9 = (bf16[1024,512]{1,0:T(8,128)(2,1)}, bf16[1024,512]{1,0:T(8,128)(2,1)}, u32[]{:S(2)}, u32[]{:S(2)}) collective-permute-start(bf16[1024,512]{1,0:T(8,128)(2,1)} %get-tuple-element.213.refs_2_), channel_id=1, source_target_pairs={{0,16},{8,24},{16,0},{24,8},{1,17},{9,25},{17,1},{25,9},{2,18},{10... | collective-permute-start | bytes 3145736 | tf_op jit(solution)/shard_map/ppermute | solution.py:1299
  189.8 11.7 %collective-permute-start.10 = (bf16[16,208,512]{2,1,0:T(8,128)(2,1)S(1)}, bf16[16,208,512]{2,1,0:T(8,128)(2,1)S(1)}, u32[]{:S(2)}, u32[]{:S(2)}) collective-permute-start(bf16[16,208,512]{2,1,0:T(8,128)(2,1)S(1)} %get-tuple-element.217), channel_id=1, source_target_pairs={{0,8},{8,0},{16,24},{24,16},{1,9},{9,1},{17,25},{25,17},{2,10},{10... | collective-permute-start | bytes 10223624 | tf_op jit(solution)/shard_map/ppermute | solution.py:44
  200.6 22.5 %collective-permute-start.13 = (bf16[16,192,512]{2,1,0:T(8,128)(2,1)}, bf16[16,192,512]{2,1,0:T(8,128)(2,1)}, u32[]{:S(2)}, u32[]{:S(2)}) collective-permute-start(bf16[16,192,512]{2,1,0:T(8,128)(2,1)} %get-tuple-element.235), channel_id=1, source_target_pairs={{0,8},{8,0},{16,24},{24,16},{1,9},{9,1},{17,25},{25,17},{2,10},{10... | collective-permute-start | bytes 9437192 | tf_op jit(solution)/shard_map/ppermute | solution.py:44
  203.7 20.9 %collective-permute-start.11 = (bf16[2,2,208,512]{3,2,1,0:T(8,128)(2,1)}, bf16[2,2,208,512]{3,2,1,0:T(8,128)(2,1)}, u32[]{:S(2)}, u32[]{:S(2)}) collective-permute-start(bf16[2,2,208,512]{3,2,1,0:T(8,128)(2,1)} %get-tuple-element.231), channel_id=1, source_target_pairs={{0,16},{8,24},{16,0},{24,8},{1,17},{9,25},{17,1},{25,9},{2,18},{10... | collective-permute-start | bytes 2555912 | tf_op jit(solution)/shard_map/ppermute | solution.py:44
  204.8 26.9 %collective-permute-start.12 = (bf16[2,2,208,512]{3,2,1,0:T(8,128)(2,1)}, bf16[2,2,208,512]{3,2,1,0:T(8,128)(2,1)}, u32[]{:S(2)}, u32[]{:S(2)}) collective-permute-start(bf16[2,2,208,512]{3,2,1,0:T(8,128)(2,1)} %get-tuple-element.233), channel_id=1, source_target_pairs={{0,1},{1,0},{2,3},{3,2},{4,5},{5,4},{6,7},{7,6},{8,9},{9,8},{10,11... | collective-permute-start | bytes 2555912 | tf_op jit(solution)/shard_map/ppermute | solution.py:44
  208.4 35.8 %all-to-all-start.4 = ((bf16[8,32,1792]{2,1,0:T(8,128)(2,1)}), bf16[8,32,1792]{2,1,0:T(8,128)(2,1)}, u32[]{:S(2)}, u32[]{:S(2)}) async-start(bf16[8,32,1792]{2,1,0:T(8,128)(2,1)} %copy-done.6), calls=%async_computation.4 | async-start | bytes 1835008 | tf_op jit(solution)/shard_map/all_to_all | solution.py:83
  237.7 32.5 %collective-permute-start.14 = (bf16[1184,512]{1,0:T(8,128)(2,1)}, bf16[1184,512]{1,0:T(8,128)(2,1)S(1)}, u32[]{:S(2)}, u32[]{:S(2)}) collective-permute-start(bf16[1184,512]{1,0:T(8,128)(2,1)} %get-tuple-element.254), channel_id=1, source_target_pairs={{0,16},{8,24},{16,0},{24,8},{1,17},{9,25},{17,1},{25,9},{2,18},{10... | collective-permute-start | bytes 3637256 | tf_op jit(solution)/shard_map/ppermute | solution.py:44
  238.2 32.0 %collective-permute-start.15 = (bf16[1184,512]{1,0:T(8,128)(2,1)}, bf16[1184,512]{1,0:T(8,128)(2,1)}, u32[]{:S(2)}, u32[]{:S(2)}) collective-permute-start(bf16[1184,512]{1,0:T(8,128)(2,1)} %get-tuple-element.255), channel_id=1, source_target_pairs={{0,1},{1,0},{2,3},{3,2},{4,5},{5,4},{6,7},{7,6},{8,9},{9,8},{10,11... | collective-permute-start | bytes 3637256 | tf_op jit(solution)/shard_map/ppermute | solution.py:44
  246.4 23.9 %collective-permute-start.16 = (bf16[464,512]{1,0:T(8,128)(2,1)S(1)}, bf16[464,512]{1,0:T(8,128)(2,1)S(1)}, u32[]{:S(2)}, u32[]{:S(2)}) collective-permute-start(bf16[464,512]{1,0:T(8,128)(2,1)S(1)} %get-tuple-element.256.refs_4_), channel_id=1, source_target_pairs={{0,8},{8,0},{16,24},{24,16},{1,9},{9,1},{17,25},{25,17},{2,10},{10... | collective-permute-start | bytes 1425416 | tf_op jit(solution)/shard_map/ppermute | solution.py:1299
  248.9 12.0 %collective-permute-start.18 = (bf16[2,400,128]{2,1,0:T(8,128)(2,1)S(1)}, bf16[2,400,128]{2,1,0:T(8,128)(2,1)S(1)}, u32[]{:S(2)}, u32[]{:S(2)}) collective-permute-start(bf16[2,400,128]{2,1,0:T(8,128)(2,1)S(1)} %get-tuple-element.259), channel_id=1, source_target_pairs={{0,4},{1,5},{2,6},{3,7},{4,0},{5,1},{6,2},{7,3},{8,12},{9,13},{10,... | collective-permute-start | bytes 614408 | tf_op jit(solution)/shard_map/ppermute | solution.py:44
  257.7 12.5 %collective-permute-start.19 = (bf16[2,400,128]{2,1,0:T(8,128)(2,1)S(1)}, bf16[2,400,128]{2,1,0:T(8,128)(2,1)S(1)}, u32[]{:S(2)}, u32[]{:S(2)}) collective-permute-start(bf16[2,400,128]{2,1,0:T(8,128)(2,1)S(1)} %get-tuple-element.260), channel_id=1, source_target_pairs={{0,6},{1,7},{2,4},{3,5},{4,2},{5,3},{6,0},{7,1},{8,14},{9,15},{10,... | collective-permute-start | bytes 614408 | tf_op jit(solution)/shard_map/ppermute | solution.py:44
  272.4 21.5 %collective-permute-start.23 = (bf16[848,512]{1,0:T(8,128)(2,1)S(1)}, bf16[848,512]{1,0:T(8,128)(2,1)S(1)}, u32[]{:S(2)}, u32[]{:S(2)}) collective-permute-start(bf16[848,512]{1,0:T(8,128)(2,1)S(1)} %get-tuple-element.266.refs_5_), channel_id=1, source_target_pairs={{0,16},{8,24},{16,0},{24,8},{1,17},{9,25},{17,1},{25,9},{2,18},{10... | collective-permute-start | bytes 2605064 | tf_op jit(solution)/shard_map/ppermute | solution.py:44
  273.5 20.4 %collective-permute-start.24 = (bf16[496,512]{1,0:T(8,128)(2,1)S(1)}, bf16[496,512]{1,0:T(8,128)(2,1)S(1)}, u32[]{:S(2)}, u32[]{:S(2)}) collective-permute-start(bf16[496,512]{1,0:T(8,128)(2,1)S(1)} %get-tuple-element.267), channel_id=1, source_target_pairs={{0,1},{1,0},{2,3},{3,2},{4,5},{5,4},{6,7},{7,6},{8,9},{9,8},{10,11... | collective-permute-start | bytes 1523720 | tf_op jit(solution)/shard_map/ppermute | solution.py:44
  275.6 18.4 %collective-permute-start.22 = (bf16[208,512]{1,0:T(8,128)(2,1)S(1)}, bf16[208,512]{1,0:T(8,128)(2,1)S(1)}, u32[]{:S(2)}, u32[]{:S(2)}) collective-permute-start(bf16[208,512]{1,0:T(8,128)(2,1)S(1)} %get-tuple-element.265), channel_id=1, source_target_pairs={{0,6},{1,7},{2,4},{3,5},{4,2},{5,3},{6,0},{7,1},{8,14},{9,15},{10,... | collective-permute-start | bytes 638984 | tf_op jit(solution)/shard_map/ppermute | solution.py:44
  295.5 19.8 %collective-permute-start.28 = (bf16[320,512]{1,0:T(8,128)(2,1)S(1)}, bf16[320,512]{1,0:T(8,128)(2,1)S(1)}, u32[]{:S(2)}, u32[]{:S(2)}) collective-permute-start(bf16[320,512]{1,0:T(8,128)(2,1)S(1)} %get-tuple-element.273.refs_5_), channel_id=1, source_target_pairs={{0,16},{8,24},{16,0},{24,8},{1,17},{9,25},{17,1},{25,9},{2,18},{10... | collective-permute-start | bytes 983048 | tf_op jit(solution)/shard_map/ppermute | solution.py:44
  297.6 17.7 %collective-permute-start.27 = (bf16[192,512]{1,0:T(8,128)(2,1)S(1)}, bf16[192,512]{1,0:T(8,128)(2,1)S(1)}, u32[]{:S(2)}, u32[]{:S(2)}) collective-permute-start(bf16[192,512]{1,0:T(8,128)(2,1)S(1)} %get-tuple-element.272), channel_id=1, source_target_pairs={{0,6},{1,7},{2,4},{3,5},{4,2},{5,3},{6,0},{7,1},{8,14},{9,15},{10,... | collective-permute-start | bytes 589832 | tf_op jit(solution)/shard_map/ppermute | solution.py:44
  316.4 11.4 %collective-permute-start.29 = (bf16[2,320,512]{2,1,0:T(8,128)(2,1)S(1)}, bf16[2,320,512]{2,1,0:T(8,128)(2,1)S(1)}, u32[]{:S(2)}, u32[]{:S(2)}) collective-permute-start(bf16[2,320,512]{2,1,0:T(8,128)(2,1)S(1)} %get-tuple-element.276.refs_2_), channel_id=1, source_target_pairs={{0,8},{8,0},{16,24},{24,16},{1,9},{9,1},{17,25},{25,17},{2,10},{10... | collective-permute-start | bytes 1966088 | tf_op jit(solution)/shard_map/ppermute | solution.py:44
  (86 other events, 747.6 us)
Sparse Core Ops, SparseCore 0:
  16.3 79.5 all-gather.3

commit v6 on v5

--- a/solution.py
+++ b/solution.py
@@ -227,9 +227,9 @@
 
 
 def later_convs(
-    act_a_ref, fm_ref, packed_ref, scale_b_ref, shift_b_ref, scale_c_ref, shift_c_ref, pool_ref, w_reduce_ref, w_query_ref,
+    act_a_ref, fm_ref, packed_ref, scale_b_ref, shift_b_ref, scale_c_ref, shift_c_ref, pool_ref, w_reduce_ref, w_query_far_ref,
     pre_b_out_ref, act_b_out_ref, pre_c_ref, regions_out_ref, reduced_out_ref, queries_ref,
-    weight_b, weight_c, out_low, held_map, held_pre, held_reduce, pre_b_ref, act_b_ref, regions_ref, reduced_ref, sems_b, sems_c, sems,
+    weight_b, weight_c, out_low, held_map, held_pre, held_reduce, pre_b_ref, act_b_ref, regions_ref, reduced_ref, w_query_ref, sems_b, sems_c, sems,
 ):
     sites, channels = act_a_ref.shape
     blocks = packed_ref.shape[0]
@@ -242,6 +242,7 @@
         [
             pltpu.make_async_copy(fm_ref, held_map, sems.at[0]),
             pltpu.make_async_copy(w_reduce_ref, held_reduce, sems.at[1]),
+            pltpu.make_async_copy(w_query_far_ref, w_query_ref, sems.at[6 + groups_c]),
         ]
     )
     act_a = act_a_ref[...]
@@ -1087,7 +1088,7 @@
             jax.ShapeDtypeStruct((own, channels), jnp.float32),
             jax.ShapeDtypeStruct((group, own, channels), jnp.bfloat16),
         ],
-        in_specs=[HELD] + [ANY] * 2 + [HELD] * 5 + [ANY, HELD],
+        in_specs=[HELD] + [ANY] * 2 + [HELD] * 5 + [ANY] * 2,
         out_specs=[ANY] * 5 + [HELD],
         scratch_shapes=[
             pltpu.VMEM((blocks * groups_b, LANE_ROWS, channels), jnp.bfloat16),
@@ -1100,9 +1101,10 @@
             pltpu.VMEM((sites, channels), jnp.bfloat16),
             pltpu.VMEM((own, features), jnp.bfloat16),
             pltpu.VMEM((own, channels), jnp.float32),
+            pltpu.VMEM(w_query.shape, jnp.bfloat16),
             pltpu.SemaphoreType.DMA((blocks,)),
             pltpu.SemaphoreType.DMA((blocks,)),
-            pltpu.SemaphoreType.DMA((6 + groups_c,)),
+            pltpu.SemaphoreType.DMA((7 + groups_c,)),
         ],
         compiler_params=params(52),
         cost_estimate=pl.CostEstimate(flops=int(15 * COST), bytes_accessed=int(15 * COST / 1000), transcendentals=0),

time: 339 us -> 338 us (level)
  no operation moved by 1% of the time
where the time goes in v6:
time: 338 us; the launch traced here: 336 us
  waiting for transfers between devices  112 us (33%)
  Pallas kernels  99.7 us (29%)
  starting transfers between devices  56.5 us (17%)
  local copies, waits for them, and re-layouts  29 us (9%)
  blocking collectives  22.6 us (7%)
  between operations  14.9 us (4%)
    ppermute x27, waiting for transfers between devices, swap(): return lax.ppermute(value, self.name, pairs)  96.6 us
    pallas_call x23, Pallas kernels, run_kernel(): pl.pallas_call(wrapped, out_shape=[shape_of(places.shape, jnp.int32)] + l...  78.3 us
    ppermute x27, starting transfers between devices, swap(): return lax.ppermute(value, self.name, pairs)  30.8 us
    unnamed x160, local copies, waits for them, and re-layouts  27.4 us
    all_to_all x4, starting transfers between devices, to_owners(): lax.all_to_all(value, 'bank', split_axis=0, concat_axis=0, tiled=True)  18.2 us
    all_to_all x1, blocking collectives, to_owners(): lax.all_to_all(value, 'bank', split_axis=0, concat_axis=0, tiled=True)  13.9 us
    pallas_call x1, Pallas kernels, run_later_convs(): pl.pallas_call(later_convs, out_shape=[jax.ShapeDtypeStruct((sites, chann...  13.1 us
    all_gather x1, blocking collectives, body(): done_a = lax.all_gather(part_a, 'dp', axis=0, tiled=False)  8.7 us
  transfers between devices with their start and end apart: 35, of which 21 were waited for; matrix products, arithmetic and copies ran while one was open for 2% of the time, Pallas kernels for 21%

profile of v6, /device:TPU:9, one launch (start us, length us, event | category | flops | bytes accessed | tf_op | source)
XLA Modules:
  0.0 336.4 jit_solution(6407677096745817642)
XLA Ops:
  27.1 4.5 %collective-permute-done.1 = bf16[12,16,512]{2,1,0:T(8,128)(2,1)} collective-permute-done((bf16[12,16,512]{2,1,0:T(8,128)(2,1)S(1)}, bf16[12,16,512]{2,1,0:T(8,128)(2,1)}, u32[]{:S(2)}, u32[]{:S(2)}) %collective-permute-start.1) | collective-permute-done | bytes 196640 | tf_op jit(solution)/shard_map/ppermute | solution.py:44
  47.0 20.6 %collective-permute-done.6 = bf16[4,12,16,512]{3,2,1,0:T(8,128)(2,1)S(1)} collective-permute-done((bf16[4,12,16,512]{3,2,1,0:T(8,128)(2,1)S(1)}, bf16[4,12,16,512]{3,2,1,0:T(8,128)(2,1)S(1)}, u32[]{:S(2)}, u32[]{:S(2)}) %collective-permute-start.6) | collective-permute-done | bytes 786464 | tf_op jit(solution)/shard_map/ppermute | solution.py:44
  70.1 7.1 %collective-permute-done.7.refs_1_ = bf16[16,12,16,512]{3,2,1,0:T(8,128)(2,1)S(1)} collective-permute-done((bf16[16,12,16,512]{3,2,1,0:T(8,128)(2,1)S(1)}, bf16[16,12,16,512]{3,2,1,0:T(8,128)(2,1)S(1)}, u32[]{:S(2)}, u32[]{:S(2)}) %collective-permute-start.7) | collective-permute-done | bytes 3145760 | tf_op jit(solution)/shard_map/ppermute | solution.py:44
  78.9 8.3 %first_conv.1 = (f32[512,512]{1,0:T(8,128)S(1)}, bf16[512,512]{1,0:T(8,128)(2,1)S(1)}, bf16[384,16,512]{2,1,0:T(8,128)(2,1)}) custom-call(s32[10]{0:T(128)S(1)} %get-tuple-element.178.places_ref.refs_0_, bf16[512,2048]{1,0:T(8,128)(2,1)} %refs_4_.5, bf16[16,12,16,512]{3,2,1,0:T(8,128)(2,1)} %copy-done.69, bf16[16,12,16,512]{3,2,1,0:T(8,128)(2,1)} %copy-done.74, ...), custom_call_target="tpu_custom_call" | custom-call | flops 89999998976 | bytes 90000000 | tf_op jit(solution)/shard_map/first_conv/pallas_call | solution.py:1052
  88.1 7.8 %all-gather.4.cloned.1.call-done = bf16[416,16,512]{2,1,0:T(8,128)(2,1)} async-done(((bf16[13,16,512]{2,1,0:T(8,128)(2,1)}), bf16[416,16,512]{2,1,0:T(8,128)(2,1)}) %all-gather.4.cloned.1.call-update) | async-done | bytes 6815760 | tf_op jit(solution)/shard_map/all_gather | solution.py:1181
  96.0 13.1 %later_convs.1 = (f32[512,512]{1,0:T(8,128)}, bf16[512,512]{1,0:T(8,128)(2,1)S(1)}, f32[512,2048]{1,0:T(8,128)}, bf16[32,2048]{1,0:T(8,128)(2,1)S(1)}, f32[32,51...) custom-call(bf16[512,512]{1,0:T(8,128)(2,1)S(1)} %get-tuple-element.181.act_a_ref.refs_9_, bf16[512,2048]{1,0:T(8,128)(2,1)} %refs_4_.5, ...), custom_call_target="tpu_custom_call" | custom-call | flops 224999997440 | bytes 225000000 | tf_op jit(solution)/shard_map/later_convs/pallas_call | solution.py:1081
  109.1 4.0 %all-to-all-start = ((bf16[8,32,512]{2,1,0:T(8,128)(2,1)}), bf16[8,32,512]{2,1,0:T(8,128)(2,1)S(1)}, u32[]{:S(2)}, u32[]{:S(2)}) async-start(bf16[8,32,512]{2,1,0:T(8,128)(2,1)} %get-tuple-element.184), calls=%async_computation | async-start | bytes 524288 | tf_op jit(solution)/shard_map/all_to_all | solution.py:83
  113.2 6.4 %all-to-all-done = bf16[8,32,512]{2,1,0:T(8,128)(2,1)S(1)} async-done(((bf16[8,32,512]{2,1,0:T(8,128)(2,1)}), bf16[8,32,512]{2,1,0:T(8,128)(2,1)S(1)}, u32[]{:S(2)}, u32[]{:S(2)}) %all-to-all-start) | async-done | bytes 262176 | tf_op jit(solution)/shard_map/all_to_all | solution.py:83
  120.9 13.9 %all_to_all.25.refs_1_ = bf16[8,32,640]{2,1,0:T(8,128)(2,1)S(1)} all-to-all(bf16[8,32,640]{2,1,0:T(8,128)(2,1)S(1)} %bitcast.45), channel_id=1, replica_groups=mesh['dp'=4,'bank'=8] {'bank'}, dimensions={0} | all-to-all | bytes 655360 | tf_op jit(solution)/shard_map/all_to_all | solution.py:83
  136.7 5.6 %all-to-all-start.2 = ((bf16[8,32,640]{2,1,0:T(8,128)(2,1)}), bf16[8,32,640]{2,1,0:T(8,128)(2,1)S(1)}, u32[]{:S(2)}, u32[]{:S(2)}) async-start(bf16[8,32,640]{2,1,0:T(8,128)(2,1)} %get-tuple-element.194), calls=%async_computation.2 | async-start | bytes 655360 | tf_op jit(solution)/shard_map/all_to_all | solution.py:83
  142.3 6.4 %slopes_outer.1 = (s32[10]{0:T(128)S(1)}, bf16[512,2048]{1,0:T(8,128)(2,1)}) custom-call(s32[10]{0:T(128)S(1)} %get-tuple-element.191.refs_0_, f32[1,2048]{1,0:T(1,128)S(1)} %bitcast.52, f32[1,2048]{1,0:T(1,128)S(1)} %bitcast.50, f32[512,2048]{1,0:T(8,128)} %get-tuple-element.192.refs_3_.refs_5_, bf16[512,2048]{1,0:T(8,128)(2,1)} %refs_4_.5), custom_call_target="tpu_custom_call" | custom-call | flops 1500000000 | bytes 1500000 | tf_op jit(solution)/shard_map/slopes_outer/pallas_call | solution.py:1034
  156.9 4.0 %all-to-all-start.3 = ((bf16[8,32,512]{2,1,0:T(8,128)(2,1)}), bf16[8,32,512]{2,1,0:T(8,128)(2,1)S(1)}, u32[]{:S(2)}, u32[]{:S(2)}) async-start(bf16[8,32,512]{2,1,0:T(8,128)(2,1)} %bitcast.27), calls=%async_computation.3 | async-start | bytes 524288 | tf_op jit(solution)/shard_map/all_to_all | solution.py:83
  171.2 17.5 %later_back.1 = (s32[10]{0:T(128)S(1)}, bf16[16,208,512]{2,1,0:T(8,128)(2,1)S(1)}, bf16[16,208,512]{2,1,0:T(8,128)(2,1)}, bf16[512,2048]{1,0:T(8,128)(2,1)S(1)},...) custom-call(s32[10]{0:T(128)S(1)} %get-tuple-element.204.refs_0_, ...), custom_call_target="tpu_custom_call" | custom-call | flops 420000006144 | bytes 420000000 | tf_op jit(solution)/shard_map/later_back/pallas_call | solution.py:1034
  191.3 8.2 %first_back.1 = (s32[10]{0:T(128)S(1)}, bf16[16,192,512]{2,1,0:T(8,128)(2,1)}, bf16[16,192,512]{2,1,0:T(8,128)(2,1)S(1)}, bf16[1024,512]{1,0:T(8,128)(2,1)S(1)}) custom-call(s32[10]{0:T(128)S(1)} %get-tuple-element.211.refs_0_, bf16[512,512]{1,0:T(8,128)(2,1)S(1)} %get-tuple-element.212.refs_1_, bf16[1024,512]{1,0:T(8,128)(2,1)} %get-tuple-element.213.refs_2_, ...), custom_call_target="tpu_custom_call" | custom-call | flops 89999998976 | bytes 90000000 | tf_op jit(solution)/shard_map/first_back/pallas_call | solution.py:1034
  207.4 4.5 %all-to-all-start.4 = ((bf16[8,32,1792]{2,1,0:T(8,128)(2,1)}), bf16[8,32,1792]{2,1,0:T(8,128)(2,1)}, u32[]{:S(2)}, u32[]{:S(2)}) async-start(bf16[8,32,1792]{2,1,0:T(8,128)(2,1)} %copy-done.6), calls=%async_computation.4 | async-start | bytes 1835008 | tf_op jit(solution)/shard_map/all_to_all | solution.py:83
  215.8 6.3 %map_back.1 = (s32[10]{0:T(128)S(1)}, bf16[512,2048]{1,0:T(8,128)(2,1)}) custom-call(s32[10]{0:T(128)S(1)} %get-tuple-element.225.refs_0_, bf16[512,512]{1,0:T(8,128)(2,1)S(1)} %copy-done.16, bf16[384,16,512]{2,1,0:T(8,128)(2,1)S(1)} %copy-done, bf16[512,2048]{1,0:T(8,128)(2,1)S(1)} %get-tuple-element.227.refs_3_), custom_call_target="tpu_custom_call" | custom-call | flops 1500000000 | bytes 1500000 | tf_op jit(solution)/shard_map/map_back/pallas_call | solution.py:1034
  223.6 7.1 %collective-permute-done.12.refs_4_ = bf16[2,2,208,512]{3,2,1,0:T(8,128)(2,1)} collective-permute-done((bf16[2,2,208,512]{3,2,1,0:T(8,128)(2,1)}, bf16[2,2,208,512]{3,2,1,0:T(8,128)(2,1)}, u32[]{:S(2)}, u32[]{:S(2)}) %collective-permute-start.12) | collective-permute-done | bytes 852000 | tf_op jit(solution)/shard_map/ppermute | solution.py:44
  230.7 4.6 %round_two.1 = (s32[10]{0:T(128)S(1)}, bf16[2368,512]{1,0:T(8,128)(2,1)S(1)}, bf16[1184,512]{1,0:T(8,128)(2,1)}, bf16[1184,512]{1,0:T(8,128)(2,1)}) custom-call(s32[10]{0:T(128)S(1)} %get-tuple-element.229.refs_0_, bf16[2,2,208,512]{3,2,1,0:T(8,128)(2,1)S(1)} %copy-done.55, bf16[2,2,208,512]{3,2,1,0:T(8,128)(2,1)} %collective-permute-done.11.refs_2_, ...), custom_call_target="tpu_custom_call" | custom-call | flops 74999996416 | bytes 75000000 | tf_op jit(solution)/shard_map/round_two/pallas_call | solution.py:1034
  250.2 6.4 %collective-permute-done.17.refs_7_ = bf16[2,400,128]{2,1,0:T(8,128)(2,1)S(1)} collective-permute-done((bf16[2,400,128]{2,1,0:T(8,128)(2,1)S(1)}, bf16[2,400,128]{2,1,0:T(8,128)(2,1)S(1)}, u32[]{:S(2)}, u32[]{:S(2)}) %collective-permute-start.17) | collective-permute-done | bytes 204832 | tf_op jit(solution)/shard_map/ppermute | solution.py:44
  259.8 9.3 %collective-permute-done.19.refs_9_ = bf16[2,400,128]{2,1,0:T(8,128)(2,1)S(1)} collective-permute-done((bf16[2,400,128]{2,1,0:T(8,128)(2,1)S(1)}, bf16[2,400,128]{2,1,0:T(8,128)(2,1)S(1)}, u32[]{:S(2)}, u32[]{:S(2)}) %collective-permute-start.19) | collective-permute-done | bytes 204832 | tf_op jit(solution)/shard_map/ppermute | solution.py:44
  278.2 4.4 %collective-permute-done.21.refs_3_ = bf16[208,512]{1,0:T(8,128)(2,1)S(1)} collective-permute-done((bf16[208,512]{1,0:T(8,128)(2,1)S(1)}, bf16[208,512]{1,0:T(8,128)(2,1)S(1)}, u32[]{:S(2)}, u32[]{:S(2)}) %collective-permute-start.21) | collective-permute-done | bytes 213024 | tf_op jit(solution)/shard_map/ppermute | solution.py:44
  282.7 10.3 %collective-permute-done.22.refs_4_ = bf16[208,512]{1,0:T(8,128)(2,1)S(1)} collective-permute-done((bf16[208,512]{1,0:T(8,128)(2,1)S(1)}, bf16[208,512]{1,0:T(8,128)(2,1)S(1)}, u32[]{:S(2)}, u32[]{:S(2)}) %collective-permute-start.22) | collective-permute-done | bytes 213024 | tf_op jit(solution)/shard_map/ppermute | solution.py:44
  302.5 11.7 %collective-permute-done.27.refs_4_ = bf16[192,512]{1,0:T(8,128)(2,1)S(1)} collective-permute-done((bf16[192,512]{1,0:T(8,128)(2,1)S(1)}, bf16[192,512]{1,0:T(8,128)(2,1)S(1)}, u32[]{:S(2)}, u32[]{:S(2)}) %collective-permute-start.27) | collective-permute-done | bytes 196640 | tf_op jit(solution)/shard_map/ppermute | solution.py:44
  318.2 8.7 %all-gather.1 = bf16[768,512]{1,0:T(8,128)(2,1)S(1)} all-gather(bf16[192,512]{1,0:T(8,128)(2,1)S(1)} %get-tuple-element.275), channel_id=3, replica_groups=mesh['dp'=4,'bank'=8] {'dp'}, dimensions={0}, use_global_device_ids=true | all-gather | bytes 983040 | tf_op jit(solution)/shard_map/all_gather | solution.py:1516
  (244 shorter events, 120.6 us)
Async XLA Ops:
  7.2 88.7 %all-gather.4.cloned.1.call-start = ((), (), s32[]{:S(2)}) async-start(), calls=%async_computation.5 | async-start | bytes 7028736 | tf_op jit(solution)/shard_map/all_gather | solution.py:1181
  12.6 14.6 %collective-permute-start.2 = (bf16[12,16,512]{2,1,0:T(8,128)(2,1)S(1)}, bf16[12,16,512]{2,1,0:T(8,128)(2,1)}, u32[]{:S(2)}, u32[]{:S(2)}) collective-permute-start(bf16[12,16,512]{2,1,0:T(8,128)(2,1)S(1)} %get-tuple-element.161), channel_id=1, source_target_pairs={{0,6},{1,7},{2,4},{3,5},{4,2},{5,3},{6,0},{7,1},{8,14},{9,15},{10,... | collective-permute-start | bytes 589832 | tf_op jit(solution)/shard_map/ppermute | solution.py:44
  14.0 17.7 %collective-permute-start.1 = (bf16[12,16,512]{2,1,0:T(8,128)(2,1)S(1)}, bf16[12,16,512]{2,1,0:T(8,128)(2,1)}, u32[]{:S(2)}, u32[]{:S(2)}) collective-permute-start(bf16[12,16,512]{2,1,0:T(8,128)(2,1)S(1)} %get-tuple-element.161), channel_id=1, source_target_pairs={{0,4},{1,5},{2,6},{3,7},{4,0},{5,1},{6,2},{7,3},{8,12},{9,13},{10,... | collective-permute-start | bytes 589832 | tf_op jit(solution)/shard_map/ppermute | solution.py:44
  15.0 16.6 %collective-permute-start = (bf16[12,16,512]{2,1,0:T(8,128)(2,1)S(1)}, bf16[12,16,512]{2,1,0:T(8,128)(2,1)}, u32[]{:S(2)}, u32[]{:S(2)}) collective-permute-start(bf16[12,16,512]{2,1,0:T(8,128)(2,1)S(1)} %get-tuple-element.161), channel_id=1, source_target_pairs={{0,2},{1,3},{2,0},{3,1},{4,6},{5,7},{6,4},{7,5},{8,10},{9,11},{10,... | collective-permute-start | bytes 589832 | tf_op jit(solution)/shard_map/ppermute | solution.py:44
  43.6 23.9 %collective-permute-start.6 = (bf16[4,12,16,512]{3,2,1,0:T(8,128)(2,1)S(1)}, bf16[4,12,16,512]{3,2,1,0:T(8,128)(2,1)S(1)}, u32[]{:S(2)}, u32[]{:S(2)}) collective-permute-start(bf16[4,12,16,512]{3,2,1,0:T(8,128)(2,1)S(1)} %constant_dynamic-update-slice_fusion.2), channel_id=1, source_target_pairs={{0,16},{8,24},{16,0},{24,8},{1,17},{9,25},{17,1},{25,9},{2,18},{10... | collective-permute-start | bytes 2359304 | tf_op jit(solution)/shard_map/ppermute | solution.py:44
  44.9 22.7 %collective-permute-start.5 = (bf16[4,12,16,512]{3,2,1,0:T(8,128)(2,1)S(1)}, bf16[4,12,16,512]{3,2,1,0:T(8,128)(2,1)S(1)}, u32[]{:S(2)}, u32[]{:S(2)}) collective-permute-start(bf16[4,12,16,512]{3,2,1,0:T(8,128)(2,1)S(1)} %constant_dynamic-update-slice_fusion), channel_id=1, source_target_pairs={{0,1},{1,0},{2,3},{3,2},{4,5},{5,4},{6,7},{7,6},{8,9},{9,8},{10,11... | collective-permute-start | bytes 2359304 | tf_op jit(solution)/shard_map/ppermute | solution.py:44
  136.7 12.4 %all-to-all-start.2 = ((bf16[8,32,640]{2,1,0:T(8,128)(2,1)}), bf16[8,32,640]{2,1,0:T(8,128)(2,1)S(1)}, u32[]{:S(2)}, u32[]{:S(2)}) async-start(bf16[8,32,640]{2,1,0:T(8,128)(2,1)} %get-tuple-element.194), calls=%async_computation.2 | async-start | bytes 655360 | tf_op jit(solution)/shard_map/all_to_all | solution.py:83
  166.2 25.1 %collective-permute-start.9 = (bf16[1024,512]{1,0:T(8,128)(2,1)}, bf16[1024,512]{1,0:T(8,128)(2,1)}, u32[]{:S(2)}, u32[]{:S(2)}) collective-permute-start(bf16[1024,512]{1,0:T(8,128)(2,1)} %get-tuple-element.213.refs_2_), channel_id=1, source_target_pairs={{0,16},{8,24},{16,0},{24,8},{1,17},{9,25},{17,1},{25,9},{2,18},{10... | collective-permute-start | bytes 3145736 | tf_op jit(solution)/shard_map/ppermute | solution.py:1301
  188.7 11.7 %collective-permute-start.10 = (bf16[16,208,512]{2,1,0:T(8,128)(2,1)S(1)}, bf16[16,208,512]{2,1,0:T(8,128)(2,1)S(1)}, u32[]{:S(2)}, u32[]{:S(2)}) collective-permute-start(bf16[16,208,512]{2,1,0:T(8,128)(2,1)S(1)} %get-tuple-element.217), channel_id=1, source_target_pairs={{0,8},{8,0},{16,24},{24,16},{1,9},{9,1},{17,25},{25,17},{2,10},{10... | collective-permute-start | bytes 10223624 | tf_op jit(solution)/shard_map/ppermute | solution.py:44
  199.5 22.5 %collective-permute-start.13 = (bf16[16,192,512]{2,1,0:T(8,128)(2,1)}, bf16[16,192,512]{2,1,0:T(8,128)(2,1)}, u32[]{:S(2)}, u32[]{:S(2)}) collective-permute-start(bf16[16,192,512]{2,1,0:T(8,128)(2,1)} %get-tuple-element.235), channel_id=1, source_target_pairs={{0,8},{8,0},{16,24},{24,16},{1,9},{9,1},{17,25},{25,17},{2,10},{10... | collective-permute-start | bytes 9437192 | tf_op jit(solution)/shard_map/ppermute | solution.py:44
  202.7 20.9 %collective-permute-start.11 = (bf16[2,2,208,512]{3,2,1,0:T(8,128)(2,1)}, bf16[2,2,208,512]{3,2,1,0:T(8,128)(2,1)}, u32[]{:S(2)}, u32[]{:S(2)}) collective-permute-start(bf16[2,2,208,512]{3,2,1,0:T(8,128)(2,1)} %get-tuple-element.231), channel_id=1, source_target_pairs={{0,16},{8,24},{16,0},{24,8},{1,17},{9,25},{17,1},{25,9},{2,18},{10... | collective-permute-start | bytes 2555912 | tf_op jit(solution)/shard_map/ppermute | solution.py:44
  203.8 26.9 %collective-permute-start.12 = (bf16[2,2,208,512]{3,2,1,0:T(8,128)(2,1)}, bf16[2,2,208,512]{3,2,1,0:T(8,128)(2,1)}, u32[]{:S(2)}, u32[]{:S(2)}) collective-permute-start(bf16[2,2,208,512]{3,2,1,0:T(8,128)(2,1)} %get-tuple-element.233), channel_id=1, source_target_pairs={{0,1},{1,0},{2,3},{3,2},{4,5},{5,4},{6,7},{7,6},{8,9},{9,8},{10,11... | collective-permute-start | bytes 2555912 | tf_op jit(solution)/shard_map/ppermute | solution.py:44
  207.4 35.8 %all-to-all-start.4 = ((bf16[8,32,1792]{2,1,0:T(8,128)(2,1)}), bf16[8,32,1792]{2,1,0:T(8,128)(2,1)}, u32[]{:S(2)}, u32[]{:S(2)}) async-start(bf16[8,32,1792]{2,1,0:T(8,128)(2,1)} %copy-done.6), calls=%async_computation.4 | async-start | bytes 1835008 | tf_op jit(solution)/shard_map/all_to_all | solution.py:83
  236.7 32.4 %collective-permute-start.14 = (bf16[1184,512]{1,0:T(8,128)(2,1)}, bf16[1184,512]{1,0:T(8,128)(2,1)S(1)}, u32[]{:S(2)}, u32[]{:S(2)}) collective-permute-start(bf16[1184,512]{1,0:T(8,128)(2,1)} %get-tuple-element.254), channel_id=1, source_target_pairs={{0,16},{8,24},{16,0},{24,8},{1,17},{9,25},{17,1},{25,9},{2,18},{10... | collective-permute-start | bytes 3637256 | tf_op jit(solution)/shard_map/ppermute | solution.py:44
  237.2 32.0 %collective-permute-start.15 = (bf16[1184,512]{1,0:T(8,128)(2,1)}, bf16[1184,512]{1,0:T(8,128)(2,1)}, u32[]{:S(2)}, u32[]{:S(2)}) collective-permute-start(bf16[1184,512]{1,0:T(8,128)(2,1)} %get-tuple-element.255), channel_id=1, source_target_pairs={{0,1},{1,0},{2,3},{3,2},{4,5},{5,4},{6,7},{7,6},{8,9},{9,8},{10,11... | collective-permute-start | bytes 3637256 | tf_op jit(solution)/shard_map/ppermute | solution.py:44
  245.3 23.9 %collective-permute-start.16 = (bf16[464,512]{1,0:T(8,128)(2,1)S(1)}, bf16[464,512]{1,0:T(8,128)(2,1)S(1)}, u32[]{:S(2)}, u32[]{:S(2)}) collective-permute-start(bf16[464,512]{1,0:T(8,128)(2,1)S(1)} %get-tuple-element.256.refs_4_), channel_id=1, source_target_pairs={{0,8},{8,0},{16,24},{24,16},{1,9},{9,1},{17,25},{25,17},{2,10},{10... | collective-permute-start | bytes 1425416 | tf_op jit(solution)/shard_map/ppermute | solution.py:1301
  247.9 12.0 %collective-permute-start.18 = (bf16[2,400,128]{2,1,0:T(8,128)(2,1)S(1)}, bf16[2,400,128]{2,1,0:T(8,128)(2,1)S(1)}, u32[]{:S(2)}, u32[]{:S(2)}) collective-permute-start(bf16[2,400,128]{2,1,0:T(8,128)(2,1)S(1)} %get-tuple-element.259), channel_id=1, source_target_pairs={{0,4},{1,5},{2,6},{3,7},{4,0},{5,1},{6,2},{7,3},{8,12},{9,13},{10,... | collective-permute-start | bytes 614408 | tf_op jit(solution)/shard_map/ppermute | solution.py:44
  256.7 12.5 %collective-permute-start.19 = (bf16[2,400,128]{2,1,0:T(8,128)(2,1)S(1)}, bf16[2,400,128]{2,1,0:T(8,128)(2,1)S(1)}, u32[]{:S(2)}, u32[]{:S(2)}) collective-permute-start(bf16[2,400,128]{2,1,0:T(8,128)(2,1)S(1)} %get-tuple-element.260), channel_id=1, source_target_pairs={{0,6},{1,7},{2,4},{3,5},{4,2},{5,3},{6,0},{7,1},{8,14},{9,15},{10,... | collective-permute-start | bytes 614408 | tf_op jit(solution)/shard_map/ppermute | solution.py:44
  271.4 21.5 %collective-permute-start.23 = (bf16[848,512]{1,0:T(8,128)(2,1)S(1)}, bf16[848,512]{1,0:T(8,128)(2,1)S(1)}, u32[]{:S(2)}, u32[]{:S(2)}) collective-permute-start(bf16[848,512]{1,0:T(8,128)(2,1)S(1)} %get-tuple-element.266.refs_5_), channel_id=1, source_target_pairs={{0,16},{8,24},{16,0},{24,8},{1,17},{9,25},{17,1},{25,9},{2,18},{10... | collective-permute-start | bytes 2605064 | tf_op jit(solution)/shard_map/ppermute | solution.py:44
  272.5 20.4 %collective-permute-start.24 = (bf16[496,512]{1,0:T(8,128)(2,1)S(1)}, bf16[496,512]{1,0:T(8,128)(2,1)S(1)}, u32[]{:S(2)}, u32[]{:S(2)}) collective-permute-start(bf16[496,512]{1,0:T(8,128)(2,1)S(1)} %get-tuple-element.267), channel_id=1, source_target_pairs={{0,1},{1,0},{2,3},{3,2},{4,5},{5,4},{6,7},{7,6},{8,9},{9,8},{10,11... | collective-permute-start | bytes 1523720 | tf_op jit(solution)/shard_map/ppermute | solution.py:44
  274.6 18.4 %collective-permute-start.22 = (bf16[208,512]{1,0:T(8,128)(2,1)S(1)}, bf16[208,512]{1,0:T(8,128)(2,1)S(1)}, u32[]{:S(2)}, u32[]{:S(2)}) collective-permute-start(bf16[208,512]{1,0:T(8,128)(2,1)S(1)} %get-tuple-element.265), channel_id=1, source_target_pairs={{0,6},{1,7},{2,4},{3,5},{4,2},{5,3},{6,0},{7,1},{8,14},{9,15},{10,... | collective-permute-start | bytes 638984 | tf_op jit(solution)/shard_map/ppermute | solution.py:44
  294.5 19.7 %collective-permute-start.28 = (bf16[320,512]{1,0:T(8,128)(2,1)S(1)}, bf16[320,512]{1,0:T(8,128)(2,1)S(1)}, u32[]{:S(2)}, u32[]{:S(2)}) collective-permute-start(bf16[320,512]{1,0:T(8,128)(2,1)S(1)} %get-tuple-element.273.refs_5_), channel_id=1, source_target_pairs={{0,16},{8,24},{16,0},{24,8},{1,17},{9,25},{17,1},{25,9},{2,18},{10... | collective-permute-start | bytes 983048 | tf_op jit(solution)/shard_map/ppermute | solution.py:44
  296.6 17.7 %collective-permute-start.27 = (bf16[192,512]{1,0:T(8,128)(2,1)S(1)}, bf16[192,512]{1,0:T(8,128)(2,1)S(1)}, u32[]{:S(2)}, u32[]{:S(2)}) collective-permute-start(bf16[192,512]{1,0:T(8,128)(2,1)S(1)} %get-tuple-element.272), channel_id=1, source_target_pairs={{0,6},{1,7},{2,4},{3,5},{4,2},{5,3},{6,0},{7,1},{8,14},{9,15},{10,... | collective-permute-start | bytes 589832 | tf_op jit(solution)/shard_map/ppermute | solution.py:44
  315.4 11.5 %collective-permute-start.29 = (bf16[2,320,512]{2,1,0:T(8,128)(2,1)S(1)}, bf16[2,320,512]{2,1,0:T(8,128)(2,1)S(1)}, u32[]{:S(2)}, u32[]{:S(2)}) collective-permute-start(bf16[2,320,512]{2,1,0:T(8,128)(2,1)S(1)} %get-tuple-element.276.refs_2_), channel_id=1, source_target_pairs={{0,8},{8,0},{16,24},{24,16},{1,9},{9,1},{17,25},{25,17},{2,10},{10... | collective-permute-start | bytes 1966088 | tf_op jit(solution)/shard_map/ppermute | solution.py:44
  (86 other events, 742.6 us)
Sparse Core Ops, SparseCore 0:
  16.3 79.5 all-gather.3

commit v7 on v6

--- a/solution.py
+++ b/solution.py
@@ -364,16 +364,17 @@
         message_ref[place, :, channels:] = tile
 
 
-def attend_back(places_ref, arrived_ref, scores_ref, keys_ref, values_ref, part_ref, score_grad_ref, weights_ref):
-    channels = keys_ref.shape[1]
+def attend_back(places_ref, arrived_ref, scores_ref, keys_ref, values_ref, queries_ref, part_ref, sums_ref):
+    keys_here, channels = keys_ref.shape
     top = from_tile(arrived_ref[:, channels:], 0)
     centre = from_tile(arrived_ref[:, channels:], 1)
+    numer_grad = arrived_ref[:, :channels]
     weights = jnp.exp(scores_ref[...] - top)
-    weights_ref[...] = low(weights)
-    prob_grad = dot_nt(arrived_ref[:, :channels], values_ref[...])
+    prob_grad = dot_nt(numer_grad, values_ref[...])
     score_grad = low(weights * (prob_grad - centre) * (channels ** (-0.5)))
-    score_grad_ref[...] = score_grad
     part_ref[...] = low(product(score_grad, keys_ref[...]))
+    sums_ref[:keys_here] = low(dot_tn(score_grad, queries_ref[...]))
+    sums_ref[keys_here:] = low(dot_tn(low(weights), numer_grad))
 
 
 def half_of(place_ref, bit):
@@ -888,12 +889,6 @@
         if spare:
             pieces.append(jnp.zeros((reduced.shape[0], spare), BF16))
         message_ref[place] = jnp.concatenate(pieces, axis=1)
-
-
-def key_value_parts(places_ref, score_grad_ref, queries_ref, weights_ref, arrived_ref, out_ref):
-    keys_here = score_grad_ref.shape[1]
-    out_ref[:keys_here] = low(dot_tn(score_grad_ref[...], queries_ref[...]))
-    out_ref[keys_here:] = low(dot_tn(weights_ref[...], arrived_ref[:, : queries_ref.shape[1]]))
 
 
 def region_sums(widths, places_ref, group_ref, branch_grad_ref, logit_grad_ref, out_ref):
@@ -1277,26 +1272,15 @@
         raw_out=(0,),
         limit=52,
     )
-    group_shape = shape_of((group_rows, channels), BF16)
-    weight_shape = shape_of((group_rows, keys_here), BF16)
-    places, query_part, score_grad, weights_low = run_kernel(
+    places, query_part, key_value = run_kernel(
         attend_back,
         places,
-        [arrived, scores, keys, values],
-        [group_shape, weight_shape, weight_shape],
+        [arrived, scores, keys, values, queries],
+        [shape_of((group_rows, channels), BF16), shape_of((2 * keys_here, channels), BF16)],
         "attend_back",
         2,
     )
     query_parts = to_owners(query_part.reshape(bank_count, own_count, channels))
-    places, key_value = run_kernel(
-        key_value_parts,
-        places,
-        [score_grad, queries, weights_low, arrived],
-        [shape_of((2 * keys_here, channels), BF16)],
-        "key_value_parts",
-        3,
-    )
-
     def dp_swap(value, step):
         return lax.ppermute(value, "dp", [(i, i ^ step) for i in range(dp_count)])
 

time: 338 us -> 338 us (level)
    unnamed x160 -> x164, local copies, waits for them, and re-layouts: 27.4 us -> 29.2 us
    pallas_call x23 -> x22, Pallas kernels: 78.3 us -> 77.2 us  [run_kernel(): pl.pallas_call(wrapped, out_shape=[shape_of(places.shape, jnp.int32)] + l...]
where the time goes in v7:
time: 338 us; the launch traced here: 337 us
  waiting for transfers between devices  112 us (33%)
  Pallas kernels  98.5 us (29%)
  starting transfers between devices  56.5 us (17%)
  local copies, waits for them, and re-layouts  30.8 us (9%)
  blocking collectives  22.7 us (7%)
  between operations  14.9 us (4%)
    ppermute x27, waiting for transfers between devices, swap(): return lax.ppermute(value, self.name, pairs)  96.5 us
    pallas_call x22, Pallas kernels, run_kernel(): pl.pallas_call(wrapped, out_shape=[shape_of(places.shape, jnp.int32)] + l...  77.2 us
    ppermute x27, starting transfers between devices, swap(): return lax.ppermute(value, self.name, pairs)  30.9 us
    unnamed x164, local copies, waits for them, and re-layouts  29.2 us
    all_to_all x4, starting transfers between devices, to_owners(): lax.all_to_all(value, 'bank', split_axis=0, concat_axis=0, tiled=True)  18.1 us
    all_to_all x1, blocking collectives, to_owners(): lax.all_to_all(value, 'bank', split_axis=0, concat_axis=0, tiled=True)  14 us
    pallas_call x1, Pallas kernels, run_later_convs(): pl.pallas_call(later_convs, out_shape=[jax.ShapeDtypeStruct((sites, chann...  13.1 us
    all_gather x1, blocking collectives, body(): done_a = lax.all_gather(part_a, 'dp', axis=0, tiled=False)  8.7 us
  transfers between devices with their start and end apart: 35, of which 21 were waited for; matrix products, arithmetic and copies ran while one was open for 2% of the time, Pallas kernels for 21%

profile of v7, /device:TPU:9, one launch (start us, length us, event | category | flops | bytes accessed | tf_op | source)
XLA Modules:
  0.0 337.0 jit_solution(15947819919937584135)
XLA Ops:
  27.1 4.5 %collective-permute-done.1 = bf16[12,16,512]{2,1,0:T(8,128)(2,1)} collective-permute-done((bf16[12,16,512]{2,1,0:T(8,128)(2,1)S(1)}, bf16[12,16,512]{2,1,0:T(8,128)(2,1)}, u32[]{:S(2)}, u32[]{:S(2)}) %collective-permute-start.1) | collective-permute-done | bytes 196640 | tf_op jit(solution)/shard_map/ppermute | solution.py:44
  47.0 20.6 %collective-permute-done.6 = bf16[4,12,16,512]{3,2,1,0:T(8,128)(2,1)S(1)} collective-permute-done((bf16[4,12,16,512]{3,2,1,0:T(8,128)(2,1)S(1)}, bf16[4,12,16,512]{3,2,1,0:T(8,128)(2,1)S(1)}, u32[]{:S(2)}, u32[]{:S(2)}) %collective-permute-start.6) | collective-permute-done | bytes 786464 | tf_op jit(solution)/shard_map/ppermute | solution.py:44
  70.1 7.1 %collective-permute-done.7.refs_1_ = bf16[16,12,16,512]{3,2,1,0:T(8,128)(2,1)S(1)} collective-permute-done((bf16[16,12,16,512]{3,2,1,0:T(8,128)(2,1)S(1)}, bf16[16,12,16,512]{3,2,1,0:T(8,128)(2,1)S(1)}, u32[]{:S(2)}, u32[]{:S(2)}) %collective-permute-start.7) | collective-permute-done | bytes 3145760 | tf_op jit(solution)/shard_map/ppermute | solution.py:44
  78.9 8.3 %first_conv.1 = (f32[512,512]{1,0:T(8,128)S(1)}, bf16[512,512]{1,0:T(8,128)(2,1)S(1)}, bf16[384,16,512]{2,1,0:T(8,128)(2,1)}) custom-call(s32[10]{0:T(128)S(1)} %get-tuple-element.175.places_ref.refs_0_, bf16[512,2048]{1,0:T(8,128)(2,1)} %refs_4_.5, bf16[16,12,16,512]{3,2,1,0:T(8,128)(2,1)} %copy-done.71, bf16[16,12,16,512]{3,2,1,0:T(8,128)(2,1)} %copy-done.76, ...), custom_call_target="tpu_custom_call" | custom-call | flops 89999998976 | bytes 90000000 | tf_op jit(solution)/shard_map/first_conv/pallas_call | solution.py:1047
  88.1 7.8 %all-gather.4.cloned.1.call-done = bf16[416,16,512]{2,1,0:T(8,128)(2,1)} async-done(((bf16[13,16,512]{2,1,0:T(8,128)(2,1)}), bf16[416,16,512]{2,1,0:T(8,128)(2,1)}) %all-gather.4.cloned.1.call-update) | async-done | bytes 6815760 | tf_op jit(solution)/shard_map/all_gather | solution.py:1176
  95.9 13.1 %later_convs.1 = (f32[512,512]{1,0:T(8,128)}, bf16[512,512]{1,0:T(8,128)(2,1)S(1)}, f32[512,2048]{1,0:T(8,128)}, bf16[32,2048]{1,0:T(8,128)(2,1)S(1)}, f32[32,51...) custom-call(bf16[512,512]{1,0:T(8,128)(2,1)S(1)} %get-tuple-element.178.act_a_ref.refs_9_, bf16[512,2048]{1,0:T(8,128)(2,1)} %refs_4_.5, ...), custom_call_target="tpu_custom_call" | custom-call | flops 224999997440 | bytes 225000000 | tf_op jit(solution)/shard_map/later_convs/pallas_call | solution.py:1076
  109.8 4.0 %all-to-all-start = ((bf16[8,32,512]{2,1,0:T(8,128)(2,1)}), bf16[8,32,512]{2,1,0:T(8,128)(2,1)S(1)}, u32[]{:S(2)}, u32[]{:S(2)}) async-start(bf16[8,32,512]{2,1,0:T(8,128)(2,1)} %get-tuple-element.181), calls=%async_computation | async-start | bytes 524288 | tf_op jit(solution)/shard_map/all_to_all | solution.py:83
  114.0 6.4 %all-to-all-done = bf16[8,32,512]{2,1,0:T(8,128)(2,1)S(1)} async-done(((bf16[8,32,512]{2,1,0:T(8,128)(2,1)}), bf16[8,32,512]{2,1,0:T(8,128)(2,1)S(1)}, u32[]{:S(2)}, u32[]{:S(2)}) %all-to-all-start) | async-done | bytes 262176 | tf_op jit(solution)/shard_map/all_to_all | solution.py:83
  121.7 14.0 %all_to_all.25.refs_1_ = bf16[8,32,640]{2,1,0:T(8,128)(2,1)S(1)} all-to-all(bf16[8,32,640]{2,1,0:T(8,128)(2,1)S(1)} %bitcast.44), channel_id=1, replica_groups=mesh['dp'=4,'bank'=8] {'bank'}, dimensions={0} | all-to-all | bytes 655360 | tf_op jit(solution)/shard_map/all_to_all | solution.py:83
  137.5 5.6 %all-to-all-start.2 = ((bf16[8,32,640]{2,1,0:T(8,128)(2,1)}), bf16[8,32,640]{2,1,0:T(8,128)(2,1)S(1)}, u32[]{:S(2)}, u32[]{:S(2)}) async-start(bf16[8,32,640]{2,1,0:T(8,128)(2,1)} %get-tuple-element.191), calls=%async_computation.2 | async-start | bytes 655360 | tf_op jit(solution)/shard_map/all_to_all | solution.py:83
  143.1 6.4 %slopes_outer.1 = (s32[10]{0:T(128)S(1)}, bf16[512,2048]{1,0:T(8,128)(2,1)}) custom-call(s32[10]{0:T(128)S(1)} %get-tuple-element.188.refs_0_, f32[1,2048]{1,0:T(1,128)S(1)} %bitcast.51, f32[1,2048]{1,0:T(1,128)S(1)} %bitcast.49, f32[512,2048]{1,0:T(8,128)} %get-tuple-element.189.refs_3_.refs_5_, bf16[512,2048]{1,0:T(8,128)(2,1)} %refs_4_.5), custom_call_target="tpu_custom_call" | custom-call | flops 1500000000 | bytes 1500000 | tf_op jit(solution)/shard_map/slopes_outer/pallas_call | solution.py:1029
  157.6 4.0 %all-to-all-start.3 = ((bf16[8,32,512]{2,1,0:T(8,128)(2,1)}), bf16[8,32,512]{2,1,0:T(8,128)(2,1)S(1)}, u32[]{:S(2)}, u32[]{:S(2)}) async-start(bf16[8,32,512]{2,1,0:T(8,128)(2,1)} %bitcast.27), calls=%async_computation.3 | async-start | bytes 524288 | tf_op jit(solution)/shard_map/all_to_all | solution.py:83
  171.9 17.5 %later_back.1 = (s32[10]{0:T(128)S(1)}, bf16[16,208,512]{2,1,0:T(8,128)(2,1)S(1)}, bf16[16,208,512]{2,1,0:T(8,128)(2,1)}, bf16[512,2048]{1,0:T(8,128)(2,1)S(1)},...) custom-call(s32[10]{0:T(128)S(1)} %get-tuple-element.198.refs_0_, ...), custom_call_target="tpu_custom_call" | custom-call | flops 420000006144 | bytes 420000000 | tf_op jit(solution)/shard_map/later_back/pallas_call | solution.py:1029
  191.9 8.2 %first_back.1 = (s32[10]{0:T(128)S(1)}, bf16[16,192,512]{2,1,0:T(8,128)(2,1)}, bf16[16,192,512]{2,1,0:T(8,128)(2,1)S(1)}, bf16[1024,512]{1,0:T(8,128)(2,1)S(1)}) custom-call(s32[10]{0:T(128)S(1)} %get-tuple-element.205.refs_0_, bf16[512,512]{1,0:T(8,128)(2,1)S(1)} %get-tuple-element.206.refs_1_, bf16[1024,512]{1,0:T(8,128)(2,1)} %get-tuple-element.207.refs_2_, ...), custom_call_target="tpu_custom_call" | custom-call | flops 89999998976 | bytes 90000000 | tf_op jit(solution)/shard_map/first_back/pallas_call | solution.py:1029
  208.0 4.5 %all-to-all-start.4 = ((bf16[8,32,1792]{2,1,0:T(8,128)(2,1)}), bf16[8,32,1792]{2,1,0:T(8,128)(2,1)}, u32[]{:S(2)}, u32[]{:S(2)}) async-start(bf16[8,32,1792]{2,1,0:T(8,128)(2,1)} %copy-done.6), calls=%async_computation.4 | async-start | bytes 1835008 | tf_op jit(solution)/shard_map/all_to_all | solution.py:83
  216.4 6.3 %map_back.1 = (s32[10]{0:T(128)S(1)}, bf16[512,2048]{1,0:T(8,128)(2,1)}) custom-call(s32[10]{0:T(128)S(1)} %get-tuple-element.219.refs_0_, bf16[512,512]{1,0:T(8,128)(2,1)S(1)} %copy-done.16, bf16[384,16,512]{2,1,0:T(8,128)(2,1)S(1)} %copy-done, bf16[512,2048]{1,0:T(8,128)(2,1)S(1)} %get-tuple-element.221.refs_3_), custom_call_target="tpu_custom_call" | custom-call | flops 1500000000 | bytes 1500000 | tf_op jit(solution)/shard_map/map_back/pallas_call | solution.py:1029
  224.3 7.0 %collective-permute-done.12.refs_4_ = bf16[2,2,208,512]{3,2,1,0:T(8,128)(2,1)} collective-permute-done((bf16[2,2,208,512]{3,2,1,0:T(8,128)(2,1)}, bf16[2,2,208,512]{3,2,1,0:T(8,128)(2,1)}, u32[]{:S(2)}, u32[]{:S(2)}) %collective-permute-start.12) | collective-permute-done | bytes 852000 | tf_op jit(solution)/shard_map/ppermute | solution.py:44
  231.3 4.6 %round_two.1 = (s32[10]{0:T(128)S(1)}, bf16[2368,512]{1,0:T(8,128)(2,1)S(1)}, bf16[1184,512]{1,0:T(8,128)(2,1)}, bf16[1184,512]{1,0:T(8,128)(2,1)}) custom-call(s32[10]{0:T(128)S(1)} %get-tuple-element.223.refs_0_, bf16[2,2,208,512]{3,2,1,0:T(8,128)(2,1)S(1)} %copy-done.57, bf16[2,2,208,512]{3,2,1,0:T(8,128)(2,1)} %collective-permute-done.11.refs_2_, ...), custom_call_target="tpu_custom_call" | custom-call | flops 74999996416 | bytes 75000000 | tf_op jit(solution)/shard_map/round_two/pallas_call | solution.py:1029
  250.9 6.4 %collective-permute-done.17.refs_7_ = bf16[2,400,128]{2,1,0:T(8,128)(2,1)S(1)} collective-permute-done((bf16[2,400,128]{2,1,0:T(8,128)(2,1)S(1)}, bf16[2,400,128]{2,1,0:T(8,128)(2,1)S(1)}, u32[]{:S(2)}, u32[]{:S(2)}) %collective-permute-start.17) | collective-permute-done | bytes 204832 | tf_op jit(solution)/shard_map/ppermute | solution.py:44
  260.5 9.3 %collective-permute-done.19.refs_9_ = bf16[2,400,128]{2,1,0:T(8,128)(2,1)S(1)} collective-permute-done((bf16[2,400,128]{2,1,0:T(8,128)(2,1)S(1)}, bf16[2,400,128]{2,1,0:T(8,128)(2,1)S(1)}, u32[]{:S(2)}, u32[]{:S(2)}) %collective-permute-start.19) | collective-permute-done | bytes 204832 | tf_op jit(solution)/shard_map/ppermute | solution.py:44
  278.8 4.4 %collective-permute-done.21.refs_3_ = bf16[208,512]{1,0:T(8,128)(2,1)S(1)} collective-permute-done((bf16[208,512]{1,0:T(8,128)(2,1)S(1)}, bf16[208,512]{1,0:T(8,128)(2,1)S(1)}, u32[]{:S(2)}, u32[]{:S(2)}) %collective-permute-start.21) | collective-permute-done | bytes 213024 | tf_op jit(solution)/shard_map/ppermute | solution.py:44
  283.3 10.3 %collective-permute-done.22.refs_4_ = bf16[208,512]{1,0:T(8,128)(2,1)S(1)} collective-permute-done((bf16[208,512]{1,0:T(8,128)(2,1)S(1)}, bf16[208,512]{1,0:T(8,128)(2,1)S(1)}, u32[]{:S(2)}, u32[]{:S(2)}) %collective-permute-start.22) | collective-permute-done | bytes 213024 | tf_op jit(solution)/shard_map/ppermute | solution.py:44
  303.2 11.7 %collective-permute-done.27.refs_4_ = bf16[192,512]{1,0:T(8,128)(2,1)S(1)} collective-permute-done((bf16[192,512]{1,0:T(8,128)(2,1)S(1)}, bf16[192,512]{1,0:T(8,128)(2,1)S(1)}, u32[]{:S(2)}, u32[]{:S(2)}) %collective-permute-start.27) | collective-permute-done | bytes 196640 | tf_op jit(solution)/shard_map/ppermute | solution.py:44
  318.8 8.7 %all-gather.1 = bf16[768,512]{1,0:T(8,128)(2,1)S(1)} all-gather(bf16[192,512]{1,0:T(8,128)(2,1)S(1)} %get-tuple-element.269), channel_id=3, replica_groups=mesh['dp'=4,'bank'=8] {'dp'}, dimensions={0}, use_global_device_ids=true | all-gather | bytes 983040 | tf_op jit(solution)/shard_map/all_gather | solution.py:1500
  (247 shorter events, 121.4 us)
Async XLA Ops:
  7.2 88.7 %all-gather.4.cloned.1.call-start = ((), (), s32[]{:S(2)}) async-start(), calls=%async_computation.5 | async-start | bytes 7028736 | tf_op jit(solution)/shard_map/all_gather | solution.py:1176
  12.6 14.6 %collective-permute-start.2 = (bf16[12,16,512]{2,1,0:T(8,128)(2,1)S(1)}, bf16[12,16,512]{2,1,0:T(8,128)(2,1)}, u32[]{:S(2)}, u32[]{:S(2)}) collective-permute-start(bf16[12,16,512]{2,1,0:T(8,128)(2,1)S(1)} %get-tuple-element.158), channel_id=1, source_target_pairs={{0,6},{1,7},{2,4},{3,5},{4,2},{5,3},{6,0},{7,1},{8,14},{9,15},{10,... | collective-permute-start | bytes 589832 | tf_op jit(solution)/shard_map/ppermute | solution.py:44
  14.0 17.7 %collective-permute-start.1 = (bf16[12,16,512]{2,1,0:T(8,128)(2,1)S(1)}, bf16[12,16,512]{2,1,0:T(8,128)(2,1)}, u32[]{:S(2)}, u32[]{:S(2)}) collective-permute-start(bf16[12,16,512]{2,1,0:T(8,128)(2,1)S(1)} %get-tuple-element.158), channel_id=1, source_target_pairs={{0,4},{1,5},{2,6},{3,7},{4,0},{5,1},{6,2},{7,3},{8,12},{9,13},{10,... | collective-permute-start | bytes 589832 | tf_op jit(solution)/shard_map/ppermute | solution.py:44
  15.0 16.6 %collective-permute-start = (bf16[12,16,512]{2,1,0:T(8,128)(2,1)S(1)}, bf16[12,16,512]{2,1,0:T(8,128)(2,1)}, u32[]{:S(2)}, u32[]{:S(2)}) collective-permute-start(bf16[12,16,512]{2,1,0:T(8,128)(2,1)S(1)} %get-tuple-element.158), channel_id=1, source_target_pairs={{0,2},{1,3},{2,0},{3,1},{4,6},{5,7},{6,4},{7,5},{8,10},{9,11},{10,... | collective-permute-start | bytes 589832 | tf_op jit(solution)/shard_map/ppermute | solution.py:44
  43.6 23.9 %collective-permute-start.6 = (bf16[4,12,16,512]{3,2,1,0:T(8,128)(2,1)S(1)}, bf16[4,12,16,512]{3,2,1,0:T(8,128)(2,1)S(1)}, u32[]{:S(2)}, u32[]{:S(2)}) collective-permute-start(bf16[4,12,16,512]{3,2,1,0:T(8,128)(2,1)S(1)} %constant_dynamic-update-slice_fusion.2), channel_id=1, source_target_pairs={{0,16},{8,24},{16,0},{24,8},{1,17},{9,25},{17,1},{25,9},{2,18},{10... | collective-permute-start | bytes 2359304 | tf_op jit(solution)/shard_map/ppermute | solution.py:44
  44.9 22.7 %collective-permute-start.5 = (bf16[4,12,16,512]{3,2,1,0:T(8,128)(2,1)S(1)}, bf16[4,12,16,512]{3,2,1,0:T(8,128)(2,1)S(1)}, u32[]{:S(2)}, u32[]{:S(2)}) collective-permute-start(bf16[4,12,16,512]{3,2,1,0:T(8,128)(2,1)S(1)} %constant_dynamic-update-slice_fusion), channel_id=1, source_target_pairs={{0,1},{1,0},{2,3},{3,2},{4,5},{5,4},{6,7},{7,6},{8,9},{9,8},{10,11... | collective-permute-start | bytes 2359304 | tf_op jit(solution)/shard_map/ppermute | solution.py:44
  137.5 12.4 %all-to-all-start.2 = ((bf16[8,32,640]{2,1,0:T(8,128)(2,1)}), bf16[8,32,640]{2,1,0:T(8,128)(2,1)S(1)}, u32[]{:S(2)}, u32[]{:S(2)}) async-start(bf16[8,32,640]{2,1,0:T(8,128)(2,1)} %get-tuple-element.191), calls=%async_computation.2 | async-start | bytes 655360 | tf_op jit(solution)/shard_map/all_to_all | solution.py:83
  166.8 25.1 %collective-permute-start.9 = (bf16[1024,512]{1,0:T(8,128)(2,1)}, bf16[1024,512]{1,0:T(8,128)(2,1)}, u32[]{:S(2)}, u32[]{:S(2)}) collective-permute-start(bf16[1024,512]{1,0:T(8,128)(2,1)} %get-tuple-element.207.refs_2_), channel_id=1, source_target_pairs={{0,16},{8,24},{16,0},{24,8},{1,17},{9,25},{17,1},{25,9},{2,18},{10... | collective-permute-start | bytes 3145736 | tf_op jit(solution)/shard_map/ppermute | solution.py:1285
  189.4 11.7 %collective-permute-start.10 = (bf16[16,208,512]{2,1,0:T(8,128)(2,1)S(1)}, bf16[16,208,512]{2,1,0:T(8,128)(2,1)S(1)}, u32[]{:S(2)}, u32[]{:S(2)}) collective-permute-start(bf16[16,208,512]{2,1,0:T(8,128)(2,1)S(1)} %get-tuple-element.211), channel_id=1, source_target_pairs={{0,8},{8,0},{16,24},{24,16},{1,9},{9,1},{17,25},{25,17},{2,10},{10... | collective-permute-start | bytes 10223624 | tf_op jit(solution)/shard_map/ppermute | solution.py:44
  200.2 22.5 %collective-permute-start.13 = (bf16[16,192,512]{2,1,0:T(8,128)(2,1)}, bf16[16,192,512]{2,1,0:T(8,128)(2,1)}, u32[]{:S(2)}, u32[]{:S(2)}) collective-permute-start(bf16[16,192,512]{2,1,0:T(8,128)(2,1)} %get-tuple-element.229), channel_id=1, source_target_pairs={{0,8},{8,0},{16,24},{24,16},{1,9},{9,1},{17,25},{25,17},{2,10},{10... | collective-permute-start | bytes 9437192 | tf_op jit(solution)/shard_map/ppermute | solution.py:44
  203.3 20.9 %collective-permute-start.11 = (bf16[2,2,208,512]{3,2,1,0:T(8,128)(2,1)}, bf16[2,2,208,512]{3,2,1,0:T(8,128)(2,1)}, u32[]{:S(2)}, u32[]{:S(2)}) collective-permute-start(bf16[2,2,208,512]{3,2,1,0:T(8,128)(2,1)} %get-tuple-element.225), channel_id=1, source_target_pairs={{0,16},{8,24},{16,0},{24,8},{1,17},{9,25},{17,1},{25,9},{2,18},{10... | collective-permute-start | bytes 2555912 | tf_op jit(solution)/shard_map/ppermute | solution.py:44
  204.4 26.9 %collective-permute-start.12 = (bf16[2,2,208,512]{3,2,1,0:T(8,128)(2,1)}, bf16[2,2,208,512]{3,2,1,0:T(8,128)(2,1)}, u32[]{:S(2)}, u32[]{:S(2)}) collective-permute-start(bf16[2,2,208,512]{3,2,1,0:T(8,128)(2,1)} %get-tuple-element.227), channel_id=1, source_target_pairs={{0,1},{1,0},{2,3},{3,2},{4,5},{5,4},{6,7},{7,6},{8,9},{9,8},{10,11... | collective-permute-start | bytes 2555912 | tf_op jit(solution)/shard_map/ppermute | solution.py:44
  208.0 35.8 %all-to-all-start.4 = ((bf16[8,32,1792]{2,1,0:T(8,128)(2,1)}), bf16[8,32,1792]{2,1,0:T(8,128)(2,1)}, u32[]{:S(2)}, u32[]{:S(2)}) async-start(bf16[8,32,1792]{2,1,0:T(8,128)(2,1)} %copy-done.6), calls=%async_computation.4 | async-start | bytes 1835008 | tf_op jit(solution)/shard_map/all_to_all | solution.py:83
  237.4 32.5 %collective-permute-start.14 = (bf16[1184,512]{1,0:T(8,128)(2,1)}, bf16[1184,512]{1,0:T(8,128)(2,1)S(1)}, u32[]{:S(2)}, u32[]{:S(2)}) collective-permute-start(bf16[1184,512]{1,0:T(8,128)(2,1)} %get-tuple-element.248), channel_id=1, source_target_pairs={{0,16},{8,24},{16,0},{24,8},{1,17},{9,25},{17,1},{25,9},{2,18},{10... | collective-permute-start | bytes 3637256 | tf_op jit(solution)/shard_map/ppermute | solution.py:44
  237.8 32.0 %collective-permute-start.15 = (bf16[1184,512]{1,0:T(8,128)(2,1)}, bf16[1184,512]{1,0:T(8,128)(2,1)}, u32[]{:S(2)}, u32[]{:S(2)}) collective-permute-start(bf16[1184,512]{1,0:T(8,128)(2,1)} %get-tuple-element.249), channel_id=1, source_target_pairs={{0,1},{1,0},{2,3},{3,2},{4,5},{5,4},{6,7},{7,6},{8,9},{9,8},{10,11... | collective-permute-start | bytes 3637256 | tf_op jit(solution)/shard_map/ppermute | solution.py:44
  246.0 23.8 %collective-permute-start.16 = (bf16[464,512]{1,0:T(8,128)(2,1)S(1)}, bf16[464,512]{1,0:T(8,128)(2,1)S(1)}, u32[]{:S(2)}, u32[]{:S(2)}) collective-permute-start(bf16[464,512]{1,0:T(8,128)(2,1)S(1)} %get-tuple-element.250.refs_4_), channel_id=1, source_target_pairs={{0,8},{8,0},{16,24},{24,16},{1,9},{9,1},{17,25},{25,17},{2,10},{10... | collective-permute-start | bytes 1425416 | tf_op jit(solution)/shard_map/ppermute | solution.py:1285
  248.5 12.0 %collective-permute-start.18 = (bf16[2,400,128]{2,1,0:T(8,128)(2,1)S(1)}, bf16[2,400,128]{2,1,0:T(8,128)(2,1)S(1)}, u32[]{:S(2)}, u32[]{:S(2)}) collective-permute-start(bf16[2,400,128]{2,1,0:T(8,128)(2,1)S(1)} %get-tuple-element.253), channel_id=1, source_target_pairs={{0,4},{1,5},{2,6},{3,7},{4,0},{5,1},{6,2},{7,3},{8,12},{9,13},{10,... | collective-permute-start | bytes 614408 | tf_op jit(solution)/shard_map/ppermute | solution.py:44
  257.3 12.5 %collective-permute-start.19 = (bf16[2,400,128]{2,1,0:T(8,128)(2,1)S(1)}, bf16[2,400,128]{2,1,0:T(8,128)(2,1)S(1)}, u32[]{:S(2)}, u32[]{:S(2)}) collective-permute-start(bf16[2,400,128]{2,1,0:T(8,128)(2,1)S(1)} %get-tuple-element.254), channel_id=1, source_target_pairs={{0,6},{1,7},{2,4},{3,5},{4,2},{5,3},{6,0},{7,1},{8,14},{9,15},{10,... | collective-permute-start | bytes 614408 | tf_op jit(solution)/shard_map/ppermute | solution.py:44
  272.1 21.5 %collective-permute-start.23 = (bf16[848,512]{1,0:T(8,128)(2,1)S(1)}, bf16[848,512]{1,0:T(8,128)(2,1)S(1)}, u32[]{:S(2)}, u32[]{:S(2)}) collective-permute-start(bf16[848,512]{1,0:T(8,128)(2,1)S(1)} %get-tuple-element.260.refs_5_), channel_id=1, source_target_pairs={{0,16},{8,24},{16,0},{24,8},{1,17},{9,25},{17,1},{25,9},{2,18},{10... | collective-permute-start | bytes 2605064 | tf_op jit(solution)/shard_map/ppermute | solution.py:44
  273.1 20.4 %collective-permute-start.24 = (bf16[496,512]{1,0:T(8,128)(2,1)S(1)}, bf16[496,512]{1,0:T(8,128)(2,1)S(1)}, u32[]{:S(2)}, u32[]{:S(2)}) collective-permute-start(bf16[496,512]{1,0:T(8,128)(2,1)S(1)} %get-tuple-element.261), channel_id=1, source_target_pairs={{0,1},{1,0},{2,3},{3,2},{4,5},{5,4},{6,7},{7,6},{8,9},{9,8},{10,11... | collective-permute-start | bytes 1523720 | tf_op jit(solution)/shard_map/ppermute | solution.py:44
  275.2 18.4 %collective-permute-start.22 = (bf16[208,512]{1,0:T(8,128)(2,1)S(1)}, bf16[208,512]{1,0:T(8,128)(2,1)S(1)}, u32[]{:S(2)}, u32[]{:S(2)}) collective-permute-start(bf16[208,512]{1,0:T(8,128)(2,1)S(1)} %get-tuple-element.259), channel_id=1, source_target_pairs={{0,6},{1,7},{2,4},{3,5},{4,2},{5,3},{6,0},{7,1},{8,14},{9,15},{10,... | collective-permute-start | bytes 638984 | tf_op jit(solution)/shard_map/ppermute | solution.py:44
  295.1 19.7 %collective-permute-start.28 = (bf16[320,512]{1,0:T(8,128)(2,1)S(1)}, bf16[320,512]{1,0:T(8,128)(2,1)S(1)}, u32[]{:S(2)}, u32[]{:S(2)}) collective-permute-start(bf16[320,512]{1,0:T(8,128)(2,1)S(1)} %get-tuple-element.267.refs_5_), channel_id=1, source_target_pairs={{0,16},{8,24},{16,0},{24,8},{1,17},{9,25},{17,1},{25,9},{2,18},{10... | collective-permute-start | bytes 983048 | tf_op jit(solution)/shard_map/ppermute | solution.py:44
  297.2 17.6 %collective-permute-start.27 = (bf16[192,512]{1,0:T(8,128)(2,1)S(1)}, bf16[192,512]{1,0:T(8,128)(2,1)S(1)}, u32[]{:S(2)}, u32[]{:S(2)}) collective-permute-start(bf16[192,512]{1,0:T(8,128)(2,1)S(1)} %get-tuple-element.266), channel_id=1, source_target_pairs={{0,6},{1,7},{2,4},{3,5},{4,2},{5,3},{6,0},{7,1},{8,14},{9,15},{10,... | collective-permute-start | bytes 589832 | tf_op jit(solution)/shard_map/ppermute | solution.py:44
  316.0 11.5 %collective-permute-start.29 = (bf16[2,320,512]{2,1,0:T(8,128)(2,1)S(1)}, bf16[2,320,512]{2,1,0:T(8,128)(2,1)S(1)}, u32[]{:S(2)}, u32[]{:S(2)}) collective-permute-start(bf16[2,320,512]{2,1,0:T(8,128)(2,1)S(1)} %get-tuple-element.270.refs_2_), channel_id=1, source_target_pairs={{0,8},{8,0},{16,24},{24,16},{1,9},{9,1},{17,25},{25,17},{2,10},{10... | collective-permute-start | bytes 1966088 | tf_op jit(solution)/shard_map/ppermute | solution.py:44
  (88 other events, 750.9 us)
Sparse Core Ops, SparseCore 0:
  16.3 79.5 all-gather.3
